TPU v7x, 256 devices: a whole 4x4x8 slice. The times are simulated.
256 devices in a mesh: rows: 16 (over z, core), feat: 16 (over y, x).
Axes of the slice: x: 4, y: 4, z: 8, core: 2. Of those that a mesh axis runs over, the one named last changes fastest.
Arguments:
- features: bfloat16 [4096, 2048], P('rows', 'feat'), may hold values from -6 to 6
- w_self: bfloat16 [2048, 2048], P(None, 'feat'), may hold values from -0.125 to 0.125
- w_neigh: bfloat16 [2048, 2048], P(None, 'feat'), may hold values from -0.25 to 0.25
- out_grad: bfloat16 [4096, 2048], P('rows', 'feat'), may hold values from -6 to 6
- tile_count: int32 [16], P('rows'), may hold values from 0 to 80, as said below
- tile_dst: int32 [16, 80], P('rows'), may hold values from 0 to 1
- tile_src: int32 [16, 80], P('rows'), may hold values from 0 to 31, as said below
- tile_weight: int32 [16, 80, 128, 128], P('rows'), may hold values from 0 to 3
Outputs:
- output: bfloat16 [4096, 2048], P('rows', 'feat')
- grad_features: bfloat16 [4096, 2048], P('rows', 'feat')
- grad_self: float32 [2048, 2048], P('rows', 'feat')
- grad_neigh: float32 [2048, 2048], P('rows', 'feat')
Inputs may be any that keep to these rules, and one draw needn't show every extreme that they name: Row group g uses the first tile_count[g] slots of its lists; the others are ignored. One row group has exactly 80 in every draw. `tile_src`: A destination and source pair may repeat; repeated tiles add. Over all its slots, row group g names at most one distinct source tile among the 2 tiles of any one row group, and in every draw some row group names exactly 1 of one row group's tiles within its used slots.
All inputs are finite; a program needn't handle non-finite values.
Results may differ from a plain program's by a relative error of at most 0.005.
Values may be sent and summed in bfloat16 or wider, within the bound.
No kernel may reach another device: no remote copies, remote signals or barrier semaphores. Data moves between devices by JAX's collectives and lax.ppermute only.
A program may use at most 64 MiB of HBM per device.

v0:
```python
import jax
import jax.numpy as jnp
from jax import lax
from jax.sharding import PartitionSpec as P


def per_device(features, w_self, w_neigh, out_grad, tile_count, tile_dst, tile_src, tile_weight):
    rows_dev = features.shape[0]
    width_dev = features.shape[1]
    tile_size = tile_weight.shape[2]
    used_tiles = tile_count[0]
    dst_tiles = tile_dst[0]
    src_tiles = tile_src[0]
    weights = tile_weight[0]
    contract_rows = (((0,), (0,)), ((), ()))
    all_rows = lax.all_gather(features, "rows", axis=0, tiled=True)
    source_start = src_tiles * tile_size
    back_rows = all_rows.shape[0]

    def gather_step(index, state):
        total, degree = state
        tile_w = weights[index]
        dst_row = dst_tiles[index] * tile_size
        source_rows = lax.dynamic_slice_in_dim(all_rows, source_start[index], tile_size, 0)
        product = jnp.dot(
            tile_w.astype(jnp.bfloat16), source_rows, preferred_element_type=jnp.float32
        )
        current = lax.dynamic_slice_in_dim(total, dst_row, tile_size, 0)
        total = lax.dynamic_update_slice_in_dim(total, current + product, dst_row, 0)
        row_sums = jnp.sum(tile_w, axis=1).astype(jnp.float32)
        current_degree = lax.dynamic_slice_in_dim(degree, dst_row, tile_size, 0)
        degree = lax.dynamic_update_slice_in_dim(degree, current_degree + row_sums, dst_row, 0)
        return (total, degree)

    start_state = (
        jnp.zeros((rows_dev, width_dev), jnp.float32),
        jnp.zeros((rows_dev,), jnp.float32),
    )
    summed, degree = lax.fori_loop(0, used_tiles, gather_step, start_state)
    inverse = 1.0 / jnp.maximum(degree, jnp.float32(1.0))
    aggregated = (summed * inverse[:, None]).astype(jnp.bfloat16)
    whole_features, whole_aggregated = (
        lax.all_gather(features, "feat", axis=1, tiled=True),
        lax.all_gather(aggregated, "feat", axis=1, tiled=True),
    )
    preact = jnp.dot(whole_features, w_self, preferred_element_type=jnp.float32) + jnp.dot(
        whole_aggregated, w_neigh, preferred_element_type=jnp.float32
    )
    sigmoid_pre = jax.nn.sigmoid(preact)
    output = (preact * sigmoid_pre).astype(jnp.bfloat16)
    preact_grad = (
        out_grad.astype(jnp.float32) * sigmoid_pre * (1.0 + preact * (1.0 - sigmoid_pre))
    ).astype(jnp.bfloat16)
    self_terms = lax.dot_general(
        whole_features, preact_grad, contract_rows, preferred_element_type=jnp.float32
    )
    neigh_terms = lax.dot_general(
        whole_aggregated, preact_grad, contract_rows, preferred_element_type=jnp.float32
    )
    grad_self, grad_neigh = (
        lax.psum_scatter(self_terms, "rows", scatter_dimension=0, tiled=True),
        lax.psum_scatter(neigh_terms, "rows", scatter_dimension=0, tiled=True),
    )
    contract_cols = (((1,), (1,)), ((), ()))
    self_part = lax.dot_general(
        w_self, preact_grad, contract_cols, preferred_element_type=jnp.float32
    )
    neigh_part = lax.dot_general(
        w_neigh, preact_grad, contract_cols, preferred_element_type=jnp.float32
    )
    reduced = lax.psum_scatter(
        jnp.concatenate([self_part, neigh_part], axis=1), "feat", scatter_dimension=0, tiled=True
    )
    direct_grad = reduced[:, :rows_dev].T
    aggregated_grad = reduced[:, rows_dev:].T
    scaled_grad = (aggregated_grad * inverse[:, None]).astype(jnp.bfloat16)

    def adjoint_step(index, total):
        tile_w = weights[index]
        dst_row = dst_tiles[index] * tile_size
        source_rows = lax.dynamic_slice_in_dim(scaled_grad, dst_row, tile_size, 0)
        product = lax.dot_general(
            tile_w.astype(jnp.bfloat16),
            source_rows,
            contract_rows,
            preferred_element_type=jnp.float32,
        )
        current = lax.dynamic_slice_in_dim(total, source_start[index], tile_size, 0)
        return lax.dynamic_update_slice_in_dim(total, current + product, source_start[index], 0)

    transported = lax.fori_loop(
        0, used_tiles, adjoint_step, jnp.zeros((back_rows, width_dev), jnp.float32)
    )
    spread = lax.psum_scatter(transported, "rows", scatter_dimension=0, tiled=True)
    grad_features = (direct_grad + spread).astype(jnp.bfloat16)
    return (output, grad_features, grad_self, grad_neigh)


def solution(mesh):
    placed = (
        P("rows", "feat"),
        P(None, "feat"),
        P(None, "feat"),
        P("rows", "feat"),
        P("rows"),
        P("rows", None),
        P("rows", None),
        P("rows", None, None, None),
    )
    return jax.shard_map(
        per_device,
        mesh=mesh,
        in_specs=placed,
        out_specs=(P("rows", "feat"), P("rows", "feat"), P("rows", "feat"), P("rows", "feat")),
        check_vma=False,
    )
```

profile of v0, /device:TPU:1, one launch (start us, length us, event | category | flops | bytes accessed | tf_op | source)
XLA Modules:
  0.0 1368.2 jit_solution(16796646104263723871)
XLA Ops:
  9.4 43.3 %all-gather.6.cloned.1.call-done = bf16[4096,128]{1,0:T(8,128)(2,1)} async-done(((bf16[256,128]{1,0:T(8,128)(2,1)}), bf16[4096,128]{1,0:T(8,128)(2,1)}) %all-gather.6.cloned.1.call-update) | async-done | bytes 1048592 | tf_op jit(solution)/shard_map/all_gather | solution.py:16
  52.7 180.8 %while.22 = (s32[]{:T(128)}, f32[256,128]{1,0:T(8,128)S(1)}, f32[256]{0:T(256)S(1)}, s32[]{:T(128)}, s32[80]{0:T(128)}, /*index=5*/s32[80,128,128]{2,1,0:T(8,128...) while((s32[]{:T(128)}, f32[256,128]{1,0:T(8,128)S(1)}, ...), condition=%wide.region_2.0_spmd, body=%wide.region_0.0_spmd.sunk | while | flops 4243596 | bytes 297259 | solution.py:39
  53.4 1.2 dynamic_slice.67
  60.6 1.2 dynamic_slice.67
  67.8 1.2 dynamic_slice.67
  75.0 1.2 dynamic_slice.67
  82.2 1.2 dynamic_slice.67
  89.4 1.2 dynamic_slice.67
  96.6 1.2 dynamic_slice.67
  103.8 1.2 dynamic_slice.67
  111.0 1.2 dynamic_slice.67
  118.2 1.2 dynamic_slice.67
  125.5 1.2 dynamic_slice.67
  132.7 1.2 dynamic_slice.67
  147.1 1.2 dynamic_slice.67
  154.3 1.2 dynamic_slice.67
  161.5 1.2 dynamic_slice.67
  219.1 1.2 dynamic_slice.67
  226.3 1.2 dynamic_slice.67
  234.4 1.6 fusion.13
  236.0 438.0 %all-gather.8.cloned.1.call-done = bf16[256,2048]{1,0:T(8,128)(2,1)} async-done(((bf16[256,128]{1,0:T(8,128)(2,1)}), bf16[256,2048]{1,0:T(8,128)(2,1)}) %all-gather.8.cloned.1.call-update) | async-done | bytes 1048592 | tf_op jit(solution)/shard_map/all_gather | solution.py:44
  674.0 2.3 multiply_convert_fusion
  677.2 2.5 pad_maximum_fusion
  680.9 1.3 convolution_bitcast_fusion.2
  682.3 79.3 %reduce-scatter.5.cloned.1.call-done = f32[128,512]{0,1:T(8,128)} async-done(((f32[2048,512]{0,1:T(8,128)}), f32[128,512]{0,1:T(8,128)}) %reduce-scatter.5.cloned.1.call-update) | async-done | bytes 262160 | tf_op jit(solution)/shard_map/reduce_scatter | solution.py:71
  762.8 151.7 %while.23 = (s32[]{:T(128)}, f32[4096,128]{1,0:T(8,128)S(1)}, s32[]{:T(128)}, s32[80]{0:T(128)S(1)}, s32[80,128,128]{2,1,0:T(8,128)}, /*index=5*/s32[80]{0:T(128...) while((s32[]{:T(128)}, f32[4096,128]{1,0:T(8,128)S(1)}, ...), condition=%wide.region_5.0_spmd, body=%wide.region_4.0_spmd.sunk | while | flops 4227084 | bytes 360735 | solution.py:91
  914.5 1.3 copy-done.1
  915.9 2.7 fusion.14
  918.7 1.6 copy.12
  920.3 382.0 %reduce-scatter.7.cloned.1.call-done = f32[256,128]{1,0:T(8,128)} async-done(((f32[4096,128]{1,0:T(8,128)}), f32[256,128]{1,0:T(8,128)}) %reduce-scatter.7.cloned.1.call-update) | async-done | bytes 131088 | tf_op jit(solution)/shard_map/reduce_scatter | solution.py:94
  1302.3 1.5 fusion.11
  1303.8 57.5 %reduce-scatter.11.cloned.1.call-done = f32[128,128]{1,0:T(8,128)} async-done(((f32[2048,128]{1,0:T(8,128)}), f32[128,128]{1,0:T(8,128)}) %reduce-scatter.11.cloned.1.call-update) | async-done | bytes 65552 | tf_op jit(solution)/shard_map/reduce_scatter | solution.py:62
  (246 shorter events, 152.6 us)
Async XLA Ops:
  7.2 666.9 %copy-start = (bf16[2048,128]{1,0:T(8,128)(2,1)S(1)}, bf16[2048,128]{1,0:T(8,128)(2,1)}, u32[]{:S(2)}) copy-start(bf16[2048,128]{1,0:T(8,128)(2,1)} %param.14) | copy-start | bytes 1572868
  7.2 227.2 %copy-start.3 = (bf16[2048,128]{1,0:T(8,128)(2,1)S(1)}, bf16[2048,128]{1,0:T(8,128)(2,1)}, u32[]{:S(2)}) copy-start(bf16[2048,128]{1,0:T(8,128)(2,1)} %param.13) | copy-start | bytes 1572868
  7.2 666.8 %copy-start.5 = (bf16[256,128]{1,0:T(8,128)(2,1)S(1)}, bf16[256,128]{1,0:T(8,128)(2,1)}, u32[]{:S(2)}) copy-start(bf16[256,128]{1,0:T(8,128)(2,1)} %param.15) | copy-start | bytes 196612
  7.2 45.5 %all-gather.6.cloned.1.call-start = ((), (), s32[]{:S(2)}) async-start(), calls=%async_computation.5 | async-start | bytes 1114112 | tf_op jit(solution)/shard_map/all_gather | solution.py:16
  7.9 226.4 %all-gather.4.cloned.1.call-start = ((), (), s32[]{:S(2)}) async-start(), calls=%async_computation.4 | async-start | bytes 1114112 | tf_op jit(solution)/shard_map/all_gather | solution.py:43
  8.7 665.3 %all-gather.8.cloned.1.call-start = ((), (), s32[]{:S(2)}) async-start(), calls=%async_computation.6 | async-start | bytes 1114112 | tf_op jit(solution)/shard_map/all_gather | solution.py:44
  234.3 527.3 %reduce-scatter.5.cloned.1.call-start = ((), (), s32[]{:S(2)}) async-start(), calls=%async_computation.7 | async-start | bytes 4456448 | tf_op jit(solution)/shard_map/reduce_scatter | solution.py:71
  679.7 1.2 copy-start.2
  679.7 239.0 %reduce-scatter.9.cloned.1.call-start = ((), (), s32[]{:S(2)}) async-start(), calls=%async_computation.9 | async-start | bytes 1114112 | tf_op jit(solution)/shard_map/reduce_scatter | solution.py:61
  682.2 80.5 %copy-start.6 = (s32[80]{0:T(128)S(1)}, s32[80]{0:T(128)}, u32[]{:S(2)}) copy-start(s32[80]{0:T(128)} %get-tuple-element.329) | copy-start | bytes 964
  682.3 620.0 %reduce-scatter.7.cloned.1.call-start = ((), (), s32[]{:S(2)}) async-start(), calls=%async_computation.8 | async-start | bytes 2228224 | tf_op jit(solution)/shard_map/reduce_scatter | solution.py:94
  914.5 1.3 copy-start.1
  915.9 386.4 %copy-start.4 = (f32[128,512]{0,1:T(8,128)S(1)}, f32[128,512]{0,1:T(8,128)}, u32[]{:S(2)}) copy-start(f32[128,512]{0,1:T(8,128)} %reduce-scatter.5.cloned.1.call-done) | copy-start | bytes 786436
  915.9 445.5 %reduce-scatter.11.cloned.1.call-start = ((), (), s32[]{:S(2)}) async-start(), calls=%async_computation.10 | async-start | bytes 1114112 | tf_op jit(solution)/shard_map/reduce_scatter | solution.py:62
Sparse Core Ops, SparseCore 0:
  9.9 42.7 all-gather.5
  55.1 45.5 all-gather.3
  234.4 439.5 all-gather.7
  679.8 81.7 reduce-scatter.4
  764.1 55.8 reduce-scatter.8
  916.0 386.2 reduce-scatter.6
  1305.4 55.9 reduce-scatter.10
where the time goes:
time: 1390 us; the launch traced here: 1370 us
  waiting for transfers between devices  1000 us (72%)
  loops' own time  165 us (12%)
  local copies, waits for them, and re-layouts  93.3 us (7%)
  matrix products  59.1 us (4%)
  other arithmetic  34.3 us (2%)
  between operations  14.3 us (1%)
    all_gather x1, waiting for transfers between devices, per_device(): lax.all_gather(aggregated, 'feat', axis=1, tiled=True)  438 us
    reduce_scatter x1, waiting for transfers between devices, per_device(): lax.psum_scatter(transported, 'rows', scatter_dimension=0, tiled=True)  382 us
    another operation x1, loops' own time, per_device(): summed, degree = lax.fori_loop(0, used_tiles, gather_step, start_state)  82.7 us
    another operation x1, loops' own time, per_device(): lax.fori_loop(0, used_tiles, adjoint_step, jnp.zeros((back_rows, width_de...  82.5 us
    reduce_scatter x1, waiting for transfers between devices, per_device(): lax.psum_scatter(jnp.concatenate([self_part, neigh_part], axis=1), 'feat'...  79.3 us
    reduce_scatter x1, waiting for transfers between devices, per_device(): lax.psum_scatter(neigh_terms, 'rows', scatter_dimension=0, tiled=True)  57.5 us
    all_gather x1, waiting for transfers between devices, per_device(): all_rows = lax.all_gather(features, 'rows', axis=0, tiled=True)  43.3 us
    dynamic_slice x25, local copies, waits for them, and re-layouts, gather_step(): dst_row = dst_tiles[index] * tile_size  31.1 us
  transfers between devices with their start and end apart: 7, of which 5 were waited for; matrix products, arithmetic and copies ran while one was open for 13% of the time, Pallas kernels for 0%

commit v1 on v0

v1 whole, which is shorter than its diff:
```python
import functools

import jax
import jax.numpy as jnp
from jax import lax
from jax.experimental import pallas as pl
from jax.experimental.pallas import tpu as pltpu
from jax.sharding import Mesh, PartitionSpec as P

F32 = jnp.float32
BF16 = jnp.bfloat16
T = 128
CHUNK = 10
LIMIT = 48 * 1024 * 1024
VMEM = pl.BlockSpec(memory_space=pltpu.VMEM)
SMEM = pl.BlockSpec(memory_space=pltpu.SMEM)
HBM = pl.BlockSpec(memory_space=pl.ANY)
PARAMS = pltpu.CompilerParams(vmem_limit_bytes=LIMIT)


def dot(a, b):
    return jnp.dot(a, b, preferred_element_type=F32)


def adjacency_kernel(count_ref, dst_ref, src_ref, weight_ref, adj_ref, inv_ref, flag_ref, sel_ref, buf, acc, sems):
    count = count_ref[0]
    slots = weight_ref.shape[0]
    groups = acc.shape[0]

    def chunk_copy(index):
        part = pl.ds(index * CHUNK, CHUNK)
        return pltpu.make_async_copy(weight_ref.at[part], buf.at[part], sems.at[index])

    for index in range(slots // CHUNK):

        @pl.when(index * CHUNK < count)
        def _():
            chunk_copy(index).start()

    acc[...] = jnp.zeros_like(acc)
    for owner in range(groups):
        sel_ref[owner] = 0
    for index in range(slots // CHUNK):

        @pl.when(index * CHUNK < count)
        def _():
            chunk_copy(index).wait()

            def add_tile(slot, carry):
                source = src_ref[slot]
                owner = source // 2
                sel_ref[owner] = source - 2 * owner
                rows = pl.ds(pl.multiple_of(dst_ref[slot] * T, T), T)
                acc[owner, rows, :] = acc[owner, rows, :] + buf[slot]
                return carry

            lax.fori_loop(index * CHUNK, jnp.minimum(count, (index + 1) * CHUNK), add_tile, 0)

    total = acc[0]
    for owner in range(groups):
        if owner > 0:
            total = total + acc[owner]
        adj_ref[:, owner * T : (owner + 1) * T] = acc[owner].astype(F32).astype(BF16)
    degree = jnp.sum(total.astype(F32), axis=1, keepdims=True)
    inv_ref[...] = jnp.broadcast_to(1.0 / jnp.maximum(degree, 1.0), inv_ref.shape)
    row = lax.broadcasted_iota(jnp.int32, flag_ref.shape, 0)
    flags = jnp.zeros(flag_ref.shape, F32)
    for owner in range(groups):
        flags = jnp.where(row == owner, sel_ref[owner].astype(F32), flags)
    flag_ref[...] = flags.astype(BF16)


def neighbour_product_kernel(x_ref, w_ref, flag_ref, pay_ref):
    parts = x_ref.shape[0]
    rows = x_ref.shape[1]
    total = dot(x_ref[0], w_ref[0:T, :])
    for part in range(1, parts):
        total = total + dot(x_ref[part], w_ref[part * T : (part + 1) * T, :])
    product = total.astype(BF16)
    flags = flag_ref[...]
    for copy in range(pay_ref.shape[0]):
        pay_ref[copy, 0:rows, :] = product
        pay_ref[copy, rows:, :] = flags


def self_product_kernel(x_ref, w_ref, z_ref):
    parts = x_ref.shape[0]
    total = dot(x_ref[0], w_ref[0:T, :])
    for part in range(1, parts):
        total = total + dot(x_ref[part], w_ref[part * T : (part + 1) * T, :])
    z_ref[...] = total


def activation_kernel(
    place_ref, sel_ref, adj_ref, inv_ref, own_ref, other_ref, z_ref, og_ref,
    out_ref, gt_ref, pay_ref, mask_ref, chosen,
):
    core = place_ref[0]
    me = place_ref[1]
    rows = z_ref.shape[0]
    flag_rows = own_ref.shape[1] - rows
    row = lax.broadcasted_iota(jnp.int32, (flag_rows, T), 0)
    for chip in range(own_ref.shape[0]):
        for ref, owner in ((own_ref, 2 * chip + core), (other_ref, 2 * chip + 1 - core)):
            start = pl.multiple_of(sel_ref[owner] * T, T)
            chosen[pl.ds(pl.multiple_of(owner * T, T), T), :] = ref[chip, pl.ds(start, T), :]
            flags = ref[chip, rows:, :].astype(F32)
            mask_ref[pl.ds(owner, 1), :] = jnp.sum(jnp.where(row == me, flags, 0.0), axis=0, keepdims=True)
    adj = adj_ref[...]
    inverse = inv_ref[...]
    z = z_ref[...] + inverse * dot(adj, chosen[...])
    sig = 1.0 / (1.0 + jnp.exp(-z))
    out_ref[...] = (z * sig).astype(BF16)
    grad = (og_ref[...].astype(F32) * sig * (1.0 + z * (1.0 - sig))).astype(BF16).astype(F32)
    gt_ref[...] = grad.T.astype(BF16)
    scaled = (grad * inverse).T.astype(BF16)
    spread = dot(scaled, adj)
    for owner in range(pay_ref.shape[0]):
        pay_ref[owner] = spread[:, owner * T : (owner + 1) * T].astype(BF16)


def self_grad_kernel(gt_ref, x_ref, part_ref):
    gt = gt_ref[...]
    for part in range(x_ref.shape[0]):
        part_ref[part] = dot(gt, x_ref[part])


def feature_grad_kernel(came_ref, mask_ref, gt_ref, ws_ref, wn_ref, bt_ref, pay_ref):
    low = jnp.zeros((T, T), F32)
    high = jnp.zeros((T, T), F32)
    for sender in range(came_ref.shape[0]):
        came = came_ref[sender].astype(F32)
        is_high = mask_ref[sender : sender + 1, :] > 0.5
        low = low + jnp.where(is_high, 0.0, came)
        high = high + jnp.where(is_high, came, 0.0)
    bt = jnp.concatenate([low, high], axis=1).astype(BF16)
    bt_ref[...] = bt
    gt = gt_ref[...]
    for part in range(pay_ref.shape[0]):
        span = slice(part * T, (part + 1) * T)
        pay_ref[part] = (dot(ws_ref[span, :], gt) + dot(wn_ref[span, :], bt)).astype(BF16)


def neigh_grad_kernel(place_ref, bt_ref, x_ref, keep_ref, send_ref):
    core = place_ref[0]
    bt = bt_ref[...]
    for chip in range(keep_ref.shape[0]):
        keep_ref[chip] = dot(bt, x_ref[2 * chip + core])
        send_ref[chip] = dot(bt, x_ref[2 * chip + 1 - core]).astype(BF16)


def sum_kernel(parts_ref, out_ref):
    total = parts_ref[0].astype(F32)
    for part in range(1, parts_ref.shape[0]):
        total = total + parts_ref[part].astype(F32)
    out_ref[...] = total.T.astype(out_ref.dtype)


def call(kernel, ins, outs, in_specs=None, out_specs=None, scratch=()):
    shapes = tuple(jax.ShapeDtypeStruct(shape, dtype) for shape, dtype in outs)
    return pl.pallas_call(
        kernel,
        out_shape=shapes,
        in_specs=in_specs or [VMEM] * len(ins),
        out_specs=tuple(out_specs or [VMEM] * len(outs)),
        scratch_shapes=list(scratch),
        compiler_params=PARAMS,
        name=kernel.__name__,
    )(*ins)


def per_device(features, w_self, w_neigh, out_grad, tile_count, tile_dst, tile_src, tile_weight, chips, parts):
    rows = features.shape[0]
    groups = 2 * chips
    slots = tile_weight.shape[1]
    core = lax.axis_index("c")
    place = jnp.stack([core, lax.axis_index("z") * 2 + core]).astype(jnp.int32)
    swap = [(0, 1), (1, 0)]

    x_all = lax.all_to_all(
        jnp.broadcast_to(features[None], (parts, rows, T)), ("y", "x"), 0, 0, tiled=True
    )
    adj, inverse, flags, sel = call(
        adjacency_kernel,
        (tile_count, tile_dst[0], tile_src[0], tile_weight[0]),
        [((rows, groups * T), BF16), ((rows, T), F32), ((groups, T), BF16), ((groups,), jnp.int32)],
        in_specs=[SMEM, SMEM, SMEM, HBM],
        out_specs=[VMEM, VMEM, VMEM, SMEM],
        scratch=[
            pltpu.VMEM((slots, T, T), jnp.int32),
            pltpu.VMEM((groups, rows, T), jnp.int32),
            pltpu.SemaphoreType.DMA((slots // CHUNK,)),
        ],
    )
    (y_pay,) = call(
        neighbour_product_kernel, (x_all, w_neigh, flags), [((chips, rows + groups, T), BF16)]
    )
    y_own = lax.all_to_all(y_pay, "z", 0, 0, tiled=True)
    (z_self,) = call(self_product_kernel, (x_all, w_self), [((rows, T), F32)])
    y_other = lax.ppermute(y_own, "c", swap)
    output, gt, c_pay, mask = call(
        activation_kernel,
        (place, sel, adj, inverse, y_own, y_other, z_self, out_grad),
        [((rows, T), BF16), ((T, rows), BF16), ((groups, T, T), BF16), ((groups, T), F32)],
        in_specs=[SMEM, SMEM] + [VMEM] * 6,
        scratch=[pltpu.VMEM((groups * T, T), BF16)],
    )
    c_all = lax.all_to_all(c_pay, ("z", "c"), 0, 0, tiled=True)
    (self_part,) = call(self_grad_kernel, (gt, x_all), [((groups, T, T), F32)])
    grad_self = lax.psum_scatter(self_part, ("z", "c"), scatter_dimension=0, tiled=True)[0].T
    bt, p_pay = call(
        feature_grad_kernel,
        (c_all, mask, gt, w_self, w_neigh),
        [((T, rows), BF16), ((parts, T, rows), BF16)],
    )
    p_all = lax.all_to_all(p_pay, ("y", "x"), 0, 0, tiled=True)
    keep, send = call(
        neigh_grad_kernel,
        (place, bt, x_all),
        [((chips, T, T), F32), ((chips, T, T), BF16)],
        in_specs=[SMEM, VMEM, VMEM],
    )
    came = lax.ppermute(send, "c", swap)
    n_all = lax.all_to_all((keep + came.astype(F32)).astype(BF16), "z", 0, 0, tiled=True)
    (grad_features,) = call(sum_kernel, (p_all,), [((rows, T), BF16)])
    (grad_neigh,) = call(sum_kernel, (n_all,), [((T, T), F32)])
    return output, grad_features, grad_self, grad_neigh


def solution(mesh):
    row_count, part_count = mesh.shape["rows"], mesh.shape["feat"]
    split = Mesh(mesh.devices.reshape(row_count // 2, 2, 4, part_count // 4), ("z", "c", "y", "x"))
    rows, feat = ("z", "c"), ("y", "x")
    return jax.shard_map(
        functools.partial(per_device, chips=row_count // 2, parts=part_count),
        mesh=split,
        in_specs=(
            P(rows, feat),
            P(None, feat),
            P(None, feat),
            P(rows, feat),
            P(rows),
            P(rows, None),
            P(rows, None),
            P(rows, None, None, None),
        ),
        out_specs=(P(rows, feat),) * 4,
        check_vma=False,
    )
```

time: 1390 us -> 139 us (0.10); the launches traced: 1370 us -> 136 us
  waiting for transfers between devices: 1000 us -> 44.3 us
  loops' own time: 165 us -> 0 us
  local copies, waits for them, and re-layouts: 93.3 us -> 8.93 us
  matrix products: 59.1 us -> 0 us
  blocking collectives: 0 us -> 37.1 us
  other arithmetic: 34.3 us -> 0.14 us
  starting transfers between devices: 0.28 us -> 20.9 us
    reduce_scatter x4 -> x1, waiting for transfers between devices: 519 us -> 0.13 us  [per_device(): lax.psum_scatter(self_part, ('z', 'c'), scatter_dimension=0, tiled=True)[0]]
    all_gather x3 -> x0, waiting for transfers between devices: 481 us -> none  [the longest x1 438 us: per_device(): lax.all_gather(aggregated, 'feat', axis=1, tiled=True)]
    another operation x2 -> x0, loops' own time: 165 us -> none  [the longest x1 82.7 us: per_device(): summed, degree = lax.fori_loop(0, used_tiles, gather_step, start_state)]
    dynamic_slice x100 -> x0, local copies, waits for them, and re-layouts: 75.2 us -> none  [the longest x25 31.1 us: gather_step(): dst_row = dst_tiles[index] * tile_size]
    dot_general x56 -> x0, matrix products: 59.1 us -> none  [the longest x25 25.9 us: adjoint_step(): lax.dot_general(tile_w.astype(jnp.bfloat16), source_rows, contract_rows,...]
    all_to_all x0 -> x3, waiting for transfers between devices: none -> 41.5 us  [the longest x1 15.9 us: per_device(): c_all = lax.all_to_all(c_pay, ('z', 'c'), 0, 0, tiled=True)]
    all_to_all x0 -> x2, blocking collectives: none -> 37.1 us  [the longest x1 22.6 us: per_device(): y_own = lax.all_to_all(y_pay, 'z', 0, 0, tiled=True)]
    reduce_sum x25 -> x0, other arithmetic: 23.6 us -> none  [gather_step(): row_sums = jnp.sum(tile_w, axis=1).astype(jnp.float32)]
  transfers between devices with their start and end apart: 7 -> 6, of which waited for: 5 -> 6; matrix products, arithmetic and copies ran while one was open for 13% -> 0% of each run, Pallas kernels for 0% -> 6%
where the time goes in v1:
time: 139 us; the launch traced here: 136 us
  waiting for transfers between devices  44.3 us (32%)
  blocking collectives  37.1 us (27%)
  starting transfers between devices  20.9 us (15%)
  between operations  14.8 us (11%)
  Pallas kernels  10.1 us (7%)
  local copies, waits for them, and re-layouts  8.93 us (6%)
    all_to_all x1, blocking collectives, per_device(): y_own = lax.all_to_all(y_pay, 'z', 0, 0, tiled=True)  22.6 us
    all_to_all x1, waiting for transfers between devices, per_device(): c_all = lax.all_to_all(c_pay, ('z', 'c'), 0, 0, tiled=True)  15.9 us
    all_to_all x1, waiting for transfers between devices, per_device(): p_all = lax.all_to_all(p_pay, ('y', 'x'), 0, 0, tiled=True)  15.4 us
    all_to_all x1, blocking collectives, per_device(): lax.all_to_all((keep + came.astype(F32)).astype(BF16), 'z', 0, 0, tiled=T...  14.5 us
    all_to_all x1, waiting for transfers between devices, per_device(): lax.all_to_all(jnp.broadcast_to(features[None], (parts, rows, T)), ('y',...  10.2 us
    pallas_call x9, Pallas kernels, call(): pl.pallas_call(kernel, out_shape=shapes, in_specs=in_specs or [VMEM] * le...  10.1 us
    all_to_all x1, starting transfers between devices, per_device(): lax.all_to_all(jnp.broadcast_to(features[None], (parts, rows, T)), ('y',...  7.72 us
    unnamed x19, local copies, waits for them, and re-layouts  6.86 us
  transfers between devices with their start and end apart: 6, of which 6 were waited for; matrix products, arithmetic and copies ran while one was open for 0% of the time, Pallas kernels for 6%

profile of v1, /device:TPU:1, one launch (start us, length us, event | category | flops | bytes accessed | tf_op | source)
XLA Modules:
  0.0 136.4 jit_solution(15344212715882634997)
XLA Ops:
  7.2 2.1 %broadcast_in_dim.2 = bf16[16,256,128]{2,1,0:T(8,128)(2,1)} broadcast(bf16[256,128]{1,0:T(8,128)(2,1)} %param.8), dimensions={1,2} | broadcast | bytes 1114112 | tf_op jit(solution)/shard_map/broadcast_in_dim | solution.py:181
  9.3 7.7 %all-to-all-start = ((bf16[16,256,128]{2,1,0:T(8,128)(2,1)}), bf16[16,256,128]{2,1,0:T(8,128)(2,1)S(1)}, u32[]{:S(2)}, u32[]{:S(2)}) async-start(bf16[16,256,128]{2,1,0:T(8,128)(2,1)} %broadcast_in_dim.2), calls=%async_computation | async-start | bytes 2097152 | tf_op jit(solution)/shard_map/all_to_all | solution.py:180
  17.7 0.6 copy-done.7
  18.3 0.7 copy-done.8
  19.0 2.8 %adjacency_kernel.1 = (bf16[256,2048]{1,0:T(8,128)(2,1)S(1)}, f32[256,128]{1,0:T(8,128)S(1)}, bf16[16,128]{1,0:T(8,128)(2,1)S(1)}, s32[16]{0:T(128)S(1)}) custom-call(s32[1]{0:T(128)S(6)} %copy.13.count_ref, s32[80]{0:T(128)S(1)} %bitcast.8, s32[80]{0:T(128)S(1)} %bitcast.9, s32[80,128,128]{2,1,0:T(8,128)} %bitcast.10), custom_call_target="tpu_custom_call" | custom-call | tf_op jit(solution)/shard_map/adjacency_kernel/pallas_call | solution.py:161
  21.8 1.0 copy-done.2
  22.8 10.2 %all-to-all-done.x_ref = bf16[16,256,128]{2,1,0:T(8,128)(2,1)S(1)} async-done(((bf16[16,256,128]{2,1,0:T(8,128)(2,1)}), bf16[16,256,128]{2,1,0:T(8,128)(2,1)S(1)}, u32[]{:S(2)}, u32[]{:S(2)}) %all-to-all-start) | async-done | bytes 1048608 | tf_op jit(solution)/shard_map/all_to_all | solution.py:180
  33.0 0.4 neighbour_product_kernel.1
  33.4 22.6 %all_to_all.25.own_ref = bf16[8,272,128]{2,1,0:T(8,128)(2,1)S(1)} all-to-all(bf16[8,272,128]{2,1,0:T(8,128)(2,1)S(1)} %neighbour_product_kernel.1), channel_id=1, replica_groups=mesh['z'=8,'c'=2,'y'=4,'x'=4] {'z'}, dimensions={0} | all-to-all | bytes 1114112 | tf_op jit(solution)/shard_map/all_to_all | solution.py:198
  56.0 4.5 %collective-permute-start = (bf16[8,272,128]{2,1,0:T(8,128)(2,1)S(1)}, bf16[8,272,128]{2,1,0:T(8,128)(2,1)S(1)}, u32[]{:S(2)}, u32[]{:S(2)}) collective-permute-start(bf16[8,272,128]{2,1,0:T(8,128)(2,1)S(1)} %all_to_all.25.own_ref), channel_id=1, source_target_pairs={{0,16},{16,0},{1,17},{17,1},{2,18},{18,2},{3,19},{19,3},{4,20},{20... | collective-permute-start | bytes 1671176 | tf_op jit(solution)/shard_map/ppermute | solution.py:200
  60.5 0.1 pad_add_fusion.place_ref
  60.6 0.4 self_product_kernel.1.z_ref
  61.0 1.1 collective-permute-done.other_ref
  62.1 1.2 copy-done.3
  63.3 1.7 %activation_kernel.1 = (bf16[256,128]{1,0:T(8,128)(2,1)}, bf16[128,256]{1,0:T(8,128)(2,1)S(1)}, bf16[16,128,128]{2,1,0:T(8,128)(2,1)S(1)}, f32[16,128]{1,0:T(8,128)S(1)}) custom-call(s32[2]{0:T(128)S(1)} %pad_add_fusion.place_ref, s32[16]{0:T(128)S(1)} %get-tuple-element.16.sel_ref, bf16[256,2048]{1,0:T(8,128)(2,1)S(1)} %copy-done.3, ...), custom_call_target="tpu_custom_call" | custom-call | tf_op jit(solution)/shard_map/activation_kernel/pallas_call | solution.py:161
  65.0 0.8 copy-done.5
  65.8 3.7 %all-to-all-start.2 = ((bf16[16,128,128]{2,1,0:T(8,128)(2,1)}), bf16[16,128,128]{2,1,0:T(8,128)(2,1)S(1)}, u32[]{:S(2)}, u32[]{:S(2)}) async-start(bf16[16,128,128]{2,1,0:T(8,128)(2,1)} %copy-done.5), calls=%async_computation.2 | async-start | bytes 1048576 | tf_op jit(solution)/shard_map/all_to_all | solution.py:208
  69.6 1.4 %self_grad_kernel.1 = f32[16,128,128]{2,1,0:T(8,128)} custom-call(bf16[128,256]{1,0:T(8,128)(2,1)S(1)} %get-tuple-element.23.gt_ref, bf16[16,256,128]{2,1,0:T(8,128)(2,1)S(1)} %all-to-all-done.x_ref), custom_call_target="tpu_custom_call" | custom-call | tf_op jit(solution)/shard_map/self_grad_kernel/pallas_call | solution.py:161
  71.0 15.9 %all-to-all-done.2.came_ref = bf16[16,128,128]{2,1,0:T(8,128)(2,1)S(1)} async-done(((bf16[16,128,128]{2,1,0:T(8,128)(2,1)}), bf16[16,128,128]{2,1,0:T(8,128)(2,1)S(1)}, u32[]{:S(2)}, u32[]{:S(2)}) %all-to-all-start.2) | async-done | bytes 524320 | tf_op jit(solution)/shard_map/all_to_all | solution.py:208
  86.9 0.9 feature_grad_kernel.1
  87.8 1.0 copy-done.4
  88.8 1.0 neigh_grad_kernel.1
  89.7 0.1 collective-permute-start.1
  89.8 1.5 %collective-permute-done.1 = bf16[8,128,128]{2,1,0:T(8,128)(2,1)S(1)} collective-permute-done((bf16[8,128,128]{2,1,0:T(8,128)(2,1)S(1)}, bf16[8,128,128]{2,1,0:T(8,128)(2,1)S(1)}, u32[]{:S(2)}, u32[]{:S(2)}) %collective-permute-start.1) | collective-permute-done | bytes 262176 | tf_op jit(solution)/shard_map/ppermute | solution.py:223
  91.4 0.1 add_convert_fusion
  91.4 14.5 %all_to_all.26.parts_ref = bf16[8,128,128]{2,1,0:T(8,128)(2,1)S(1)} all-to-all(bf16[8,128,128]{2,1,0:T(8,128)(2,1)S(1)} %add_convert_fusion), channel_id=1, replica_groups=mesh['z'=8,'c'=2,'y'=4,'x'=4] {'z'}, dimensions={0} | all-to-all | bytes 524288 | tf_op jit(solution)/shard_map/all_to_all | solution.py:224
  106.0 4.8 %all-to-all-start.3 = ((bf16[16,128,256]{2,1,0:T(8,128)(2,1)}), bf16[16,128,256]{2,1,0:T(8,128)(2,1)S(1)}, u32[]{:S(2)}, u32[]{:S(2)}) async-start(bf16[16,128,256]{2,1,0:T(8,128)(2,1)} %copy-done.4), calls=%async_computation.3 | async-start | bytes 2097152 | tf_op jit(solution)/shard_map/all_to_all | solution.py:216
  110.8 0.7 sum_kernel.3
  111.5 15.4 %all-to-all-done.3.parts_ref = bf16[16,128,256]{2,1,0:T(8,128)(2,1)S(1)} async-done(((bf16[16,128,256]{2,1,0:T(8,128)(2,1)}), bf16[16,128,256]{2,1,0:T(8,128)(2,1)S(1)}, u32[]{:S(2)}, u32[]{:S(2)}) %all-to-all-start.3) | async-done | bytes 1048608 | tf_op jit(solution)/shard_map/all_to_all | solution.py:216
  127.0 0.8 sum_kernel.2
  127.8 0.1 reduce-scatter.2.cloned.1.call-done
  127.9 1.6 %copy.12 = f32[128,128]{1,0:T(8,128)} copy(f32[128,128]{0,1:T(8,128)} %bitcast.11) | data formatting | bytes 131072
  (14 shorter events, 0.1 us)
Async XLA Ops:
  7.2 25.8 %copy-start.1 = (bf16[2048,128]{1,0:T(8,128)(2,1)S(1)}, bf16[2048,128]{1,0:T(8,128)(2,1)}, u32[]{:S(2)}) copy-start(bf16[2048,128]{1,0:T(8,128)(2,1)} %wn_ref.1) | copy-start | bytes 1572868
  9.2 51.4 %copy-start = (bf16[2048,128]{1,0:T(8,128)(2,1)S(1)}, bf16[2048,128]{1,0:T(8,128)(2,1)}, u32[]{:S(2)}) copy-start(bf16[2048,128]{1,0:T(8,128)(2,1)} %ws_ref.1) | copy-start | bytes 1572868
  9.3 23.7 %all-to-all-start = ((bf16[16,256,128]{2,1,0:T(8,128)(2,1)}), bf16[16,256,128]{2,1,0:T(8,128)(2,1)S(1)}, u32[]{:S(2)}, u32[]{:S(2)}) async-start(bf16[16,256,128]{2,1,0:T(8,128)(2,1)} %broadcast_in_dim.2), calls=%async_computation | async-start | bytes 2097152 | tf_op jit(solution)/shard_map/all_to_all | solution.py:180
  17.0 45.1 %copy-start.6 = (bf16[256,128]{1,0:T(8,128)(2,1)S(1)}, bf16[256,128]{1,0:T(8,128)(2,1)}, u32[]{:S(2)}) copy-start(bf16[256,128]{1,0:T(8,128)(2,1)} %og_ref.1) | copy-start | bytes 196612
  17.7 0.7 copy-start.7
  18.3 0.7 copy-start.8
  21.8 1.0 copy-start.2
  56.0 6.1 %collective-permute-start = (bf16[8,272,128]{2,1,0:T(8,128)(2,1)S(1)}, bf16[8,272,128]{2,1,0:T(8,128)(2,1)S(1)}, u32[]{:S(2)}, u32[]{:S(2)}) collective-permute-start(bf16[8,272,128]{2,1,0:T(8,128)(2,1)S(1)} %all_to_all.25.own_ref), channel_id=1, source_target_pairs={{0,16},{16,0},{1,17},{17,1},{2,18},{18,2},{3,19},{19,3},{4,20},{20... | collective-permute-start | bytes 1671176 | tf_op jit(solution)/shard_map/ppermute | solution.py:200
  62.1 1.2 copy-start.3
  65.0 0.8 copy-start.5
  65.8 21.1 %all-to-all-start.2 = ((bf16[16,128,128]{2,1,0:T(8,128)(2,1)}), bf16[16,128,128]{2,1,0:T(8,128)(2,1)S(1)}, u32[]{:S(2)}, u32[]{:S(2)}) async-start(bf16[16,128,128]{2,1,0:T(8,128)(2,1)} %copy-done.5), calls=%async_computation.2 | async-start | bytes 1048576 | tf_op jit(solution)/shard_map/all_to_all | solution.py:208
  69.5 58.4 %reduce-scatter.2.cloned.1.call-start = ((), (), s32[]{:S(2)}) async-start(), calls=%async_computation.6 | async-start | bytes 1114112 | tf_op jit(solution)/shard_map/reduce_scatter | solution.py:210
  87.8 1.0 copy-start.4
  89.7 1.6 %collective-permute-start.1 = (bf16[8,128,128]{2,1,0:T(8,128)(2,1)S(1)}, bf16[8,128,128]{2,1,0:T(8,128)(2,1)S(1)}, u32[]{:S(2)}, u32[]{:S(2)}) collective-permute-start(bf16[8,128,128]{2,1,0:T(8,128)(2,1)S(1)} %get-tuple-element.27), channel_id=1, source_target_pairs={{0,16},{16,0},{1,17},{17,1},{2,18},{18,2},{3,19},{19,3},{4,20},{20... | collective-permute-start | bytes 786440 | tf_op jit(solution)/shard_map/ppermute | solution.py:223
  106.0 21.0 %all-to-all-start.3 = ((bf16[16,128,256]{2,1,0:T(8,128)(2,1)}), bf16[16,128,256]{2,1,0:T(8,128)(2,1)S(1)}, u32[]{:S(2)}, u32[]{:S(2)}) async-start(bf16[16,128,256]{2,1,0:T(8,128)(2,1)} %copy-done.4), calls=%async_computation.3 | async-start | bytes 2097152 | tf_op jit(solution)/shard_map/all_to_all | solution.py:216
Sparse Core Ops, SparseCore 0:
  72.9 55.0 reduce-scatter.1

commit v2 on v1

--- a/solution.py
+++ b/solution.py
@@ -20,6 +20,11 @@
 
 def dot(a, b):
     return jnp.dot(a, b, preferred_element_type=F32)
+
+
+def halves(block):
+    high = block.astype(BF16)
+    return jnp.concatenate([high, (block - high.astype(F32)).astype(BF16)], axis=0)
 
 
 def adjacency_kernel(count_ref, dst_ref, src_ref, weight_ref, adj_ref, inv_ref, flag_ref, sel_ref, buf, acc, sems):
@@ -68,6 +73,12 @@
     for owner in range(groups):
         flags = jnp.where(row == owner, sel_ref[owner].astype(F32), flags)
     flag_ref[...] = flags.astype(BF16)
+
+
+def spread_kernel(x_ref, pay_ref):
+    block = x_ref[...]
+    for copy in range(pay_ref.shape[0]):
+        pay_ref[copy] = block
 
 
 def neighbour_product_kernel(x_ref, w_ref, flag_ref, pay_ref):
@@ -113,16 +124,10 @@
     out_ref[...] = (z * sig).astype(BF16)
     grad = (og_ref[...].astype(F32) * sig * (1.0 + z * (1.0 - sig))).astype(BF16).astype(F32)
     gt_ref[...] = grad.T.astype(BF16)
-    scaled = (grad * inverse).T.astype(BF16)
-    spread = dot(scaled, adj)
+    spread = dot(halves((grad * inverse).T), adj)
+    spread = spread[0:T] + spread[T:]
     for owner in range(pay_ref.shape[0]):
         pay_ref[owner] = spread[:, owner * T : (owner + 1) * T].astype(BF16)
-
-
-def self_grad_kernel(gt_ref, x_ref, part_ref):
-    gt = gt_ref[...]
-    for part in range(x_ref.shape[0]):
-        part_ref[part] = dot(gt, x_ref[part])
 
 
 def feature_grad_kernel(came_ref, mask_ref, gt_ref, ws_ref, wn_ref, bt_ref, pay_ref):
@@ -133,20 +138,37 @@
         is_high = mask_ref[sender : sender + 1, :] > 0.5
         low = low + jnp.where(is_high, 0.0, came)
         high = high + jnp.where(is_high, came, 0.0)
-    bt = jnp.concatenate([low, high], axis=1).astype(BF16)
-    bt_ref[...] = bt
+    both = halves(jnp.concatenate([low, high], axis=1))
+    bt = both[0:T]
+    bt_ref[...] = both
     gt = gt_ref[...]
     for part in range(pay_ref.shape[0]):
         span = slice(part * T, (part + 1) * T)
         pay_ref[part] = (dot(ws_ref[span, :], gt) + dot(wn_ref[span, :], bt)).astype(BF16)
 
 
-def neigh_grad_kernel(place_ref, bt_ref, x_ref, keep_ref, send_ref):
+def weight_grad_kernel(place_ref, gt_ref, bt_ref, x_ref, keep_ref, send_ref):
     core = place_ref[0]
-    bt = bt_ref[...]
+    left = jnp.concatenate([gt_ref[...], bt_ref[...]], axis=0)
     for chip in range(keep_ref.shape[0]):
-        keep_ref[chip] = dot(bt, x_ref[2 * chip + core])
-        send_ref[chip] = dot(bt, x_ref[2 * chip + 1 - core]).astype(BF16)
+        kept = dot(left, x_ref[2 * chip + core])
+        sent = dot(left, x_ref[2 * chip + 1 - core])
+        keep_ref[chip, 0:T] = kept[0:T]
+        keep_ref[chip, T:] = kept[T : 2 * T] + kept[2 * T :]
+        send_ref[chip, 0:T] = sent[0:T].astype(BF16)
+        send_ref[chip, T:] = (sent[T : 2 * T] + sent[2 * T :]).astype(BF16)
+
+
+def pair_kernel(keep_ref, came_ref, pay_ref):
+    pay_ref[...] = (keep_ref[...] + came_ref[...].astype(F32)).astype(BF16)
+
+
+def weight_sum_kernel(parts_ref, self_ref, neigh_ref):
+    total = parts_ref[0].astype(F32)
+    for part in range(1, parts_ref.shape[0]):
+        total = total + parts_ref[part].astype(F32)
+    self_ref[...] = total[0:T].T
+    neigh_ref[...] = total[T:].T
 
 
 def sum_kernel(parts_ref, out_ref):
@@ -177,9 +199,8 @@
     place = jnp.stack([core, lax.axis_index("z") * 2 + core]).astype(jnp.int32)
     swap = [(0, 1), (1, 0)]
 
-    x_all = lax.all_to_all(
-        jnp.broadcast_to(features[None], (parts, rows, T)), ("y", "x"), 0, 0, tiled=True
-    )
+    (x_pay,) = call(spread_kernel, (features,), [((parts, rows, T), BF16)])
+    x_all = lax.all_to_all(x_pay, ("y", "x"), 0, 0, tiled=True)
     adj, inverse, flags, sel = call(
         adjacency_kernel,
         (tile_count, tile_dst[0], tile_src[0], tile_weight[0]),
@@ -206,24 +227,23 @@
         scratch=[pltpu.VMEM((groups * T, T), BF16)],
     )
     c_all = lax.all_to_all(c_pay, ("z", "c"), 0, 0, tiled=True)
-    (self_part,) = call(self_grad_kernel, (gt, x_all), [((groups, T, T), F32)])
-    grad_self = lax.psum_scatter(self_part, ("z", "c"), scatter_dimension=0, tiled=True)[0].T
     bt, p_pay = call(
         feature_grad_kernel,
         (c_all, mask, gt, w_self, w_neigh),
-        [((T, rows), BF16), ((parts, T, rows), BF16)],
+        [((2 * T, rows), BF16), ((parts, T, rows), BF16)],
     )
     p_all = lax.all_to_all(p_pay, ("y", "x"), 0, 0, tiled=True)
     keep, send = call(
-        neigh_grad_kernel,
-        (place, bt, x_all),
-        [((chips, T, T), F32), ((chips, T, T), BF16)],
-        in_specs=[SMEM, VMEM, VMEM],
+        weight_grad_kernel,
+        (place, gt, bt, x_all),
+        [((chips, 2 * T, T), F32), ((chips, 2 * T, T), BF16)],
+        in_specs=[SMEM, VMEM, VMEM, VMEM],
     )
     came = lax.ppermute(send, "c", swap)
-    n_all = lax.all_to_all((keep + came.astype(F32)).astype(BF16), "z", 0, 0, tiled=True)
+    (w_pay,) = call(pair_kernel, (keep, came), [((chips, 2 * T, T), BF16)])
+    w_all = lax.all_to_all(w_pay, "z", 0, 0, tiled=True)
     (grad_features,) = call(sum_kernel, (p_all,), [((rows, T), BF16)])
-    (grad_neigh,) = call(sum_kernel, (n_all,), [((T, T), F32)])
+    grad_self, grad_neigh = call(weight_sum_kernel, (w_all,), [((T, T), F32)] * 2)
     return output, grad_features, grad_self, grad_neigh
 
 

time: 139 us -> 126 us (0.906); the launches traced: 136 us -> 126 us
  between operations: 14.8 us -> 1.44 us
  blocking collectives: 37.1 us -> 42.7 us
  local copies, waits for them, and re-layouts: 8.93 us -> 5.39 us
    all_to_all x1, blocking collectives: 14.5 us -> 20.1 us  [per_device(): c_all = lax.all_to_all(c_pay, ('z', 'c'), 0, 0, tiled=True)]
    broadcast_in_dim x1 -> x0, local copies, waits for them, and re-layouts: 2.08 us -> none  [per_device(): jnp.broadcast_to(features[None], (parts, rows, T))]
    unnamed x19 -> x18, local copies, waits for them, and re-layouts: 6.86 us -> 5.39 us
    pallas_call x9 -> x10, Pallas kernels: 10.1 us -> 11.3 us  [call(): pl.pallas_call(kernel, out_shape=shapes, in_specs=in_specs or [VMEM] * le...]
  transfers between devices with their start and end apart: 6 -> 5, of which waited for: 6 -> 5; matrix products, arithmetic and copies ran while one was open for 0% -> 0% of each run, Pallas kernels for 6% -> 5%
where the time goes in v2:
time: 126 us
  waiting for transfers between devices  44.8 us (36%)
  blocking collectives  42.7 us (34%)
  starting transfers between devices  20 us (16%)
  Pallas kernels  11.3 us (9%)
  local copies, waits for them, and re-layouts  5.39 us (4%)
  between operations  1.44 us (1%)
    all_to_all x1, blocking collectives, per_device(): y_own = lax.all_to_all(y_pay, 'z', 0, 0, tiled=True)  22.6 us
    all_to_all x1, blocking collectives, per_device(): c_all = lax.all_to_all(c_pay, ('z', 'c'), 0, 0, tiled=True)  20.1 us
    all_to_all x1, waiting for transfers between devices, per_device(): w_all = lax.all_to_all(w_pay, 'z', 0, 0, tiled=True)  17.1 us
    all_to_all x1, waiting for transfers between devices, per_device(): p_all = lax.all_to_all(p_pay, ('y', 'x'), 0, 0, tiled=True)  14.4 us
    pallas_call x10, Pallas kernels, call(): pl.pallas_call(kernel, out_shape=shapes, in_specs=in_specs or [VMEM] * le...  11.3 us
    all_to_all x1, waiting for transfers between devices, per_device(): x_all = lax.all_to_all(x_pay, ('y', 'x'), 0, 0, tiled=True)  10.3 us
    all_to_all x1, starting transfers between devices, per_device(): x_all = lax.all_to_all(x_pay, ('y', 'x'), 0, 0, tiled=True)  7.72 us
    unnamed x18, local copies, waits for them, and re-layouts  5.39 us
  transfers between devices with their start and end apart: 5, of which 5 were waited for; matrix products, arithmetic and copies ran while one was open for 0% of the time, Pallas kernels for 5%

profile of v2, /device:TPU:1, one launch (start us, length us, event | category | flops | bytes accessed | tf_op | source)
XLA Modules:
  0.0 125.7 jit_solution(10052856817708686713)
XLA Ops:
  0.6 0.0 copy-start.1
  0.7 0.9 copy-done.5
  1.5 1.2 spread_kernel.1
  2.7 7.7 %all-to-all-start = ((bf16[16,256,128]{2,1,0:T(8,128)(2,1)}), bf16[16,256,128]{2,1,0:T(8,128)(2,1)S(1)}, u32[]{:S(2)}, u32[]{:S(2)}) async-start(bf16[16,256,128]{2,1,0:T(8,128)(2,1)} %spread_kernel.1), calls=%async_computation | async-start | bytes 2097152 | tf_op jit(solution)/shard_map/all_to_all | solution.py:203
  10.4 0.0 copy-start.6
  11.1 0.0 copy-start.7
  11.1 0.6 copy-done.7
  11.8 0.7 copy-done.8
  12.4 2.6 %adjacency_kernel.1 = (bf16[256,2048]{1,0:T(8,128)(2,1)S(1)}, f32[256,128]{1,0:T(8,128)S(1)}, bf16[16,128]{1,0:T(8,128)(2,1)S(1)}, s32[16]{0:T(128)S(1)}) custom-call(s32[1]{0:T(128)S(6)} %copy.12.count_ref, s32[80]{0:T(128)S(1)} %bitcast.5, s32[80]{0:T(128)S(1)} %bitcast.6, s32[80,128,128]{2,1,0:T(8,128)} %bitcast.7), custom_call_target="tpu_custom_call" | custom-call | tf_op jit(solution)/shard_map/adjacency_kernel/pallas_call | solution.py:183
  15.1 1.0 copy-done.2
  16.1 10.3 %all-to-all-done.x_ref = bf16[16,256,128]{2,1,0:T(8,128)(2,1)S(1)} async-done(((bf16[16,256,128]{2,1,0:T(8,128)(2,1)}), bf16[16,256,128]{2,1,0:T(8,128)(2,1)S(1)}, u32[]{:S(2)}, u32[]{:S(2)}) %all-to-all-start) | async-done | bytes 1048608 | tf_op jit(solution)/shard_map/all_to_all | solution.py:203
  26.4 0.4 neighbour_product_kernel.1
  26.9 22.6 %all_to_all.25.own_ref = bf16[8,272,128]{2,1,0:T(8,128)(2,1)S(1)} all-to-all(bf16[8,272,128]{2,1,0:T(8,128)(2,1)S(1)} %neighbour_product_kernel.1), channel_id=1, replica_groups=mesh['z'=8,'c'=2,'y'=4,'x'=4] {'z'}, dimensions={0} | all-to-all | bytes 1114112 | tf_op jit(solution)/shard_map/all_to_all | solution.py:219
  49.5 4.5 %collective-permute-start = (bf16[8,272,128]{2,1,0:T(8,128)(2,1)S(1)}, bf16[8,272,128]{2,1,0:T(8,128)(2,1)S(1)}, u32[]{:S(2)}, u32[]{:S(2)}) collective-permute-start(bf16[8,272,128]{2,1,0:T(8,128)(2,1)S(1)} %all_to_all.25.own_ref), channel_id=1, source_target_pairs={{0,16},{16,0},{1,17},{17,1},{2,18},{18,2},{3,19},{19,3},{4,20},{20... | collective-permute-start | bytes 1671176 | tf_op jit(solution)/shard_map/ppermute | solution.py:221
  54.0 0.1 pad_add_fusion.place_ref
  54.1 0.4 self_product_kernel.1.z_ref
  54.5 1.1 collective-permute-done.other_ref
  55.6 1.2 copy-done.3
  56.8 1.7 %activation_kernel.1 = (bf16[256,128]{1,0:T(8,128)(2,1)}, bf16[128,256]{1,0:T(8,128)(2,1)S(1)}, bf16[16,128,128]{2,1,0:T(8,128)(2,1)S(1)}, f32[16,128]{1,0:T(8,128)S(1)}) custom-call(s32[2]{0:T(128)S(1)} %pad_add_fusion.place_ref, s32[16]{0:T(128)S(1)} %get-tuple-element.18.sel_ref, bf16[256,2048]{1,0:T(8,128)(2,1)S(1)} %copy-done.3, ...), custom_call_target="tpu_custom_call" | custom-call | tf_op jit(solution)/shard_map/activation_kernel/pallas_call | solution.py:183
  58.5 20.1 %all_to_all.26.came_ref = bf16[16,128,128]{2,1,0:T(8,128)(2,1)S(1)} all-to-all(bf16[16,128,128]{2,1,0:T(8,128)(2,1)S(1)} %get-tuple-element.23), channel_id=1, replica_groups=mesh['z'=8,'c'=2,'y'=4,'x'=4] {'z','c'}, dimensions={0} | all-to-all | bytes 1048576 | tf_op jit(solution)/shard_map/all_to_all | solution.py:229
  78.6 0.9 feature_grad_kernel.1
  79.5 1.0 copy-done.4
  80.5 4.2 %all-to-all-start.3 = ((bf16[16,128,256]{2,1,0:T(8,128)(2,1)}), bf16[16,128,256]{2,1,0:T(8,128)(2,1)S(1)}, u32[]{:S(2)}, u32[]{:S(2)}) async-start(bf16[16,128,256]{2,1,0:T(8,128)(2,1)} %copy-done.4), calls=%async_computation.3 | async-start | bytes 2097152 | tf_op jit(solution)/shard_map/all_to_all | solution.py:235
  84.7 1.5 %weight_grad_kernel.1 = (f32[8,256,128]{2,1,0:T(8,128)S(1)}, bf16[8,256,128]{2,1,0:T(8,128)(2,1)S(1)}) custom-call(s32[2]{0:T(128)S(1)} %pad_add_fusion.place_ref, bf16[128,256]{1,0:T(8,128)(2,1)S(1)} %get-tuple-element.25.gt_ref, bf16[256,256]{1,0:T(8,128)(2,1)S(1)} %get-tuple-element.27.bt_ref, bf16[16,256,128]{2,1,0:T(8,128)(2,1)S(1)} %all-to-all-done.x_ref), custom_call_target="tpu_custom_call" | custom-call | tf_op jit(solution)/shard_map/weight_grad_kernel/pallas_call | solution.py:183
  86.3 0.1 collective-permute-start.1
  86.4 1.9 %collective-permute-done.1.came_ref = bf16[8,256,128]{2,1,0:T(8,128)(2,1)S(1)} collective-permute-done((bf16[8,256,128]{2,1,0:T(8,128)(2,1)S(1)}, bf16[8,256,128]{2,1,0:T(8,128)(2,1)S(1)}, u32[]{:S(2)}, u32[]{:S(2)}) %collective-permute-start.1) | collective-permute-done | bytes 524320 | tf_op jit(solution)/shard_map/ppermute | solution.py:242
  88.3 0.9 pair_kernel.1
  89.1 14.4 %all-to-all-done.3.parts_ref = bf16[16,128,256]{2,1,0:T(8,128)(2,1)S(1)} async-done(((bf16[16,128,256]{2,1,0:T(8,128)(2,1)}), bf16[16,128,256]{2,1,0:T(8,128)(2,1)S(1)}, u32[]{:S(2)}, u32[]{:S(2)}) %all-to-all-start.3) | async-done | bytes 1048608 | tf_op jit(solution)/shard_map/all_to_all | solution.py:235
  103.5 3.5 %all-to-all-start.4 = ((bf16[8,256,128]{2,1,0:T(8,128)(2,1)}), bf16[8,256,128]{2,1,0:T(8,128)(2,1)S(1)}, u32[]{:S(2)}, u32[]{:S(2)}) async-start(bf16[8,256,128]{2,1,0:T(8,128)(2,1)} %pair_kernel.1), calls=%async_computation.4 | async-start | bytes 1048576 | tf_op jit(solution)/shard_map/all_to_all | solution.py:244
  107.0 0.8 sum_kernel.1
  107.8 17.1 %all-to-all-done.4.parts_ref = bf16[8,256,128]{2,1,0:T(8,128)(2,1)S(1)} async-done(((bf16[8,256,128]{2,1,0:T(8,128)(2,1)}), bf16[8,256,128]{2,1,0:T(8,128)(2,1)S(1)}, u32[]{:S(2)}, u32[]{:S(2)}) %all-to-all-start.4) | async-done | bytes 524320 | tf_op jit(solution)/shard_map/all_to_all | solution.py:244
  124.9 0.8 weight_sum_kernel.1
  (9 shorter events, 0.0 us)
Async XLA Ops:
  0.6 25.8 %copy-start.1 = (bf16[2048,128]{1,0:T(8,128)(2,1)S(1)}, bf16[2048,128]{1,0:T(8,128)(2,1)}, u32[]{:S(2)}) copy-start(bf16[2048,128]{1,0:T(8,128)(2,1)} %wn_ref.1) | copy-start | bytes 1572868
  0.6 0.9 copy-start.5
  2.7 51.4 %copy-start = (bf16[2048,128]{1,0:T(8,128)(2,1)S(1)}, bf16[2048,128]{1,0:T(8,128)(2,1)}, u32[]{:S(2)}) copy-start(bf16[2048,128]{1,0:T(8,128)(2,1)} %ws_ref.1) | copy-start | bytes 1572868
  2.7 23.7 %all-to-all-start = ((bf16[16,256,128]{2,1,0:T(8,128)(2,1)}), bf16[16,256,128]{2,1,0:T(8,128)(2,1)S(1)}, u32[]{:S(2)}, u32[]{:S(2)}) async-start(bf16[16,256,128]{2,1,0:T(8,128)(2,1)} %spread_kernel.1), calls=%async_computation | async-start | bytes 2097152 | tf_op jit(solution)/shard_map/all_to_all | solution.py:203
  10.4 45.1 %copy-start.6 = (bf16[256,128]{1,0:T(8,128)(2,1)S(1)}, bf16[256,128]{1,0:T(8,128)(2,1)}, u32[]{:S(2)}) copy-start(bf16[256,128]{1,0:T(8,128)(2,1)} %og_ref.1) | copy-start | bytes 196612
  11.1 0.7 copy-start.7
  11.8 0.7 copy-start.8
  15.1 1.0 copy-start.2
  49.5 6.1 %collective-permute-start = (bf16[8,272,128]{2,1,0:T(8,128)(2,1)S(1)}, bf16[8,272,128]{2,1,0:T(8,128)(2,1)S(1)}, u32[]{:S(2)}, u32[]{:S(2)}) collective-permute-start(bf16[8,272,128]{2,1,0:T(8,128)(2,1)S(1)} %all_to_all.25.own_ref), channel_id=1, source_target_pairs={{0,16},{16,0},{1,17},{17,1},{2,18},{18,2},{3,19},{19,3},{4,20},{20... | collective-permute-start | bytes 1671176 | tf_op jit(solution)/shard_map/ppermute | solution.py:221
  55.6 1.2 copy-start.3
  79.5 1.0 copy-start.4
  80.5 23.0 %all-to-all-start.3 = ((bf16[16,128,256]{2,1,0:T(8,128)(2,1)}), bf16[16,128,256]{2,1,0:T(8,128)(2,1)S(1)}, u32[]{:S(2)}, u32[]{:S(2)}) async-start(bf16[16,128,256]{2,1,0:T(8,128)(2,1)} %copy-done.4), calls=%async_computation.3 | async-start | bytes 2097152 | tf_op jit(solution)/shard_map/all_to_all | solution.py:235
  86.3 2.0 %collective-permute-start.1 = (bf16[8,256,128]{2,1,0:T(8,128)(2,1)S(1)}, bf16[8,256,128]{2,1,0:T(8,128)(2,1)S(1)}, u32[]{:S(2)}, u32[]{:S(2)}) collective-permute-start(bf16[8,256,128]{2,1,0:T(8,128)(2,1)S(1)} %get-tuple-element.29), channel_id=1, source_target_pairs={{0,16},{16,0},{1,17},{17,1},{2,18},{18,2},{3,19},{19,3},{4,20},{20... | collective-permute-start | bytes 1572872 | tf_op jit(solution)/shard_map/ppermute | solution.py:242
  103.5 21.4 %all-to-all-start.4 = ((bf16[8,256,128]{2,1,0:T(8,128)(2,1)}), bf16[8,256,128]{2,1,0:T(8,128)(2,1)S(1)}, u32[]{:S(2)}, u32[]{:S(2)}) async-start(bf16[8,256,128]{2,1,0:T(8,128)(2,1)} %pair_kernel.1), calls=%async_computation.4 | async-start | bytes 1048576 | tf_op jit(solution)/shard_map/all_to_all | solution.py:244

commit v3 on v2

--- a/solution.py
+++ b/solution.py
@@ -11,11 +11,11 @@
 BF16 = jnp.bfloat16
 T = 128
 CHUNK = 10
-LIMIT = 48 * 1024 * 1024
+MIB = 1024 * 1024
 VMEM = pl.BlockSpec(memory_space=pltpu.VMEM)
 SMEM = pl.BlockSpec(memory_space=pltpu.SMEM)
-HBM = pl.BlockSpec(memory_space=pl.ANY)
-PARAMS = pltpu.CompilerParams(vmem_limit_bytes=LIMIT)
+ANY = pl.BlockSpec(memory_space=pl.ANY)
+HBM = pl.BlockSpec(memory_space=pltpu.HBM)
 
 
 def dot(a, b):
@@ -75,10 +75,14 @@
     flag_ref[...] = flags.astype(BF16)
 
 
-def spread_kernel(x_ref, pay_ref):
-    block = x_ref[...]
-    for copy in range(pay_ref.shape[0]):
-        pay_ref[copy] = block
+def spread_kernel(x_ref, pay_ref, sems):
+    copies = [
+        pltpu.make_async_copy(x_ref, pay_ref.at[copy], sems.at[copy]) for copy in range(pay_ref.shape[0])
+    ]
+    for copy in copies:
+        copy.start()
+    for copy in copies:
+        copy.wait()
 
 
 def neighbour_product_kernel(x_ref, w_ref, flag_ref, pay_ref):
@@ -130,7 +134,7 @@
         pay_ref[owner] = spread[:, owner * T : (owner + 1) * T].astype(BF16)
 
 
-def feature_grad_kernel(came_ref, mask_ref, gt_ref, ws_ref, wn_ref, bt_ref, pay_ref):
+def feature_grad_kernel(came_ref, mask_ref, gt_ref, ws_ref, wn_ref, bt_ref, pay_ref, buf, sems):
     low = jnp.zeros((T, T), F32)
     high = jnp.zeros((T, T), F32)
     for sender in range(came_ref.shape[0]):
@@ -142,31 +146,42 @@
     bt = both[0:T]
     bt_ref[...] = both
     gt = gt_ref[...]
+    copies = []
     for part in range(pay_ref.shape[0]):
         span = slice(part * T, (part + 1) * T)
-        pay_ref[part] = (dot(ws_ref[span, :], gt) + dot(wn_ref[span, :], bt)).astype(BF16)
+        buf[part] = (dot(ws_ref[span, :], gt) + dot(wn_ref[span, :], bt)).astype(BF16)
+        copies.append(pltpu.make_async_copy(buf.at[part], pay_ref.at[part], sems.at[part]))
+        copies[-1].start()
+    for copy in copies:
+        copy.wait()
 
 
 def weight_grad_kernel(place_ref, gt_ref, bt_ref, x_ref, keep_ref, send_ref):
     core = place_ref[0]
+    here = place_ref[2]
+    chips = keep_ref.shape[0]
     left = jnp.concatenate([gt_ref[...], bt_ref[...]], axis=0)
-    for chip in range(keep_ref.shape[0]):
+    for step in range(chips):
+        chip = lax.rem(here + step, chips)
         kept = dot(left, x_ref[2 * chip + core])
         sent = dot(left, x_ref[2 * chip + 1 - core])
-        keep_ref[chip, 0:T] = kept[0:T]
-        keep_ref[chip, T:] = kept[T : 2 * T] + kept[2 * T :]
-        send_ref[chip, 0:T] = sent[0:T].astype(BF16)
-        send_ref[chip, T:] = (sent[T : 2 * T] + sent[2 * T :]).astype(BF16)
-
-
-def pair_kernel(keep_ref, came_ref, pay_ref):
-    pay_ref[...] = (keep_ref[...] + came_ref[...].astype(F32)).astype(BF16)
-
-
-def weight_sum_kernel(parts_ref, self_ref, neigh_ref):
-    total = parts_ref[0].astype(F32)
-    for part in range(1, parts_ref.shape[0]):
-        total = total + parts_ref[part].astype(F32)
+        keep_ref[step, 0:T] = kept[0:T]
+        keep_ref[step, T:] = kept[T : 2 * T] + kept[2 * T :]
+        send_ref[step, 0:T] = sent[0:T].astype(BF16)
+        send_ref[step, T:] = (sent[T : 2 * T] + sent[2 * T :]).astype(BF16)
+
+
+def pair_kernel(keep_ref, came_ref, own_ref, *pay_refs):
+    own_ref[...] = keep_ref[0] + came_ref[0].astype(F32)
+    for step, pay_ref in enumerate(pay_refs, 1):
+        pay_ref[...] = (keep_ref[step] + came_ref[step].astype(F32)).astype(BF16)
+
+
+def weight_sum_kernel(own_ref, *refs):
+    parts, (self_ref, neigh_ref) = refs[:-2], refs[-2:]
+    total = own_ref[...]
+    for part in parts:
+        total = total + part[...].astype(F32)
     self_ref[...] = total[0:T].T
     neigh_ref[...] = total[T:].T
 
@@ -178,7 +193,7 @@
     out_ref[...] = total.T.astype(out_ref.dtype)
 
 
-def call(kernel, ins, outs, in_specs=None, out_specs=None, scratch=()):
+def call(kernel, ins, outs, in_specs=None, out_specs=None, scratch=(), limit=12):
     shapes = tuple(jax.ShapeDtypeStruct(shape, dtype) for shape, dtype in outs)
     return pl.pallas_call(
         kernel,
@@ -186,7 +201,7 @@
         in_specs=in_specs or [VMEM] * len(ins),
         out_specs=tuple(out_specs or [VMEM] * len(outs)),
         scratch_shapes=list(scratch),
-        compiler_params=PARAMS,
+        compiler_params=pltpu.CompilerParams(vmem_limit_bytes=limit * MIB),
         name=kernel.__name__,
     )(*ins)
 
@@ -196,22 +211,31 @@
     groups = 2 * chips
     slots = tile_weight.shape[1]
     core = lax.axis_index("c")
-    place = jnp.stack([core, lax.axis_index("z") * 2 + core]).astype(jnp.int32)
+    here = lax.axis_index("z")
+    place = jnp.stack([core, here * 2 + core, here]).astype(jnp.int32)
     swap = [(0, 1), (1, 0)]
 
-    (x_pay,) = call(spread_kernel, (features,), [((parts, rows, T), BF16)])
+    (x_pay,) = call(
+        spread_kernel,
+        (features,),
+        [((parts, rows, T), BF16)],
+        in_specs=[ANY],
+        out_specs=[HBM],
+        scratch=[pltpu.SemaphoreType.DMA((parts,))],
+    )
     x_all = lax.all_to_all(x_pay, ("y", "x"), 0, 0, tiled=True)
     adj, inverse, flags, sel = call(
         adjacency_kernel,
         (tile_count, tile_dst[0], tile_src[0], tile_weight[0]),
         [((rows, groups * T), BF16), ((rows, T), F32), ((groups, T), BF16), ((groups,), jnp.int32)],
-        in_specs=[SMEM, SMEM, SMEM, HBM],
+        in_specs=[SMEM, SMEM, SMEM, ANY],
         out_specs=[VMEM, VMEM, VMEM, SMEM],
         scratch=[
             pltpu.VMEM((slots, T, T), jnp.int32),
             pltpu.VMEM((groups, rows, T), jnp.int32),
             pltpu.SemaphoreType.DMA((slots // CHUNK,)),
         ],
+        limit=20,
     )
     (y_pay,) = call(
         neighbour_product_kernel, (x_all, w_neigh, flags), [((chips, rows + groups, T), BF16)]
@@ -231,6 +255,8 @@
         feature_grad_kernel,
         (c_all, mask, gt, w_self, w_neigh),
         [((2 * T, rows), BF16), ((parts, T, rows), BF16)],
+        out_specs=[VMEM, HBM],
+        scratch=[pltpu.VMEM((parts, T, rows), BF16), pltpu.SemaphoreType.DMA((parts,))],
     )
     p_all = lax.all_to_all(p_pay, ("y", "x"), 0, 0, tiled=True)
     keep, send = call(
@@ -240,10 +266,17 @@
         in_specs=[SMEM, VMEM, VMEM, VMEM],
     )
     came = lax.ppermute(send, "c", swap)
-    (w_pay,) = call(pair_kernel, (keep, came), [((chips, 2 * T, T), BF16)])
-    w_all = lax.all_to_all(w_pay, "z", 0, 0, tiled=True)
+    own, *w_pay = call(
+        pair_kernel,
+        (keep, came),
+        [((2 * T, T), F32)] + [((2 * T, T), BF16)] * (chips - 1),
+    )
+    w_came = [
+        lax.ppermute(block, "z", [(chip, (chip + step) % chips) for chip in range(chips)])
+        for step, block in enumerate(w_pay, 1)
+    ]
     (grad_features,) = call(sum_kernel, (p_all,), [((rows, T), BF16)])
-    grad_self, grad_neigh = call(weight_sum_kernel, (w_all,), [((T, T), F32)] * 2)
+    grad_self, grad_neigh = call(weight_sum_kernel, (own, *w_came), [((T, T), F32)] * 2)
     return output, grad_features, grad_self, grad_neigh
 
 

time: 126 us -> 110 us (0.87)
  waiting for transfers between devices: 44.8 us -> 20.3 us
  starting transfers between devices: 20 us -> 27.4 us
  local copies, waits for them, and re-layouts: 5.39 us -> 6.93 us
    all_to_all x1 -> x0, waiting for transfers between devices: 17.1 us -> none  [per_device(): w_all = lax.all_to_all(w_pay, 'z', 0, 0, tiled=True)]
    all_to_all x1, waiting for transfers between devices: 14.4 us -> 0.01 us  [per_device(): p_all = lax.all_to_all(p_pay, ('y', 'x'), 0, 0, tiled=True)]
    ppermute x0 -> x7, starting transfers between devices: none -> 10.8 us  [per_device(): lax.ppermute(block, 'z', [(chip, (chip + step) % chips) for chip in range...]
    ppermute x0 -> x7, waiting for transfers between devices: none -> 9.17 us  [per_device(): lax.ppermute(block, 'z', [(chip, (chip + step) % chips) for chip in range...]
    all_to_all x1 -> x0, starting transfers between devices: 3.49 us -> none  [per_device(): w_all = lax.all_to_all(w_pay, 'z', 0, 0, tiled=True)]
    all_to_all x1, waiting for transfers between devices: 10.3 us -> 8.11 us  [per_device(): x_all = lax.all_to_all(x_pay, ('y', 'x'), 0, 0, tiled=True)]
    unnamed x18, local copies, waits for them, and re-layouts: 5.39 us -> 6.93 us
  transfers between devices with their start and end apart: 5 -> 11, of which waited for: 5 -> 6; matrix products, arithmetic and copies ran while one was open for 0% -> 0% of each run, Pallas kernels for 5% -> 5%
where the time goes in v3:
time: 110 us
  blocking collectives  42.7 us (39%)
  starting transfers between devices  27.4 us (25%)
  waiting for transfers between devices  20.3 us (18%)
  Pallas kernels  10.9 us (10%)
  local copies, waits for them, and re-layouts  6.93 us (6%)
  between operations  1.42 us (1%)
    all_to_all x1, blocking collectives, per_device(): y_own = lax.all_to_all(y_pay, 'z', 0, 0, tiled=True)  22.6 us
    all_to_all x1, blocking collectives, per_device(): c_all = lax.all_to_all(c_pay, ('z', 'c'), 0, 0, tiled=True)  20.1 us
    pallas_call x10, Pallas kernels, call(): pl.pallas_call(kernel, out_shape=shapes, in_specs=in_specs or [VMEM] * le...  10.9 us
    ppermute x7, starting transfers between devices, per_device(): lax.ppermute(block, 'z', [(chip, (chip + step) % chips) for chip in range...  10.8 us
    ppermute x7, waiting for transfers between devices, per_device(): lax.ppermute(block, 'z', [(chip, (chip + step) % chips) for chip in range...  9.17 us
    all_to_all x1, waiting for transfers between devices, per_device(): x_all = lax.all_to_all(x_pay, ('y', 'x'), 0, 0, tiled=True)  8.11 us
    all_to_all x1, starting transfers between devices, per_device(): x_all = lax.all_to_all(x_pay, ('y', 'x'), 0, 0, tiled=True)  7.73 us
    unnamed x18, local copies, waits for them, and re-layouts  6.93 us
  transfers between devices with their start and end apart: 11, of which 6 were waited for; matrix products, arithmetic and copies ran while one was open for 0% of the time, Pallas kernels for 5%

profile of v3, /device:TPU:1, one launch (start us, length us, event | category | flops | bytes accessed | tf_op | source)
XLA Modules:
  0.0 109.8 jit_solution(226540089629810141)
XLA Ops:
  0.7 0.9 copy-done.5
  1.5 1.1 spread_kernel.1
  2.7 7.7 %all-to-all-start = ((bf16[16,256,128]{2,1,0:T(8,128)(2,1)}), bf16[16,256,128]{2,1,0:T(8,128)(2,1)S(1)}, u32[]{:S(2)}, u32[]{:S(2)}) async-start(bf16[16,256,128]{2,1,0:T(8,128)(2,1)} %spread_kernel.1), calls=%async_computation | async-start | bytes 2097152 | tf_op jit(solution)/shard_map/all_to_all | solution.py:226
  11.1 2.5 %copy-done = s32[1,80,128,128]{3,2,1,0:T(8,128)S(1)} copy-done((s32[1,80,128,128]{3,2,1,0:T(8,128)S(1)}, s32[1,80,128,128]{3,2,1,0:T(8,128)}, u32[]{:S(2)}) %copy-start) | copy-done | bytes 5242904
  13.5 0.7 copy-done.7
  14.2 0.7 copy-done.8
  14.8 2.4 %adjacency_kernel.1 = (bf16[256,2048]{1,0:T(8,128)(2,1)S(1)}, f32[256,128]{1,0:T(8,128)S(1)}, bf16[16,128]{1,0:T(8,128)(2,1)S(1)}, s32[16]{0:T(128)S(1)}) custom-call(s32[1]{0:T(128)S(6)} %copy.12.count_ref, s32[80]{0:T(128)S(1)} %bitcast.7, s32[80]{0:T(128)S(1)} %bitcast.8, s32[80,128,128]{2,1,0:T(8,128)S(1)} %bitcast.6), custom_call_target="tpu_custom_call" | custom-call | tf_op jit(solution)/shard_map/adjacency_kernel/pallas_call | solution.py:198
  17.3 1.0 copy-done.3
  18.3 8.1 %all-to-all-done.x_ref = bf16[16,256,128]{2,1,0:T(8,128)(2,1)S(1)} async-done(((bf16[16,256,128]{2,1,0:T(8,128)(2,1)}), bf16[16,256,128]{2,1,0:T(8,128)(2,1)S(1)}, u32[]{:S(2)}, u32[]{:S(2)}) %all-to-all-start) | async-done | bytes 1048608 | tf_op jit(solution)/shard_map/all_to_all | solution.py:226
  26.4 0.4 neighbour_product_kernel.1
  26.8 22.6 %all_to_all.20.own_ref = bf16[8,272,128]{2,1,0:T(8,128)(2,1)S(1)} all-to-all(bf16[8,272,128]{2,1,0:T(8,128)(2,1)S(1)} %neighbour_product_kernel.1), channel_id=1, replica_groups=mesh['z'=8,'c'=2,'y'=4,'x'=4] {'z'}, dimensions={0} | all-to-all | bytes 1114112 | tf_op jit(solution)/shard_map/all_to_all | solution.py:243
  49.4 4.5 %collective-permute-start = (bf16[8,272,128]{2,1,0:T(8,128)(2,1)S(1)}, bf16[8,272,128]{2,1,0:T(8,128)(2,1)S(1)}, u32[]{:S(2)}, u32[]{:S(2)}) collective-permute-start(bf16[8,272,128]{2,1,0:T(8,128)(2,1)S(1)} %all_to_all.20.own_ref), channel_id=1, source_target_pairs={{0,16},{16,0},{1,17},{17,1},{2,18},{18,2},{3,19},{19,3},{4,20},{20... | collective-permute-start | bytes 1671176 | tf_op jit(solution)/shard_map/ppermute | solution.py:245
  54.0 0.4 self_product_kernel.1.z_ref
  54.5 1.1 collective-permute-done.other_ref
  55.5 1.2 %copy-done.4 = bf16[256,2048]{1,0:T(8,128)(2,1)S(1)} copy-done((bf16[256,2048]{1,0:T(8,128)(2,1)S(1)}, bf16[256,2048]{1,0:T(8,128)(2,1)}, u32[]{:S(2)}) %copy-start.4) | copy-done | bytes 1048600
  56.8 1.7 %activation_kernel.1 = (bf16[256,128]{1,0:T(8,128)(2,1)}, bf16[128,256]{1,0:T(8,128)(2,1)S(1)}, bf16[16,128,128]{2,1,0:T(8,128)(2,1)S(1)}, f32[16,128]{1,0:T(8,128)S(1)}) custom-call(s32[3]{0:T(128)S(1)} %pad_add_fusion.place_ref, s32[16]{0:T(128)S(1)} %get-tuple-element.26.sel_ref, bf16[256,2048]{1,0:T(8,128)(2,1)S(1)} %copy-done.4, ...), custom_call_target="tpu_custom_call" | custom-call | tf_op jit(solution)/shard_map/activation_kernel/pallas_call | solution.py:198
  58.4 20.1 %all_to_all.21.came_ref = bf16[16,128,128]{2,1,0:T(8,128)(2,1)S(1)} all-to-all(bf16[16,128,128]{2,1,0:T(8,128)(2,1)S(1)} %get-tuple-element.31), channel_id=1, replica_groups=mesh['z'=8,'c'=2,'y'=4,'x'=4] {'z','c'}, dimensions={0} | all-to-all | bytes 1048576 | tf_op jit(solution)/shard_map/all_to_all | solution.py:253
  78.6 1.7 %feature_grad_kernel.1 = (bf16[256,256]{1,0:T(8,128)(2,1)S(1)}, bf16[16,128,256]{2,1,0:T(8,128)(2,1)}) custom-call(bf16[16,128,128]{2,1,0:T(8,128)(2,1)S(1)} %all_to_all.21.came_ref, f32[16,128]{1,0:T(8,128)S(1)} %get-tuple-element.32.mask_ref, bf16[128,256]{1,0:T(8,128)(2,1)S(1)} %get-tuple-element.33.gt_ref, bf16[2048,128]{1,0:T(8,128)(2,1)S(1)} %copy-done.1, ...), custom_call_target="tpu_custom_call" | custom-call | tf_op jit(solution)/shard_map/feature_grad_kernel/pallas_call | solution.py:198
  80.3 4.2 %all-to-all-start.3 = ((bf16[16,128,256]{2,1,0:T(8,128)(2,1)}), bf16[16,128,256]{2,1,0:T(8,128)(2,1)S(1)}, u32[]{:S(2)}, u32[]{:S(2)}) async-start(bf16[16,128,256]{2,1,0:T(8,128)(2,1)} %get-tuple-element.34), calls=%async_computation.3 | async-start | bytes 2097152 | tf_op jit(solution)/shard_map/all_to_all | solution.py:261
  84.5 1.5 %weight_grad_kernel.1 = (f32[8,256,128]{2,1,0:T(8,128)S(1)}, bf16[8,256,128]{2,1,0:T(8,128)(2,1)S(1)}) custom-call(s32[3]{0:T(128)S(1)} %pad_add_fusion.place_ref, bf16[128,256]{1,0:T(8,128)(2,1)S(1)} %get-tuple-element.33.gt_ref, bf16[256,256]{1,0:T(8,128)(2,1)S(1)} %get-tuple-element.35.bt_ref, bf16[16,256,128]{2,1,0:T(8,128)(2,1)S(1)} %all-to-all-done.x_ref), custom_call_target="tpu_custom_call" | custom-call | tf_op jit(solution)/shard_map/weight_grad_kernel/pallas_call | solution.py:198
  86.1 1.9 %collective-permute-done.1.came_ref = bf16[8,256,128]{2,1,0:T(8,128)(2,1)S(1)} collective-permute-done((bf16[8,256,128]{2,1,0:T(8,128)(2,1)S(1)}, bf16[8,256,128]{2,1,0:T(8,128)(2,1)S(1)}, u32[]{:S(2)}, u32[]{:S(2)}) %collective-permute-start.1) | collective-permute-done | bytes 524320 | tf_op jit(solution)/shard_map/ppermute | solution.py:268
  88.2 1.4 %collective-permute-start.3 = (bf16[256,128]{1,0:T(8,128)(2,1)S(1)}, bf16[256,128]{1,0:T(8,128)(2,1)S(1)}, u32[]{:S(2)}, u32[]{:S(2)}) collective-permute-start(bf16[256,128]{1,0:T(8,128)(2,1)S(1)} %get-tuple-element.40), channel_id=1, source_target_pairs={{0,64},{32,96},{64,128},{96,160},{128,192},{160,224},{192,0},{224,... | collective-permute-start | bytes 196616 | tf_op jit(solution)/shard_map/ppermute | solution.py:275
  89.6 1.2 %collective-permute-start.4 = (bf16[256,128]{1,0:T(8,128)(2,1)S(1)}, bf16[256,128]{1,0:T(8,128)(2,1)S(1)}, u32[]{:S(2)}, u32[]{:S(2)}) collective-permute-start(bf16[256,128]{1,0:T(8,128)(2,1)S(1)} %get-tuple-element.41), channel_id=1, source_target_pairs={{0,96},{32,128},{64,160},{96,192},{128,224},{160,0},{192,32},{224,... | collective-permute-start | bytes 196616 | tf_op jit(solution)/shard_map/ppermute | solution.py:275
  90.9 3.2 %collective-permute-start.5 = (bf16[256,128]{1,0:T(8,128)(2,1)S(1)}, bf16[256,128]{1,0:T(8,128)(2,1)S(1)}, u32[]{:S(2)}, u32[]{:S(2)}) collective-permute-start(bf16[256,128]{1,0:T(8,128)(2,1)S(1)} %get-tuple-element.42), channel_id=1, source_target_pairs={{0,128},{32,160},{64,192},{96,224},{128,0},{160,32},{192,64},{224,... | collective-permute-start | bytes 196616 | tf_op jit(solution)/shard_map/ppermute | solution.py:275
  94.1 1.2 %collective-permute-start.6 = (bf16[256,128]{1,0:T(8,128)(2,1)S(1)}, bf16[256,128]{1,0:T(8,128)(2,1)S(1)}, u32[]{:S(2)}, u32[]{:S(2)}) collective-permute-start(bf16[256,128]{1,0:T(8,128)(2,1)S(1)} %get-tuple-element.43), channel_id=1, source_target_pairs={{0,160},{32,192},{64,224},{96,0},{128,32},{160,64},{192,96},{224,1... | collective-permute-start | bytes 196616 | tf_op jit(solution)/shard_map/ppermute | solution.py:275
  95.3 3.4 %collective-permute-start.7 = (bf16[256,128]{1,0:T(8,128)(2,1)S(1)}, bf16[256,128]{1,0:T(8,128)(2,1)S(1)}, u32[]{:S(2)}, u32[]{:S(2)}) collective-permute-start(bf16[256,128]{1,0:T(8,128)(2,1)S(1)} %get-tuple-element.44), channel_id=1, source_target_pairs={{0,192},{32,224},{64,0},{96,32},{128,64},{160,96},{192,128},{224,1... | collective-permute-start | bytes 196616 | tf_op jit(solution)/shard_map/ppermute | solution.py:275
  98.7 0.3 collective-permute-start.8
  99.0 2.3 %collective-permute-done.4.refs_2_ = bf16[256,128]{1,0:T(8,128)(2,1)S(1)} collective-permute-done((bf16[256,128]{1,0:T(8,128)(2,1)S(1)}, bf16[256,128]{1,0:T(8,128)(2,1)S(1)}, u32[]{:S(2)}, u32[]{:S(2)}) %collective-permute-start.4) | collective-permute-done | bytes 65568 | tf_op jit(solution)/shard_map/ppermute | solution.py:275
  101.3 5.8 %collective-permute-done.7.refs_5_ = bf16[256,128]{1,0:T(8,128)(2,1)S(1)} collective-permute-done((bf16[256,128]{1,0:T(8,128)(2,1)S(1)}, bf16[256,128]{1,0:T(8,128)(2,1)S(1)}, u32[]{:S(2)}, u32[]{:S(2)}) %collective-permute-start.7) | collective-permute-done | bytes 65568 | tf_op jit(solution)/shard_map/ppermute | solution.py:275
  107.1 1.0 collective-permute-done.8.refs_6_
  108.1 0.8 weight_sum_kernel.1
  108.9 0.8 sum_kernel.1
  (21 shorter events, 0.4 us)
Async XLA Ops:
  0.6 25.8 %copy-start.2 = (bf16[2048,128]{1,0:T(8,128)(2,1)S(1)}, bf16[2048,128]{1,0:T(8,128)(2,1)}, u32[]{:S(2)}) copy-start(bf16[2048,128]{1,0:T(8,128)(2,1)} %wn_ref.1) | copy-start | bytes 1572868
  0.6 0.9 copy-start.5
  2.6 51.4 %copy-start.1 = (bf16[2048,128]{1,0:T(8,128)(2,1)S(1)}, bf16[2048,128]{1,0:T(8,128)(2,1)}, u32[]{:S(2)}) copy-start(bf16[2048,128]{1,0:T(8,128)(2,1)} %ws_ref.1) | copy-start | bytes 1572868
  2.6 52.9 %copy-start.6 = (bf16[256,128]{1,0:T(8,128)(2,1)S(1)}, bf16[256,128]{1,0:T(8,128)(2,1)}, u32[]{:S(2)}) copy-start(bf16[256,128]{1,0:T(8,128)(2,1)} %og_ref.1) | copy-start | bytes 196612
  2.7 23.7 %all-to-all-start = ((bf16[16,256,128]{2,1,0:T(8,128)(2,1)}), bf16[16,256,128]{2,1,0:T(8,128)(2,1)S(1)}, u32[]{:S(2)}, u32[]{:S(2)}) async-start(bf16[16,256,128]{2,1,0:T(8,128)(2,1)} %spread_kernel.1), calls=%async_computation | async-start | bytes 2097152 | tf_op jit(solution)/shard_map/all_to_all | solution.py:226
  11.0 2.5 %copy-start = (s32[1,80,128,128]{3,2,1,0:T(8,128)S(1)}, s32[1,80,128,128]{3,2,1,0:T(8,128)}, u32[]{:S(2)}) copy-start(s32[1,80,128,128]{3,2,1,0:T(8,128)} %param.15) | copy-start | bytes 15728644
  13.5 0.7 copy-start.7
  14.2 0.7 copy-start.8
  17.3 1.0 copy-start.3
  49.4 6.1 %collective-permute-start = (bf16[8,272,128]{2,1,0:T(8,128)(2,1)S(1)}, bf16[8,272,128]{2,1,0:T(8,128)(2,1)S(1)}, u32[]{:S(2)}, u32[]{:S(2)}) collective-permute-start(bf16[8,272,128]{2,1,0:T(8,128)(2,1)S(1)} %all_to_all.20.own_ref), channel_id=1, source_target_pairs={{0,16},{16,0},{1,17},{17,1},{2,18},{18,2},{3,19},{19,3},{4,20},{20... | collective-permute-start | bytes 1671176 | tf_op jit(solution)/shard_map/ppermute | solution.py:245
  55.5 1.2 %copy-start.4 = (bf16[256,2048]{1,0:T(8,128)(2,1)S(1)}, bf16[256,2048]{1,0:T(8,128)(2,1)}, u32[]{:S(2)}) copy-start(bf16[256,2048]{1,0:T(8,128)(2,1)} %copy-done.3) | copy-start | bytes 3145732
  80.3 28.6 %all-to-all-start.3 = ((bf16[16,128,256]{2,1,0:T(8,128)(2,1)}), bf16[16,128,256]{2,1,0:T(8,128)(2,1)S(1)}, u32[]{:S(2)}, u32[]{:S(2)}) async-start(bf16[16,128,256]{2,1,0:T(8,128)(2,1)} %get-tuple-element.34), calls=%async_computation.3 | async-start | bytes 2097152 | tf_op jit(solution)/shard_map/all_to_all | solution.py:261
  86.0 2.0 %collective-permute-start.1 = (bf16[8,256,128]{2,1,0:T(8,128)(2,1)S(1)}, bf16[8,256,128]{2,1,0:T(8,128)(2,1)S(1)}, u32[]{:S(2)}, u32[]{:S(2)}) collective-permute-start(bf16[8,256,128]{2,1,0:T(8,128)(2,1)S(1)} %get-tuple-element.37), channel_id=1, source_target_pairs={{0,16},{16,0},{1,17},{17,1},{2,18},{18,2},{3,19},{19,3},{4,20},{20... | collective-permute-start | bytes 1572872 | tf_op jit(solution)/shard_map/ppermute | solution.py:268
  88.1 7.1 %collective-permute-start.2 = (bf16[256,128]{1,0:T(8,128)(2,1)S(1)}, bf16[256,128]{1,0:T(8,128)(2,1)S(1)}, u32[]{:S(2)}, u32[]{:S(2)}) collective-permute-start(bf16[256,128]{1,0:T(8,128)(2,1)S(1)} %get-tuple-element.39), channel_id=1, source_target_pairs={{0,32},{32,64},{64,96},{96,128},{128,160},{160,192},{192,224},{224... | collective-permute-start | bytes 196616 | tf_op jit(solution)/shard_map/ppermute | solution.py:275
  88.2 10.5 %collective-permute-start.3 = (bf16[256,128]{1,0:T(8,128)(2,1)S(1)}, bf16[256,128]{1,0:T(8,128)(2,1)S(1)}, u32[]{:S(2)}, u32[]{:S(2)}) collective-permute-start(bf16[256,128]{1,0:T(8,128)(2,1)S(1)} %get-tuple-element.40), channel_id=1, source_target_pairs={{0,64},{32,96},{64,128},{96,160},{128,192},{160,224},{192,0},{224,... | collective-permute-start | bytes 196616 | tf_op jit(solution)/shard_map/ppermute | solution.py:275
  89.6 11.7 %collective-permute-start.4 = (bf16[256,128]{1,0:T(8,128)(2,1)S(1)}, bf16[256,128]{1,0:T(8,128)(2,1)S(1)}, u32[]{:S(2)}, u32[]{:S(2)}) collective-permute-start(bf16[256,128]{1,0:T(8,128)(2,1)S(1)} %get-tuple-element.41), channel_id=1, source_target_pairs={{0,96},{32,128},{64,160},{96,192},{128,224},{160,0},{192,32},{224,... | collective-permute-start | bytes 196616 | tf_op jit(solution)/shard_map/ppermute | solution.py:275
  90.9 10.4 %collective-permute-start.5 = (bf16[256,128]{1,0:T(8,128)(2,1)S(1)}, bf16[256,128]{1,0:T(8,128)(2,1)S(1)}, u32[]{:S(2)}, u32[]{:S(2)}) collective-permute-start(bf16[256,128]{1,0:T(8,128)(2,1)S(1)} %get-tuple-element.42), channel_id=1, source_target_pairs={{0,128},{32,160},{64,192},{96,224},{128,0},{160,32},{192,64},{224,... | collective-permute-start | bytes 196616 | tf_op jit(solution)/shard_map/ppermute | solution.py:275
  94.1 7.3 %collective-permute-start.6 = (bf16[256,128]{1,0:T(8,128)(2,1)S(1)}, bf16[256,128]{1,0:T(8,128)(2,1)S(1)}, u32[]{:S(2)}, u32[]{:S(2)}) collective-permute-start(bf16[256,128]{1,0:T(8,128)(2,1)S(1)} %get-tuple-element.43), channel_id=1, source_target_pairs={{0,160},{32,192},{64,224},{96,0},{128,32},{160,64},{192,96},{224,1... | collective-permute-start | bytes 196616 | tf_op jit(solution)/shard_map/ppermute | solution.py:275
  95.3 11.8 %collective-permute-start.7 = (bf16[256,128]{1,0:T(8,128)(2,1)S(1)}, bf16[256,128]{1,0:T(8,128)(2,1)S(1)}, u32[]{:S(2)}, u32[]{:S(2)}) collective-permute-start(bf16[256,128]{1,0:T(8,128)(2,1)S(1)} %get-tuple-element.44), channel_id=1, source_target_pairs={{0,192},{32,224},{64,0},{96,32},{128,64},{160,96},{192,128},{224,1... | collective-permute-start | bytes 196616 | tf_op jit(solution)/shard_map/ppermute | solution.py:275
  98.7 9.4 %collective-permute-start.8 = (bf16[256,128]{1,0:T(8,128)(2,1)S(1)}, bf16[256,128]{1,0:T(8,128)(2,1)S(1)}, u32[]{:S(2)}, u32[]{:S(2)}) collective-permute-start(bf16[256,128]{1,0:T(8,128)(2,1)S(1)} %get-tuple-element.45), channel_id=1, source_target_pairs={{0,224},{32,0},{64,32},{96,64},{128,96},{160,128},{192,160},{224,1... | collective-permute-start | bytes 196616 | tf_op jit(solution)/shard_map/ppermute | solution.py:275

commit v4 on v3

--- a/solution.py
+++ b/solution.py
@@ -22,6 +22,10 @@
     return jnp.dot(a, b, preferred_element_type=F32)
 
 
+def far_first(chips):
+    return tuple(sorted(range(1, chips), key=lambda step: abs(step - chips // 2)))
+
+
 def halves(block):
     high = block.astype(BF16)
     return jnp.concatenate([high, (block - high.astype(F32)).astype(BF16)], axis=0)
@@ -52,10 +56,10 @@
             chunk_copy(index).wait()
 
             def add_tile(slot, carry):
-                source = src_ref[slot]
+                source = src_ref[0, slot]
                 owner = source // 2
                 sel_ref[owner] = source - 2 * owner
-                rows = pl.ds(pl.multiple_of(dst_ref[slot] * T, T), T)
+                rows = pl.ds(pl.multiple_of(dst_ref[0, slot] * T, T), T)
                 acc[owner, rows, :] = acc[owner, rows, :] + buf[slot]
                 return carry
 
@@ -65,7 +69,7 @@
     for owner in range(groups):
         if owner > 0:
             total = total + acc[owner]
-        adj_ref[:, owner * T : (owner + 1) * T] = acc[owner].astype(F32).astype(BF16)
+        adj_ref[owner] = acc[owner].astype(F32).astype(BF16)
     degree = jnp.sum(total.astype(F32), axis=1, keepdims=True)
     inv_ref[...] = jnp.broadcast_to(1.0 / jnp.maximum(degree, 1.0), inv_ref.shape)
     row = lax.broadcasted_iota(jnp.int32, flag_ref.shape, 0)
@@ -98,40 +102,52 @@
         pay_ref[copy, rows:, :] = flags
 
 
-def self_product_kernel(x_ref, w_ref, z_ref):
-    parts = x_ref.shape[0]
+def chosen_tile(ref, sel_ref, chip, owner):
+    return ref[chip, pl.ds(pl.multiple_of(sel_ref[owner] * T, T), T), :]
+
+
+def half_kernel(place_ref, sel_ref, x_ref, w_ref, adj_ref, inv_ref, own_ref, z_ref):
+    core = place_ref[0]
     total = dot(x_ref[0], w_ref[0:T, :])
-    for part in range(1, parts):
+    for part in range(1, x_ref.shape[0]):
         total = total + dot(x_ref[part], w_ref[part * T : (part + 1) * T, :])
-    z_ref[...] = total
+    summed = jnp.zeros(z_ref.shape, F32)
+    for chip in range(own_ref.shape[0]):
+        owner = 2 * chip + core
+        summed = summed + dot(adj_ref[owner], chosen_tile(own_ref, sel_ref, chip, owner))
+    z_ref[...] = total + inv_ref[...] * summed
 
 
 def activation_kernel(
-    place_ref, sel_ref, adj_ref, inv_ref, own_ref, other_ref, z_ref, og_ref,
-    out_ref, gt_ref, pay_ref, mask_ref, chosen,
+    place_ref, sel_ref, adj_ref, inv_ref, other_ref, z_ref, og_ref, x_ref, out_ref, gt_ref, pay_ref, x_same_ref
 ):
     core = place_ref[0]
+    summed = jnp.zeros(z_ref.shape, F32)
+    for chip in range(other_ref.shape[0]):
+        owner = 2 * chip + 1 - core
+        summed = summed + dot(adj_ref[owner], chosen_tile(other_ref, sel_ref, chip, owner))
+    inverse = inv_ref[...]
+    z = z_ref[...] + inverse * summed
+    sig = 1.0 / (1.0 + jnp.exp(-z))
+    grad = (og_ref[...].astype(F32) * sig * (1.0 + z * (1.0 - sig))).astype(BF16).astype(F32)
+    scaled = halves((grad * inverse).T)
+    for owner in range(pay_ref.shape[0]):
+        spread = dot(scaled, adj_ref[owner])
+        pay_ref[owner] = (spread[0:T] + spread[T:]).astype(BF16)
+    out_ref[...] = (z * sig).astype(BF16)
+    gt_ref[...] = grad.T.astype(BF16)
+
+
+def mask_kernel(place_ref, own_ref, other_ref, mask_ref):
+    core = place_ref[0]
     me = place_ref[1]
-    rows = z_ref.shape[0]
-    flag_rows = own_ref.shape[1] - rows
+    flag_rows = mask_ref.shape[0]
+    start = own_ref.shape[1] - flag_rows
     row = lax.broadcasted_iota(jnp.int32, (flag_rows, T), 0)
     for chip in range(own_ref.shape[0]):
         for ref, owner in ((own_ref, 2 * chip + core), (other_ref, 2 * chip + 1 - core)):
-            start = pl.multiple_of(sel_ref[owner] * T, T)
-            chosen[pl.ds(pl.multiple_of(owner * T, T), T), :] = ref[chip, pl.ds(start, T), :]
-            flags = ref[chip, rows:, :].astype(F32)
+            flags = ref[chip, start:, :].astype(F32)
             mask_ref[pl.ds(owner, 1), :] = jnp.sum(jnp.where(row == me, flags, 0.0), axis=0, keepdims=True)
-    adj = adj_ref[...]
-    inverse = inv_ref[...]
-    z = z_ref[...] + inverse * dot(adj, chosen[...])
-    sig = 1.0 / (1.0 + jnp.exp(-z))
-    out_ref[...] = (z * sig).astype(BF16)
-    grad = (og_ref[...].astype(F32) * sig * (1.0 + z * (1.0 - sig))).astype(BF16).astype(F32)
-    gt_ref[...] = grad.T.astype(BF16)
-    spread = dot(halves((grad * inverse).T), adj)
-    spread = spread[0:T] + spread[T:]
-    for owner in range(pay_ref.shape[0]):
-        pay_ref[owner] = spread[:, owner * T : (owner + 1) * T].astype(BF16)
 
 
 def feature_grad_kernel(came_ref, mask_ref, gt_ref, ws_ref, wn_ref, bt_ref, pay_ref, buf, sems):
@@ -156,25 +172,17 @@
         copy.wait()
 
 
-def weight_grad_kernel(place_ref, gt_ref, bt_ref, x_ref, keep_ref, send_ref):
+def weight_grad_kernel(place_ref, gt_ref, bt_ref, gt_pair_ref, bt_pair_ref, x_ref, x_pair_ref, own_ref, *pay_refs):
     core = place_ref[0]
     here = place_ref[2]
-    chips = keep_ref.shape[0]
+    chips = len(pay_refs) + 1
     left = jnp.concatenate([gt_ref[...], bt_ref[...]], axis=0)
-    for step in range(chips):
-        chip = lax.rem(here + step, chips)
-        kept = dot(left, x_ref[2 * chip + core])
-        sent = dot(left, x_ref[2 * chip + 1 - core])
-        keep_ref[step, 0:T] = kept[0:T]
-        keep_ref[step, T:] = kept[T : 2 * T] + kept[2 * T :]
-        send_ref[step, 0:T] = sent[0:T].astype(BF16)
-        send_ref[step, T:] = (sent[T : 2 * T] + sent[2 * T :]).astype(BF16)
-
-
-def pair_kernel(keep_ref, came_ref, own_ref, *pay_refs):
-    own_ref[...] = keep_ref[0] + came_ref[0].astype(F32)
-    for step, pay_ref in enumerate(pay_refs, 1):
-        pay_ref[...] = (keep_ref[step] + came_ref[step].astype(F32)).astype(BF16)
+    left_pair = jnp.concatenate([gt_pair_ref[...], bt_pair_ref[...]], axis=0)
+    for step, pay_ref in zip(far_first(chips) + (0,), pay_refs + (own_ref,)):
+        owner = 2 * lax.rem(here + step, chips) + core
+        total = dot(left, x_ref[owner]) + dot(left_pair, x_pair_ref[owner])
+        pay_ref[0:T] = total[0:T].astype(pay_ref.dtype)
+        pay_ref[T:] = (total[T : 2 * T] + total[2 * T :]).astype(pay_ref.dtype)
 
 
 def weight_sum_kernel(own_ref, *refs):
@@ -193,14 +201,22 @@
     out_ref[...] = total.T.astype(out_ref.dtype)
 
 
-def call(kernel, ins, outs, in_specs=None, out_specs=None, scratch=(), limit=12):
-    shapes = tuple(jax.ShapeDtypeStruct(shape, dtype) for shape, dtype in outs)
+def call(kernel, ins, outs, in_specs=None, out_specs=None, scratch=(), limit=12, aliases=None):
+    shapes = tuple(
+        pltpu.HBM(shape, dtype) if spec is HBM else jax.ShapeDtypeStruct(shape, dtype)
+        for (shape, dtype), spec in zip(outs, out_specs or [VMEM] * len(outs))
+    )
+    ins = [
+        pltpu.with_memory_space_constraint(value, pltpu.HBM) if spec is HBM else value
+        for value, spec in zip(ins, in_specs or [VMEM] * len(ins))
+    ]
     return pl.pallas_call(
         kernel,
         out_shape=shapes,
         in_specs=in_specs or [VMEM] * len(ins),
         out_specs=tuple(out_specs or [VMEM] * len(outs)),
         scratch_shapes=list(scratch),
+        input_output_aliases=aliases or {},
         compiler_params=pltpu.CompilerParams(vmem_limit_bytes=limit * MIB),
         name=kernel.__name__,
     )(*ins)
@@ -219,16 +235,16 @@
         spread_kernel,
         (features,),
         [((parts, rows, T), BF16)],
-        in_specs=[ANY],
+        in_specs=[HBM],
         out_specs=[HBM],
         scratch=[pltpu.SemaphoreType.DMA((parts,))],
     )
     x_all = lax.all_to_all(x_pay, ("y", "x"), 0, 0, tiled=True)
     adj, inverse, flags, sel = call(
         adjacency_kernel,
-        (tile_count, tile_dst[0], tile_src[0], tile_weight[0]),
-        [((rows, groups * T), BF16), ((rows, T), F32), ((groups, T), BF16), ((groups,), jnp.int32)],
-        in_specs=[SMEM, SMEM, SMEM, ANY],
+        (tile_count, tile_dst, tile_src, tile_weight[0]),
+        [((groups, rows, T), BF16), ((rows, T), F32), ((groups, T), BF16), ((groups,), jnp.int32)],
+        in_specs=[SMEM, SMEM, SMEM, HBM],
         out_specs=[VMEM, VMEM, VMEM, SMEM],
         scratch=[
             pltpu.VMEM((slots, T, T), jnp.int32),
@@ -241,16 +257,27 @@
         neighbour_product_kernel, (x_all, w_neigh, flags), [((chips, rows + groups, T), BF16)]
     )
     y_own = lax.all_to_all(y_pay, "z", 0, 0, tiled=True)
-    (z_self,) = call(self_product_kernel, (x_all, w_self), [((rows, T), F32)])
     y_other = lax.ppermute(y_own, "c", swap)
-    output, gt, c_pay, mask = call(
+    (z_half,) = call(
+        half_kernel,
+        (place, sel, x_all, w_self, adj, inverse, y_own),
+        [((rows, T), F32)],
+        in_specs=[SMEM, SMEM] + [VMEM] * 5,
+    )
+    output, gt, c_pay, x_late = call(
         activation_kernel,
-        (place, sel, adj, inverse, y_own, y_other, z_self, out_grad),
-        [((rows, T), BF16), ((T, rows), BF16), ((groups, T, T), BF16), ((groups, T), F32)],
-        in_specs=[SMEM, SMEM] + [VMEM] * 6,
-        scratch=[pltpu.VMEM((groups * T, T), BF16)],
+        (place, sel, adj, inverse, y_other, z_half, out_grad, x_all),
+        [((rows, T), BF16), ((T, rows), BF16), ((groups, T, T), BF16), (x_all.shape, BF16)],
+        in_specs=[SMEM, SMEM] + [VMEM] * 5 + [ANY],
+        out_specs=[VMEM] * 3 + [ANY],
+        aliases={7: 3},
     )
     c_all = lax.all_to_all(c_pay, ("z", "c"), 0, 0, tiled=True)
+    gt_pair = lax.ppermute(gt, "c", swap)
+    x_pair = lax.ppermute(x_late, "c", swap)
+    (mask,) = call(
+        mask_kernel, (place, y_own, y_other), [((groups, T), F32)], in_specs=[SMEM, VMEM, VMEM]
+    )
     bt, p_pay = call(
         feature_grad_kernel,
         (c_all, mask, gt, w_self, w_neigh),
@@ -258,22 +285,17 @@
         out_specs=[VMEM, HBM],
         scratch=[pltpu.VMEM((parts, T, rows), BF16), pltpu.SemaphoreType.DMA((parts,))],
     )
+    bt_pair = lax.ppermute(bt, "c", swap)
     p_all = lax.all_to_all(p_pay, ("y", "x"), 0, 0, tiled=True)
-    keep, send = call(
+    own, *w_pay = call(
         weight_grad_kernel,
-        (place, gt, bt, x_all),
-        [((chips, 2 * T, T), F32), ((chips, 2 * T, T), BF16)],
-        in_specs=[SMEM, VMEM, VMEM, VMEM],
-    )
-    came = lax.ppermute(send, "c", swap)
-    own, *w_pay = call(
-        pair_kernel,
-        (keep, came),
+        (place, gt, bt, gt_pair, bt_pair, x_late, x_pair),
         [((2 * T, T), F32)] + [((2 * T, T), BF16)] * (chips - 1),
+        in_specs=[SMEM] + [VMEM] * 6,
     )
     w_came = [
         lax.ppermute(block, "z", [(chip, (chip + step) % chips) for chip in range(chips)])
-        for step, block in enumerate(w_pay, 1)
+        for step, block in zip(far_first(chips), w_pay)
     ]
     (grad_features,) = call(sum_kernel, (p_all,), [((rows, T), BF16)])
     grad_self, grad_neigh = call(weight_sum_kernel, (own, *w_came), [((T, T), F32)] * 2)

time: 110 us -> 141 us (1.28)
  Pallas kernels: 10.9 us -> 45.1 us
  blocking collectives: 42.7 us -> 22.6 us
  waiting for transfers between devices: 20.3 us -> 31.6 us
  starting transfers between devices: 27.4 us -> 34.4 us
  local copies, waits for them, and re-layouts: 6.93 us -> 5.24 us
    pallas_call x10, Pallas kernels: 10.9 us -> 45.1 us  [call(): pl.pallas_call(kernel, out_shape=shapes, in_specs=in_specs or [VMEM] * le...]
    all_to_all x1 -> x0, blocking collectives: 20.1 us -> none  [per_device(): c_all = lax.all_to_all(c_pay, ('z', 'c'), 0, 0, tiled=True)]
    all_to_all x0 -> x1, waiting for transfers between devices: none -> 16.5 us  [per_device(): c_all = lax.all_to_all(c_pay, ('z', 'c'), 0, 0, tiled=True)]
    ppermute x7, waiting for transfers between devices: 9.17 us -> 2.76 us  [per_device(): lax.ppermute(block, 'z', [(chip, (chip + step) % chips) for chip in range...]
    all_to_all x0 -> x1, starting transfers between devices: none -> 3.47 us  [per_device(): c_all = lax.all_to_all(c_pay, ('z', 'c'), 0, 0, tiled=True)]
    all_to_all x1, waiting for transfers between devices: 8.11 us -> 11.4 us  [per_device(): x_all = lax.all_to_all(x_pay, ('y', 'x'), 0, 0, tiled=True)]
    ppermute x7, starting transfers between devices: 10.8 us -> 13.8 us  [per_device(): lax.ppermute(block, 'z', [(chip, (chip + step) % chips) for chip in range...]
    unnamed x18 -> x16, local copies, waits for them, and re-layouts: 6.93 us -> 5.24 us
  transfers between devices with their start and end apart: 11 -> 14, of which waited for: 6 -> 7; matrix products, arithmetic and copies ran while one was open for 0% -> 0% of each run, Pallas kernels for 5% -> 6%
where the time goes in v4:
time: 141 us; the launch traced here: 140 us
  Pallas kernels  45.1 us (32%)
  starting transfers between devices  34.4 us (24%)
  waiting for transfers between devices  31.6 us (22%)
  blocking collectives  22.6 us (16%)
  local copies, waits for them, and re-layouts  5.24 us (4%)
  between operations  1.43 us (1%)
    pallas_call x10, Pallas kernels, call(): pl.pallas_call(kernel, out_shape=shapes, in_specs=in_specs or [VMEM] * le...  45.1 us
    all_to_all x1, blocking collectives, per_device(): y_own = lax.all_to_all(y_pay, 'z', 0, 0, tiled=True)  22.6 us
    all_to_all x1, waiting for transfers between devices, per_device(): c_all = lax.all_to_all(c_pay, ('z', 'c'), 0, 0, tiled=True)  16.5 us
    ppermute x7, starting transfers between devices, per_device(): lax.ppermute(block, 'z', [(chip, (chip + step) % chips) for chip in range...  13.8 us
    all_to_all x1, waiting for transfers between devices, per_device(): x_all = lax.all_to_all(x_pay, ('y', 'x'), 0, 0, tiled=True)  11.4 us
    all_to_all x1, starting transfers between devices, per_device(): x_all = lax.all_to_all(x_pay, ('y', 'x'), 0, 0, tiled=True)  7.6 us
    unnamed x16, local copies, waits for them, and re-layouts  5.24 us
    ppermute x1, starting transfers between devices, per_device(): y_other = lax.ppermute(y_own, 'c', swap)  4.54 us
  transfers between devices with their start and end apart: 14, of which 7 were waited for; matrix products, arithmetic and copies ran while one was open for 0% of the time, Pallas kernels for 6%

profile of v4, /device:TPU:1, one launch (start us, length us, event | category | flops | bytes accessed | tf_op | source)
XLA Modules:
  0.0 140.4 jit_solution(17267295879365779894)
XLA Ops:
  0.6 33.0 %spread_kernel.1 = bf16[16,256,128]{2,1,0:T(8,128)(2,1)} custom-call(bf16[256,128]{1,0:T(8,128)(2,1)} %x_ref.1), custom_call_target="tpu_custom_call" | custom-call | tf_op jit(solution)/shard_map/spread_kernel/pallas_call | solution.py:213
  33.7 7.6 %all-to-all-start = ((bf16[16,256,128]{2,1,0:T(8,128)(2,1)}), bf16[16,256,128]{2,1,0:T(8,128)(2,1)S(1)}, u32[]{:S(2)}, u32[]{:S(2)}) async-start(bf16[16,256,128]{2,1,0:T(8,128)(2,1)} %spread_kernel.1), calls=%async_computation | async-start | bytes 2097152 | tf_op jit(solution)/shard_map/all_to_all | solution.py:242
  41.9 0.6 copy-done.6
  42.6 0.7 copy-done.7
  43.2 2.6 %adjacency_kernel.1 = (bf16[16,256,128]{2,1,0:T(8,128)(2,1)S(1)}, f32[256,128]{1,0:T(8,128)S(1)}, bf16[16,128]{1,0:T(8,128)(2,1)S(1)}, s32[16]{0:T(128)S(1)}) custom-call(s32[1]{0:T(128)S(6)} %copy.14.count_ref, s32[1,80]{1,0:T(1,128)S(1)} %copy-done.6, s32[1,80]{1,0:T(1,128)S(1)} %copy-done.7, s32[80,128,128]{2,1,0:T(8,128)} %bitcast.4), custom_call_target="tpu_custom_call" | custom-call | tf_op jit(solution)/shard_map/adjacency_kernel/pallas_call | solution.py:213
  45.8 11.4 %all-to-all-done.x_ref = bf16[16,256,128]{2,1,0:T(8,128)(2,1)S(1)} async-done(((bf16[16,256,128]{2,1,0:T(8,128)(2,1)}), bf16[16,256,128]{2,1,0:T(8,128)(2,1)S(1)}, u32[]{:S(2)}, u32[]{:S(2)}) %all-to-all-start) | async-done | bytes 1048608 | tf_op jit(solution)/shard_map/all_to_all | solution.py:242
  57.7 22.6 %all_to_all.20.own_ref = bf16[8,272,128]{2,1,0:T(8,128)(2,1)S(1)} all-to-all(bf16[8,272,128]{2,1,0:T(8,128)(2,1)S(1)} %neighbour_product_kernel.1), channel_id=1, replica_groups=mesh['z'=8,'c'=2,'y'=4,'x'=4] {'z'}, dimensions={0} | all-to-all | bytes 1114112 | tf_op jit(solution)/shard_map/all_to_all | solution.py:259
  80.3 4.5 %collective-permute-start = (bf16[8,272,128]{2,1,0:T(8,128)(2,1)S(1)}, bf16[8,272,128]{2,1,0:T(8,128)(2,1)S(1)}, u32[]{:S(2)}, u32[]{:S(2)}) collective-permute-start(bf16[8,272,128]{2,1,0:T(8,128)(2,1)S(1)} %all_to_all.20.own_ref), channel_id=1, source_target_pairs={{0,16},{16,0},{1,17},{17,1},{2,18},{18,2},{3,19},{19,3},{4,20},{20... | collective-permute-start | bytes 1671176 | tf_op jit(solution)/shard_map/ppermute | solution.py:260
  84.9 1.0 copy-done
  85.9 1.1 half_kernel.1.z_ref
  87.1 1.9 %activation_kernel.1 = (bf16[256,128]{1,0:T(8,128)(2,1)}, bf16[128,256]{1,0:T(8,128)(2,1)S(1)}, bf16[16,128,128]{2,1,0:T(8,128)(2,1)S(1)}, bf16[16,256,128]{2,1,0:T(8,128)(2,1)S(1)}) custom-call(s32[3]{0:T(128)S(1)} %pad_add_fusion.place_ref, s32[16]{0:T(128)S(1)} %get-tuple-element.24.sel_ref, ...), custom_call_target="tpu_custom_call", output_to_operand_aliasing={{3}: (7, {})} | custom-call | tf_op jit(solution)/shard_map/activation_kernel/pallas_call | solution.py:213
  88.9 0.8 copy-done.4
  89.7 3.5 %all-to-all-start.2 = ((bf16[16,128,128]{2,1,0:T(8,128)(2,1)}), bf16[16,128,128]{2,1,0:T(8,128)(2,1)S(1)}, u32[]{:S(2)}, u32[]{:S(2)}) async-start(bf16[16,128,128]{2,1,0:T(8,128)(2,1)} %copy-done.4), calls=%async_computation.2 | async-start | bytes 1048576 | tf_op jit(solution)/shard_map/all_to_all | solution.py:275
  93.4 0.6 mask_kernel.1.mask_ref
  94.0 16.5 %all-to-all-done.2.came_ref = bf16[16,128,128]{2,1,0:T(8,128)(2,1)S(1)} async-done(((bf16[16,128,128]{2,1,0:T(8,128)(2,1)}), bf16[16,128,128]{2,1,0:T(8,128)(2,1)S(1)}, u32[]{:S(2)}, u32[]{:S(2)}) %all-to-all-start.2) | async-done | bytes 524320 | tf_op jit(solution)/shard_map/all_to_all | solution.py:275
  110.5 1.0 copy-done.1
  111.5 1.0 copy-done.3
  112.5 1.7 %feature_grad_kernel.1 = (bf16[256,256]{1,0:T(8,128)(2,1)S(1)}, bf16[16,128,256]{2,1,0:T(8,128)(2,1)}) custom-call(bf16[16,128,128]{2,1,0:T(8,128)(2,1)S(1)} %all-to-all-done.2.came_ref, f32[16,128]{1,0:T(8,128)S(1)} %mask_kernel.1.mask_ref, bf16[128,256]{1,0:T(8,128)(2,1)S(1)} %get-tuple-element.30.gt_ref, bf16[2048,128]{1,0:T(8,128)(2,1)S(1)} %copy-done.1, ...), custom_call_target="tpu_custom_call" | custom-call | tf_op jit(solution)/shard_map/feature_grad_kernel/pallas_call | solution.py:213
  114.2 4.2 %all-to-all-start.3 = ((bf16[16,128,256]{2,1,0:T(8,128)(2,1)}), bf16[16,128,256]{2,1,0:T(8,128)(2,1)S(1)}, u32[]{:S(2)}, u32[]{:S(2)}) async-start(bf16[16,128,256]{2,1,0:T(8,128)(2,1)} %get-tuple-element.31), calls=%async_computation.3 | async-start | bytes 2097152 | tf_op jit(solution)/shard_map/all_to_all | solution.py:289
  119.0 0.9 collective-permute-done.1.gt_pair_ref
  120.0 2.2 %weight_grad_kernel.1 = (f32[256,128]{1,0:T(8,128)S(1)}, bf16[256,128]{1,0:T(8,128)(2,1)S(1)}, bf16[256,128]{1,0:T(8,128)(2,1)S(1)}, bf16[256,128]{1,0:T(8,128)(...) custom-call(s32[3]{0:T(128)S(1)} %pad_add_fusion.place_ref, ...), custom_call_target="tpu_custom_call" | custom-call | tf_op jit(solution)/shard_map/weight_grad_kernel/pallas_call | solution.py:213
  122.2 1.5 %collective-permute-start.4 = (bf16[256,128]{1,0:T(8,128)(2,1)S(1)}, bf16[256,128]{1,0:T(8,128)(2,1)S(1)}, u32[]{:S(2)}, u32[]{:S(2)}) collective-permute-start(bf16[256,128]{1,0:T(8,128)(2,1)S(1)} %get-tuple-element.35), channel_id=1, source_target_pairs={{0,128},{32,160},{64,192},{96,224},{128,0},{160,32},{192,64},{224,... | collective-permute-start | bytes 196616 | tf_op jit(solution)/shard_map/ppermute | solution.py:297
  123.7 1.1 collective-permute-start.5
  124.8 3.4 %collective-permute-start.6 = (bf16[256,128]{1,0:T(8,128)(2,1)S(1)}, bf16[256,128]{1,0:T(8,128)(2,1)S(1)}, u32[]{:S(2)}, u32[]{:S(2)}) collective-permute-start(bf16[256,128]{1,0:T(8,128)(2,1)S(1)} %get-tuple-element.37), channel_id=1, source_target_pairs={{0,160},{32,192},{64,224},{96,0},{128,32},{160,64},{192,96},{224,1... | collective-permute-start | bytes 196616 | tf_op jit(solution)/shard_map/ppermute | solution.py:297
  128.2 1.1 collective-permute-start.7
  129.3 2.5 %collective-permute-start.8 = (bf16[256,128]{1,0:T(8,128)(2,1)S(1)}, bf16[256,128]{1,0:T(8,128)(2,1)S(1)}, u32[]{:S(2)}, u32[]{:S(2)}) collective-permute-start(bf16[256,128]{1,0:T(8,128)(2,1)S(1)} %get-tuple-element.39), channel_id=1, source_target_pairs={{0,192},{32,224},{64,0},{96,32},{128,64},{160,96},{192,128},{224,1... | collective-permute-start | bytes 196616 | tf_op jit(solution)/shard_map/ppermute | solution.py:297
  131.8 1.2 collective-permute-start.9
  133.0 1.0 collective-permute-done.5.refs_1_
  134.0 3.0 %collective-permute-start.10 = (bf16[256,128]{1,0:T(8,128)(2,1)S(1)}, bf16[256,128]{1,0:T(8,128)(2,1)S(1)}, u32[]{:S(2)}, u32[]{:S(2)}) collective-permute-start(bf16[256,128]{1,0:T(8,128)(2,1)S(1)} %get-tuple-element.41), channel_id=1, source_target_pairs={{0,224},{32,0},{64,32},{96,64},{128,96},{160,128},{192,160},{224,1... | collective-permute-start | bytes 196616 | tf_op jit(solution)/shard_map/ppermute | solution.py:297
  137.6 1.2 collective-permute-done.10.refs_6_
  138.8 0.8 weight_sum_kernel.1
  139.6 0.8 sum_kernel.1
  (24 shorter events, 1.9 us)
Async XLA Ops:
  0.6 56.6 %copy-start.2 = (bf16[2048,128]{1,0:T(8,128)(2,1)S(1)}, bf16[2048,128]{1,0:T(8,128)(2,1)}, u32[]{:S(2)}) copy-start(bf16[2048,128]{1,0:T(8,128)(2,1)} %wn_ref.1) | copy-start | bytes 1572868
  33.7 23.6 %all-to-all-start = ((bf16[16,256,128]{2,1,0:T(8,128)(2,1)}), bf16[16,256,128]{2,1,0:T(8,128)(2,1)S(1)}, u32[]{:S(2)}, u32[]{:S(2)}) async-start(bf16[16,256,128]{2,1,0:T(8,128)(2,1)} %spread_kernel.1), calls=%async_computation | async-start | bytes 2097152 | tf_op jit(solution)/shard_map/all_to_all | solution.py:242
  41.9 0.7 copy-start.6
  42.6 0.7 copy-start.7
  43.2 43.8 %copy-start.5 = (bf16[256,128]{1,0:T(8,128)(2,1)S(1)}, bf16[256,128]{1,0:T(8,128)(2,1)}, u32[]{:S(2)}) copy-start(bf16[256,128]{1,0:T(8,128)(2,1)} %og_ref.1) | copy-start | bytes 196612
  80.3 6.8 %collective-permute-start = (bf16[8,272,128]{2,1,0:T(8,128)(2,1)S(1)}, bf16[8,272,128]{2,1,0:T(8,128)(2,1)S(1)}, u32[]{:S(2)}, u32[]{:S(2)}) collective-permute-start(bf16[8,272,128]{2,1,0:T(8,128)(2,1)S(1)} %all_to_all.20.own_ref), channel_id=1, source_target_pairs={{0,16},{16,0},{1,17},{17,1},{2,18},{18,2},{3,19},{19,3},{4,20},{20... | collective-permute-start | bytes 1671176 | tf_op jit(solution)/shard_map/ppermute | solution.py:260
  84.9 1.0 copy-start
  88.9 0.8 copy-start.4
  89.7 20.7 %all-to-all-start.2 = ((bf16[16,128,128]{2,1,0:T(8,128)(2,1)}), bf16[16,128,128]{2,1,0:T(8,128)(2,1)S(1)}, u32[]{:S(2)}, u32[]{:S(2)}) async-start(bf16[16,128,128]{2,1,0:T(8,128)(2,1)} %copy-done.4), calls=%async_computation.2 | async-start | bytes 1048576 | tf_op jit(solution)/shard_map/all_to_all | solution.py:275
  93.2 26.8 %collective-permute-start.3 = (bf16[16,256,128]{2,1,0:T(8,128)(2,1)S(1)}, bf16[16,256,128]{2,1,0:T(8,128)(2,1)}, u32[]{:S(2)}, u32[]{:S(2)}) collective-permute-start(bf16[16,256,128]{2,1,0:T(8,128)(2,1)S(1)} %get-tuple-element.33.x_ref), channel_id=1, source_target_pairs={{0,16},{16,0},{1,17},{17,1},{2,18},{18,2},{3,19},{19,3},{4,20},{20... | collective-permute-start | bytes 3145736 | tf_op jit(solution)/shard_map/ppermute | solution.py:277
  110.5 1.0 copy-start.1
  111.5 1.0 copy-start.3
  114.2 25.3 %all-to-all-start.3 = ((bf16[16,128,256]{2,1,0:T(8,128)(2,1)}), bf16[16,128,256]{2,1,0:T(8,128)(2,1)S(1)}, u32[]{:S(2)}, u32[]{:S(2)}) async-start(bf16[16,128,256]{2,1,0:T(8,128)(2,1)} %get-tuple-element.31), calls=%async_computation.3 | async-start | bytes 2097152 | tf_op jit(solution)/shard_map/all_to_all | solution.py:289
  118.4 1.5 %collective-permute-start.2 = (bf16[256,256]{1,0:T(8,128)(2,1)S(1)}, bf16[256,256]{1,0:T(8,128)(2,1)S(1)}, u32[]{:S(2)}, u32[]{:S(2)}) collective-permute-start(bf16[256,256]{1,0:T(8,128)(2,1)S(1)} %get-tuple-element.32.bt_ref), channel_id=1, source_target_pairs={{0,16},{16,0},{1,17},{17,1},{2,18},{18,2},{3,19},{19,3},{4,20},{20... | collective-permute-start | bytes 393224 | tf_op jit(solution)/shard_map/ppermute | solution.py:288
  118.5 1.4 %collective-permute-start.1 = (bf16[128,256]{1,0:T(8,128)(2,1)S(1)}, bf16[128,256]{1,0:T(8,128)(2,1)S(1)}, u32[]{:S(2)}, u32[]{:S(2)}) collective-permute-start(bf16[128,256]{1,0:T(8,128)(2,1)S(1)} %get-tuple-element.30.gt_ref), channel_id=1, source_target_pairs={{0,16},{16,0},{1,17},{17,1},{2,18},{18,2},{3,19},{19,3},{4,20},{20... | collective-permute-start | bytes 196616 | tf_op jit(solution)/shard_map/ppermute | solution.py:276
  122.2 9.6 %collective-permute-start.4 = (bf16[256,128]{1,0:T(8,128)(2,1)S(1)}, bf16[256,128]{1,0:T(8,128)(2,1)S(1)}, u32[]{:S(2)}, u32[]{:S(2)}) collective-permute-start(bf16[256,128]{1,0:T(8,128)(2,1)S(1)} %get-tuple-element.35), channel_id=1, source_target_pairs={{0,128},{32,160},{64,192},{96,224},{128,0},{160,32},{192,64},{224,... | collective-permute-start | bytes 196616 | tf_op jit(solution)/shard_map/ppermute | solution.py:297
  123.7 10.3 %collective-permute-start.5 = (bf16[256,128]{1,0:T(8,128)(2,1)S(1)}, bf16[256,128]{1,0:T(8,128)(2,1)S(1)}, u32[]{:S(2)}, u32[]{:S(2)}) collective-permute-start(bf16[256,128]{1,0:T(8,128)(2,1)S(1)} %get-tuple-element.36), channel_id=1, source_target_pairs={{0,96},{32,128},{64,160},{96,192},{128,224},{160,0},{192,32},{224,... | collective-permute-start | bytes 196616 | tf_op jit(solution)/shard_map/ppermute | solution.py:297
  124.8 12.2 %collective-permute-start.6 = (bf16[256,128]{1,0:T(8,128)(2,1)S(1)}, bf16[256,128]{1,0:T(8,128)(2,1)S(1)}, u32[]{:S(2)}, u32[]{:S(2)}) collective-permute-start(bf16[256,128]{1,0:T(8,128)(2,1)S(1)} %get-tuple-element.37), channel_id=1, source_target_pairs={{0,160},{32,192},{64,224},{96,0},{128,32},{160,64},{192,96},{224,1... | collective-permute-start | bytes 196616 | tf_op jit(solution)/shard_map/ppermute | solution.py:297
  128.2 9.2 %collective-permute-start.7 = (bf16[256,128]{1,0:T(8,128)(2,1)S(1)}, bf16[256,128]{1,0:T(8,128)(2,1)S(1)}, u32[]{:S(2)}, u32[]{:S(2)}) collective-permute-start(bf16[256,128]{1,0:T(8,128)(2,1)S(1)} %get-tuple-element.38), channel_id=1, source_target_pairs={{0,64},{32,96},{64,128},{96,160},{128,192},{160,224},{192,0},{224,... | collective-permute-start | bytes 196616 | tf_op jit(solution)/shard_map/ppermute | solution.py:297
  129.3 8.1 %collective-permute-start.8 = (bf16[256,128]{1,0:T(8,128)(2,1)S(1)}, bf16[256,128]{1,0:T(8,128)(2,1)S(1)}, u32[]{:S(2)}, u32[]{:S(2)}) collective-permute-start(bf16[256,128]{1,0:T(8,128)(2,1)S(1)} %get-tuple-element.39), channel_id=1, source_target_pairs={{0,192},{32,224},{64,0},{96,32},{128,64},{160,96},{192,128},{224,1... | collective-permute-start | bytes 196616 | tf_op jit(solution)/shard_map/ppermute | solution.py:297
  131.8 5.8 %collective-permute-start.9 = (bf16[256,128]{1,0:T(8,128)(2,1)S(1)}, bf16[256,128]{1,0:T(8,128)(2,1)S(1)}, u32[]{:S(2)}, u32[]{:S(2)}) collective-permute-start(bf16[256,128]{1,0:T(8,128)(2,1)S(1)} %get-tuple-element.40), channel_id=1, source_target_pairs={{0,32},{32,64},{64,96},{96,128},{128,160},{160,192},{192,224},{224... | collective-permute-start | bytes 196616 | tf_op jit(solution)/shard_map/ppermute | solution.py:297
  134.0 4.8 %collective-permute-start.10 = (bf16[256,128]{1,0:T(8,128)(2,1)S(1)}, bf16[256,128]{1,0:T(8,128)(2,1)S(1)}, u32[]{:S(2)}, u32[]{:S(2)}) collective-permute-start(bf16[256,128]{1,0:T(8,128)(2,1)S(1)} %get-tuple-element.41), channel_id=1, source_target_pairs={{0,224},{32,0},{64,32},{96,64},{128,96},{160,128},{192,160},{224,1... | collective-permute-start | bytes 196616 | tf_op jit(solution)/shard_map/ppermute | solution.py:297

commit v5 on v4

--- a/solution.py
+++ b/solution.py
@@ -31,7 +31,10 @@
     return jnp.concatenate([high, (block - high.astype(F32)).astype(BF16)], axis=0)
 
 
-def adjacency_kernel(count_ref, dst_ref, src_ref, weight_ref, adj_ref, inv_ref, flag_ref, sel_ref, buf, acc, sems):
+def setup_kernel(
+    count_ref, dst_hbm, src_hbm, x_hbm, weight_ref, pay_ref, adj_ref, inv_ref, flag_ref, sel_ref,
+    dst_ref, src_ref, x_ref, buf, acc, in_sems, out_sems, sems,
+):
     count = count_ref[0]
     slots = weight_ref.shape[0]
     groups = acc.shape[0]
@@ -40,6 +43,15 @@
         part = pl.ds(index * CHUNK, CHUNK)
         return pltpu.make_async_copy(weight_ref.at[part], buf.at[part], sems.at[index])
 
+    ins = [
+        pltpu.make_async_copy(source, target, in_sems.at[index])
+        for index, (source, target) in enumerate(((x_hbm, x_ref), (dst_hbm, dst_ref), (src_hbm, src_ref)))
+    ]
+    outs = [
+        pltpu.make_async_copy(x_ref, pay_ref.at[copy], out_sems.at[copy]) for copy in range(pay_ref.shape[0])
+    ]
+    for copy in ins:
+        copy.start()
     for index in range(slots // CHUNK):
 
         @pl.when(index * CHUNK < count)
@@ -49,6 +61,11 @@
     acc[...] = jnp.zeros_like(acc)
     for owner in range(groups):
         sel_ref[owner] = 0
+    ins[0].wait()
+    for copy in outs:
+        copy.start()
+    ins[1].wait()
+    ins[2].wait()
     for index in range(slots // CHUNK):
 
         @pl.when(index * CHUNK < count)
@@ -77,15 +94,7 @@
     for owner in range(groups):
         flags = jnp.where(row == owner, sel_ref[owner].astype(F32), flags)
     flag_ref[...] = flags.astype(BF16)
-
-
-def spread_kernel(x_ref, pay_ref, sems):
-    copies = [
-        pltpu.make_async_copy(x_ref, pay_ref.at[copy], sems.at[copy]) for copy in range(pay_ref.shape[0])
-    ]
-    for copy in copies:
-        copy.start()
-    for copy in copies:
+    for copy in outs:
         copy.wait()
 
 
@@ -119,9 +128,12 @@
 
 
 def activation_kernel(
-    place_ref, sel_ref, adj_ref, inv_ref, other_ref, z_ref, og_ref, x_ref, out_ref, gt_ref, pay_ref, x_same_ref
+    place_ref, sel_ref, adj_ref, inv_ref, own_ref, other_ref, z_ref, og_ref,
+    out_ref, gt_ref, pay_ref, mask_ref,
 ):
     core = place_ref[0]
+    me = place_ref[1]
+    rows = z_ref.shape[0]
     summed = jnp.zeros(z_ref.shape, F32)
     for chip in range(other_ref.shape[0]):
         owner = 2 * chip + 1 - core
@@ -136,17 +148,10 @@
         pay_ref[owner] = (spread[0:T] + spread[T:]).astype(BF16)
     out_ref[...] = (z * sig).astype(BF16)
     gt_ref[...] = grad.T.astype(BF16)
-
-
-def mask_kernel(place_ref, own_ref, other_ref, mask_ref):
-    core = place_ref[0]
-    me = place_ref[1]
-    flag_rows = mask_ref.shape[0]
-    start = own_ref.shape[1] - flag_rows
-    row = lax.broadcasted_iota(jnp.int32, (flag_rows, T), 0)
+    row = lax.broadcasted_iota(jnp.int32, mask_ref.shape, 0)
     for chip in range(own_ref.shape[0]):
         for ref, owner in ((own_ref, 2 * chip + core), (other_ref, 2 * chip + 1 - core)):
-            flags = ref[chip, start:, :].astype(F32)
+            flags = ref[chip, rows:, :].astype(F32)
             mask_ref[pl.ds(owner, 1), :] = jnp.sum(jnp.where(row == me, flags, 0.0), axis=0, keepdims=True)
 
 
@@ -172,21 +177,28 @@
         copy.wait()
 
 
-def weight_grad_kernel(place_ref, gt_ref, bt_ref, gt_pair_ref, bt_pair_ref, x_ref, x_pair_ref, own_ref, *pay_refs):
+def weight_grad_kernel(place_ref, gt_ref, bt_ref, x_ref, keep_ref, send_ref):
     core = place_ref[0]
     here = place_ref[2]
-    chips = len(pay_refs) + 1
+    chips = keep_ref.shape[0]
     left = jnp.concatenate([gt_ref[...], bt_ref[...]], axis=0)
-    left_pair = jnp.concatenate([gt_pair_ref[...], bt_pair_ref[...]], axis=0)
-    for step, pay_ref in zip(far_first(chips) + (0,), pay_refs + (own_ref,)):
-        owner = 2 * lax.rem(here + step, chips) + core
-        total = dot(left, x_ref[owner]) + dot(left_pair, x_pair_ref[owner])
-        pay_ref[0:T] = total[0:T].astype(pay_ref.dtype)
-        pay_ref[T:] = (total[T : 2 * T] + total[2 * T :]).astype(pay_ref.dtype)
-
-
-def weight_sum_kernel(own_ref, *refs):
-    parts, (self_ref, neigh_ref) = refs[:-2], refs[-2:]
+    for slot, step in enumerate(far_first(chips) + (0,)):
+        chip = lax.rem(here + step, chips)
+        kept = dot(left, x_ref[2 * chip + core])
+        sent = dot(left, x_ref[2 * chip + 1 - core])
+        keep_ref[slot, 0:T] = kept[0:T]
+        keep_ref[slot, T:] = kept[T : 2 * T] + kept[2 * T :]
+        send_ref[slot, 0:T] = sent[0:T].astype(BF16)
+        send_ref[slot, T:] = (sent[T : 2 * T] + sent[2 * T :]).astype(BF16)
+
+
+def pair_kernel(keep_ref, came_ref, *pay_refs):
+    for slot, pay_ref in enumerate(pay_refs):
+        pay_ref[...] = (keep_ref[slot] + came_ref[slot].astype(F32)).astype(pay_ref.dtype)
+
+
+def weight_sum_kernel(own_ref, done_ref, *refs):
+    parts, (self_ref, neigh_ref, same_ref) = refs[:-3], refs[-3:]
     total = own_ref[...]
     for part in parts:
         total = total + part[...].astype(F32)
@@ -231,28 +243,31 @@
     place = jnp.stack([core, here * 2 + core, here]).astype(jnp.int32)
     swap = [(0, 1), (1, 0)]
 
-    (x_pay,) = call(
-        spread_kernel,
-        (features,),
-        [((parts, rows, T), BF16)],
-        in_specs=[HBM],
-        out_specs=[HBM],
-        scratch=[pltpu.SemaphoreType.DMA((parts,))],
-    )
-    x_all = lax.all_to_all(x_pay, ("y", "x"), 0, 0, tiled=True)
-    adj, inverse, flags, sel = call(
-        adjacency_kernel,
-        (tile_count, tile_dst, tile_src, tile_weight[0]),
-        [((groups, rows, T), BF16), ((rows, T), F32), ((groups, T), BF16), ((groups,), jnp.int32)],
-        in_specs=[SMEM, SMEM, SMEM, HBM],
-        out_specs=[VMEM, VMEM, VMEM, SMEM],
+    x_pay, adj, inverse, flags, sel = call(
+        setup_kernel,
+        (tile_count, tile_dst, tile_src, features, tile_weight[0]),
+        [
+            ((parts, rows, T), BF16),
+            ((groups, rows, T), BF16),
+            ((rows, T), F32),
+            ((groups, T), BF16),
+            ((groups,), jnp.int32),
+        ],
+        in_specs=[SMEM, HBM, HBM, HBM, HBM],
+        out_specs=[HBM, VMEM, VMEM, VMEM, SMEM],
         scratch=[
+            pltpu.SMEM(tile_dst.shape, jnp.int32),
+            pltpu.SMEM(tile_src.shape, jnp.int32),
+            pltpu.VMEM((rows, T), BF16),
             pltpu.VMEM((slots, T, T), jnp.int32),
             pltpu.VMEM((groups, rows, T), jnp.int32),
+            pltpu.SemaphoreType.DMA((3,)),
+            pltpu.SemaphoreType.DMA((parts,)),
             pltpu.SemaphoreType.DMA((slots // CHUNK,)),
         ],
         limit=20,
     )
+    x_all = lax.all_to_all(x_pay, ("y", "x"), 0, 0, tiled=True)
     (y_pay,) = call(
         neighbour_product_kernel, (x_all, w_neigh, flags), [((chips, rows + groups, T), BF16)]
     )
@@ -264,20 +279,13 @@
         [((rows, T), F32)],
         in_specs=[SMEM, SMEM] + [VMEM] * 5,
     )
-    output, gt, c_pay, x_late = call(
+    output, gt, c_pay, mask = call(
         activation_kernel,
-        (place, sel, adj, inverse, y_other, z_half, out_grad, x_all),
-        [((rows, T), BF16), ((T, rows), BF16), ((groups, T, T), BF16), (x_all.shape, BF16)],
-        in_specs=[SMEM, SMEM] + [VMEM] * 5 + [ANY],
-        out_specs=[VMEM] * 3 + [ANY],
-        aliases={7: 3},
+        (place, sel, adj, inverse, y_own, y_other, z_half, out_grad),
+        [((rows, T), BF16), ((T, rows), BF16), ((groups, T, T), BF16), ((groups, T), F32)],
+        in_specs=[SMEM, SMEM] + [VMEM] * 6,
     )
     c_all = lax.all_to_all(c_pay, ("z", "c"), 0, 0, tiled=True)
-    gt_pair = lax.ppermute(gt, "c", swap)
-    x_pair = lax.ppermute(x_late, "c", swap)
-    (mask,) = call(
-        mask_kernel, (place, y_own, y_other), [((groups, T), F32)], in_specs=[SMEM, VMEM, VMEM]
-    )
     bt, p_pay = call(
         feature_grad_kernel,
         (c_all, mask, gt, w_self, w_neigh),
@@ -285,20 +293,30 @@
         out_specs=[VMEM, HBM],
         scratch=[pltpu.VMEM((parts, T, rows), BF16), pltpu.SemaphoreType.DMA((parts,))],
     )
-    bt_pair = lax.ppermute(bt, "c", swap)
     p_all = lax.all_to_all(p_pay, ("y", "x"), 0, 0, tiled=True)
-    own, *w_pay = call(
+    keep, send = call(
         weight_grad_kernel,
-        (place, gt, bt, gt_pair, bt_pair, x_late, x_pair),
-        [((2 * T, T), F32)] + [((2 * T, T), BF16)] * (chips - 1),
-        in_specs=[SMEM] + [VMEM] * 6,
+        (place, gt, bt, x_all),
+        [((chips, 2 * T, T), F32), ((chips, 2 * T, T), BF16)],
+        in_specs=[SMEM] + [VMEM] * 3,
+    )
+    came = lax.ppermute(send, "c", swap)
+    *w_pay, own = call(
+        pair_kernel, (keep, came), [((2 * T, T), BF16)] * (chips - 1) + [((2 * T, T), F32)]
     )
     w_came = [
         lax.ppermute(block, "z", [(chip, (chip + step) % chips) for chip in range(chips)])
         for step, block in zip(far_first(chips), w_pay)
     ]
     (grad_features,) = call(sum_kernel, (p_all,), [((rows, T), BF16)])
-    grad_self, grad_neigh = call(weight_sum_kernel, (own, *w_came), [((T, T), F32)] * 2)
+    grad_self, grad_neigh, grad_features = call(
+        weight_sum_kernel,
+        (own, grad_features, *w_came),
+        [((T, T), F32), ((T, T), F32), ((rows, T), BF16)],
+        in_specs=[VMEM, ANY] + [VMEM] * (chips - 1),
+        out_specs=[VMEM, VMEM, ANY],
+        aliases={1: 2},
+    )
     return output, grad_features, grad_self, grad_neigh
 
 

time: 141 us -> 107 us (0.76)
  blocking collectives: 22.6 us -> 67.3 us
  Pallas kernels: 45.1 us -> 12.2 us
  waiting for transfers between devices: 31.6 us -> 3.9 us
  starting transfers between devices: 34.4 us -> 21.6 us
  local copies, waits for them, and re-layouts: 5.24 us -> 0.02 us
    all_to_all x0 -> x2, blocking collectives: none -> 43.9 us  [the longest x1 23.8 us: per_device(): x_all = lax.all_to_all(x_pay, ('y', 'x'), 0, 0, tiled=True)]
    pallas_call x10 -> x9, Pallas kernels: 45.1 us -> 12.2 us  [call(): pl.pallas_call(kernel, out_shape=shapes, in_specs=in_specs or [VMEM] * le...]
    all_to_all x2 -> x0, waiting for transfers between devices: 27.9 us -> none  [the longest x1 16.5 us: per_device(): c_all = lax.all_to_all(c_pay, ('z', 'c'), 0, 0, tiled=True)]
    all_to_all x2 -> x0, starting transfers between devices: 11.1 us -> none  [the longest x1 7.6 us: per_device(): x_all = lax.all_to_all(x_pay, ('y', 'x'), 0, 0, tiled=True)]
    unnamed x16 -> x8, local copies, waits for them, and re-layouts: 5.24 us -> 0.02 us
  transfers between devices with their start and end apart: 14 -> 10, of which waited for: 7 -> 4; matrix products, arithmetic and copies ran while one was open for 0% -> 0% of each run, Pallas kernels for 6% -> 3%
where the time goes in v5:
time: 107 us
  blocking collectives  67.3 us (63%)
  starting transfers between devices  21.6 us (20%)
  Pallas kernels  12.2 us (11%)
  waiting for transfers between devices  3.9 us (4%)
  between operations  1.45 us (1%)
    all_to_all x1, blocking collectives, per_device(): x_all = lax.all_to_all(x_pay, ('y', 'x'), 0, 0, tiled=True)  23.8 us
    all_to_all x1, blocking collectives, per_device(): y_own = lax.all_to_all(y_pay, 'z', 0, 0, tiled=True)  23.4 us
    all_to_all x1, blocking collectives, per_device(): c_all = lax.all_to_all(c_pay, ('z', 'c'), 0, 0, tiled=True)  20.2 us
    ppermute x7, starting transfers between devices, per_device(): lax.ppermute(block, 'z', [(chip, (chip + step) % chips) for chip in range...  13.8 us
    pallas_call x9, Pallas kernels, call(): pl.pallas_call(kernel, out_shape=shapes, in_specs=in_specs or [VMEM] * le...  12.2 us
    ppermute x1, starting transfers between devices, per_device(): y_other = lax.ppermute(y_own, 'c', swap)  3.98 us
    all_to_all x1, starting transfers between devices, per_device(): p_all = lax.all_to_all(p_pay, ('y', 'x'), 0, 0, tiled=True)  3.66 us
  transfers between devices with their start and end apart: 10, of which 4 were waited for; matrix products, arithmetic and copies ran while one was open for 0% of the time, Pallas kernels for 3%

profile of v5, /device:TPU:1, one launch (start us, length us, event | category | flops | bytes accessed | tf_op | source)
XLA Modules:
  0.0 106.5 jit_solution(7666002386698973591)
XLA Ops:
  0.6 0.0 copy-start.1
  1.4 3.3 %setup_kernel.1 = (bf16[16,256,128]{2,1,0:T(8,128)(2,1)}, bf16[16,256,128]{2,1,0:T(8,128)(2,1)S(1)}, f32[256,128]{1,0:T(8,128)S(1)}, bf16[16,128]{1,0:T(8,128)(2,1)S(1)}, s32[16]{0:T(128)S(1)}) custom-call(s32[1]{0:T(128)S(6)} %copy.14.count_ref, s32[1,80]{1,0:T(1,128)} %dst_hbm.1, s32[1,80]{1,0:T(1,128)} %src_hbm.1, bf16[256,128]{1,0:T(8,128)(2,1)} %x_hbm.1, ...), custom_call_target="tpu_custom_call" | custom-call | tf_op jit(solution)/shard_map/setup_kernel/pallas_call | solution.py:225
  4.7 0.0 copy-start.3
  4.7 23.8 %all_to_all.20.x_ref = bf16[16,256,128]{2,1,0:T(8,128)(2,1)S(1)} all-to-all(bf16[16,256,128]{2,1,0:T(8,128)(2,1)} %get-tuple-element.31), channel_id=1, replica_groups=mesh['z'=8,'c'=2,'y'=4,'x'=4] {'y','x'}, dimensions={0} | all-to-all | bytes 2097152 | tf_op jit(solution)/shard_map/all_to_all | solution.py:270
  28.5 0.4 neighbour_product_kernel.1
  28.9 23.4 %all_to_all.21.own_ref = bf16[8,272,128]{2,1,0:T(8,128)(2,1)S(1)} all-to-all(bf16[8,272,128]{2,1,0:T(8,128)(2,1)S(1)} %neighbour_product_kernel.1), channel_id=1, replica_groups=mesh['z'=8,'c'=2,'y'=4,'x'=4] {'z'}, dimensions={0} | all-to-all | bytes 1114112 | tf_op jit(solution)/shard_map/all_to_all | solution.py:274
  52.3 4.0 %collective-permute-start = (bf16[8,272,128]{2,1,0:T(8,128)(2,1)S(1)}, bf16[8,272,128]{2,1,0:T(8,128)(2,1)}, u32[]{:S(2)}, u32[]{:S(2)}) collective-permute-start(bf16[8,272,128]{2,1,0:T(8,128)(2,1)S(1)} %all_to_all.21.own_ref), channel_id=1, source_target_pairs={{0,16},{16,0},{1,17},{17,1},{2,18},{18,2},{3,19},{19,3},{4,20},{20... | collective-permute-start | bytes 1671176 | tf_op jit(solution)/shard_map/ppermute | solution.py:275
  56.3 0.1 pad_add_fusion.place_ref
  56.4 1.1 %half_kernel.1.z_ref = f32[256,128]{1,0:T(8,128)S(1)} custom-call(s32[3]{0:T(128)S(1)} %pad_add_fusion.place_ref, s32[16]{0:T(128)S(1)} %get-tuple-element.28.sel_ref, bf16[16,256,128]{2,1,0:T(8,128)(2,1)S(1)} %all_to_all.20.x_ref, bf16[2048,128]{1,0:T(8,128)(2,1)S(1)} %copy-done, bf16[16,256,128]{2,1,0:T(8,128)(2,1)S(1)} %get-tuple-element.29.adj_ref, ...), custom_call_target="tpu_custom_call" | custom-call | tf_op jit(solution)/shard_map/half_kernel/pallas_call | solution.py:225
  57.5 0.5 collective-permute-done.other_ref
  58.0 2.4 %activation_kernel.1 = (bf16[256,128]{1,0:T(8,128)(2,1)}, bf16[128,256]{1,0:T(8,128)(2,1)S(1)}, bf16[16,128,128]{2,1,0:T(8,128)(2,1)S(1)}, f32[16,128]{1,0:T(8,128)S(1)}) custom-call(s32[3]{0:T(128)S(1)} %pad_add_fusion.place_ref, s32[16]{0:T(128)S(1)} %get-tuple-element.28.sel_ref, bf16[16,256,128]{2,1,0:T(8,128)(2,1)S(1)} %get-tuple-element.29.adj_ref, ...), custom_call_target="tpu_custom_call" | custom-call | tf_op jit(solution)/shard_map/activation_kernel/pallas_call | solution.py:225
  60.4 20.2 %all_to_all.22.came_ref = bf16[16,128,128]{2,1,0:T(8,128)(2,1)S(1)} all-to-all(bf16[16,128,128]{2,1,0:T(8,128)(2,1)S(1)} %get-tuple-element.35), channel_id=1, replica_groups=mesh['z'=8,'c'=2,'y'=4,'x'=4] {'z','c'}, dimensions={0} | all-to-all | bytes 1048576 | tf_op jit(solution)/shard_map/all_to_all | solution.py:288
  80.6 1.7 %feature_grad_kernel.1 = (bf16[256,256]{1,0:T(8,128)(2,1)S(1)}, bf16[16,128,256]{2,1,0:T(8,128)(2,1)}) custom-call(bf16[16,128,128]{2,1,0:T(8,128)(2,1)S(1)} %all_to_all.22.came_ref, f32[16,128]{1,0:T(8,128)S(1)} %get-tuple-element.36.mask_ref, bf16[128,256]{1,0:T(8,128)(2,1)S(1)} %get-tuple-element.34.gt_ref, bf16[2048,128]{1,0:T(8,128)(2,1)S(1)} %copy-done, ...), custom_call_target="tpu_custom_call" | custom-call | tf_op jit(solution)/shard_map/feature_grad_kernel/pallas_call | solution.py:225
  82.3 3.7 %all-to-all-start.3 = ((bf16[16,128,256]{2,1,0:T(8,128)(2,1)}), bf16[16,128,256]{2,1,0:T(8,128)(2,1)S(1)}, u32[]{:S(2)}, u32[]{:S(2)}) async-start(bf16[16,128,256]{2,1,0:T(8,128)(2,1)} %get-tuple-element.41), calls=%async_computation.3 | async-start | bytes 2097152 | tf_op jit(solution)/shard_map/all_to_all | solution.py:296
  85.9 1.5 %weight_grad_kernel.1 = (f32[8,256,128]{2,1,0:T(8,128)S(1)}, bf16[8,256,128]{2,1,0:T(8,128)(2,1)S(1)}) custom-call(s32[3]{0:T(128)S(1)} %pad_add_fusion.place_ref, bf16[128,256]{1,0:T(8,128)(2,1)S(1)} %get-tuple-element.34.gt_ref, bf16[256,256]{1,0:T(8,128)(2,1)S(1)} %get-tuple-element.37.bt_ref, bf16[16,256,128]{2,1,0:T(8,128)(2,1)S(1)} %all_to_all.20.x_ref), custom_call_target="tpu_custom_call" | custom-call | tf_op jit(solution)/shard_map/weight_grad_kernel/pallas_call | solution.py:225
  87.5 0.1 collective-permute-start.1
  87.6 1.9 %collective-permute-done.1.came_ref = bf16[8,256,128]{2,1,0:T(8,128)(2,1)S(1)} collective-permute-done((bf16[8,256,128]{2,1,0:T(8,128)(2,1)S(1)}, bf16[8,256,128]{2,1,0:T(8,128)(2,1)S(1)}, u32[]{:S(2)}, u32[]{:S(2)}) %collective-permute-start.1) | collective-permute-done | bytes 524320 | tf_op jit(solution)/shard_map/ppermute | solution.py:303
  89.5 0.1 pair_kernel.1
  89.6 1.2 %collective-permute-start.2 = (bf16[256,128]{1,0:T(8,128)(2,1)S(1)}, bf16[256,128]{1,0:T(8,128)(2,1)S(1)}, u32[]{:S(2)}, u32[]{:S(2)}) collective-permute-start(bf16[256,128]{1,0:T(8,128)(2,1)S(1)} %get-tuple-element.42), channel_id=1, source_target_pairs={{0,128},{32,160},{64,192},{96,224},{128,0},{160,32},{192,64},{224,... | collective-permute-start | bytes 196616 | tf_op jit(solution)/shard_map/ppermute | solution.py:308
  90.7 1.1 %collective-permute-start.3 = (bf16[256,128]{1,0:T(8,128)(2,1)S(1)}, bf16[256,128]{1,0:T(8,128)(2,1)S(1)}, u32[]{:S(2)}, u32[]{:S(2)}) collective-permute-start(bf16[256,128]{1,0:T(8,128)(2,1)S(1)} %get-tuple-element.43), channel_id=1, source_target_pairs={{0,96},{32,128},{64,160},{96,192},{128,224},{160,0},{192,32},{224,... | collective-permute-start | bytes 196616 | tf_op jit(solution)/shard_map/ppermute | solution.py:308
  91.8 3.4 %collective-permute-start.4 = (bf16[256,128]{1,0:T(8,128)(2,1)S(1)}, bf16[256,128]{1,0:T(8,128)(2,1)S(1)}, u32[]{:S(2)}, u32[]{:S(2)}) collective-permute-start(bf16[256,128]{1,0:T(8,128)(2,1)S(1)} %get-tuple-element.44), channel_id=1, source_target_pairs={{0,160},{32,192},{64,224},{96,0},{128,32},{160,64},{192,96},{224,1... | collective-permute-start | bytes 196616 | tf_op jit(solution)/shard_map/ppermute | solution.py:308
  95.2 1.3 %collective-permute-start.5 = (bf16[256,128]{1,0:T(8,128)(2,1)S(1)}, bf16[256,128]{1,0:T(8,128)(2,1)S(1)}, u32[]{:S(2)}, u32[]{:S(2)}) collective-permute-start(bf16[256,128]{1,0:T(8,128)(2,1)S(1)} %get-tuple-element.45), channel_id=1, source_target_pairs={{0,64},{32,96},{64,128},{96,160},{128,192},{160,224},{192,0},{224,... | collective-permute-start | bytes 196616 | tf_op jit(solution)/shard_map/ppermute | solution.py:308
  96.5 2.3 %collective-permute-start.6 = (bf16[256,128]{1,0:T(8,128)(2,1)S(1)}, bf16[256,128]{1,0:T(8,128)(2,1)S(1)}, u32[]{:S(2)}, u32[]{:S(2)}) collective-permute-start(bf16[256,128]{1,0:T(8,128)(2,1)S(1)} %get-tuple-element.46), channel_id=1, source_target_pairs={{0,192},{32,224},{64,0},{96,32},{128,64},{160,96},{192,128},{224,1... | collective-permute-start | bytes 196616 | tf_op jit(solution)/shard_map/ppermute | solution.py:308
  98.8 0.0 collective-permute-done.2.refs_0_
  98.8 1.2 %collective-permute-start.7 = (bf16[256,128]{1,0:T(8,128)(2,1)S(1)}, bf16[256,128]{1,0:T(8,128)(2,1)S(1)}, u32[]{:S(2)}, u32[]{:S(2)}) collective-permute-start(bf16[256,128]{1,0:T(8,128)(2,1)S(1)} %get-tuple-element.47), channel_id=1, source_target_pairs={{0,32},{32,64},{64,96},{96,128},{128,160},{160,192},{192,224},{224... | collective-permute-start | bytes 196616 | tf_op jit(solution)/shard_map/ppermute | solution.py:308
  100.0 1.0 collective-permute-done.3.refs_1_
  101.0 3.4 %collective-permute-start.8 = (bf16[256,128]{1,0:T(8,128)(2,1)S(1)}, bf16[256,128]{1,0:T(8,128)(2,1)S(1)}, u32[]{:S(2)}, u32[]{:S(2)}) collective-permute-start(bf16[256,128]{1,0:T(8,128)(2,1)S(1)} %get-tuple-element.48), channel_id=1, source_target_pairs={{0,224},{32,0},{64,32},{96,64},{128,96},{160,128},{192,160},{224,1... | collective-permute-start | bytes 196616 | tf_op jit(solution)/shard_map/ppermute | solution.py:308
  104.4 0.0 all-to-all-done.3.parts_ref
  104.4 0.8 sum_kernel.1.done_ref
  105.2 0.0 collective-permute-done.4.refs_2_
  105.3 0.5 collective-permute-done.8.refs_6_
  105.7 0.8 weight_sum_kernel.1
  (9 shorter events, 0.0 us)
Async XLA Ops:
  0.6 27.8 %copy-start.1 = (bf16[2048,128]{1,0:T(8,128)(2,1)S(1)}, bf16[2048,128]{1,0:T(8,128)(2,1)}, u32[]{:S(2)}) copy-start(bf16[2048,128]{1,0:T(8,128)(2,1)} %wn_ref.1) | copy-start | bytes 1572868
  1.3 55.0 %copy-start = (bf16[2048,128]{1,0:T(8,128)(2,1)S(1)}, bf16[2048,128]{1,0:T(8,128)(2,1)}, u32[]{:S(2)}) copy-start(bf16[2048,128]{1,0:T(8,128)(2,1)} %ws_ref.1) | copy-start | bytes 1572868
  4.7 53.3 %copy-start.3 = (bf16[256,128]{1,0:T(8,128)(2,1)S(1)}, bf16[256,128]{1,0:T(8,128)(2,1)}, u32[]{:S(2)}) copy-start(bf16[256,128]{1,0:T(8,128)(2,1)} %og_ref.1) | copy-start | bytes 196612
  52.3 5.7 %collective-permute-start = (bf16[8,272,128]{2,1,0:T(8,128)(2,1)S(1)}, bf16[8,272,128]{2,1,0:T(8,128)(2,1)}, u32[]{:S(2)}, u32[]{:S(2)}) collective-permute-start(bf16[8,272,128]{2,1,0:T(8,128)(2,1)S(1)} %all_to_all.21.own_ref), channel_id=1, source_target_pairs={{0,16},{16,0},{1,17},{17,1},{2,18},{18,2},{3,19},{19,3},{4,20},{20... | collective-permute-start | bytes 1671176 | tf_op jit(solution)/shard_map/ppermute | solution.py:275
  56.3 24.3 %copy-start.2 = (bf16[2048,128]{1,0:T(8,128)(2,1)S(1)}, bf16[2048,128]{1,0:T(8,128)(2,1)}, u32[]{:S(2)}) copy-start(bf16[2048,128]{1,0:T(8,128)(2,1)} %wn_ref.1) | copy-start | bytes 1572868
  82.3 22.1 %all-to-all-start.3 = ((bf16[16,128,256]{2,1,0:T(8,128)(2,1)}), bf16[16,128,256]{2,1,0:T(8,128)(2,1)S(1)}, u32[]{:S(2)}, u32[]{:S(2)}) async-start(bf16[16,128,256]{2,1,0:T(8,128)(2,1)} %get-tuple-element.41), calls=%async_computation.3 | async-start | bytes 2097152 | tf_op jit(solution)/shard_map/all_to_all | solution.py:296
  87.5 2.0 %collective-permute-start.1 = (bf16[8,256,128]{2,1,0:T(8,128)(2,1)S(1)}, bf16[8,256,128]{2,1,0:T(8,128)(2,1)S(1)}, u32[]{:S(2)}, u32[]{:S(2)}) collective-permute-start(bf16[8,256,128]{2,1,0:T(8,128)(2,1)S(1)} %get-tuple-element.39), channel_id=1, source_target_pairs={{0,16},{16,0},{1,17},{17,1},{2,18},{18,2},{3,19},{19,3},{4,20},{20... | collective-permute-start | bytes 1572872 | tf_op jit(solution)/shard_map/ppermute | solution.py:303
  89.6 9.2 %collective-permute-start.2 = (bf16[256,128]{1,0:T(8,128)(2,1)S(1)}, bf16[256,128]{1,0:T(8,128)(2,1)S(1)}, u32[]{:S(2)}, u32[]{:S(2)}) collective-permute-start(bf16[256,128]{1,0:T(8,128)(2,1)S(1)} %get-tuple-element.42), channel_id=1, source_target_pairs={{0,128},{32,160},{64,192},{96,224},{128,0},{160,32},{192,64},{224,... | collective-permute-start | bytes 196616 | tf_op jit(solution)/shard_map/ppermute | solution.py:308
  90.7 10.3 %collective-permute-start.3 = (bf16[256,128]{1,0:T(8,128)(2,1)S(1)}, bf16[256,128]{1,0:T(8,128)(2,1)S(1)}, u32[]{:S(2)}, u32[]{:S(2)}) collective-permute-start(bf16[256,128]{1,0:T(8,128)(2,1)S(1)} %get-tuple-element.43), channel_id=1, source_target_pairs={{0,96},{32,128},{64,160},{96,192},{128,224},{160,0},{192,32},{224,... | collective-permute-start | bytes 196616 | tf_op jit(solution)/shard_map/ppermute | solution.py:308
  91.8 13.4 %collective-permute-start.4 = (bf16[256,128]{1,0:T(8,128)(2,1)S(1)}, bf16[256,128]{1,0:T(8,128)(2,1)S(1)}, u32[]{:S(2)}, u32[]{:S(2)}) collective-permute-start(bf16[256,128]{1,0:T(8,128)(2,1)S(1)} %get-tuple-element.44), channel_id=1, source_target_pairs={{0,160},{32,192},{64,224},{96,0},{128,32},{160,64},{192,96},{224,1... | collective-permute-start | bytes 196616 | tf_op jit(solution)/shard_map/ppermute | solution.py:308
  95.2 10.1 %collective-permute-start.5 = (bf16[256,128]{1,0:T(8,128)(2,1)S(1)}, bf16[256,128]{1,0:T(8,128)(2,1)S(1)}, u32[]{:S(2)}, u32[]{:S(2)}) collective-permute-start(bf16[256,128]{1,0:T(8,128)(2,1)S(1)} %get-tuple-element.45), channel_id=1, source_target_pairs={{0,64},{32,96},{64,128},{96,160},{128,192},{160,224},{192,0},{224,... | collective-permute-start | bytes 196616 | tf_op jit(solution)/shard_map/ppermute | solution.py:308
  96.5 8.8 %collective-permute-start.6 = (bf16[256,128]{1,0:T(8,128)(2,1)S(1)}, bf16[256,128]{1,0:T(8,128)(2,1)S(1)}, u32[]{:S(2)}, u32[]{:S(2)}) collective-permute-start(bf16[256,128]{1,0:T(8,128)(2,1)S(1)} %get-tuple-element.46), channel_id=1, source_target_pairs={{0,192},{32,224},{64,0},{96,32},{128,64},{160,96},{192,128},{224,1... | collective-permute-start | bytes 196616 | tf_op jit(solution)/shard_map/ppermute | solution.py:308
  98.8 6.5 %collective-permute-start.7 = (bf16[256,128]{1,0:T(8,128)(2,1)S(1)}, bf16[256,128]{1,0:T(8,128)(2,1)S(1)}, u32[]{:S(2)}, u32[]{:S(2)}) collective-permute-start(bf16[256,128]{1,0:T(8,128)(2,1)S(1)} %get-tuple-element.47), channel_id=1, source_target_pairs={{0,32},{32,64},{64,96},{96,128},{128,160},{160,192},{192,224},{224... | collective-permute-start | bytes 196616 | tf_op jit(solution)/shard_map/ppermute | solution.py:308
  101.0 4.7 %collective-permute-start.8 = (bf16[256,128]{1,0:T(8,128)(2,1)S(1)}, bf16[256,128]{1,0:T(8,128)(2,1)S(1)}, u32[]{:S(2)}, u32[]{:S(2)}) collective-permute-start(bf16[256,128]{1,0:T(8,128)(2,1)S(1)} %get-tuple-element.48), channel_id=1, source_target_pairs={{0,224},{32,0},{64,32},{96,64},{128,96},{160,128},{192,160},{224,1... | collective-permute-start | bytes 196616 | tf_op jit(solution)/shard_map/ppermute | solution.py:308

commit v6 on v4

v6 whole, which is shorter than its diff:
```python
import functools

import jax
import jax.numpy as jnp
from jax import lax
from jax.experimental import pallas as pl
from jax.experimental.pallas import tpu as pltpu
from jax.sharding import Mesh, PartitionSpec as P

F32 = jnp.float32
BF16 = jnp.bfloat16
T = 128
CHUNK = 10
MIB = 1024 * 1024
VMEM = pl.BlockSpec(memory_space=pltpu.VMEM)
SMEM = pl.BlockSpec(memory_space=pltpu.SMEM)
ANY = pl.BlockSpec(memory_space=pl.ANY)
HBM = pl.BlockSpec(memory_space=pltpu.HBM)


def dot(a, b):
    return jnp.dot(a, b, preferred_element_type=F32)


def halves(block):
    high = block.astype(BF16)
    return jnp.concatenate([high, (block - high.astype(F32)).astype(BF16)], axis=0)


def add_halves(block):
    half = block.shape[0] // 2
    return block[0:half] + block[half:]


def spread_kernel(x_hbm, pay_ref, x_ref, in_sem, sems):
    copies = [
        pltpu.make_async_copy(x_ref, pay_ref.at[copy], sems.at[copy]) for copy in range(pay_ref.shape[0])
    ]
    came = pltpu.make_async_copy(x_hbm, x_ref, in_sem)
    came.start()
    came.wait()
    for copy in copies:
        copy.start()
    for copy in copies:
        copy.wait()


def neighbour_kernel(x_ref, w_ref, y_ref):
    total = dot(x_ref[0], w_ref[0:T, :])
    for part in range(1, x_ref.shape[0]):
        total = total + dot(x_ref[part], w_ref[part * T : (part + 1) * T, :])
    y_ref[...] = total.astype(BF16)


def self_kernel(x_ref, w_ref, z_ref):
    total = dot(x_ref[0], w_ref[0:T, :])
    for part in range(1, x_ref.shape[0]):
        total = total + dot(x_ref[part], w_ref[part * T : (part + 1) * T, :])
    z_ref[...] = total


def pair_kernel(place_ref, y_ref, y_pair_ref, pair_ref):
    core = place_ref[0]
    pair_ref[core] = y_ref[...]
    pair_ref[1 - core] = y_pair_ref[...]


def adjacency_kernel(
    count_ref, dst_hbm, src_hbm, weight_ref, adj_ref, inv_ref, sel_ref, dst_ref, src_ref, buf, acc, in_sems, sems
):
    count = count_ref[0]
    slots = weight_ref.shape[0]
    groups = acc.shape[0]

    def chunk_copy(index):
        part = pl.ds(index * CHUNK, CHUNK)
        return pltpu.make_async_copy(weight_ref.at[part], buf.at[part], sems.at[index])

    ins = [
        pltpu.make_async_copy(source, target, in_sems.at[index])
        for index, (source, target) in enumerate(((dst_hbm, dst_ref), (src_hbm, src_ref)))
    ]
    for copy in ins:
        copy.start()
    for index in range(slots // CHUNK):

        @pl.when(index * CHUNK < count)
        def _():
            chunk_copy(index).start()

    acc[...] = jnp.zeros_like(acc)
    for owner in range(groups):
        sel_ref[owner] = 0
    for copy in ins:
        copy.wait()
    for index in range(slots // CHUNK):

        @pl.when(index * CHUNK < count)
        def _():
            chunk_copy(index).wait()

            def add_tile(slot, carry):
                source = src_ref[0, slot]
                owner = source // 2
                sel_ref[owner] = source - 2 * owner
                rows = pl.ds(pl.multiple_of(dst_ref[0, slot] * T, T), T)
                acc[owner, rows, :] = acc[owner, rows, :] + buf[slot]
                return carry

            lax.fori_loop(index * CHUNK, jnp.minimum(count, (index + 1) * CHUNK), add_tile, 0)

    total = acc[0]
    for owner in range(groups):
        if owner > 0:
            total = total + acc[owner]
        adj_ref[owner] = acc[owner].astype(F32).astype(BF16)
    degree = jnp.sum(total.astype(F32), axis=1, keepdims=True)
    inv_ref[...] = jnp.broadcast_to(1.0 / jnp.maximum(degree, 1.0), inv_ref.shape)


def chip_at(place_ref, step):
    chips = 8
    return lax.rem(place_ref[1] + step + chips, chips)


def aggregate_kernel(
    place_ref, sel_ref, sel_pair_ref, adj_ref, adj_pair_ref, pair_ref, one_ref, two_ref, three_ref, far_ref,
    mine_ref, theirs_ref,
):
    core, here, way = place_ref[0], place_ref[1], place_ref[2]
    sources = []
    for step, ref in ((1, one_ref), (2, two_ref), (3, three_ref)):
        chip = chip_at(place_ref, -step * way)
        sources += [(ref.at[side], 2 * chip + side) for side in range(2)]
    sources.append((far_ref, 2 * chip_at(place_ref, 4) + core))
    local = [(pair_ref.at[side], 2 * here + side) for side in range(2)]

    def summed(adj, sel, tiles):
        total = jnp.zeros(mine_ref.shape, F32)
        for ref, owner in tiles:
            total = total + dot(adj[owner], ref[pl.ds(pl.multiple_of(sel[owner] * T, T), T), :])
        return total

    theirs_ref[...] = summed(adj_pair_ref, sel_pair_ref, sources)
    mine_ref[...] = summed(adj_ref, sel_ref, sources + local)


def activation_kernel(inv_ref, mine_ref, came_ref, z_ref, og_ref, out_ref, both_ref):
    inverse = inv_ref[...]
    z = z_ref[...] + inverse * (mine_ref[...] + came_ref[...])
    sig = 1.0 / (1.0 + jnp.exp(-z))
    out_ref[...] = (z * sig).astype(BF16)
    grad = (og_ref[...].astype(F32) * sig * (1.0 + z * (1.0 - sig))).astype(BF16).astype(F32)
    both_ref[0:T, :] = grad.T.astype(BF16)
    both_ref[T:, :] = halves((grad * inverse).T)


def targets(place_ref, one_ref, two_ref, three_ref, far_ref, own_ref):
    core, here, way = place_ref[0], place_ref[1], place_ref[2]
    places = [(far_ref, 2 * chip_at(place_ref, 4) + core)]
    for step, ref in ((3, three_ref), (2, two_ref), (1, one_ref)):
        chip = chip_at(place_ref, step * way)
        places += [(ref.at[side], 2 * chip + side) for side in range(2)]
    places.append((own_ref, 2 * here + core))
    return places


def transpose_kernel(
    place_ref, sel_ref, sel_pair_ref, adj_ref, adj_pair_ref, both_ref, both_pair_ref, x_ref, *out_refs
):
    left = both_ref[T:, :]
    left_pair = both_pair_ref[T:, :]
    for ref, owner in targets(place_ref, *out_refs[:-1]):
        ours = add_halves(dot(left, adj_ref[owner]))
        theirs = add_halves(dot(left_pair, adj_pair_ref[owner]))
        ours_high = sel_ref[owner] == 1
        theirs_high = sel_pair_ref[owner] == 1
        low = jnp.where(ours_high, 0.0, ours) + jnp.where(theirs_high, 0.0, theirs)
        high = jnp.where(ours_high, ours, 0.0) + jnp.where(theirs_high, theirs, 0.0)
        ref[:, 0:T] = low.astype(ref.dtype)
        ref[:, T:] = high.astype(ref.dtype)


def weight_grad_kernel(place_ref, both_ref, both_pair_ref, bt_ref, x_ref, x_pair_ref, *out_refs):
    left = jnp.concatenate([both_ref[0:T, :], bt_ref[0]], axis=0)
    left_pair = jnp.concatenate([both_pair_ref[0:T, :], bt_ref[1]], axis=0)
    for ref, owner in targets(place_ref, *out_refs):
        total = dot(left, x_ref[owner]) + dot(left_pair, x_pair_ref[owner])
        ref[0:T] = total[0:T].astype(ref.dtype)
        ref[T:] = add_halves(total[T:]).astype(ref.dtype)


def fold_kernel(place_ref, one_ref, two_ref, three_ref, far_ref, own_ref, fold_ref):
    core = place_ref[0]
    mine = own_ref[...] + far_ref[...].astype(F32)
    theirs = jnp.zeros(own_ref.shape, F32)
    for ref in (one_ref, two_ref, three_ref):
        mine = mine + ref[core].astype(F32)
        theirs = theirs + ref[1 - core].astype(F32)
    fold_ref[0] = mine
    fold_ref[1] = theirs


def feature_grad_kernel(fold_ref, came_ref, both_ref, ws_ref, wn_ref, bt_ref, pay_ref, buf, sems):
    split = halves(fold_ref[0] + came_ref[1])
    bt_ref[0] = split
    bt_ref[1] = halves(fold_ref[1] + came_ref[0])
    bt = split[0:T]
    gt = both_ref[0:T, :]
    copies = []
    for part in range(pay_ref.shape[0]):
        span = slice(part * T, (part + 1) * T)
        buf[part] = (dot(ws_ref[span, :], gt) + dot(wn_ref[span, :], bt)).astype(BF16)
        copies.append(pltpu.make_async_copy(buf.at[part], pay_ref.at[part], sems.at[part]))
        copies[-1].start()
    for copy in copies:
        copy.wait()


def sum_kernel(parts_ref, out_ref):
    total = parts_ref[0].astype(F32)
    for part in range(1, parts_ref.shape[0]):
        total = total + parts_ref[part].astype(F32)
    out_ref[...] = total.T.astype(out_ref.dtype)


def last_kernel(fold_ref, came_ref, done_ref, self_ref, neigh_ref, same_ref):
    total = fold_ref[0] + came_ref[1]
    self_ref[...] = total[0:T].T
    neigh_ref[...] = total[T:].T


def call(kernel, ins, outs, in_specs=None, out_specs=None, scratch=(), limit=12, aliases=None):
    shapes = tuple(
        pltpu.HBM(shape, dtype) if spec is HBM else jax.ShapeDtypeStruct(shape, dtype)
        for (shape, dtype), spec in zip(outs, out_specs or [VMEM] * len(outs))
    )
    ins = [
        pltpu.with_memory_space_constraint(value, pltpu.HBM) if spec is HBM else value
        for value, spec in zip(ins, in_specs or [VMEM] * len(ins))
    ]
    return pl.pallas_call(
        kernel,
        out_shape=shapes,
        in_specs=in_specs or [VMEM] * len(ins),
        out_specs=tuple(out_specs or [VMEM] * len(outs)),
        scratch_shapes=list(scratch),
        input_output_aliases=aliases or {},
        compiler_params=pltpu.CompilerParams(vmem_limit_bytes=limit * MIB),
        name=kernel.__name__,
    )(*ins)


def swap(value):
    return lax.ppermute(value, "c", [(0, 1), (1, 0)])


def along(value, step):
    pairs = [(2 * chip, 2 * ((chip + step) % 8)) for chip in range(8)]
    pairs += [(2 * chip + 1, 2 * ((chip - step) % 8) + 1) for chip in range(8)]
    return lax.ppermute(value, ("z", "c"), pairs)


def exchange(one, two, three, far):
    far = along(far, 4)
    three, two, one = along(three, 3), along(two, 2), along(one, 1)
    return one, two, three, far


def exchange_shapes(shape):
    return [((2,) + shape, BF16)] * 3 + [(shape, BF16), (shape, F32)]


def per_device(features, w_self, w_neigh, out_grad, tile_count, tile_dst, tile_src, tile_weight, chips, parts):
    rows = features.shape[0]
    groups = 2 * chips
    slots = tile_weight.shape[1]
    core = lax.axis_index("c")
    place = jnp.stack([core, lax.axis_index("z"), 1 - 2 * core]).astype(jnp.int32)

    (x_pay,) = call(
        spread_kernel,
        (features,),
        [((parts, rows, T), BF16)],
        in_specs=[HBM],
        out_specs=[HBM],
        scratch=[pltpu.VMEM((rows, T), BF16), pltpu.SemaphoreType.DMA, pltpu.SemaphoreType.DMA((parts,))],
    )
    x_all = lax.all_to_all(x_pay, "f", 0, 0, tiled=True)
    (y,) = call(neighbour_kernel, (x_all, w_neigh), [((rows, T), BF16)])
    (pair,) = call(pair_kernel, (place, y, swap(y)), [((2, rows, T), BF16)], in_specs=[SMEM, VMEM, VMEM])
    y_came = exchange(pair, pair, pair, y)
    adj, inverse, sel = call(
        adjacency_kernel,
        (tile_count, tile_dst, tile_src, tile_weight[0]),
        [((groups, rows, T), BF16), ((rows, T), F32), ((groups,), jnp.int32)],
        in_specs=[SMEM, HBM, HBM, HBM],
        out_specs=[VMEM, VMEM, SMEM],
        scratch=[
            pltpu.SMEM(tile_dst.shape, jnp.int32),
            pltpu.SMEM(tile_src.shape, jnp.int32),
            pltpu.VMEM((slots, T, T), jnp.int32),
            pltpu.VMEM((groups, rows, T), jnp.int32),
            pltpu.SemaphoreType.DMA((2,)),
            pltpu.SemaphoreType.DMA((slots // CHUNK,)),
        ],
        limit=20,
    )
    adj_pair, sel_pair = swap(adj), swap(sel)
    (z_self,) = call(self_kernel, (x_all, w_self), [((rows, T), F32)])
    scalars = [SMEM] * 3
    mine, theirs = call(
        aggregate_kernel,
        (place, sel, sel_pair, adj, adj_pair, pair, *y_came),
        [((rows, T), F32)] * 2,
        in_specs=scalars + [VMEM] * 7,
    )
    output, both = call(
        activation_kernel,
        (inverse, mine, swap(theirs), z_self, out_grad),
        [((rows, T), BF16), ((3 * T, rows), BF16)],
    )
    both_pair = swap(both)

    *sends, own, x_late = call(
        transpose_kernel,
        (place, sel, sel_pair, adj, adj_pair, both, both_pair, x_all),
        exchange_shapes((T, rows)) + [(x_all.shape, BF16)],
        in_specs=scalars + [VMEM] * 4 + [ANY],
        out_specs=[VMEM] * 5 + [ANY],
        aliases={7: 5},
    )
    x_pair = swap(x_late)
    b_came = exchange(*sends)
    (fold,) = call(
        fold_kernel, (place, *b_came, own), [((2, T, rows), F32)], in_specs=[SMEM] + [VMEM] * 5
    )
    bt, p_pay = call(
        feature_grad_kernel,
        (fold, swap(fold), both, w_self, w_neigh),
        [((2, 2 * T, rows), BF16), ((parts, T, rows), BF16)],
        out_specs=[VMEM, HBM],
        scratch=[pltpu.VMEM((parts, T, rows), BF16), pltpu.SemaphoreType.DMA((parts,))],
    )
    p_all = lax.all_to_all(p_pay, "f", 0, 0, tiled=True)
    *sends, own = call(
        weight_grad_kernel,
        (place, both, both_pair, bt, x_late, x_pair),
        exchange_shapes((2 * T, T)),
        in_specs=[SMEM] + [VMEM] * 5,
    )
    w_came = exchange(*sends)
    (fold,) = call(
        fold_kernel, (place, *w_came, own), [((2, 2 * T, T), F32)], in_specs=[SMEM] + [VMEM] * 5
    )
    (grad_features,) = call(sum_kernel, (p_all,), [((rows, T), BF16)])
    grad_self, grad_neigh, grad_features = call(
        last_kernel,
        (fold, swap(fold), grad_features),
        [((T, T), F32), ((T, T), F32), ((rows, T), BF16)],
        in_specs=[VMEM, VMEM, ANY],
        out_specs=[VMEM, VMEM, ANY],
        aliases={2: 2},
    )
    return output, grad_features, grad_self, grad_neigh


def solution(mesh):
    row_count, part_count = mesh.shape["rows"], mesh.shape["feat"]
    split = Mesh(mesh.devices.reshape(row_count // 2, 2, part_count), ("z", "c", "f"))
    rows = ("z", "c")
    return jax.shard_map(
        functools.partial(per_device, chips=row_count // 2, parts=part_count),
        mesh=split,
        in_specs=(
            P(rows, "f"),
            P(None, "f"),
            P(None, "f"),
            P(rows, "f"),
            P(rows),
            P(rows, None),
            P(rows, None),
            P(rows, None, None, None),
        ),
        out_specs=(P(rows, "f"),) * 4,
        check_vma=False,
    )
```

time: 141 us -> 109 us (0.77)
  Pallas kernels: 45.1 us -> 14.5 us
  blocking collectives: 22.6 us -> 0 us
  starting transfers between devices: 34.4 us -> 49.8 us
  waiting for transfers between devices: 31.6 us -> 38.8 us
  local copies, waits for them, and re-layouts: 5.24 us -> 3.73 us
    pallas_call x10 -> x14, Pallas kernels: 45.1 us -> 14.5 us  [call(): pl.pallas_call(kernel, out_shape=shapes, in_specs=in_specs or [VMEM] * le...]
    ppermute x11 -> x20, waiting for transfers between devices: 3.69 us -> 26.9 us  [the longest x12 22.3 us: along(): return lax.ppermute(value, ('z', 'c'), pairs)]
    all_to_all x1 -> x0, blocking collectives: 22.6 us -> none  [per_device(): y_own = lax.all_to_all(y_pay, 'z', 0, 0, tiled=True)]
    ppermute x11 -> x20, starting transfers between devices: 19.1 us -> 38.5 us  [the longest x12 25.6 us: along(): return lax.ppermute(value, ('z', 'c'), pairs)]
    all_to_all x3 -> x2, waiting for transfers between devices: 27.9 us -> 11.9 us  [the longest x1 11.9 us: per_device(): x_all = lax.all_to_all(x_pay, 'f', 0, 0, tiled=True)]
    all_to_all x3 -> x2, starting transfers between devices: 15.3 us -> 11.2 us  [the longest x1 7.6 us: per_device(): x_all = lax.all_to_all(x_pay, 'f', 0, 0, tiled=True)]
    unnamed x16 -> x14, local copies, waits for them, and re-layouts: 5.24 us -> 3.73 us
  transfers between devices with their start and end apart: 14 -> 22, of which waited for: 7 -> 9; matrix products, arithmetic and copies ran while one was open for 0% -> 0% of each run, Pallas kernels for 6% -> 8%
where the time goes in v6:
time: 109 us; the launch traced here: 108 us
  starting transfers between devices  49.8 us (46%)
  waiting for transfers between devices  38.8 us (36%)
  Pallas kernels  14.5 us (13%)
  local copies, waits for them, and re-layouts  3.73 us (3%)
  between operations  1.47 us (1%)
    ppermute x12, starting transfers between devices, along(): return lax.ppermute(value, ('z', 'c'), pairs)  25.6 us
    ppermute x12, waiting for transfers between devices, along(): return lax.ppermute(value, ('z', 'c'), pairs)  22.3 us
    pallas_call x14, Pallas kernels, call(): pl.pallas_call(kernel, out_shape=shapes, in_specs=in_specs or [VMEM] * le...  14.5 us
    ppermute x8, starting transfers between devices, swap(): return lax.ppermute(value, 'c', [(0, 1), (1, 0)])  13 us
    all_to_all x1, waiting for transfers between devices, per_device(): x_all = lax.all_to_all(x_pay, 'f', 0, 0, tiled=True)  11.9 us
    all_to_all x1, starting transfers between devices, per_device(): x_all = lax.all_to_all(x_pay, 'f', 0, 0, tiled=True)  7.6 us
    ppermute x8, waiting for transfers between devices, swap(): return lax.ppermute(value, 'c', [(0, 1), (1, 0)])  4.56 us
    unnamed x14, local copies, waits for them, and re-layouts  3.73 us
  transfers between devices with their start and end apart: 22, of which 9 were waited for; matrix products, arithmetic and copies ran while one was open for 0% of the time, Pallas kernels for 8%

profile of v6, /device:TPU:1, one launch (start us, length us, event | category | flops | bytes accessed | tf_op | source)
XLA Modules:
  0.0 108.3 jit_solution(2606476917782845535)
XLA Ops:
  0.6 2.0 %spread_kernel.1 = bf16[16,256,128]{2,1,0:T(8,128)(2,1)} custom-call(bf16[256,128]{1,0:T(8,128)(2,1)} %x_hbm.1), custom_call_target="tpu_custom_call" | custom-call | tf_op jit(solution)/shard_map/spread_kernel/pallas_call | solution.py:242
  2.6 7.6 %all-to-all-start = ((bf16[16,256,128]{2,1,0:T(8,128)(2,1)}), bf16[16,256,128]{2,1,0:T(8,128)(2,1)S(1)}, u32[]{:S(2)}, u32[]{:S(2)}) async-start(bf16[16,256,128]{2,1,0:T(8,128)(2,1)} %spread_kernel.1), calls=%async_computation | async-start | bytes 2097152 | tf_op jit(solution)/shard_map/all_to_all | solution.py:289
  10.9 2.3 %adjacency_kernel.1 = (bf16[16,256,128]{2,1,0:T(8,128)(2,1)S(1)}, f32[256,128]{1,0:T(8,128)S(1)}, s32[16]{0:T(128)S(1)}) custom-call(s32[1]{0:T(128)S(6)} %copy.16.count_ref, s32[1,80]{1,0:T(1,128)} %dst_hbm.1, s32[1,80]{1,0:T(1,128)} %src_hbm.1, s32[80,128,128]{2,1,0:T(8,128)} %bitcast.4), custom_call_target="tpu_custom_call" | custom-call | tf_op jit(solution)/shard_map/adjacency_kernel/pallas_call | solution.py:242
  13.2 1.1 %collective-permute-start.1 = (bf16[16,256,128]{2,1,0:T(8,128)(2,1)S(1)}, bf16[16,256,128]{2,1,0:T(8,128)(2,1)S(1)}, u32[]{:S(2)}, u32[]{:S(2)}) collective-permute-start(bf16[16,256,128]{2,1,0:T(8,128)(2,1)S(1)} %get-tuple-element.29.adj_ref), channel_id=1, source_target_pairs={{0,16},{16,0},{1,17},{17,1},{2,18},{18,2},{3,19},{19,3},{4,20},{20... | collective-permute-start | bytes 3145736 | tf_op jit(solution)/shard_map/ppermute | solution.py:255
  14.3 11.9 %all-to-all-done.x_ref = bf16[16,256,128]{2,1,0:T(8,128)(2,1)S(1)} async-done(((bf16[16,256,128]{2,1,0:T(8,128)(2,1)}), bf16[16,256,128]{2,1,0:T(8,128)(2,1)S(1)}, u32[]{:S(2)}, u32[]{:S(2)}) %all-to-all-start) | async-done | bytes 1048608 | tf_op jit(solution)/shard_map/all_to_all | solution.py:289
  26.2 1.0 copy-done
  27.7 2.7 %collective-permute-start.2 = (bf16[256,128]{1,0:T(8,128)(2,1)S(1)}, bf16[256,128]{1,0:T(8,128)(2,1)S(1)}, u32[]{:S(2)}, u32[]{:S(2)}) collective-permute-start(bf16[256,128]{1,0:T(8,128)(2,1)S(1)} %neighbour_kernel.1.y_ref), channel_id=1, source_target_pairs={{0,16},{16,0},{1,17},{17,1},{2,18},{18,2},{3,19},{19,3},{4,20},{20... | collective-permute-start | bytes 196616 | tf_op jit(solution)/shard_map/ppermute | solution.py:255
  31.9 6.5 %collective-permute-start.5 = (bf16[2,256,128]{2,1,0:T(8,128)(2,1)S(1)}, bf16[2,256,128]{2,1,0:T(8,128)(2,1)S(1)}, u32[]{:S(2)}, u32[]{:S(2)}) collective-permute-start(bf16[2,256,128]{2,1,0:T(8,128)(2,1)S(1)} %pair_kernel.1.pair_ref), channel_id=1, source_target_pairs={{0,96},{32,128},{64,160},{96,192},{128,224},{160,0},{192,32},{224,... | collective-permute-start | bytes 393224 | tf_op jit(solution)/shard_map/ppermute | solution.py:261
  39.1 2.4 %collective-permute-start = (s32[16]{0:T(128)S(1)}, s32[16]{0:T(128)S(1)}, u32[]{:S(2)}, u32[]{:S(2)}) collective-permute-start(s32[16]{0:T(128)S(1)} %get-tuple-element.28.sel_ref), channel_id=1, source_target_pairs={{0,16},{16,0},{1,17},{17,1},{2,18},{18,2},{3,19},{19,3},{4,20},{20... | collective-permute-start | bytes 200 | tf_op jit(solution)/shard_map/ppermute | solution.py:255
  42.3 2.4 %collective-permute-start.6 = (bf16[256,128]{1,0:T(8,128)(2,1)S(1)}, bf16[256,128]{1,0:T(8,128)(2,1)S(1)}, u32[]{:S(2)}, u32[]{:S(2)}) collective-permute-start(bf16[256,128]{1,0:T(8,128)(2,1)S(1)} %neighbour_kernel.1.y_ref), channel_id=1, source_target_pairs={{0,128},{32,160},{64,192},{96,224},{128,0},{160,32},{192,64},{224,... | collective-permute-start | bytes 196616 | tf_op jit(solution)/shard_map/ppermute | solution.py:261
  44.7 8.2 %collective-permute-done.6.far_ref = bf16[256,128]{1,0:T(8,128)(2,1)S(1)} collective-permute-done((bf16[256,128]{1,0:T(8,128)(2,1)S(1)}, bf16[256,128]{1,0:T(8,128)(2,1)S(1)}, u32[]{:S(2)}, u32[]{:S(2)}) %collective-permute-start.6) | collective-permute-done | bytes 65568 | tf_op jit(solution)/shard_map/ppermute | solution.py:261
  52.9 1.0 aggregate_kernel.1
  54.6 1.0 copy-done.2
  56.9 1.4 %collective-permute-done.8.both_pair_ref = bf16[384,256]{1,0:T(8,128)(2,1)S(1)} collective-permute-done((bf16[384,256]{1,0:T(8,128)(2,1)S(1)}, bf16[384,256]{1,0:T(8,128)(2,1)S(1)}, u32[]{:S(2)}, u32[]{:S(2)}) %collective-permute-start.8) | collective-permute-done | bytes 196640 | tf_op jit(solution)/shard_map/ppermute | solution.py:255
  58.3 1.3 %transpose_kernel.1 = (bf16[2,128,256]{2,1,0:T(8,128)(2,1)S(1)}, bf16[2,128,256]{2,1,0:T(8,128)(2,1)S(1)}, bf16[2,128,256]{2,1,0:T(8,128)(2,1)S(1)}, bf16[128,25...) custom-call(s32[3]{0:T(128)S(1)} %pad_add_fusion.place_ref, ...), custom_call_target="tpu_custom_call", output_to_operand_aliasing={{5}: (7, {})} | custom-call | tf_op jit(solution)/shard_map/transpose_kernel/pallas_call | solution.py:242
  60.4 1.0 collective-permute-start.10
  61.4 1.9 %collective-permute-start.11 = (bf16[2,128,256]{2,1,0:T(8,128)(2,1)S(1)}, bf16[2,128,256]{2,1,0:T(8,128)(2,1)S(1)}, u32[]{:S(2)}, u32[]{:S(2)}) collective-permute-start(bf16[2,128,256]{2,1,0:T(8,128)(2,1)S(1)} %get-tuple-element.36), channel_id=1, source_target_pairs={{0,96},{32,128},{64,160},{96,192},{128,224},{160,0},{192,32},{224,... | collective-permute-start | bytes 393224 | tf_op jit(solution)/shard_map/ppermute | solution.py:261
  63.3 3.7 %collective-permute-start.12 = (bf16[128,256]{1,0:T(8,128)(2,1)S(1)}, bf16[128,256]{1,0:T(8,128)(2,1)S(1)}, u32[]{:S(2)}, u32[]{:S(2)}) collective-permute-start(bf16[128,256]{1,0:T(8,128)(2,1)S(1)} %get-tuple-element.37), channel_id=1, source_target_pairs={{0,128},{32,160},{64,192},{96,224},{128,0},{160,32},{192,64},{224,... | collective-permute-start | bytes 196616 | tf_op jit(solution)/shard_map/ppermute | solution.py:261
  67.0 6.7 %collective-permute-done.12.far_ref = bf16[128,256]{1,0:T(8,128)(2,1)S(1)} collective-permute-done((bf16[128,256]{1,0:T(8,128)(2,1)S(1)}, bf16[128,256]{1,0:T(8,128)(2,1)S(1)}, u32[]{:S(2)}, u32[]{:S(2)}) %collective-permute-start.12) | collective-permute-done | bytes 65568 | tf_op jit(solution)/shard_map/ppermute | solution.py:261
  74.3 1.9 %collective-permute-start.13 = (f32[2,128,256]{2,1,0:T(8,128)S(1)}, f32[2,128,256]{2,1,0:T(8,128)S(1)}, u32[]{:S(2)}, u32[]{:S(2)}) collective-permute-start(f32[2,128,256]{2,1,0:T(8,128)S(1)} %fold_kernel.2.fold_ref), channel_id=1, source_target_pairs={{0,16},{16,0},{1,17},{17,1},{2,18},{18,2},{3,19},{19,3},{4,20},{20... | collective-permute-start | bytes 786440 | tf_op jit(solution)/shard_map/ppermute | solution.py:255
  76.2 1.2 %collective-permute-done.13.came_ref = f32[2,128,256]{2,1,0:T(8,128)S(1)} collective-permute-done((f32[2,128,256]{2,1,0:T(8,128)S(1)}, f32[2,128,256]{2,1,0:T(8,128)S(1)}, u32[]{:S(2)}, u32[]{:S(2)}) %collective-permute-start.13) | collective-permute-done | bytes 262176 | tf_op jit(solution)/shard_map/ppermute | solution.py:255
  77.3 1.5 %feature_grad_kernel.1 = (bf16[2,256,256]{2,1,0:T(8,128)(2,1)S(1)}, bf16[16,128,256]{2,1,0:T(8,128)(2,1)}) custom-call(f32[2,128,256]{2,1,0:T(8,128)S(1)} %fold_kernel.2.fold_ref, f32[2,128,256]{2,1,0:T(8,128)S(1)} %collective-permute-done.13.came_ref, bf16[384,256]{1,0:T(8,128)(2,1)S(1)} %get-tuple-element.33.both_ref, bf16[2048,128]{1,0:T(8,128)(2,1)S(1)} %copy-done.3, ...), custom_call_target="tpu_custom_call" | custom-call | tf_op jit(solution)/shard_map/feature_grad_kernel/pallas_call | solution.py:242
  79.5 3.7 %all-to-all-start.1 = ((bf16[16,128,256]{2,1,0:T(8,128)(2,1)}), bf16[16,128,256]{2,1,0:T(8,128)(2,1)S(1)}, u32[]{:S(2)}, u32[]{:S(2)}) async-start(bf16[16,128,256]{2,1,0:T(8,128)(2,1)} %get-tuple-element.46), calls=%async_computation.1 | async-start | bytes 2097152 | tf_op jit(solution)/shard_map/all_to_all | solution.py:345
  83.2 0.9 copy-done.5
  84.2 1.5 %weight_grad_kernel.1 = (bf16[2,256,128]{2,1,0:T(8,128)(2,1)S(1)}, bf16[2,256,128]{2,1,0:T(8,128)(2,1)S(1)}, bf16[2,256,128]{2,1,0:T(8,128)(2,1)S(1)}, bf16[256,128]{1,0:T(8,128)(2,1)S(1)}, f32[256,128]{1,0:T(8,128)S(1)}) custom-call(s32[3]{0:T(128)S(1)} %pad_add_fusion.place_ref, bf16[384,256]{1,0:T(8,128)(2,1)S(1)} %get-tuple-element.33.both_ref, ...), custom_call_target="tpu_custom_call" | custom-call | tf_op jit(solution)/shard_map/weight_grad_kernel/pallas_call | solution.py:242
  85.7 1.0 collective-permute-start.15
  86.7 2.2 %collective-permute-start.16 = (bf16[2,256,128]{2,1,0:T(8,128)(2,1)S(1)}, bf16[2,256,128]{2,1,0:T(8,128)(2,1)S(1)}, u32[]{:S(2)}, u32[]{:S(2)}) collective-permute-start(bf16[2,256,128]{2,1,0:T(8,128)(2,1)S(1)} %get-tuple-element.42), channel_id=1, source_target_pairs={{0,64},{32,96},{64,128},{96,160},{128,192},{160,224},{192,0},{224,... | collective-permute-start | bytes 393224 | tf_op jit(solution)/shard_map/ppermute | solution.py:261
  89.0 3.5 %collective-permute-start.17 = (bf16[2,256,128]{2,1,0:T(8,128)(2,1)S(1)}, bf16[2,256,128]{2,1,0:T(8,128)(2,1)S(1)}, u32[]{:S(2)}, u32[]{:S(2)}) collective-permute-start(bf16[2,256,128]{2,1,0:T(8,128)(2,1)S(1)} %get-tuple-element.43), channel_id=1, source_target_pairs={{0,96},{32,128},{64,160},{96,192},{128,224},{160,0},{192,32},{224,... | collective-permute-start | bytes 393224 | tf_op jit(solution)/shard_map/ppermute | solution.py:261
  92.4 2.0 %collective-permute-start.18 = (bf16[256,128]{1,0:T(8,128)(2,1)S(1)}, bf16[256,128]{1,0:T(8,128)(2,1)S(1)}, u32[]{:S(2)}, u32[]{:S(2)}) collective-permute-start(bf16[256,128]{1,0:T(8,128)(2,1)S(1)} %get-tuple-element.44), channel_id=1, source_target_pairs={{0,128},{32,160},{64,192},{96,224},{128,0},{160,32},{192,64},{224,... | collective-permute-start | bytes 196616 | tf_op jit(solution)/shard_map/ppermute | solution.py:261
  94.4 7.4 %collective-permute-done.18.far_ref = bf16[256,128]{1,0:T(8,128)(2,1)S(1)} collective-permute-done((bf16[256,128]{1,0:T(8,128)(2,1)S(1)}, bf16[256,128]{1,0:T(8,128)(2,1)S(1)}, u32[]{:S(2)}, u32[]{:S(2)}) %collective-permute-start.18) | collective-permute-done | bytes 65568 | tf_op jit(solution)/shard_map/ppermute | solution.py:261
  102.5 4.0 %collective-permute-start.19 = (f32[2,256,128]{2,1,0:T(8,128)S(1)}, f32[2,256,128]{2,1,0:T(8,128)S(1)}, u32[]{:S(2)}, u32[]{:S(2)}) collective-permute-start(f32[2,256,128]{2,1,0:T(8,128)S(1)} %fold_kernel.3.fold_ref), channel_id=1, source_target_pairs={{0,16},{16,0},{1,17},{17,1},{2,18},{18,2},{3,19},{19,3},{4,20},{20... | collective-permute-start | bytes 786440 | tf_op jit(solution)/shard_map/ppermute | solution.py:255
  106.4 0.8 sum_kernel.1.done_ref
  (41 shorter events, 9.2 us)
Async XLA Ops:
  2.6 23.6 %all-to-all-start = ((bf16[16,256,128]{2,1,0:T(8,128)(2,1)}), bf16[16,256,128]{2,1,0:T(8,128)(2,1)S(1)}, u32[]{:S(2)}, u32[]{:S(2)}) async-start(bf16[16,256,128]{2,1,0:T(8,128)(2,1)} %spread_kernel.1), calls=%async_computation | async-start | bytes 2097152 | tf_op jit(solution)/shard_map/all_to_all | solution.py:289
  10.9 45.3 %copy-start.6 = (bf16[256,128]{1,0:T(8,128)(2,1)S(1)}, bf16[256,128]{1,0:T(8,128)(2,1)}, u32[]{:S(2)}) copy-start(bf16[256,128]{1,0:T(8,128)(2,1)} %og_ref.1) | copy-start | bytes 196612
  13.2 31.5 %collective-permute-start.1 = (bf16[16,256,128]{2,1,0:T(8,128)(2,1)S(1)}, bf16[16,256,128]{2,1,0:T(8,128)(2,1)S(1)}, u32[]{:S(2)}, u32[]{:S(2)}) collective-permute-start(bf16[16,256,128]{2,1,0:T(8,128)(2,1)S(1)} %get-tuple-element.29.adj_ref), channel_id=1, source_target_pairs={{0,16},{16,0},{1,17},{17,1},{2,18},{18,2},{3,19},{19,3},{4,20},{20... | collective-permute-start | bytes 3145736 | tf_op jit(solution)/shard_map/ppermute | solution.py:255
  26.2 1.0 copy-start
  27.7 49.7 %copy-start.1 = (bf16[2048,128]{1,0:T(8,128)(2,1)S(1)}, bf16[2048,128]{1,0:T(8,128)(2,1)}, u32[]{:S(2)}) copy-start(bf16[2048,128]{1,0:T(8,128)(2,1)} %wn_ref.1) | copy-start | bytes 1572868
  27.7 49.6 %copy-start.3 = (bf16[2048,128]{1,0:T(8,128)(2,1)S(1)}, bf16[2048,128]{1,0:T(8,128)(2,1)}, u32[]{:S(2)}) copy-start(bf16[2048,128]{1,0:T(8,128)(2,1)} %ws_ref.1) | copy-start | bytes 1572868
  27.7 3.6 %collective-permute-start.2 = (bf16[256,128]{1,0:T(8,128)(2,1)S(1)}, bf16[256,128]{1,0:T(8,128)(2,1)S(1)}, u32[]{:S(2)}, u32[]{:S(2)}) collective-permute-start(bf16[256,128]{1,0:T(8,128)(2,1)S(1)} %neighbour_kernel.1.y_ref), channel_id=1, source_target_pairs={{0,16},{16,0},{1,17},{17,1},{2,18},{18,2},{3,19},{19,3},{4,20},{20... | collective-permute-start | bytes 196616 | tf_op jit(solution)/shard_map/ppermute | solution.py:255
  31.9 21.1 %collective-permute-start.5 = (bf16[2,256,128]{2,1,0:T(8,128)(2,1)S(1)}, bf16[2,256,128]{2,1,0:T(8,128)(2,1)S(1)}, u32[]{:S(2)}, u32[]{:S(2)}) collective-permute-start(bf16[2,256,128]{2,1,0:T(8,128)(2,1)S(1)} %pair_kernel.1.pair_ref), channel_id=1, source_target_pairs={{0,96},{32,128},{64,160},{96,192},{128,224},{160,0},{192,32},{224,... | collective-permute-start | bytes 393224 | tf_op jit(solution)/shard_map/ppermute | solution.py:261
  38.4 14.5 %collective-permute-start.4 = (bf16[2,256,128]{2,1,0:T(8,128)(2,1)S(1)}, bf16[2,256,128]{2,1,0:T(8,128)(2,1)S(1)}, u32[]{:S(2)}, u32[]{:S(2)}) collective-permute-start(bf16[2,256,128]{2,1,0:T(8,128)(2,1)S(1)} %pair_kernel.1.pair_ref), channel_id=1, source_target_pairs={{0,64},{32,96},{64,128},{96,160},{128,192},{160,224},{192,0},{224,... | collective-permute-start | bytes 393224 | tf_op jit(solution)/shard_map/ppermute | solution.py:261
  38.7 14.3 %collective-permute-start.3 = (bf16[2,256,128]{2,1,0:T(8,128)(2,1)S(1)}, bf16[2,256,128]{2,1,0:T(8,128)(2,1)S(1)}, u32[]{:S(2)}, u32[]{:S(2)}) collective-permute-start(bf16[2,256,128]{2,1,0:T(8,128)(2,1)S(1)} %pair_kernel.1.pair_ref), channel_id=1, source_target_pairs={{0,32},{32,64},{64,96},{96,128},{128,160},{160,192},{192,224},{224... | collective-permute-start | bytes 393224 | tf_op jit(solution)/shard_map/ppermute | solution.py:261
  39.1 3.2 %collective-permute-start = (s32[16]{0:T(128)S(1)}, s32[16]{0:T(128)S(1)}, u32[]{:S(2)}, u32[]{:S(2)}) collective-permute-start(s32[16]{0:T(128)S(1)} %get-tuple-element.28.sel_ref), channel_id=1, source_target_pairs={{0,16},{16,0},{1,17},{17,1},{2,18},{18,2},{3,19},{19,3},{4,20},{20... | collective-permute-start | bytes 200 | tf_op jit(solution)/shard_map/ppermute | solution.py:255
  42.3 10.6 %collective-permute-start.6 = (bf16[256,128]{1,0:T(8,128)(2,1)S(1)}, bf16[256,128]{1,0:T(8,128)(2,1)S(1)}, u32[]{:S(2)}, u32[]{:S(2)}) collective-permute-start(bf16[256,128]{1,0:T(8,128)(2,1)S(1)} %neighbour_kernel.1.y_ref), channel_id=1, source_target_pairs={{0,128},{32,160},{64,192},{96,224},{128,0},{160,32},{192,64},{224,... | collective-permute-start | bytes 196616 | tf_op jit(solution)/shard_map/ppermute | solution.py:261
  53.9 2.2 %collective-permute-start.7 = (f32[256,128]{1,0:T(8,128)S(1)}, f32[256,128]{1,0:T(8,128)S(1)}, u32[]{:S(2)}, u32[]{:S(2)}) collective-permute-start(f32[256,128]{1,0:T(8,128)S(1)} %get-tuple-element.31), channel_id=1, source_target_pairs={{0,16},{16,0},{1,17},{17,1},{2,18},{18,2},{3,19},{19,3},{4,20},{20... | collective-permute-start | bytes 393224 | tf_op jit(solution)/shard_map/ppermute | solution.py:255
  54.6 1.0 copy-start.2
  56.8 1.4 %collective-permute-start.8 = (bf16[384,256]{1,0:T(8,128)(2,1)S(1)}, bf16[384,256]{1,0:T(8,128)(2,1)S(1)}, u32[]{:S(2)}, u32[]{:S(2)}) collective-permute-start(bf16[384,256]{1,0:T(8,128)(2,1)S(1)} %get-tuple-element.33.both_ref), channel_id=1, source_target_pairs={{0,16},{16,0},{1,17},{17,1},{2,18},{18,2},{3,19},{19,3},{4,20},{20... | collective-permute-start | bytes 589832 | tf_op jit(solution)/shard_map/ppermute | solution.py:255
  59.5 23.7 %collective-permute-start.14 = (bf16[16,256,128]{2,1,0:T(8,128)(2,1)S(1)}, bf16[16,256,128]{2,1,0:T(8,128)(2,1)S(1)}, u32[]{:S(2)}, u32[]{:S(2)}) collective-permute-start(bf16[16,256,128]{2,1,0:T(8,128)(2,1)S(1)} %get-tuple-element.40.x_ref), channel_id=1, source_target_pairs={{0,16},{16,0},{1,17},{17,1},{2,18},{18,2},{3,19},{19,3},{4,20},{20... | collective-permute-start | bytes 3145736 | tf_op jit(solution)/shard_map/ppermute | solution.py:255
  59.8 13.9 %collective-permute-start.9 = (bf16[2,128,256]{2,1,0:T(8,128)(2,1)S(1)}, bf16[2,128,256]{2,1,0:T(8,128)(2,1)S(1)}, u32[]{:S(2)}, u32[]{:S(2)}) collective-permute-start(bf16[2,128,256]{2,1,0:T(8,128)(2,1)S(1)} %get-tuple-element.34), channel_id=1, source_target_pairs={{0,32},{32,64},{64,96},{96,128},{128,160},{160,192},{192,224},{224... | collective-permute-start | bytes 393224 | tf_op jit(solution)/shard_map/ppermute | solution.py:261
  60.4 13.2 %collective-permute-start.10 = (bf16[2,128,256]{2,1,0:T(8,128)(2,1)S(1)}, bf16[2,128,256]{2,1,0:T(8,128)(2,1)S(1)}, u32[]{:S(2)}, u32[]{:S(2)}) collective-permute-start(bf16[2,128,256]{2,1,0:T(8,128)(2,1)S(1)} %get-tuple-element.35), channel_id=1, source_target_pairs={{0,64},{32,96},{64,128},{96,160},{128,192},{160,224},{192,0},{224,... | collective-permute-start | bytes 393224 | tf_op jit(solution)/shard_map/ppermute | solution.py:261
  61.4 12.3 %collective-permute-start.11 = (bf16[2,128,256]{2,1,0:T(8,128)(2,1)S(1)}, bf16[2,128,256]{2,1,0:T(8,128)(2,1)S(1)}, u32[]{:S(2)}, u32[]{:S(2)}) collective-permute-start(bf16[2,128,256]{2,1,0:T(8,128)(2,1)S(1)} %get-tuple-element.36), channel_id=1, source_target_pairs={{0,96},{32,128},{64,160},{96,192},{128,224},{160,0},{192,32},{224,... | collective-permute-start | bytes 393224 | tf_op jit(solution)/shard_map/ppermute | solution.py:261
  63.3 10.3 %collective-permute-start.12 = (bf16[128,256]{1,0:T(8,128)(2,1)S(1)}, bf16[128,256]{1,0:T(8,128)(2,1)S(1)}, u32[]{:S(2)}, u32[]{:S(2)}) collective-permute-start(bf16[128,256]{1,0:T(8,128)(2,1)S(1)} %get-tuple-element.37), channel_id=1, source_target_pairs={{0,128},{32,160},{64,192},{96,224},{128,0},{160,32},{192,64},{224,... | collective-permute-start | bytes 196616 | tf_op jit(solution)/shard_map/ppermute | solution.py:261
  74.3 3.0 %collective-permute-start.13 = (f32[2,128,256]{2,1,0:T(8,128)S(1)}, f32[2,128,256]{2,1,0:T(8,128)S(1)}, u32[]{:S(2)}, u32[]{:S(2)}) collective-permute-start(f32[2,128,256]{2,1,0:T(8,128)S(1)} %fold_kernel.2.fold_ref), channel_id=1, source_target_pairs={{0,16},{16,0},{1,17},{17,1},{2,18},{18,2},{3,19},{19,3},{4,20},{20... | collective-permute-start | bytes 786440 | tf_op jit(solution)/shard_map/ppermute | solution.py:255
  78.8 0.7 copy-start.4
  79.5 26.9 %all-to-all-start.1 = ((bf16[16,128,256]{2,1,0:T(8,128)(2,1)}), bf16[16,128,256]{2,1,0:T(8,128)(2,1)S(1)}, u32[]{:S(2)}, u32[]{:S(2)}) async-start(bf16[16,128,256]{2,1,0:T(8,128)(2,1)} %get-tuple-element.46), calls=%async_computation.1 | async-start | bytes 2097152 | tf_op jit(solution)/shard_map/all_to_all | solution.py:345
  83.2 1.0 copy-start.5
  85.7 16.1 %collective-permute-start.15 = (bf16[2,256,128]{2,1,0:T(8,128)(2,1)S(1)}, bf16[2,256,128]{2,1,0:T(8,128)(2,1)S(1)}, u32[]{:S(2)}, u32[]{:S(2)}) collective-permute-start(bf16[2,256,128]{2,1,0:T(8,128)(2,1)S(1)} %get-tuple-element.41), channel_id=1, source_target_pairs={{0,32},{32,64},{64,96},{96,128},{128,160},{160,192},{192,224},{224... | collective-permute-start | bytes 393224 | tf_op jit(solution)/shard_map/ppermute | solution.py:261
  86.7 15.1 %collective-permute-start.16 = (bf16[2,256,128]{2,1,0:T(8,128)(2,1)S(1)}, bf16[2,256,128]{2,1,0:T(8,128)(2,1)S(1)}, u32[]{:S(2)}, u32[]{:S(2)}) collective-permute-start(bf16[2,256,128]{2,1,0:T(8,128)(2,1)S(1)} %get-tuple-element.42), channel_id=1, source_target_pairs={{0,64},{32,96},{64,128},{96,160},{128,192},{160,224},{192,0},{224,... | collective-permute-start | bytes 393224 | tf_op jit(solution)/shard_map/ppermute | solution.py:261
  89.0 12.9 %collective-permute-start.17 = (bf16[2,256,128]{2,1,0:T(8,128)(2,1)S(1)}, bf16[2,256,128]{2,1,0:T(8,128)(2,1)S(1)}, u32[]{:S(2)}, u32[]{:S(2)}) collective-permute-start(bf16[2,256,128]{2,1,0:T(8,128)(2,1)S(1)} %get-tuple-element.43), channel_id=1, source_target_pairs={{0,96},{32,128},{64,160},{96,192},{128,224},{160,0},{192,32},{224,... | collective-permute-start | bytes 393224 | tf_op jit(solution)/shard_map/ppermute | solution.py:261
  92.4 9.4 %collective-permute-start.18 = (bf16[256,128]{1,0:T(8,128)(2,1)S(1)}, bf16[256,128]{1,0:T(8,128)(2,1)S(1)}, u32[]{:S(2)}, u32[]{:S(2)}) collective-permute-start(bf16[256,128]{1,0:T(8,128)(2,1)S(1)} %get-tuple-element.44), channel_id=1, source_target_pairs={{0,128},{32,160},{64,192},{96,224},{128,0},{160,32},{192,64},{224,... | collective-permute-start | bytes 196616 | tf_op jit(solution)/shard_map/ppermute | solution.py:261
  102.5 5.1 %collective-permute-start.19 = (f32[2,256,128]{2,1,0:T(8,128)S(1)}, f32[2,256,128]{2,1,0:T(8,128)S(1)}, u32[]{:S(2)}, u32[]{:S(2)}) collective-permute-start(f32[2,256,128]{2,1,0:T(8,128)S(1)} %fold_kernel.3.fold_ref), channel_id=1, source_target_pairs={{0,16},{16,0},{1,17},{17,1},{2,18},{18,2},{3,19},{19,3},{4,20},{20... | collective-permute-start | bytes 786440 | tf_op jit(solution)/shard_map/ppermute | solution.py:255

commit v7 on v6

--- a/solution.py
+++ b/solution.py
@@ -45,9 +45,21 @@
         copy.wait()
 
 
-def neighbour_kernel(x_ref, w_ref, y_ref):
-    total = dot(x_ref[0], w_ref[0:T, :])
-    for part in range(1, x_ref.shape[0]):
+def neighbour_kernel(sel_ref, x_ref, w_hbm, y_ref, sel_same_ref, w_ref, sems):
+    parts = x_ref.shape[0]
+    chunks = sems.shape[0]
+    span = parts // chunks
+    copies = []
+    for chunk in range(chunks):
+        part = pl.ds(chunk * span * T, span * T)
+        copies.append(pltpu.make_async_copy(w_hbm.at[part], w_ref.at[part], sems.at[chunk]))
+        copies[-1].start()
+    for owner in range(sel_ref.shape[0]):
+        sel_same_ref[owner] = sel_ref[owner]
+    total = jnp.zeros(y_ref.shape, F32)
+    for part in range(parts):
+        if part % span == 0:
+            copies[part // span].wait()
         total = total + dot(x_ref[part], w_ref[part * T : (part + 1) * T, :])
     y_ref[...] = total.astype(BF16)
 
@@ -124,15 +136,14 @@
 
 
 def aggregate_kernel(
-    place_ref, sel_ref, sel_pair_ref, adj_ref, adj_pair_ref, pair_ref, one_ref, two_ref, three_ref, far_ref,
-    mine_ref, theirs_ref,
+    place_ref, sel_ref, sel_pair_ref, adj_ref, adj_pair_ref, inv_ref, z_ref, pair_ref,
+    far_ref, three_ref, two_ref, one_ref, mine_ref, theirs_ref,
 ):
-    core, here, way = place_ref[0], place_ref[1], place_ref[2]
+    here, way = place_ref[1], place_ref[2]
     sources = []
-    for step, ref in ((1, one_ref), (2, two_ref), (3, three_ref)):
+    for step, ref in ((1, one_ref), (2, two_ref), (3, three_ref), (4, far_ref)):
         chip = chip_at(place_ref, -step * way)
         sources += [(ref.at[side], 2 * chip + side) for side in range(2)]
-    sources.append((far_ref, 2 * chip_at(place_ref, 4) + core))
     local = [(pair_ref.at[side], 2 * here + side) for side in range(2)]
 
     def summed(adj, sel, tiles):
@@ -142,12 +153,12 @@
         return total
 
     theirs_ref[...] = summed(adj_pair_ref, sel_pair_ref, sources)
-    mine_ref[...] = summed(adj_ref, sel_ref, sources + local)
-
-
-def activation_kernel(inv_ref, mine_ref, came_ref, z_ref, og_ref, out_ref, both_ref):
+    mine_ref[...] = z_ref[...] + inv_ref[...] * summed(adj_ref, sel_ref, sources + local)
+
+
+def activation_kernel(inv_ref, mine_ref, came_ref, og_ref, out_ref, both_ref):
     inverse = inv_ref[...]
-    z = z_ref[...] + inverse * (mine_ref[...] + came_ref[...])
+    z = mine_ref[...] + inverse * came_ref[...]
     sig = 1.0 / (1.0 + jnp.exp(-z))
     out_ref[...] = (z * sig).astype(BF16)
     grad = (og_ref[...].astype(F32) * sig * (1.0 + z * (1.0 - sig))).astype(BF16).astype(F32)
@@ -155,10 +166,10 @@
     both_ref[T:, :] = halves((grad * inverse).T)
 
 
-def targets(place_ref, one_ref, two_ref, three_ref, far_ref, own_ref):
+def targets(place_ref, far_ref, three_ref, two_ref, one_ref, own_ref):
     core, here, way = place_ref[0], place_ref[1], place_ref[2]
-    places = [(far_ref, 2 * chip_at(place_ref, 4) + core)]
-    for step, ref in ((3, three_ref), (2, two_ref), (1, one_ref)):
+    places = []
+    for step, ref in ((4, far_ref), (3, three_ref), (2, two_ref), (1, one_ref)):
         chip = chip_at(place_ref, step * way)
         places += [(ref.at[side], 2 * chip + side) for side in range(2)]
     places.append((own_ref, 2 * here + core))
@@ -190,11 +201,11 @@
         ref[T:] = add_halves(total[T:]).astype(ref.dtype)
 
 
-def fold_kernel(place_ref, one_ref, two_ref, three_ref, far_ref, own_ref, fold_ref):
+def fold_kernel(place_ref, far_ref, three_ref, two_ref, one_ref, own_ref, fold_ref):
     core = place_ref[0]
-    mine = own_ref[...] + far_ref[...].astype(F32)
+    mine = own_ref[...]
     theirs = jnp.zeros(own_ref.shape, F32)
-    for ref in (one_ref, two_ref, three_ref):
+    for ref in (far_ref, three_ref, two_ref, one_ref):
         mine = mine + ref[core].astype(F32)
         theirs = theirs + ref[1 - core].astype(F32)
     fold_ref[0] = mine
@@ -257,18 +268,17 @@
 
 def along(value, step):
     pairs = [(2 * chip, 2 * ((chip + step) % 8)) for chip in range(8)]
-    pairs += [(2 * chip + 1, 2 * ((chip - step) % 8) + 1) for chip in range(8)]
+    if step < 4:
+        pairs += [(2 * chip + 1, 2 * ((chip - step) % 8) + 1) for chip in range(8)]
     return lax.ppermute(value, ("z", "c"), pairs)
 
 
-def exchange(one, two, three, far):
-    far = along(far, 4)
-    three, two, one = along(three, 3), along(two, 2), along(one, 1)
-    return one, two, three, far
+def exchange(far, three, two, one):
+    return along(far, 4), along(three, 3), along(two, 2), along(one, 1)
 
 
 def exchange_shapes(shape):
-    return [((2,) + shape, BF16)] * 3 + [(shape, BF16), (shape, F32)]
+    return [((2,) + shape, BF16)] * 4 + [(shape, F32)]
 
 
 def per_device(features, w_self, w_neigh, out_grad, tile_count, tile_dst, tile_src, tile_weight, chips, parts):
@@ -287,9 +297,6 @@
         scratch=[pltpu.VMEM((rows, T), BF16), pltpu.SemaphoreType.DMA, pltpu.SemaphoreType.DMA((parts,))],
     )
     x_all = lax.all_to_all(x_pay, "f", 0, 0, tiled=True)
-    (y,) = call(neighbour_kernel, (x_all, w_neigh), [((rows, T), BF16)])
-    (pair,) = call(pair_kernel, (place, y, swap(y)), [((2, rows, T), BF16)], in_specs=[SMEM, VMEM, VMEM])
-    y_came = exchange(pair, pair, pair, y)
     adj, inverse, sel = call(
         adjacency_kernel,
         (tile_count, tile_dst, tile_src, tile_weight[0]),
@@ -306,18 +313,29 @@
         ],
         limit=20,
     )
-    adj_pair, sel_pair = swap(adj), swap(sel)
+    sel_pair = swap(sel)
+    y, sel_pair = call(
+        neighbour_kernel,
+        (sel_pair, x_all, w_neigh),
+        [((rows, T), BF16), ((groups,), jnp.int32)],
+        in_specs=[SMEM, VMEM, HBM],
+        out_specs=[VMEM, SMEM],
+        scratch=[pltpu.VMEM(w_neigh.shape, BF16), pltpu.SemaphoreType.DMA((4,))],
+    )
+    (pair,) = call(pair_kernel, (place, y, swap(y)), [((2, rows, T), BF16)], in_specs=[SMEM, VMEM, VMEM])
+    y_came = exchange(pair, pair, pair, pair)
+    adj_pair = swap(adj)
     (z_self,) = call(self_kernel, (x_all, w_self), [((rows, T), F32)])
     scalars = [SMEM] * 3
     mine, theirs = call(
         aggregate_kernel,
-        (place, sel, sel_pair, adj, adj_pair, pair, *y_came),
+        (place, sel, sel_pair, adj, adj_pair, inverse, z_self, pair, *y_came),
         [((rows, T), F32)] * 2,
-        in_specs=scalars + [VMEM] * 7,
+        in_specs=scalars + [VMEM] * 9,
     )
     output, both = call(
         activation_kernel,
-        (inverse, mine, swap(theirs), z_self, out_grad),
+        (inverse, mine, swap(theirs), out_grad),
         [((rows, T), BF16), ((3 * T, rows), BF16)],
     )
     both_pair = swap(both)

time: 109 us -> 113 us (1.037)
  Pallas kernels: 14.5 us -> 16.9 us
  waiting for transfers between devices: 38.8 us -> 40.5 us
    ppermute x8, starting transfers between devices: 13 us -> 20.8 us  [swap(): return lax.ppermute(value, 'c', [(0, 1), (1, 0)])]
    ppermute x12, starting transfers between devices: 25.6 us -> 18.4 us  [along(): return lax.ppermute(value, ('z', 'c'), pairs)]
    pallas_call x14, Pallas kernels: 14.5 us -> 16.9 us  [call(): pl.pallas_call(kernel, out_shape=shapes, in_specs=in_specs or [VMEM] * le...]
    all_to_all x1, waiting for transfers between devices: 11.9 us -> 9.47 us  [per_device(): x_all = lax.all_to_all(x_pay, 'f', 0, 0, tiled=True)]
    ppermute x12, waiting for transfers between devices: 22.3 us -> 24.4 us  [along(): return lax.ppermute(value, ('z', 'c'), pairs)]
    ppermute x8, waiting for transfers between devices: 4.56 us -> 6.57 us  [swap(): return lax.ppermute(value, 'c', [(0, 1), (1, 0)])]
    unnamed x14 -> x12, local copies, waits for them, and re-layouts: 3.73 us -> 2.69 us
  transfers between devices with their start and end apart: 22 -> 22, of which waited for: 9 -> 15; matrix products, arithmetic and copies ran while one was open for 0% -> 0% of each run, Pallas kernels for 8% -> 10%
where the time goes in v7:
time: 113 us; the launch traced here: 112 us
  starting transfers between devices  50.6 us (45%)
  waiting for transfers between devices  40.5 us (36%)
  Pallas kernels  16.9 us (15%)
  local copies, waits for them, and re-layouts  2.69 us (2%)
  between operations  1.48 us (1%)
    ppermute x12, waiting for transfers between devices, along(): return lax.ppermute(value, ('z', 'c'), pairs)  24.4 us
    ppermute x8, starting transfers between devices, swap(): return lax.ppermute(value, 'c', [(0, 1), (1, 0)])  20.8 us
    ppermute x12, starting transfers between devices, along(): return lax.ppermute(value, ('z', 'c'), pairs)  18.4 us
    pallas_call x14, Pallas kernels, call(): pl.pallas_call(kernel, out_shape=shapes, in_specs=in_specs or [VMEM] * le...  16.9 us
    all_to_all x1, waiting for transfers between devices, per_device(): x_all = lax.all_to_all(x_pay, 'f', 0, 0, tiled=True)  9.47 us
    all_to_all x1, starting transfers between devices, per_device(): x_all = lax.all_to_all(x_pay, 'f', 0, 0, tiled=True)  7.6 us
    ppermute x8, waiting for transfers between devices, swap(): return lax.ppermute(value, 'c', [(0, 1), (1, 0)])  6.57 us
    all_to_all x1, starting transfers between devices, per_device(): p_all = lax.all_to_all(p_pay, 'f', 0, 0, tiled=True)  3.83 us
  transfers between devices with their start and end apart: 22, of which 15 were waited for; matrix products, arithmetic and copies ran while one was open for 0% of the time, Pallas kernels for 10%

profile of v7, /device:TPU:1, one launch (start us, length us, event | category | flops | bytes accessed | tf_op | source)
XLA Modules:
  0.0 112.3 jit_solution(3280259637839806240)
XLA Ops:
  0.6 2.0 %spread_kernel.1 = bf16[16,256,128]{2,1,0:T(8,128)(2,1)} custom-call(bf16[256,128]{1,0:T(8,128)(2,1)} %x_hbm.1), custom_call_target="tpu_custom_call" | custom-call | tf_op jit(solution)/shard_map/spread_kernel/pallas_call | solution.py:253
  2.6 7.6 %all-to-all-start = ((bf16[16,256,128]{2,1,0:T(8,128)(2,1)}), bf16[16,256,128]{2,1,0:T(8,128)(2,1)S(1)}, u32[]{:S(2)}, u32[]{:S(2)}) async-start(bf16[16,256,128]{2,1,0:T(8,128)(2,1)} %spread_kernel.1), calls=%async_computation | async-start | bytes 2097152 | tf_op jit(solution)/shard_map/all_to_all | solution.py:299
  10.9 2.3 %adjacency_kernel.1 = (bf16[16,256,128]{2,1,0:T(8,128)(2,1)S(1)}, f32[256,128]{1,0:T(8,128)S(1)}, s32[16]{0:T(128)S(1)}) custom-call(s32[1]{0:T(128)S(6)} %copy.16.count_ref, s32[1,80]{1,0:T(1,128)} %dst_hbm.1, s32[1,80]{1,0:T(1,128)} %src_hbm.1, s32[80,128,128]{2,1,0:T(8,128)} %bitcast.4), custom_call_target="tpu_custom_call" | custom-call | tf_op jit(solution)/shard_map/adjacency_kernel/pallas_call | solution.py:253
  13.2 1.2 %collective-permute-start.1 = (bf16[16,256,128]{2,1,0:T(8,128)(2,1)S(1)}, bf16[16,256,128]{2,1,0:T(8,128)(2,1)S(1)}, u32[]{:S(2)}, u32[]{:S(2)}) collective-permute-start(bf16[16,256,128]{2,1,0:T(8,128)(2,1)S(1)} %get-tuple-element.32.adj_ref), channel_id=1, source_target_pairs={{0,16},{16,0},{1,17},{17,1},{2,18},{18,2},{3,19},{19,3},{4,20},{20... | collective-permute-start | bytes 3145736 | tf_op jit(solution)/shard_map/ppermute | solution.py:266
  14.5 2.2 %collective-permute-done.sel_ref = s32[16]{0:T(128)S(1)} collective-permute-done((s32[16]{0:T(128)S(1)}, s32[16]{0:T(128)S(1)}, u32[]{:S(2)}, u32[]{:S(2)}) %collective-permute-start) | collective-permute-done | bytes 96 | tf_op jit(solution)/shard_map/ppermute | solution.py:266
  16.7 9.5 %all-to-all-done.x_ref = bf16[16,256,128]{2,1,0:T(8,128)(2,1)S(1)} async-done(((bf16[16,256,128]{2,1,0:T(8,128)(2,1)}), bf16[16,256,128]{2,1,0:T(8,128)(2,1)S(1)}, u32[]{:S(2)}, u32[]{:S(2)}) %all-to-all-start) | async-done | bytes 1048608 | tf_op jit(solution)/shard_map/all_to_all | solution.py:299
  26.2 2.6 %neighbour_kernel.1 = (bf16[256,128]{1,0:T(8,128)(2,1)S(1)}, s32[16]{0:T(128)S(1)}) custom-call(s32[16]{0:T(128)S(1)} %collective-permute-done.sel_ref, bf16[16,256,128]{2,1,0:T(8,128)(2,1)S(1)} %all-to-all-done.x_ref, bf16[2048,128]{1,0:T(8,128)(2,1)} %wn_ref.1), custom_call_target="tpu_custom_call" | custom-call | tf_op jit(solution)/shard_map/neighbour_kernel/pallas_call | solution.py:253
  28.8 2.7 %collective-permute-start.2 = (bf16[256,128]{1,0:T(8,128)(2,1)S(1)}, bf16[256,128]{1,0:T(8,128)(2,1)S(1)}, u32[]{:S(2)}, u32[]{:S(2)}) collective-permute-start(bf16[256,128]{1,0:T(8,128)(2,1)S(1)} %get-tuple-element.33.y_ref), channel_id=1, source_target_pairs={{0,16},{16,0},{1,17},{17,1},{2,18},{18,2},{3,19},{19,3},{4,20},{20... | collective-permute-start | bytes 196616 | tf_op jit(solution)/shard_map/ppermute | solution.py:266
  33.0 5.7 %collective-permute-start.6 = (bf16[2,256,128]{2,1,0:T(8,128)(2,1)S(1)}, bf16[2,256,128]{2,1,0:T(8,128)(2,1)S(1)}, u32[]{:S(2)}, u32[]{:S(2)}) collective-permute-start(bf16[2,256,128]{2,1,0:T(8,128)(2,1)S(1)} %pair_kernel.1.pair_ref), channel_id=1, source_target_pairs={{0,32},{32,64},{64,96},{96,128},{128,160},{160,192},{192,224},{224... | collective-permute-start | bytes 393224 | tf_op jit(solution)/shard_map/ppermute | solution.py:273
  38.7 1.2 %collective-permute-start.5 = (bf16[2,256,128]{2,1,0:T(8,128)(2,1)S(1)}, bf16[2,256,128]{2,1,0:T(8,128)(2,1)S(1)}, u32[]{:S(2)}, u32[]{:S(2)}) collective-permute-start(bf16[2,256,128]{2,1,0:T(8,128)(2,1)S(1)} %pair_kernel.1.pair_ref), channel_id=1, source_target_pairs={{0,64},{32,96},{64,128},{96,160},{128,192},{160,224},{192,0},{224,... | collective-permute-start | bytes 393224 | tf_op jit(solution)/shard_map/ppermute | solution.py:273
  41.0 1.0 copy-done.1
  42.5 1.3 %collective-permute-done.5.two_ref = bf16[2,256,128]{2,1,0:T(8,128)(2,1)S(1)} collective-permute-done((bf16[2,256,128]{2,1,0:T(8,128)(2,1)S(1)}, bf16[2,256,128]{2,1,0:T(8,128)(2,1)S(1)}, u32[]{:S(2)}, u32[]{:S(2)}) %collective-permute-start.5) | collective-permute-done | bytes 131104 | tf_op jit(solution)/shard_map/ppermute | solution.py:273
  43.7 1.9 %collective-permute-done.4.three_ref = bf16[2,256,128]{2,1,0:T(8,128)(2,1)S(1)} collective-permute-done((bf16[2,256,128]{2,1,0:T(8,128)(2,1)S(1)}, bf16[2,256,128]{2,1,0:T(8,128)(2,1)S(1)}, u32[]{:S(2)}, u32[]{:S(2)}) %collective-permute-start.4) | collective-permute-done | bytes 131104 | tf_op jit(solution)/shard_map/ppermute | solution.py:273
  45.6 1.0 aggregate_kernel.1
  46.6 8.6 %collective-permute-start.7 = (f32[256,128]{1,0:T(8,128)S(1)}, f32[256,128]{1,0:T(8,128)S(1)}, u32[]{:S(2)}, u32[]{:S(2)}) collective-permute-start(f32[256,128]{1,0:T(8,128)S(1)} %get-tuple-element.35), channel_id=1, source_target_pairs={{0,16},{16,0},{1,17},{17,1},{2,18},{18,2},{3,19},{19,3},{4,20},{20... | collective-permute-start | bytes 393224 | tf_op jit(solution)/shard_map/ppermute | solution.py:266
  57.3 1.1 collective-permute-done.8.both_pair_ref
  58.3 1.3 %transpose_kernel.1 = (bf16[2,128,256]{2,1,0:T(8,128)(2,1)S(1)}, bf16[2,128,256]{2,1,0:T(8,128)(2,1)S(1)}, bf16[2,128,256]{2,1,0:T(8,128)(2,1)S(1)}, bf16[2,128,...) custom-call(s32[3]{0:T(128)S(1)} %pad_add_fusion.place_ref, ...), custom_call_target="tpu_custom_call", output_to_operand_aliasing={{5}: (7, {})} | custom-call | tf_op jit(solution)/shard_map/transpose_kernel/pallas_call | solution.py:253
  60.8 1.5 %collective-permute-start.10 = (bf16[2,128,256]{2,1,0:T(8,128)(2,1)S(1)}, bf16[2,128,256]{2,1,0:T(8,128)(2,1)S(1)}, u32[]{:S(2)}, u32[]{:S(2)}) collective-permute-start(bf16[2,128,256]{2,1,0:T(8,128)(2,1)S(1)} %get-tuple-element.39), channel_id=1, source_target_pairs={{0,96},{32,128},{64,160},{96,192},{128,224},{160,0},{192,32},{224,... | collective-permute-start | bytes 393224 | tf_op jit(solution)/shard_map/ppermute | solution.py:273
  62.3 3.3 %collective-permute-start.11 = (bf16[2,128,256]{2,1,0:T(8,128)(2,1)S(1)}, bf16[2,128,256]{2,1,0:T(8,128)(2,1)S(1)}, u32[]{:S(2)}, u32[]{:S(2)}) collective-permute-start(bf16[2,128,256]{2,1,0:T(8,128)(2,1)S(1)} %get-tuple-element.40), channel_id=1, source_target_pairs={{0,64},{32,96},{64,128},{96,160},{128,192},{160,224},{192,0},{224,... | collective-permute-start | bytes 393224 | tf_op jit(solution)/shard_map/ppermute | solution.py:273
  65.6 1.1 collective-permute-done.10.three_ref
  66.7 8.3 %collective-permute-done.11.two_ref = bf16[2,128,256]{2,1,0:T(8,128)(2,1)S(1)} collective-permute-done((bf16[2,128,256]{2,1,0:T(8,128)(2,1)S(1)}, bf16[2,128,256]{2,1,0:T(8,128)(2,1)S(1)}, u32[]{:S(2)}, u32[]{:S(2)}) %collective-permute-start.11) | collective-permute-done | bytes 131104 | tf_op jit(solution)/shard_map/ppermute | solution.py:273
  75.0 1.4 %collective-permute-done.12.one_ref = bf16[2,128,256]{2,1,0:T(8,128)(2,1)S(1)} collective-permute-done((bf16[2,128,256]{2,1,0:T(8,128)(2,1)S(1)}, bf16[2,128,256]{2,1,0:T(8,128)(2,1)S(1)}, u32[]{:S(2)}, u32[]{:S(2)}) %collective-permute-start.12) | collective-permute-done | bytes 131104 | tf_op jit(solution)/shard_map/ppermute | solution.py:273
  77.0 3.3 %collective-permute-start.13 = (f32[2,128,256]{2,1,0:T(8,128)S(1)}, f32[2,128,256]{2,1,0:T(8,128)S(1)}, u32[]{:S(2)}, u32[]{:S(2)}) collective-permute-start(f32[2,128,256]{2,1,0:T(8,128)S(1)} %fold_kernel.2.fold_ref), channel_id=1, source_target_pairs={{0,16},{16,0},{1,17},{17,1},{2,18},{18,2},{3,19},{19,3},{4,20},{20... | collective-permute-start | bytes 786440 | tf_op jit(solution)/shard_map/ppermute | solution.py:266
  80.2 1.2 %collective-permute-done.13.came_ref = f32[2,128,256]{2,1,0:T(8,128)S(1)} collective-permute-done((f32[2,128,256]{2,1,0:T(8,128)S(1)}, f32[2,128,256]{2,1,0:T(8,128)S(1)}, u32[]{:S(2)}, u32[]{:S(2)}) %collective-permute-start.13) | collective-permute-done | bytes 262176 | tf_op jit(solution)/shard_map/ppermute | solution.py:266
  81.4 1.5 %feature_grad_kernel.1 = (bf16[2,256,256]{2,1,0:T(8,128)(2,1)S(1)}, bf16[16,128,256]{2,1,0:T(8,128)(2,1)}) custom-call(f32[2,128,256]{2,1,0:T(8,128)S(1)} %fold_kernel.2.fold_ref, f32[2,128,256]{2,1,0:T(8,128)S(1)} %collective-permute-done.13.came_ref, bf16[384,256]{1,0:T(8,128)(2,1)S(1)} %get-tuple-element.37.both_ref, bf16[2048,128]{1,0:T(8,128)(2,1)S(1)} %copy-done.2, ...), custom_call_target="tpu_custom_call" | custom-call | tf_op jit(solution)/shard_map/feature_grad_kernel/pallas_call | solution.py:253
  83.6 3.8 %all-to-all-start.1 = ((bf16[16,128,256]{2,1,0:T(8,128)(2,1)}), bf16[16,128,256]{2,1,0:T(8,128)(2,1)S(1)}, u32[]{:S(2)}, u32[]{:S(2)}) async-start(bf16[16,128,256]{2,1,0:T(8,128)(2,1)} %get-tuple-element.50), calls=%async_computation.1 | async-start | bytes 2097152 | tf_op jit(solution)/shard_map/all_to_all | solution.py:363
  88.4 1.6 %weight_grad_kernel.1 = (bf16[2,256,128]{2,1,0:T(8,128)(2,1)S(1)}, bf16[2,256,128]{2,1,0:T(8,128)(2,1)S(1)}, bf16[2,256,128]{2,1,0:T(8,128)(2,1)S(1)}, bf16[2,256,128]{2,1,0:T(8,128)(2,1)S(1)}, f32[256,128]{1,0:T(8,128)S(1)}) custom-call(s32[3]{0:T(128)S(1)} %pad_add_fusion.place_ref, bf16[384,256]{1,0:T(8,128)(2,1)S(1)} %get-tuple-element.37.both_ref, ...), custom_call_target="tpu_custom_call" | custom-call | tf_op jit(solution)/shard_map/weight_grad_kernel/pallas_call | solution.py:253
  90.7 2.9 %collective-permute-start.16 = (bf16[2,256,128]{2,1,0:T(8,128)(2,1)S(1)}, bf16[2,256,128]{2,1,0:T(8,128)(2,1)S(1)}, u32[]{:S(2)}, u32[]{:S(2)}) collective-permute-start(bf16[2,256,128]{2,1,0:T(8,128)(2,1)S(1)} %get-tuple-element.46), channel_id=1, source_target_pairs={{0,96},{32,128},{64,160},{96,192},{128,224},{160,0},{192,32},{224,... | collective-permute-start | bytes 393224 | tf_op jit(solution)/shard_map/ppermute | solution.py:273
  94.0 1.0 collective-permute-start.18
  95.1 5.8 %collective-permute-done.16.three_ref = bf16[2,256,128]{2,1,0:T(8,128)(2,1)S(1)} collective-permute-done((bf16[2,256,128]{2,1,0:T(8,128)(2,1)S(1)}, bf16[2,256,128]{2,1,0:T(8,128)(2,1)S(1)}, u32[]{:S(2)}, u32[]{:S(2)}) %collective-permute-start.16) | collective-permute-done | bytes 131104 | tf_op jit(solution)/shard_map/ppermute | solution.py:273
  101.1 4.5 %collective-permute-done.18.one_ref = bf16[2,256,128]{2,1,0:T(8,128)(2,1)S(1)} collective-permute-done((bf16[2,256,128]{2,1,0:T(8,128)(2,1)S(1)}, bf16[2,256,128]{2,1,0:T(8,128)(2,1)S(1)}, u32[]{:S(2)}, u32[]{:S(2)}) %collective-permute-start.18) | collective-permute-done | bytes 131104 | tf_op jit(solution)/shard_map/ppermute | solution.py:273
  106.2 4.1 %collective-permute-start.19 = (f32[2,256,128]{2,1,0:T(8,128)S(1)}, f32[2,256,128]{2,1,0:T(8,128)S(1)}, u32[]{:S(2)}, u32[]{:S(2)}) collective-permute-start(f32[2,256,128]{2,1,0:T(8,128)S(1)} %fold_kernel.3.fold_ref), channel_id=1, source_target_pairs={{0,16},{16,0},{1,17},{17,1},{2,18},{18,2},{3,19},{19,3},{4,20},{20... | collective-permute-start | bytes 786440 | tf_op jit(solution)/shard_map/ppermute | solution.py:266
  (39 shorter events, 12.4 us)
Async XLA Ops:
  2.6 23.6 %all-to-all-start = ((bf16[16,256,128]{2,1,0:T(8,128)(2,1)}), bf16[16,256,128]{2,1,0:T(8,128)(2,1)S(1)}, u32[]{:S(2)}, u32[]{:S(2)}) async-start(bf16[16,256,128]{2,1,0:T(8,128)(2,1)} %spread_kernel.1), calls=%async_computation | async-start | bytes 2097152 | tf_op jit(solution)/shard_map/all_to_all | solution.py:299
  10.9 45.3 %copy-start.5 = (bf16[256,128]{1,0:T(8,128)(2,1)S(1)}, bf16[256,128]{1,0:T(8,128)(2,1)}, u32[]{:S(2)}) copy-start(bf16[256,128]{1,0:T(8,128)(2,1)} %og_ref.1) | copy-start | bytes 196612
  13.2 29.2 %collective-permute-start.1 = (bf16[16,256,128]{2,1,0:T(8,128)(2,1)S(1)}, bf16[16,256,128]{2,1,0:T(8,128)(2,1)S(1)}, u32[]{:S(2)}, u32[]{:S(2)}) collective-permute-start(bf16[16,256,128]{2,1,0:T(8,128)(2,1)S(1)} %get-tuple-element.32.adj_ref), channel_id=1, source_target_pairs={{0,16},{16,0},{1,17},{17,1},{2,18},{18,2},{3,19},{19,3},{4,20},{20... | collective-permute-start | bytes 3145736 | tf_op jit(solution)/shard_map/ppermute | solution.py:266
  14.4 2.3 %collective-permute-start = (s32[16]{0:T(128)S(1)}, s32[16]{0:T(128)S(1)}, u32[]{:S(2)}, u32[]{:S(2)}) collective-permute-start(s32[16]{0:T(128)S(1)} %get-tuple-element.30.sel_ref), channel_id=1, source_target_pairs={{0,16},{16,0},{1,17},{17,1},{2,18},{18,2},{3,19},{19,3},{4,20},{20... | collective-permute-start | bytes 200 | tf_op jit(solution)/shard_map/ppermute | solution.py:266
  26.2 55.2 %copy-start.2 = (bf16[2048,128]{1,0:T(8,128)(2,1)S(1)}, bf16[2048,128]{1,0:T(8,128)(2,1)}, u32[]{:S(2)}) copy-start(bf16[2048,128]{1,0:T(8,128)(2,1)} %ws_ref.1) | copy-start | bytes 1572868
  28.8 52.6 %copy-start = (bf16[2048,128]{1,0:T(8,128)(2,1)S(1)}, bf16[2048,128]{1,0:T(8,128)(2,1)}, u32[]{:S(2)}) copy-start(bf16[2048,128]{1,0:T(8,128)(2,1)} %wn_ref.1) | copy-start | bytes 1572868
  28.8 3.6 %collective-permute-start.2 = (bf16[256,128]{1,0:T(8,128)(2,1)S(1)}, bf16[256,128]{1,0:T(8,128)(2,1)S(1)}, u32[]{:S(2)}, u32[]{:S(2)}) collective-permute-start(bf16[256,128]{1,0:T(8,128)(2,1)S(1)} %get-tuple-element.33.y_ref), channel_id=1, source_target_pairs={{0,16},{16,0},{1,17},{17,1},{2,18},{18,2},{3,19},{19,3},{4,20},{20... | collective-permute-start | bytes 196616 | tf_op jit(solution)/shard_map/ppermute | solution.py:266
  33.0 9.4 %collective-permute-start.6 = (bf16[2,256,128]{2,1,0:T(8,128)(2,1)S(1)}, bf16[2,256,128]{2,1,0:T(8,128)(2,1)S(1)}, u32[]{:S(2)}, u32[]{:S(2)}) collective-permute-start(bf16[2,256,128]{2,1,0:T(8,128)(2,1)S(1)} %pair_kernel.1.pair_ref), channel_id=1, source_target_pairs={{0,32},{32,64},{64,96},{96,128},{128,160},{160,192},{192,224},{224... | collective-permute-start | bytes 393224 | tf_op jit(solution)/shard_map/ppermute | solution.py:273
  38.7 5.1 %collective-permute-start.5 = (bf16[2,256,128]{2,1,0:T(8,128)(2,1)S(1)}, bf16[2,256,128]{2,1,0:T(8,128)(2,1)S(1)}, u32[]{:S(2)}, u32[]{:S(2)}) collective-permute-start(bf16[2,256,128]{2,1,0:T(8,128)(2,1)S(1)} %pair_kernel.1.pair_ref), channel_id=1, source_target_pairs={{0,64},{32,96},{64,128},{96,160},{128,192},{160,224},{192,0},{224,... | collective-permute-start | bytes 393224 | tf_op jit(solution)/shard_map/ppermute | solution.py:273
  39.8 5.7 %collective-permute-start.4 = (bf16[2,256,128]{2,1,0:T(8,128)(2,1)S(1)}, bf16[2,256,128]{2,1,0:T(8,128)(2,1)S(1)}, u32[]{:S(2)}, u32[]{:S(2)}) collective-permute-start(bf16[2,256,128]{2,1,0:T(8,128)(2,1)S(1)} %pair_kernel.1.pair_ref), channel_id=1, source_target_pairs={{0,96},{32,128},{64,160},{96,192},{128,224},{160,0},{192,32},{224,... | collective-permute-start | bytes 393224 | tf_op jit(solution)/shard_map/ppermute | solution.py:273
  40.3 5.3 %collective-permute-start.3 = (bf16[2,256,128]{2,1,0:T(8,128)(2,1)S(1)}, bf16[2,256,128]{2,1,0:T(8,128)(2,1)S(1)}, u32[]{:S(2)}, u32[]{:S(2)}) collective-permute-start(bf16[2,256,128]{2,1,0:T(8,128)(2,1)S(1)} %pair_kernel.1.pair_ref), channel_id=1, source_target_pairs={{0,128},{32,160},{64,192},{96,224},{128,0},{160,32},{192,64},{224,... | collective-permute-start | bytes 393224 | tf_op jit(solution)/shard_map/ppermute | solution.py:273
  41.0 1.0 copy-start.1
  46.6 9.6 %collective-permute-start.7 = (f32[256,128]{1,0:T(8,128)S(1)}, f32[256,128]{1,0:T(8,128)S(1)}, u32[]{:S(2)}, u32[]{:S(2)}) collective-permute-start(f32[256,128]{1,0:T(8,128)S(1)} %get-tuple-element.35), channel_id=1, source_target_pairs={{0,16},{16,0},{1,17},{17,1},{2,18},{18,2},{3,19},{19,3},{4,20},{20... | collective-permute-start | bytes 393224 | tf_op jit(solution)/shard_map/ppermute | solution.py:266
  56.9 1.4 %collective-permute-start.8 = (bf16[384,256]{1,0:T(8,128)(2,1)S(1)}, bf16[384,256]{1,0:T(8,128)(2,1)S(1)}, u32[]{:S(2)}, u32[]{:S(2)}) collective-permute-start(bf16[384,256]{1,0:T(8,128)(2,1)S(1)} %get-tuple-element.37.both_ref), channel_id=1, source_target_pairs={{0,16},{16,0},{1,17},{17,1},{2,18},{18,2},{3,19},{19,3},{4,20},{20... | collective-permute-start | bytes 589832 | tf_op jit(solution)/shard_map/ppermute | solution.py:266
  59.7 27.8 %collective-permute-start.14 = (bf16[16,256,128]{2,1,0:T(8,128)(2,1)S(1)}, bf16[16,256,128]{2,1,0:T(8,128)(2,1)S(1)}, u32[]{:S(2)}, u32[]{:S(2)}) collective-permute-start(bf16[16,256,128]{2,1,0:T(8,128)(2,1)S(1)} %get-tuple-element.44.x_ref), channel_id=1, source_target_pairs={{0,16},{16,0},{1,17},{17,1},{2,18},{18,2},{3,19},{19,3},{4,20},{20... | collective-permute-start | bytes 3145736 | tf_op jit(solution)/shard_map/ppermute | solution.py:266
  60.1 5.5 %collective-permute-start.9 = (bf16[2,128,256]{2,1,0:T(8,128)(2,1)S(1)}, bf16[2,128,256]{2,1,0:T(8,128)(2,1)S(1)}, u32[]{:S(2)}, u32[]{:S(2)}) collective-permute-start(bf16[2,128,256]{2,1,0:T(8,128)(2,1)S(1)} %get-tuple-element.38), channel_id=1, source_target_pairs={{0,128},{32,160},{64,192},{96,224},{128,0},{160,32},{192,64},{224,... | collective-permute-start | bytes 393224 | tf_op jit(solution)/shard_map/ppermute | solution.py:273
  60.8 5.9 %collective-permute-start.10 = (bf16[2,128,256]{2,1,0:T(8,128)(2,1)S(1)}, bf16[2,128,256]{2,1,0:T(8,128)(2,1)S(1)}, u32[]{:S(2)}, u32[]{:S(2)}) collective-permute-start(bf16[2,128,256]{2,1,0:T(8,128)(2,1)S(1)} %get-tuple-element.39), channel_id=1, source_target_pairs={{0,96},{32,128},{64,160},{96,192},{128,224},{160,0},{192,32},{224,... | collective-permute-start | bytes 393224 | tf_op jit(solution)/shard_map/ppermute | solution.py:273
  62.3 12.7 %collective-permute-start.11 = (bf16[2,128,256]{2,1,0:T(8,128)(2,1)S(1)}, bf16[2,128,256]{2,1,0:T(8,128)(2,1)S(1)}, u32[]{:S(2)}, u32[]{:S(2)}) collective-permute-start(bf16[2,128,256]{2,1,0:T(8,128)(2,1)S(1)} %get-tuple-element.40), channel_id=1, source_target_pairs={{0,64},{32,96},{64,128},{96,160},{128,192},{160,224},{192,0},{224,... | collective-permute-start | bytes 393224 | tf_op jit(solution)/shard_map/ppermute | solution.py:273
  65.6 10.8 %collective-permute-start.12 = (bf16[2,128,256]{2,1,0:T(8,128)(2,1)S(1)}, bf16[2,128,256]{2,1,0:T(8,128)(2,1)S(1)}, u32[]{:S(2)}, u32[]{:S(2)}) collective-permute-start(bf16[2,128,256]{2,1,0:T(8,128)(2,1)S(1)} %get-tuple-element.41), channel_id=1, source_target_pairs={{0,32},{32,64},{64,96},{96,128},{128,160},{160,192},{192,224},{224... | collective-permute-start | bytes 393224 | tf_op jit(solution)/shard_map/ppermute | solution.py:273
  77.0 4.4 %collective-permute-start.13 = (f32[2,128,256]{2,1,0:T(8,128)S(1)}, f32[2,128,256]{2,1,0:T(8,128)S(1)}, u32[]{:S(2)}, u32[]{:S(2)}) collective-permute-start(f32[2,128,256]{2,1,0:T(8,128)S(1)} %fold_kernel.2.fold_ref), channel_id=1, source_target_pairs={{0,16},{16,0},{1,17},{17,1},{2,18},{18,2},{3,19},{19,3},{4,20},{20... | collective-permute-start | bytes 786440 | tf_op jit(solution)/shard_map/ppermute | solution.py:266
  82.9 0.7 copy-start.3
  83.6 26.7 %all-to-all-start.1 = ((bf16[16,128,256]{2,1,0:T(8,128)(2,1)}), bf16[16,128,256]{2,1,0:T(8,128)(2,1)S(1)}, u32[]{:S(2)}, u32[]{:S(2)}) async-start(bf16[16,128,256]{2,1,0:T(8,128)(2,1)} %get-tuple-element.50), calls=%async_computation.1 | async-start | bytes 2097152 | tf_op jit(solution)/shard_map/all_to_all | solution.py:363
  87.5 1.0 copy-start.4
  90.1 5.0 %collective-permute-start.15 = (bf16[2,256,128]{2,1,0:T(8,128)(2,1)S(1)}, bf16[2,256,128]{2,1,0:T(8,128)(2,1)S(1)}, u32[]{:S(2)}, u32[]{:S(2)}) collective-permute-start(bf16[2,256,128]{2,1,0:T(8,128)(2,1)S(1)} %get-tuple-element.45), channel_id=1, source_target_pairs={{0,128},{32,160},{64,192},{96,224},{128,0},{160,32},{192,64},{224,... | collective-permute-start | bytes 393224 | tf_op jit(solution)/shard_map/ppermute | solution.py:273
  90.7 10.1 %collective-permute-start.16 = (bf16[2,256,128]{2,1,0:T(8,128)(2,1)S(1)}, bf16[2,256,128]{2,1,0:T(8,128)(2,1)S(1)}, u32[]{:S(2)}, u32[]{:S(2)}) collective-permute-start(bf16[2,256,128]{2,1,0:T(8,128)(2,1)S(1)} %get-tuple-element.46), channel_id=1, source_target_pairs={{0,96},{32,128},{64,160},{96,192},{128,224},{160,0},{192,32},{224,... | collective-permute-start | bytes 393224 | tf_op jit(solution)/shard_map/ppermute | solution.py:273
  93.6 7.5 %collective-permute-start.17 = (bf16[2,256,128]{2,1,0:T(8,128)(2,1)S(1)}, bf16[2,256,128]{2,1,0:T(8,128)(2,1)S(1)}, u32[]{:S(2)}, u32[]{:S(2)}) collective-permute-start(bf16[2,256,128]{2,1,0:T(8,128)(2,1)S(1)} %get-tuple-element.47), channel_id=1, source_target_pairs={{0,64},{32,96},{64,128},{96,160},{128,192},{160,224},{192,0},{224,... | collective-permute-start | bytes 393224 | tf_op jit(solution)/shard_map/ppermute | solution.py:273
  94.0 11.6 %collective-permute-start.18 = (bf16[2,256,128]{2,1,0:T(8,128)(2,1)S(1)}, bf16[2,256,128]{2,1,0:T(8,128)(2,1)S(1)}, u32[]{:S(2)}, u32[]{:S(2)}) collective-permute-start(bf16[2,256,128]{2,1,0:T(8,128)(2,1)S(1)} %get-tuple-element.48), channel_id=1, source_target_pairs={{0,32},{32,64},{64,96},{96,128},{128,160},{160,192},{192,224},{224... | collective-permute-start | bytes 393224 | tf_op jit(solution)/shard_map/ppermute | solution.py:273
  106.2 5.3 %collective-permute-start.19 = (f32[2,256,128]{2,1,0:T(8,128)S(1)}, f32[2,256,128]{2,1,0:T(8,128)S(1)}, u32[]{:S(2)}, u32[]{:S(2)}) collective-permute-start(f32[2,256,128]{2,1,0:T(8,128)S(1)} %fold_kernel.3.fold_ref), channel_id=1, source_target_pairs={{0,16},{16,0},{1,17},{17,1},{2,18},{18,2},{3,19},{19,3},{4,20},{20... | collective-permute-start | bytes 786440 | tf_op jit(solution)/shard_map/ppermute | solution.py:266

commit v8 on v5

--- a/solution.py
+++ b/solution.py
@@ -115,8 +115,8 @@
     return ref[chip, pl.ds(pl.multiple_of(sel_ref[owner] * T, T), T), :]
 
 
-def half_kernel(place_ref, sel_ref, x_ref, w_ref, adj_ref, inv_ref, own_ref, z_ref):
-    core = place_ref[0]
+def half_kernel(sel_ref, x_ref, w_ref, adj_ref, inv_ref, own_ref, z_ref):
+    core = lax.axis_index("c")
     total = dot(x_ref[0], w_ref[0:T, :])
     for part in range(1, x_ref.shape[0]):
         total = total + dot(x_ref[part], w_ref[part * T : (part + 1) * T, :])
@@ -128,11 +128,11 @@
 
 
 def activation_kernel(
-    place_ref, sel_ref, adj_ref, inv_ref, own_ref, other_ref, z_ref, og_ref,
+    sel_ref, adj_ref, inv_ref, own_ref, other_ref, z_ref, og_ref,
     out_ref, gt_ref, pay_ref, mask_ref,
 ):
-    core = place_ref[0]
-    me = place_ref[1]
+    core = lax.axis_index("c")
+    me = 2 * lax.axis_index("z") + core
     rows = z_ref.shape[0]
     summed = jnp.zeros(z_ref.shape, F32)
     for chip in range(other_ref.shape[0]):
@@ -155,7 +155,10 @@
             mask_ref[pl.ds(owner, 1), :] = jnp.sum(jnp.where(row == me, flags, 0.0), axis=0, keepdims=True)
 
 
-def feature_grad_kernel(came_ref, mask_ref, gt_ref, ws_ref, wn_ref, bt_ref, pay_ref, buf, sems):
+def weight_grad_kernel(came_ref, mask_ref, gt_ref, x_ref, bt_ref, keep_ref, send_ref):
+    core = lax.axis_index("c")
+    here = lax.axis_index("z")
+    chips = keep_ref.shape[0]
     low = jnp.zeros((T, T), F32)
     high = jnp.zeros((T, T), F32)
     for sender in range(came_ref.shape[0]):
@@ -164,9 +167,21 @@
         low = low + jnp.where(is_high, 0.0, came)
         high = high + jnp.where(is_high, came, 0.0)
     both = halves(jnp.concatenate([low, high], axis=1))
-    bt = both[0:T]
-    bt_ref[...] = both
+    bt_ref[...] = both[0:T]
+    left = jnp.concatenate([gt_ref[...], both], axis=0)
+    for slot, step in enumerate(far_first(chips) + (0,)):
+        chip = lax.rem(here + step, chips)
+        kept = dot(left, x_ref[2 * chip + core])
+        sent = dot(left, x_ref[2 * chip + 1 - core])
+        keep_ref[slot, 0:T] = kept[0:T]
+        keep_ref[slot, T:] = kept[T : 2 * T] + kept[2 * T :]
+        send_ref[slot, 0:T] = sent[0:T].astype(BF16)
+        send_ref[slot, T:] = (sent[T : 2 * T] + sent[2 * T :]).astype(BF16)
+
+
+def feature_grad_kernel(gt_ref, bt_ref, ws_ref, wn_ref, pay_ref, buf, sems):
     gt = gt_ref[...]
+    bt = bt_ref[...]
     copies = []
     for part in range(pay_ref.shape[0]):
         span = slice(part * T, (part + 1) * T)
@@ -177,23 +192,8 @@
         copy.wait()
 
 
-def weight_grad_kernel(place_ref, gt_ref, bt_ref, x_ref, keep_ref, send_ref):
-    core = place_ref[0]
-    here = place_ref[2]
-    chips = keep_ref.shape[0]
-    left = jnp.concatenate([gt_ref[...], bt_ref[...]], axis=0)
-    for slot, step in enumerate(far_first(chips) + (0,)):
-        chip = lax.rem(here + step, chips)
-        kept = dot(left, x_ref[2 * chip + core])
-        sent = dot(left, x_ref[2 * chip + 1 - core])
-        keep_ref[slot, 0:T] = kept[0:T]
-        keep_ref[slot, T:] = kept[T : 2 * T] + kept[2 * T :]
-        send_ref[slot, 0:T] = sent[0:T].astype(BF16)
-        send_ref[slot, T:] = (sent[T : 2 * T] + sent[2 * T :]).astype(BF16)
-
-
-def pair_kernel(keep_ref, came_ref, *pay_refs):
-    for slot, pay_ref in enumerate(pay_refs):
+def pair_kernel(keep_ref, came_ref, payload_ref, *pay_refs):
+    for slot, pay_ref in enumerate(pay_refs[:-1]):
         pay_ref[...] = (keep_ref[slot] + came_ref[slot].astype(F32)).astype(pay_ref.dtype)
 
 
@@ -238,9 +238,6 @@
     rows = features.shape[0]
     groups = 2 * chips
     slots = tile_weight.shape[1]
-    core = lax.axis_index("c")
-    here = lax.axis_index("z")
-    place = jnp.stack([core, here * 2 + core, here]).astype(jnp.int32)
     swap = [(0, 1), (1, 0)]
 
     x_pay, adj, inverse, flags, sel = call(
@@ -267,7 +264,7 @@
         ],
         limit=20,
     )
-    x_all = lax.all_to_all(x_pay, ("y", "x"), 0, 0, tiled=True)
+    x_all = lax.all_to_all(x_pay, "f", 0, 0, tiled=True)
     (y_pay,) = call(
         neighbour_product_kernel, (x_all, w_neigh, flags), [((chips, rows + groups, T), BF16)]
     )
@@ -275,35 +272,39 @@
     y_other = lax.ppermute(y_own, "c", swap)
     (z_half,) = call(
         half_kernel,
-        (place, sel, x_all, w_self, adj, inverse, y_own),
+        (sel, x_all, w_self, adj, inverse, y_own),
         [((rows, T), F32)],
-        in_specs=[SMEM, SMEM] + [VMEM] * 5,
+        in_specs=[SMEM] + [VMEM] * 5,
     )
     output, gt, c_pay, mask = call(
         activation_kernel,
-        (place, sel, adj, inverse, y_own, y_other, z_half, out_grad),
+        (sel, adj, inverse, y_own, y_other, z_half, out_grad),
         [((rows, T), BF16), ((T, rows), BF16), ((groups, T, T), BF16), ((groups, T), F32)],
-        in_specs=[SMEM, SMEM] + [VMEM] * 6,
+        in_specs=[SMEM] + [VMEM] * 6,
     )
     c_all = lax.all_to_all(c_pay, ("z", "c"), 0, 0, tiled=True)
-    bt, p_pay = call(
+    bt, keep, send = call(
+        weight_grad_kernel,
+        (c_all, mask, gt, x_all),
+        [((T, rows), BF16), ((chips, 2 * T, T), F32), ((chips, 2 * T, T), BF16)],
+    )
+    came = lax.ppermute(send, "c", swap)
+    (p_pay,) = call(
         feature_grad_kernel,
-        (c_all, mask, gt, w_self, w_neigh),
-        [((2 * T, rows), BF16), ((parts, T, rows), BF16)],
-        out_specs=[VMEM, HBM],
+        (gt, bt, w_self, w_neigh),
+        [((parts, T, rows), BF16)],
+        out_specs=[HBM],
         scratch=[pltpu.VMEM((parts, T, rows), BF16), pltpu.SemaphoreType.DMA((parts,))],
     )
-    p_all = lax.all_to_all(p_pay, ("y", "x"), 0, 0, tiled=True)
-    keep, send = call(
-        weight_grad_kernel,
-        (place, gt, bt, x_all),
-        [((chips, 2 * T, T), F32), ((chips, 2 * T, T), BF16)],
-        in_specs=[SMEM] + [VMEM] * 3,
-    )
-    came = lax.ppermute(send, "c", swap)
-    *w_pay, own = call(
-        pair_kernel, (keep, came), [((2 * T, T), BF16)] * (chips - 1) + [((2 * T, T), F32)]
-    )
+    *w_pay, own, p_pay = call(
+        pair_kernel,
+        (keep, came, p_pay),
+        [((2 * T, T), BF16)] * (chips - 1) + [((2 * T, T), F32), (p_pay.shape, BF16)],
+        in_specs=[VMEM, VMEM, HBM],
+        out_specs=[VMEM] * chips + [HBM],
+        aliases={2: chips},
+    )
+    p_all = lax.all_to_all(p_pay, "f", 0, 0, tiled=True)
     w_came = [
         lax.ppermute(block, "z", [(chip, (chip + step) % chips) for chip in range(chips)])
         for step, block in zip(far_first(chips), w_pay)
@@ -322,8 +323,8 @@
 
 def solution(mesh):
     row_count, part_count = mesh.shape["rows"], mesh.shape["feat"]
-    split = Mesh(mesh.devices.reshape(row_count // 2, 2, 4, part_count // 4), ("z", "c", "y", "x"))
-    rows, feat = ("z", "c"), ("y", "x")
+    split = Mesh(mesh.devices.reshape(row_count // 2, 2, part_count), ("z", "c", "f"))
+    rows, feat = ("z", "c"), "f"
     return jax.shard_map(
         functools.partial(per_device, chips=row_count // 2, parts=part_count),
         mesh=split,

time: 107 us -> 107 us (level)
  waiting for transfers between devices: 3.9 us -> 5.69 us
    all_to_all x1, waiting for transfers between devices: 0.01 us -> 3.67 us  [per_device(): p_all = lax.all_to_all(p_pay, 'f', 0, 0, tiled=True)]
    ppermute x1, waiting for transfers between devices: 1.9 us -> 0.4 us  [per_device(): came = lax.ppermute(send, 'c', swap)]
where the time goes in v8:
time: 107 us
  blocking collectives  66.9 us (63%)
  starting transfers between devices  21.4 us (20%)
  Pallas kernels  11.2 us (10%)
  waiting for transfers between devices  5.69 us (5%)
  between operations  1.46 us (1%)
    all_to_all x1, blocking collectives, per_device(): x_all = lax.all_to_all(x_pay, 'f', 0, 0, tiled=True)  23.9 us
    all_to_all x1, blocking collectives, per_device(): y_own = lax.all_to_all(y_pay, 'z', 0, 0, tiled=True)  22.9 us
    all_to_all x1, blocking collectives, per_device(): c_all = lax.all_to_all(c_pay, ('z', 'c'), 0, 0, tiled=True)  20.2 us
    ppermute x7, starting transfers between devices, per_device(): lax.ppermute(block, 'z', [(chip, (chip + step) % chips) for chip in range...  13.6 us
    pallas_call x9, Pallas kernels, call(): pl.pallas_call(kernel, out_shape=shapes, in_specs=in_specs or [VMEM] * le...  11.2 us
    ppermute x1, starting transfers between devices, per_device(): y_other = lax.ppermute(y_own, 'c', swap)  3.99 us
    all_to_all x1, waiting for transfers between devices, per_device(): p_all = lax.all_to_all(p_pay, 'f', 0, 0, tiled=True)  3.67 us
    all_to_all x1, starting transfers between devices, per_device(): p_all = lax.all_to_all(p_pay, 'f', 0, 0, tiled=True)  3.66 us
  transfers between devices with their start and end apart: 10, of which 4 were waited for; matrix products, arithmetic and copies ran while one was open for 0% of the time, Pallas kernels for 3%

profile of v8, /device:TPU:1, one launch (start us, length us, event | category | flops | bytes accessed | tf_op | source)
XLA Modules:
  0.0 106.7 jit_solution(802644113338828563)
XLA Ops:
  1.4 3.5 %setup_kernel.1 = (bf16[16,256,128]{2,1,0:T(8,128)(2,1)}, bf16[16,256,128]{2,1,0:T(8,128)(2,1)S(1)}, f32[256,128]{1,0:T(8,128)S(1)}, bf16[16,128]{1,0:T(8,128)(2,1)S(1)}, s32[16]{0:T(128)S(1)}) custom-call(s32[1]{0:T(128)S(6)} %copy.16.count_ref, s32[1,80]{1,0:T(1,128)} %dst_hbm.1, s32[1,80]{1,0:T(1,128)} %src_hbm.1, bf16[256,128]{1,0:T(8,128)(2,1)} %x_hbm.1, ...), custom_call_target="tpu_custom_call" | custom-call | tf_op jit(solution)/shard_map/setup_kernel/pallas_call | solution.py:225
  4.9 0.0 copy-start.2
  4.9 23.9 %all_to_all.20.x_ref = bf16[16,256,128]{2,1,0:T(8,128)(2,1)S(1)} all-to-all(bf16[16,256,128]{2,1,0:T(8,128)(2,1)} %get-tuple-element.31), channel_id=1, replica_groups=mesh['z'=8,'c'=2,'f'=16] {'f'}, dimensions={0} | all-to-all | bytes 2097152 | tf_op jit(solution)/shard_map/all_to_all | solution.py:267
  28.7 0.4 neighbour_product_kernel.1
  29.2 22.9 %all_to_all.21.own_ref = bf16[8,272,128]{2,1,0:T(8,128)(2,1)S(1)} all-to-all(bf16[8,272,128]{2,1,0:T(8,128)(2,1)S(1)} %neighbour_product_kernel.1), channel_id=1, replica_groups=mesh['z'=8,'c'=2,'f'=16] {'z'}, dimensions={0} | all-to-all | bytes 1114112 | tf_op jit(solution)/shard_map/all_to_all | solution.py:271
  52.1 4.0 %collective-permute-start = (bf16[8,272,128]{2,1,0:T(8,128)(2,1)S(1)}, bf16[8,272,128]{2,1,0:T(8,128)(2,1)S(1)}, u32[]{:S(2)}, u32[]{:S(2)}) collective-permute-start(bf16[8,272,128]{2,1,0:T(8,128)(2,1)S(1)} %all_to_all.21.own_ref), channel_id=1, source_target_pairs={{0,16},{16,0},{1,17},{17,1},{2,18},{18,2},{3,19},{19,3},{4,20},{20... | collective-permute-start | bytes 1671176 | tf_op jit(solution)/shard_map/ppermute | solution.py:272
  56.1 1.1 %half_kernel.1.z_ref = f32[256,128]{1,0:T(8,128)S(1)} custom-call(s32[16]{0:T(128)S(1)} %get-tuple-element.28.sel_ref, bf16[16,256,128]{2,1,0:T(8,128)(2,1)S(1)} %all_to_all.20.x_ref, bf16[2048,128]{1,0:T(8,128)(2,1)S(1)} %copy-done.1, bf16[16,256,128]{2,1,0:T(8,128)(2,1)S(1)} %get-tuple-element.29.adj_ref, f32[256,128]{1,0:T(8,128)S(1)} %get-tuple-element.30.inv_ref, ...), custom_call_target="tpu_custom_call" | custom-call | tf_op jit(solution)/shard_map/half_kernel/pallas_call | solution.py:225
  57.2 0.5 collective-permute-done.other_ref
  57.6 1.9 %activation_kernel.1 = (bf16[256,128]{1,0:T(8,128)(2,1)}, bf16[128,256]{1,0:T(8,128)(2,1)S(1)}, bf16[16,128,128]{2,1,0:T(8,128)(2,1)S(1)}, f32[16,128]{1,0:T(8,128)S(1)}) custom-call(s32[16]{0:T(128)S(1)} %get-tuple-element.28.sel_ref, bf16[16,256,128]{2,1,0:T(8,128)(2,1)S(1)} %get-tuple-element.29.adj_ref, f32[256,128]{1,0:T(8,128)S(1)} %get-tuple-element.30.inv_ref, ...), custom_call_target="tpu_custom_call" | custom-call | tf_op jit(solution)/shard_map/activation_kernel/pallas_call | solution.py:225
  59.5 20.2 %all_to_all.22.came_ref = bf16[16,128,128]{2,1,0:T(8,128)(2,1)S(1)} all-to-all(bf16[16,128,128]{2,1,0:T(8,128)(2,1)S(1)} %get-tuple-element.34), channel_id=1, replica_groups=mesh['z'=8,'c'=2,'f'=16] {'z','c'}, dimensions={0} | all-to-all | bytes 1048576 | tf_op jit(solution)/shard_map/all_to_all | solution.py:285
  79.7 1.1 %weight_grad_kernel.1 = (bf16[128,256]{1,0:T(8,128)(2,1)S(1)}, f32[8,256,128]{2,1,0:T(8,128)S(1)}, bf16[8,256,128]{2,1,0:T(8,128)(2,1)S(1)}) custom-call(bf16[16,128,128]{2,1,0:T(8,128)(2,1)S(1)} %all_to_all.22.came_ref, f32[16,128]{1,0:T(8,128)S(1)} %get-tuple-element.35.mask_ref, bf16[128,256]{1,0:T(8,128)(2,1)S(1)} %get-tuple-element.36.gt_ref, ...), custom_call_target="tpu_custom_call" | custom-call | tf_op jit(solution)/shard_map/weight_grad_kernel/pallas_call | solution.py:225
  80.8 0.1 collective-permute-start.1
  80.9 1.5 %feature_grad_kernel.1.payload_ref = bf16[16,128,256]{2,1,0:T(8,128)(2,1)} custom-call(bf16[128,256]{1,0:T(8,128)(2,1)S(1)} %get-tuple-element.36.gt_ref, bf16[128,256]{1,0:T(8,128)(2,1)S(1)} %get-tuple-element.39.bt_ref, bf16[2048,128]{1,0:T(8,128)(2,1)S(1)} %copy-done.1, bf16[2048,128]{1,0:T(8,128)(2,1)S(1)} %copy-done), custom_call_target="tpu_custom_call" | custom-call | tf_op jit(solution)/shard_map/feature_grad_kernel/pallas_call | solution.py:225
  82.4 0.4 collective-permute-done.1.came_ref
  82.8 0.1 pair_kernel.1
  82.9 3.7 %all-to-all-start.3 = ((bf16[16,128,256]{2,1,0:T(8,128)(2,1)}), bf16[16,128,256]{2,1,0:T(8,128)(2,1)S(1)}, u32[]{:S(2)}, u32[]{:S(2)}) async-start(bf16[16,128,256]{2,1,0:T(8,128)(2,1)} %get-tuple-element.41), calls=%async_computation.3 | async-start | bytes 2097152 | tf_op jit(solution)/shard_map/all_to_all | solution.py:307
  86.6 1.0 collective-permute-start.2
  87.6 1.1 %collective-permute-start.3 = (bf16[256,128]{1,0:T(8,128)(2,1)S(1)}, bf16[256,128]{1,0:T(8,128)(2,1)S(1)}, u32[]{:S(2)}, u32[]{:S(2)}) collective-permute-start(bf16[256,128]{1,0:T(8,128)(2,1)S(1)} %get-tuple-element.43), channel_id=1, source_target_pairs={{0,96},{32,128},{64,160},{96,192},{128,224},{160,0},{192,32},{224,... | collective-permute-start | bytes 196616 | tf_op jit(solution)/shard_map/ppermute | solution.py:309
  88.7 3.4 %collective-permute-start.4 = (bf16[256,128]{1,0:T(8,128)(2,1)S(1)}, bf16[256,128]{1,0:T(8,128)(2,1)S(1)}, u32[]{:S(2)}, u32[]{:S(2)}) collective-permute-start(bf16[256,128]{1,0:T(8,128)(2,1)S(1)} %get-tuple-element.44), channel_id=1, source_target_pairs={{0,160},{32,192},{64,224},{96,0},{128,32},{160,64},{192,96},{224,1... | collective-permute-start | bytes 196616 | tf_op jit(solution)/shard_map/ppermute | solution.py:309
  92.1 1.4 %collective-permute-start.5 = (bf16[256,128]{1,0:T(8,128)(2,1)S(1)}, bf16[256,128]{1,0:T(8,128)(2,1)S(1)}, u32[]{:S(2)}, u32[]{:S(2)}) collective-permute-start(bf16[256,128]{1,0:T(8,128)(2,1)S(1)} %get-tuple-element.45), channel_id=1, source_target_pairs={{0,64},{32,96},{64,128},{96,160},{128,192},{160,224},{192,0},{224,... | collective-permute-start | bytes 196616 | tf_op jit(solution)/shard_map/ppermute | solution.py:309
  93.5 2.2 %collective-permute-start.6 = (bf16[256,128]{1,0:T(8,128)(2,1)S(1)}, bf16[256,128]{1,0:T(8,128)(2,1)S(1)}, u32[]{:S(2)}, u32[]{:S(2)}) collective-permute-start(bf16[256,128]{1,0:T(8,128)(2,1)S(1)} %get-tuple-element.46), channel_id=1, source_target_pairs={{0,192},{32,224},{64,0},{96,32},{128,64},{160,96},{192,128},{224,1... | collective-permute-start | bytes 196616 | tf_op jit(solution)/shard_map/ppermute | solution.py:309
  95.6 0.0 collective-permute-done.2.refs_0_
  95.6 1.2 %collective-permute-start.7 = (bf16[256,128]{1,0:T(8,128)(2,1)S(1)}, bf16[256,128]{1,0:T(8,128)(2,1)S(1)}, u32[]{:S(2)}, u32[]{:S(2)}) collective-permute-start(bf16[256,128]{1,0:T(8,128)(2,1)S(1)} %get-tuple-element.47), channel_id=1, source_target_pairs={{0,32},{32,64},{64,96},{96,128},{128,160},{160,192},{192,224},{224... | collective-permute-start | bytes 196616 | tf_op jit(solution)/shard_map/ppermute | solution.py:309
  96.9 1.1 %collective-permute-done.3.refs_1_ = bf16[256,128]{1,0:T(8,128)(2,1)S(1)} collective-permute-done((bf16[256,128]{1,0:T(8,128)(2,1)S(1)}, bf16[256,128]{1,0:T(8,128)(2,1)S(1)}, u32[]{:S(2)}, u32[]{:S(2)}) %collective-permute-start.3) | collective-permute-done | bytes 65568 | tf_op jit(solution)/shard_map/ppermute | solution.py:309
  98.0 3.3 %collective-permute-start.8 = (bf16[256,128]{1,0:T(8,128)(2,1)S(1)}, bf16[256,128]{1,0:T(8,128)(2,1)S(1)}, u32[]{:S(2)}, u32[]{:S(2)}) collective-permute-start(bf16[256,128]{1,0:T(8,128)(2,1)S(1)} %get-tuple-element.48), channel_id=1, source_target_pairs={{0,224},{32,0},{64,32},{96,64},{128,96},{160,128},{192,160},{224,1... | collective-permute-start | bytes 196616 | tf_op jit(solution)/shard_map/ppermute | solution.py:309
  101.3 3.7 %all-to-all-done.3.parts_ref = bf16[16,128,256]{2,1,0:T(8,128)(2,1)S(1)} async-done(((bf16[16,128,256]{2,1,0:T(8,128)(2,1)}), bf16[16,128,256]{2,1,0:T(8,128)(2,1)S(1)}, u32[]{:S(2)}, u32[]{:S(2)}) %all-to-all-start.3) | async-done | bytes 1048608 | tf_op jit(solution)/shard_map/all_to_all | solution.py:307
  105.0 0.8 sum_kernel.1.done_ref
  105.8 0.0 collective-permute-done.4.refs_2_
  105.8 0.0 collective-permute-done.5.refs_3_
  105.8 0.0 collective-permute-done.7.refs_5_
  105.9 0.0 collective-permute-done.8.refs_6_
  105.9 0.8 weight_sum_kernel.1
  (6 shorter events, 0.0 us)
Async XLA Ops:
  0.6 28.1 %copy-start = (bf16[2048,128]{1,0:T(8,128)(2,1)S(1)}, bf16[2048,128]{1,0:T(8,128)(2,1)}, u32[]{:S(2)}) copy-start(bf16[2048,128]{1,0:T(8,128)(2,1)} %wn_ref.1) | copy-start | bytes 1572868
  1.3 54.7 %copy-start.1 = (bf16[2048,128]{1,0:T(8,128)(2,1)S(1)}, bf16[2048,128]{1,0:T(8,128)(2,1)}, u32[]{:S(2)}) copy-start(bf16[2048,128]{1,0:T(8,128)(2,1)} %ws_ref.1) | copy-start | bytes 1572868
  4.9 52.8 %copy-start.2 = (bf16[256,128]{1,0:T(8,128)(2,1)S(1)}, bf16[256,128]{1,0:T(8,128)(2,1)}, u32[]{:S(2)}) copy-start(bf16[256,128]{1,0:T(8,128)(2,1)} %og_ref.1) | copy-start | bytes 196612
  52.1 5.6 %collective-permute-start = (bf16[8,272,128]{2,1,0:T(8,128)(2,1)S(1)}, bf16[8,272,128]{2,1,0:T(8,128)(2,1)S(1)}, u32[]{:S(2)}, u32[]{:S(2)}) collective-permute-start(bf16[8,272,128]{2,1,0:T(8,128)(2,1)S(1)} %all_to_all.21.own_ref), channel_id=1, source_target_pairs={{0,16},{16,0},{1,17},{17,1},{2,18},{18,2},{3,19},{19,3},{4,20},{20... | collective-permute-start | bytes 1671176 | tf_op jit(solution)/shard_map/ppermute | solution.py:272
  80.8 2.0 %collective-permute-start.1 = (bf16[8,256,128]{2,1,0:T(8,128)(2,1)S(1)}, bf16[8,256,128]{2,1,0:T(8,128)(2,1)S(1)}, u32[]{:S(2)}, u32[]{:S(2)}) collective-permute-start(bf16[8,256,128]{2,1,0:T(8,128)(2,1)S(1)} %get-tuple-element.38), channel_id=1, source_target_pairs={{0,16},{16,0},{1,17},{17,1},{2,18},{18,2},{3,19},{19,3},{4,20},{20... | collective-permute-start | bytes 1572872 | tf_op jit(solution)/shard_map/ppermute | solution.py:291
  82.9 22.1 %all-to-all-start.3 = ((bf16[16,128,256]{2,1,0:T(8,128)(2,1)}), bf16[16,128,256]{2,1,0:T(8,128)(2,1)S(1)}, u32[]{:S(2)}, u32[]{:S(2)}) async-start(bf16[16,128,256]{2,1,0:T(8,128)(2,1)} %get-tuple-element.41), calls=%async_computation.3 | async-start | bytes 2097152 | tf_op jit(solution)/shard_map/all_to_all | solution.py:307
  86.6 9.1 %collective-permute-start.2 = (bf16[256,128]{1,0:T(8,128)(2,1)S(1)}, bf16[256,128]{1,0:T(8,128)(2,1)S(1)}, u32[]{:S(2)}, u32[]{:S(2)}) collective-permute-start(bf16[256,128]{1,0:T(8,128)(2,1)S(1)} %get-tuple-element.42), channel_id=1, source_target_pairs={{0,128},{32,160},{64,192},{96,224},{128,0},{160,32},{192,64},{224,... | collective-permute-start | bytes 196616 | tf_op jit(solution)/shard_map/ppermute | solution.py:309
  87.6 10.4 %collective-permute-start.3 = (bf16[256,128]{1,0:T(8,128)(2,1)S(1)}, bf16[256,128]{1,0:T(8,128)(2,1)S(1)}, u32[]{:S(2)}, u32[]{:S(2)}) collective-permute-start(bf16[256,128]{1,0:T(8,128)(2,1)S(1)} %get-tuple-element.43), channel_id=1, source_target_pairs={{0,96},{32,128},{64,160},{96,192},{128,224},{160,0},{192,32},{224,... | collective-permute-start | bytes 196616 | tf_op jit(solution)/shard_map/ppermute | solution.py:309
  88.7 17.2 %collective-permute-start.4 = (bf16[256,128]{1,0:T(8,128)(2,1)S(1)}, bf16[256,128]{1,0:T(8,128)(2,1)S(1)}, u32[]{:S(2)}, u32[]{:S(2)}) collective-permute-start(bf16[256,128]{1,0:T(8,128)(2,1)S(1)} %get-tuple-element.44), channel_id=1, source_target_pairs={{0,160},{32,192},{64,224},{96,0},{128,32},{160,64},{192,96},{224,1... | collective-permute-start | bytes 196616 | tf_op jit(solution)/shard_map/ppermute | solution.py:309
  92.1 13.8 %collective-permute-start.5 = (bf16[256,128]{1,0:T(8,128)(2,1)S(1)}, bf16[256,128]{1,0:T(8,128)(2,1)S(1)}, u32[]{:S(2)}, u32[]{:S(2)}) collective-permute-start(bf16[256,128]{1,0:T(8,128)(2,1)S(1)} %get-tuple-element.45), channel_id=1, source_target_pairs={{0,64},{32,96},{64,128},{96,160},{128,192},{160,224},{192,0},{224,... | collective-permute-start | bytes 196616 | tf_op jit(solution)/shard_map/ppermute | solution.py:309
  93.5 12.4 %collective-permute-start.6 = (bf16[256,128]{1,0:T(8,128)(2,1)S(1)}, bf16[256,128]{1,0:T(8,128)(2,1)S(1)}, u32[]{:S(2)}, u32[]{:S(2)}) collective-permute-start(bf16[256,128]{1,0:T(8,128)(2,1)S(1)} %get-tuple-element.46), channel_id=1, source_target_pairs={{0,192},{32,224},{64,0},{96,32},{128,64},{160,96},{192,128},{224,1... | collective-permute-start | bytes 196616 | tf_op jit(solution)/shard_map/ppermute | solution.py:309
  95.6 10.2 %collective-permute-start.7 = (bf16[256,128]{1,0:T(8,128)(2,1)S(1)}, bf16[256,128]{1,0:T(8,128)(2,1)S(1)}, u32[]{:S(2)}, u32[]{:S(2)}) collective-permute-start(bf16[256,128]{1,0:T(8,128)(2,1)S(1)} %get-tuple-element.47), channel_id=1, source_target_pairs={{0,32},{32,64},{64,96},{96,128},{128,160},{160,192},{192,224},{224... | collective-permute-start | bytes 196616 | tf_op jit(solution)/shard_map/ppermute | solution.py:309
  98.0 7.9 %collective-permute-start.8 = (bf16[256,128]{1,0:T(8,128)(2,1)S(1)}, bf16[256,128]{1,0:T(8,128)(2,1)S(1)}, u32[]{:S(2)}, u32[]{:S(2)}) collective-permute-start(bf16[256,128]{1,0:T(8,128)(2,1)S(1)} %get-tuple-element.48), channel_id=1, source_target_pairs={{0,224},{32,0},{64,32},{96,64},{128,96},{160,128},{192,160},{224,1... | collective-permute-start | bytes 196616 | tf_op jit(solution)/shard_map/ppermute | solution.py:309

commit v9 on v8

--- a/solution.py
+++ b/solution.py
@@ -31,9 +31,22 @@
     return jnp.concatenate([high, (block - high.astype(F32)).astype(BF16)], axis=0)
 
 
-def setup_kernel(
-    count_ref, dst_hbm, src_hbm, x_hbm, weight_ref, pay_ref, adj_ref, inv_ref, flag_ref, sel_ref,
-    dst_ref, src_ref, x_ref, buf, acc, in_sems, out_sems, sems,
+def spread_kernel(x_hbm, pay_ref, x_ref, in_sem, sems):
+    copies = [
+        pltpu.make_async_copy(x_ref, pay_ref.at[copy], sems.at[copy]) for copy in range(pay_ref.shape[0])
+    ]
+    came = pltpu.make_async_copy(x_hbm, x_ref, in_sem)
+    came.start()
+    came.wait()
+    for copy in copies:
+        copy.start()
+    for copy in copies:
+        copy.wait()
+
+
+def adjacency_kernel(
+    count_ref, dst_hbm, src_hbm, weight_ref, adj_ref, send_ref, inv_ref, flag_ref, sel_ref,
+    dst_ref, src_ref, buf, acc, in_sems, sems,
 ):
     count = count_ref[0]
     slots = weight_ref.shape[0]
@@ -45,10 +58,7 @@
 
     ins = [
         pltpu.make_async_copy(source, target, in_sems.at[index])
-        for index, (source, target) in enumerate(((x_hbm, x_ref), (dst_hbm, dst_ref), (src_hbm, src_ref)))
-    ]
-    outs = [
-        pltpu.make_async_copy(x_ref, pay_ref.at[copy], out_sems.at[copy]) for copy in range(pay_ref.shape[0])
+        for index, (source, target) in enumerate(((dst_hbm, dst_ref), (src_hbm, src_ref)))
     ]
     for copy in ins:
         copy.start()
@@ -61,11 +71,8 @@
     acc[...] = jnp.zeros_like(acc)
     for owner in range(groups):
         sel_ref[owner] = 0
-    ins[0].wait()
-    for copy in outs:
-        copy.start()
-    ins[1].wait()
-    ins[2].wait()
+    for copy in ins:
+        copy.wait()
     for index in range(slots // CHUNK):
 
         @pl.when(index * CHUNK < count)
@@ -87,6 +94,9 @@
         if owner > 0:
             total = total + acc[owner]
         adj_ref[owner] = acc[owner].astype(F32).astype(BF16)
+    other = 1 - lax.axis_index("c")
+    for chip in range(send_ref.shape[0]):
+        send_ref[chip] = adj_ref[2 * chip + other]
     degree = jnp.sum(total.astype(F32), axis=1, keepdims=True)
     inv_ref[...] = jnp.broadcast_to(1.0 / jnp.maximum(degree, 1.0), inv_ref.shape)
     row = lax.broadcasted_iota(jnp.int32, flag_ref.shape, 0)
@@ -94,52 +104,68 @@
     for owner in range(groups):
         flags = jnp.where(row == owner, sel_ref[owner].astype(F32), flags)
     flag_ref[...] = flags.astype(BF16)
-    for copy in outs:
-        copy.wait()
-
-
-def neighbour_product_kernel(x_ref, w_ref, flag_ref, pay_ref):
-    parts = x_ref.shape[0]
+
+
+def neighbour_kernel(sel_ref, x_ref, w_ref, flag_ref, adj_ref, pay_ref, sel_same_ref, adj_same_ref):
     rows = x_ref.shape[1]
     total = dot(x_ref[0], w_ref[0:T, :])
-    for part in range(1, parts):
+    for part in range(1, x_ref.shape[0]):
         total = total + dot(x_ref[part], w_ref[part * T : (part + 1) * T, :])
     product = total.astype(BF16)
     flags = flag_ref[...]
     for copy in range(pay_ref.shape[0]):
         pay_ref[copy, 0:rows, :] = product
         pay_ref[copy, rows:, :] = flags
-
-
-def chosen_tile(ref, sel_ref, chip, owner):
-    return ref[chip, pl.ds(pl.multiple_of(sel_ref[owner] * T, T), T), :]
-
-
-def half_kernel(sel_ref, x_ref, w_ref, adj_ref, inv_ref, own_ref, z_ref):
-    core = lax.axis_index("c")
+    for owner in range(sel_ref.shape[0]):
+        sel_same_ref[owner] = sel_ref[owner]
+
+
+def self_kernel(x_ref, w_ref, z_ref):
     total = dot(x_ref[0], w_ref[0:T, :])
     for part in range(1, x_ref.shape[0]):
         total = total + dot(x_ref[part], w_ref[part * T : (part + 1) * T, :])
-    summed = jnp.zeros(z_ref.shape, F32)
-    for chip in range(own_ref.shape[0]):
-        owner = 2 * chip + core
-        summed = summed + dot(adj_ref[owner], chosen_tile(own_ref, sel_ref, chip, owner))
-    z_ref[...] = total + inv_ref[...] * summed
-
-
-def activation_kernel(
-    sel_ref, adj_ref, inv_ref, own_ref, other_ref, z_ref, og_ref,
-    out_ref, gt_ref, pay_ref, mask_ref,
+    z_ref[...] = total
+
+
+def aggregate_kernel(
+    sel_ref, sel_pair_ref, adj_ref, adj_pair_ref, y_ref, x_ref, mine_ref, mask_ref, theirs_ref, x_same_ref
 ):
     core = lax.axis_index("c")
-    me = 2 * lax.axis_index("z") + core
+    here = 2 * lax.axis_index("z")
+    chips = y_ref.shape[0]
+    rows = mine_ref.shape[0]
+    row = lax.broadcasted_iota(jnp.int32, (y_ref.shape[1] - rows, T), 0)
+
+    def summed(adj, sel):
+        total = jnp.zeros(mine_ref.shape, F32)
+        for chip in range(chips):
+            owner = 2 * chip + core
+            tile = y_ref[chip, pl.ds(pl.multiple_of(sel[owner] * T, T), T), :]
+            total = total + dot(adj(chip, owner), tile)
+        return total
+
+    theirs_ref[0:rows] = summed(lambda chip, owner: adj_pair_ref[chip], sel_pair_ref)
+    mine_ref[...] = summed(lambda chip, owner: adj_ref[owner], sel_ref)
+    for chip in range(chips):
+        flags = y_ref[chip, rows:, :].astype(F32)
+        mask_ref[chip : chip + 1, :] = jnp.sum(
+            jnp.where(row == here + core, flags, 0.0), axis=0, keepdims=True
+        )
+        theirs_ref[rows + chip : rows + chip + 1, :] = jnp.sum(
+            jnp.where(row == here + 1 - core, flags, 0.0), axis=0, keepdims=True
+        )
+
+
+def activation_kernel(
+    adj_ref, inv_ref, mine_ref, own_mask_ref, came_ref, z_ref, og_ref, out_ref, gt_ref, pay_ref, mask_ref
+):
+    core = lax.axis_index("c")
     rows = z_ref.shape[0]
-    summed = jnp.zeros(z_ref.shape, F32)
-    for chip in range(other_ref.shape[0]):
-        owner = 2 * chip + 1 - core
-        summed = summed + dot(adj_ref[owner], chosen_tile(other_ref, sel_ref, chip, owner))
+    chips = own_mask_ref.shape[0]
+    mask_ref[pl.ds(pl.multiple_of(core * chips, chips), chips), :] = own_mask_ref[...]
+    mask_ref[pl.ds(pl.multiple_of((1 - core) * chips, chips), chips), :] = came_ref[rows:, :]
     inverse = inv_ref[...]
-    z = z_ref[...] + inverse * summed
+    z = z_ref[...] + inverse * (mine_ref[...] + came_ref[0:rows])
     sig = 1.0 / (1.0 + jnp.exp(-z))
     grad = (og_ref[...].astype(F32) * sig * (1.0 + z * (1.0 - sig))).astype(BF16).astype(F32)
     scaled = halves((grad * inverse).T)
@@ -148,11 +174,6 @@
         pay_ref[owner] = (spread[0:T] + spread[T:]).astype(BF16)
     out_ref[...] = (z * sig).astype(BF16)
     gt_ref[...] = grad.T.astype(BF16)
-    row = lax.broadcasted_iota(jnp.int32, mask_ref.shape, 0)
-    for chip in range(own_ref.shape[0]):
-        for ref, owner in ((own_ref, 2 * chip + core), (other_ref, 2 * chip + 1 - core)):
-            flags = ref[chip, rows:, :].astype(F32)
-            mask_ref[pl.ds(owner, 1), :] = jnp.sum(jnp.where(row == me, flags, 0.0), axis=0, keepdims=True)
 
 
 def weight_grad_kernel(came_ref, mask_ref, gt_ref, x_ref, bt_ref, keep_ref, send_ref):
@@ -163,7 +184,8 @@
     high = jnp.zeros((T, T), F32)
     for sender in range(came_ref.shape[0]):
         came = came_ref[sender].astype(F32)
-        is_high = mask_ref[sender : sender + 1, :] > 0.5
+        place = sender % 2 * chips + sender // 2
+        is_high = mask_ref[place : place + 1, :] > 0.5
         low = low + jnp.where(is_high, 0.0, came)
         high = high + jnp.where(is_high, came, 0.0)
     both = halves(jnp.concatenate([low, high], axis=1))
@@ -240,52 +262,66 @@
     slots = tile_weight.shape[1]
     swap = [(0, 1), (1, 0)]
 
-    x_pay, adj, inverse, flags, sel = call(
-        setup_kernel,
-        (tile_count, tile_dst, tile_src, features, tile_weight[0]),
+    (x_pay,) = call(
+        spread_kernel,
+        (features,),
+        [((parts, rows, T), BF16)],
+        in_specs=[HBM],
+        out_specs=[HBM],
+        scratch=[pltpu.VMEM((rows, T), BF16), pltpu.SemaphoreType.DMA, pltpu.SemaphoreType.DMA((parts,))],
+    )
+    x_all = lax.all_to_all(x_pay, "f", 0, 0, tiled=True)
+    adj, adj_send, inverse, flags, sel = call(
+        adjacency_kernel,
+        (tile_count, tile_dst, tile_src, tile_weight[0]),
         [
-            ((parts, rows, T), BF16),
             ((groups, rows, T), BF16),
+            ((chips, rows, T), BF16),
             ((rows, T), F32),
             ((groups, T), BF16),
             ((groups,), jnp.int32),
         ],
-        in_specs=[SMEM, HBM, HBM, HBM, HBM],
-        out_specs=[HBM, VMEM, VMEM, VMEM, SMEM],
+        in_specs=[SMEM, HBM, HBM, HBM],
+        out_specs=[VMEM, VMEM, VMEM, VMEM, SMEM],
         scratch=[
             pltpu.SMEM(tile_dst.shape, jnp.int32),
             pltpu.SMEM(tile_src.shape, jnp.int32),
-            pltpu.VMEM((rows, T), BF16),
             pltpu.VMEM((slots, T, T), jnp.int32),
             pltpu.VMEM((groups, rows, T), jnp.int32),
-            pltpu.SemaphoreType.DMA((3,)),
-            pltpu.SemaphoreType.DMA((parts,)),
+            pltpu.SemaphoreType.DMA((2,)),
             pltpu.SemaphoreType.DMA((slots // CHUNK,)),
         ],
         limit=20,
     )
-    x_all = lax.all_to_all(x_pay, "f", 0, 0, tiled=True)
-    (y_pay,) = call(
-        neighbour_product_kernel, (x_all, w_neigh, flags), [((chips, rows + groups, T), BF16)]
+    adj_pair = lax.ppermute(adj_send, "c", swap)
+    y_pay, sel_pair, adj_pair = call(
+        neighbour_kernel,
+        (lax.ppermute(sel, "c", swap), x_all, w_neigh, flags, adj_pair),
+        [((chips, rows + groups, T), BF16), ((groups,), jnp.int32), (adj_pair.shape, BF16)],
+        in_specs=[SMEM] + [VMEM] * 3 + [HBM],
+        out_specs=[VMEM, SMEM, HBM],
+        aliases={4: 2},
     )
     y_own = lax.all_to_all(y_pay, "z", 0, 0, tiled=True)
-    y_other = lax.ppermute(y_own, "c", swap)
-    (z_half,) = call(
-        half_kernel,
-        (sel, x_all, w_self, adj, inverse, y_own),
-        [((rows, T), F32)],
-        in_specs=[SMEM] + [VMEM] * 5,
-    )
+    mine, own_mask, theirs, x_late = call(
+        aggregate_kernel,
+        (sel, sel_pair, adj, adj_pair, y_own, x_all),
+        [((rows, T), F32), ((chips, T), F32), ((rows + chips, T), F32), (x_all.shape, BF16)],
+        in_specs=[SMEM] * 2 + [VMEM] * 3 + [ANY],
+        out_specs=[VMEM] * 3 + [ANY],
+        aliases={5: 3},
+    )
+    came = lax.ppermute(theirs, "c", swap)
+    (z_self,) = call(self_kernel, (x_late, w_self), [((rows, T), F32)])
     output, gt, c_pay, mask = call(
         activation_kernel,
-        (sel, adj, inverse, y_own, y_other, z_half, out_grad),
+        (adj, inverse, mine, own_mask, came, z_self, out_grad),
         [((rows, T), BF16), ((T, rows), BF16), ((groups, T, T), BF16), ((groups, T), F32)],
-        in_specs=[SMEM] + [VMEM] * 6,
     )
     c_all = lax.all_to_all(c_pay, ("z", "c"), 0, 0, tiled=True)
     bt, keep, send = call(
         weight_grad_kernel,
-        (c_all, mask, gt, x_all),
+        (c_all, mask, gt, x_late),
         [((T, rows), BF16), ((chips, 2 * T, T), F32), ((chips, 2 * T, T), BF16)],
     )
     came = lax.ppermute(send, "c", swap)

time: 107 us -> 105 us (0.981)
  blocking collectives: 66.9 us -> 42.7 us
  waiting for transfers between devices: 5.69 us -> 16 us
  starting transfers between devices: 21.4 us -> 30.1 us
  Pallas kernels: 11.2 us -> 13.8 us
    all_to_all x1 -> x0, blocking collectives: 23.9 us -> none  [per_device(): x_all = lax.all_to_all(x_pay, 'f', 0, 0, tiled=True)]
    all_to_all x0 -> x1, waiting for transfers between devices: none -> 9.79 us  [per_device(): x_all = lax.all_to_all(x_pay, 'f', 0, 0, tiled=True)]
    all_to_all x0 -> x1, starting transfers between devices: none -> 7.6 us  [per_device(): x_all = lax.all_to_all(x_pay, 'f', 0, 0, tiled=True)]
    pallas_call x9 -> x11, Pallas kernels: 11.2 us -> 13.8 us  [call(): pl.pallas_call(kernel, out_shape=shapes, in_specs=in_specs or [VMEM] * le...]
    ppermute x1 -> x3, waiting for transfers between devices: 0.48 us -> 2.09 us  [the longest x1 1.36 us: per_device(): lax.ppermute(sel, 'c', swap)]
    ppermute x1 -> x3, starting transfers between devices: 3.99 us -> 5.22 us  [the longest x1 4.63 us: per_device(): came = lax.ppermute(theirs, 'c', swap)]
    all_to_all x1, waiting for transfers between devices: 3.67 us -> 2.48 us  [per_device(): p_all = lax.all_to_all(p_pay, 'f', 0, 0, tiled=True)]
  transfers between devices with their start and end apart: 10 -> 13, of which waited for: 4 -> 8; matrix products, arithmetic and copies ran while one was open for 0% -> 0% of each run, Pallas kernels for 3% -> 6%
where the time goes in v9:
time: 105 us; the launch traced here: 104 us
  blocking collectives  42.7 us (41%)
  starting transfers between devices  30.1 us (29%)
  waiting for transfers between devices  16 us (15%)
  Pallas kernels  13.8 us (13%)
  between operations  1.43 us (1%)
    all_to_all x1, blocking collectives, per_device(): y_own = lax.all_to_all(y_pay, 'z', 0, 0, tiled=True)  22.6 us
    all_to_all x1, blocking collectives, per_device(): c_all = lax.all_to_all(c_pay, ('z', 'c'), 0, 0, tiled=True)  20.1 us
    pallas_call x11, Pallas kernels, call(): pl.pallas_call(kernel, out_shape=shapes, in_specs=in_specs or [VMEM] * le...  13.8 us
    ppermute x7, starting transfers between devices, per_device(): lax.ppermute(block, 'z', [(chip, (chip + step) % chips) for chip in range...  13 us
    all_to_all x1, waiting for transfers between devices, per_device(): x_all = lax.all_to_all(x_pay, 'f', 0, 0, tiled=True)  9.79 us
    all_to_all x1, starting transfers between devices, per_device(): x_all = lax.all_to_all(x_pay, 'f', 0, 0, tiled=True)  7.6 us
    ppermute x1, starting transfers between devices, per_device(): came = lax.ppermute(theirs, 'c', swap)  4.63 us
    all_to_all x1, starting transfers between devices, per_device(): p_all = lax.all_to_all(p_pay, 'f', 0, 0, tiled=True)  4.21 us
  transfers between devices with their start and end apart: 13, of which 8 were waited for; matrix products, arithmetic and copies ran while one was open for 0% of the time, Pallas kernels for 6%

profile of v9, /device:TPU:1, one launch (start us, length us, event | category | flops | bytes accessed | tf_op | source)
XLA Modules:
  0.0 104.2 jit_solution(17494290875533912348)
XLA Ops:
  0.6 2.0 %spread_kernel.1 = bf16[16,256,128]{2,1,0:T(8,128)(2,1)} custom-call(bf16[256,128]{1,0:T(8,128)(2,1)} %x_hbm.1), custom_call_target="tpu_custom_call" | custom-call | tf_op jit(solution)/shard_map/spread_kernel/pallas_call | solution.py:247
  2.7 7.6 %all-to-all-start = ((bf16[16,256,128]{2,1,0:T(8,128)(2,1)}), bf16[16,256,128]{2,1,0:T(8,128)(2,1)S(1)}, u32[]{:S(2)}, u32[]{:S(2)}) async-start(bf16[16,256,128]{2,1,0:T(8,128)(2,1)} %spread_kernel.1), calls=%async_computation | async-start | bytes 2097152 | tf_op jit(solution)/shard_map/all_to_all | solution.py:273
  10.9 3.4 %adjacency_kernel.1 = (bf16[16,256,128]{2,1,0:T(8,128)(2,1)S(1)}, bf16[8,256,128]{2,1,0:T(8,128)(2,1)S(1)}, f32[256,128]{1,0:T(8,128)S(1)}, bf16[16,128]{1,0:T(8,128)(2,1)S(1)}, s32[16]{0:T(128)S(1)}) custom-call(s32[1]{0:T(128)S(6)} %copy.20.count_ref, s32[1,80]{1,0:T(1,128)} %dst_hbm.1, s32[1,80]{1,0:T(1,128)} %src_hbm.1, s32[80,128,128]{2,1,0:T(8,128)} %bitcast.1), custom_call_target="tpu_custom_call" | custom-call | tf_op jit(solution)/shard_map/adjacency_kernel/pallas_call | solution.py:247
  14.4 0.1 collective-permute-start.1
  14.5 0.5 collective-permute-start
  14.9 1.4 %collective-permute-done.sel_ref = s32[16]{0:T(128)S(1)} collective-permute-done((s32[16]{0:T(128)S(1)}, s32[16]{0:T(128)S(1)}, u32[]{:S(2)}, u32[]{:S(2)}) %collective-permute-start) | collective-permute-done | bytes 96 | tf_op jit(solution)/shard_map/ppermute | solution.py:299
  16.3 0.2 collective-permute-done.1.adj_ref
  16.5 9.8 %all-to-all-done.x_ref = bf16[16,256,128]{2,1,0:T(8,128)(2,1)S(1)} async-done(((bf16[16,256,128]{2,1,0:T(8,128)(2,1)}), bf16[16,256,128]{2,1,0:T(8,128)(2,1)S(1)}, u32[]{:S(2)}, u32[]{:S(2)}) %all-to-all-start) | async-done | bytes 1048608 | tf_op jit(solution)/shard_map/all_to_all | solution.py:273
  26.3 1.4 %neighbour_kernel.1 = (bf16[8,272,128]{2,1,0:T(8,128)(2,1)S(1)}, s32[16]{0:T(128)S(1)}, bf16[8,256,128]{2,1,0:T(8,128)(2,1)}) custom-call(s32[16]{0:T(128)S(1)} %collective-permute-done.sel_ref, bf16[16,256,128]{2,1,0:T(8,128)(2,1)S(1)} %all-to-all-done.x_ref, bf16[2048,128]{1,0:T(8,128)(2,1)S(1)} %copy-done, ...), custom_call_target="tpu_custom_call", output_to_operand_aliasing={{2}: (4, {})} | custom-call | tf_op jit(solution)/shard_map/neighbour_kernel/pallas_call | solution.py:247
  27.6 22.6 %all_to_all.20.y_ref = bf16[8,272,128]{2,1,0:T(8,128)(2,1)S(1)} all-to-all(bf16[8,272,128]{2,1,0:T(8,128)(2,1)S(1)} %get-tuple-element.42), channel_id=1, replica_groups=mesh['z'=8,'c'=2,'f'=16] {'z'}, dimensions={0} | all-to-all | bytes 1114112 | tf_op jit(solution)/shard_map/all_to_all | solution.py:305
  50.2 1.5 %aggregate_kernel.1 = (f32[256,128]{1,0:T(8,128)S(1)}, f32[8,128]{1,0:T(8,128)S(1)}, f32[264,128]{1,0:T(8,128)S(1)}, bf16[16,256,128]{2,1,0:T(8,128)(2,1)S(1)}) custom-call(s32[16]{0:T(128)S(1)} %get-tuple-element.37.sel_ref, s32[16]{0:T(128)S(1)} %get-tuple-element.40.sel_pair_ref, ...), custom_call_target="tpu_custom_call", output_to_operand_aliasing={{3}: (5, {})} | custom-call | tf_op jit(solution)/shard_map/aggregate_kernel/pallas_call | solution.py:247
  51.7 4.6 %collective-permute-start.2 = (f32[264,128]{1,0:T(8,128)S(1)}, f32[264,128]{1,0:T(8,128)S(1)}, u32[]{:S(2)}, u32[]{:S(2)}) collective-permute-start(f32[264,128]{1,0:T(8,128)S(1)} %get-tuple-element.45), channel_id=1, source_target_pairs={{0,16},{16,0},{1,17},{17,1},{2,18},{18,2},{3,19},{19,3},{4,20},{20... | collective-permute-start | bytes 405512 | tf_op jit(solution)/shard_map/ppermute | solution.py:314
  56.4 0.4 self_kernel.1.z_ref
  56.8 0.6 collective-permute-done.2.came_ref
  57.4 0.8 activation_kernel.1
  58.2 20.1 %all_to_all.21.came_ref = bf16[16,128,128]{2,1,0:T(8,128)(2,1)S(1)} all-to-all(bf16[16,128,128]{2,1,0:T(8,128)(2,1)S(1)} %get-tuple-element.48), channel_id=1, replica_groups=mesh['z'=8,'c'=2,'f'=16] {'z','c'}, dimensions={0} | all-to-all | bytes 1048576 | tf_op jit(solution)/shard_map/all_to_all | solution.py:321
  78.3 1.1 %weight_grad_kernel.1 = (bf16[128,256]{1,0:T(8,128)(2,1)S(1)}, f32[8,256,128]{2,1,0:T(8,128)S(1)}, bf16[8,256,128]{2,1,0:T(8,128)(2,1)S(1)}) custom-call(bf16[16,128,128]{2,1,0:T(8,128)(2,1)S(1)} %all_to_all.21.came_ref, f32[16,128]{1,0:T(8,128)S(1)} %get-tuple-element.49.mask_ref, bf16[128,256]{1,0:T(8,128)(2,1)S(1)} %get-tuple-element.50.gt_ref, ...), custom_call_target="tpu_custom_call" | custom-call | tf_op jit(solution)/shard_map/weight_grad_kernel/pallas_call | solution.py:247
  79.6 1.5 %feature_grad_kernel.1.payload_ref = bf16[16,128,256]{2,1,0:T(8,128)(2,1)} custom-call(bf16[128,256]{1,0:T(8,128)(2,1)S(1)} %get-tuple-element.50.gt_ref, bf16[128,256]{1,0:T(8,128)(2,1)S(1)} %get-tuple-element.53.bt_ref, bf16[2048,128]{1,0:T(8,128)(2,1)S(1)} %copy-done.1, bf16[2048,128]{1,0:T(8,128)(2,1)S(1)} %copy-done), custom_call_target="tpu_custom_call" | custom-call | tf_op jit(solution)/shard_map/feature_grad_kernel/pallas_call | solution.py:247
  81.1 0.4 collective-permute-done.3.came_ref
  81.5 4.2 %all-to-all-start.3 = ((bf16[16,128,256]{2,1,0:T(8,128)(2,1)}), bf16[16,128,256]{2,1,0:T(8,128)(2,1)S(1)}, u32[]{:S(2)}, u32[]{:S(2)}) async-start(bf16[16,128,256]{2,1,0:T(8,128)(2,1)} %get-tuple-element.55), calls=%async_computation.3 | async-start | bytes 2097152 | tf_op jit(solution)/shard_map/all_to_all | solution.py:343
  85.8 1.0 collective-permute-start.4
  86.8 1.1 %collective-permute-start.5 = (bf16[256,128]{1,0:T(8,128)(2,1)S(1)}, bf16[256,128]{1,0:T(8,128)(2,1)S(1)}, u32[]{:S(2)}, u32[]{:S(2)}) collective-permute-start(bf16[256,128]{1,0:T(8,128)(2,1)S(1)} %get-tuple-element.57), channel_id=1, source_target_pairs={{0,96},{32,128},{64,160},{96,192},{128,224},{160,0},{192,32},{224,... | collective-permute-start | bytes 196616 | tf_op jit(solution)/shard_map/ppermute | solution.py:345
  87.9 3.4 %collective-permute-start.6 = (bf16[256,128]{1,0:T(8,128)(2,1)S(1)}, bf16[256,128]{1,0:T(8,128)(2,1)S(1)}, u32[]{:S(2)}, u32[]{:S(2)}) collective-permute-start(bf16[256,128]{1,0:T(8,128)(2,1)S(1)} %get-tuple-element.58), channel_id=1, source_target_pairs={{0,160},{32,192},{64,224},{96,0},{128,32},{160,64},{192,96},{224,1... | collective-permute-start | bytes 196616 | tf_op jit(solution)/shard_map/ppermute | solution.py:345
  91.3 1.4 %collective-permute-start.7 = (bf16[256,128]{1,0:T(8,128)(2,1)S(1)}, bf16[256,128]{1,0:T(8,128)(2,1)S(1)}, u32[]{:S(2)}, u32[]{:S(2)}) collective-permute-start(bf16[256,128]{1,0:T(8,128)(2,1)S(1)} %get-tuple-element.59), channel_id=1, source_target_pairs={{0,64},{32,96},{64,128},{96,160},{128,192},{160,224},{192,0},{224,... | collective-permute-start | bytes 196616 | tf_op jit(solution)/shard_map/ppermute | solution.py:345
  92.7 2.2 %collective-permute-start.8 = (bf16[256,128]{1,0:T(8,128)(2,1)S(1)}, bf16[256,128]{1,0:T(8,128)(2,1)S(1)}, u32[]{:S(2)}, u32[]{:S(2)}) collective-permute-start(bf16[256,128]{1,0:T(8,128)(2,1)S(1)} %get-tuple-element.60), channel_id=1, source_target_pairs={{0,192},{32,224},{64,0},{96,32},{128,64},{160,96},{192,128},{224,1... | collective-permute-start | bytes 196616 | tf_op jit(solution)/shard_map/ppermute | solution.py:345
  94.8 0.1 collective-permute-done.4.refs_0_
  94.9 1.1 %collective-permute-start.9 = (bf16[256,128]{1,0:T(8,128)(2,1)S(1)}, bf16[256,128]{1,0:T(8,128)(2,1)S(1)}, u32[]{:S(2)}, u32[]{:S(2)}) collective-permute-start(bf16[256,128]{1,0:T(8,128)(2,1)S(1)} %get-tuple-element.61), channel_id=1, source_target_pairs={{0,32},{32,64},{64,96},{96,128},{128,160},{160,192},{192,224},{224... | collective-permute-start | bytes 196616 | tf_op jit(solution)/shard_map/ppermute | solution.py:345
  96.1 1.2 %collective-permute-done.5.refs_1_ = bf16[256,128]{1,0:T(8,128)(2,1)S(1)} collective-permute-done((bf16[256,128]{1,0:T(8,128)(2,1)S(1)}, bf16[256,128]{1,0:T(8,128)(2,1)S(1)}, u32[]{:S(2)}, u32[]{:S(2)}) %collective-permute-start.5) | collective-permute-done | bytes 65568 | tf_op jit(solution)/shard_map/ppermute | solution.py:345
  97.2 2.8 %collective-permute-start.10 = (bf16[256,128]{1,0:T(8,128)(2,1)S(1)}, bf16[256,128]{1,0:T(8,128)(2,1)S(1)}, u32[]{:S(2)}, u32[]{:S(2)}) collective-permute-start(bf16[256,128]{1,0:T(8,128)(2,1)S(1)} %get-tuple-element.62), channel_id=1, source_target_pairs={{0,224},{32,0},{64,32},{96,64},{128,96},{160,128},{192,160},{224,1... | collective-permute-start | bytes 196616 | tf_op jit(solution)/shard_map/ppermute | solution.py:345
  100.0 2.5 %all-to-all-done.3.parts_ref = bf16[16,128,256]{2,1,0:T(8,128)(2,1)S(1)} async-done(((bf16[16,128,256]{2,1,0:T(8,128)(2,1)}), bf16[16,128,256]{2,1,0:T(8,128)(2,1)S(1)}, u32[]{:S(2)}, u32[]{:S(2)}) %all-to-all-start.3) | async-done | bytes 1048608 | tf_op jit(solution)/shard_map/all_to_all | solution.py:343
  102.5 0.8 sum_kernel.1.done_ref
  103.4 0.8 weight_sum_kernel.1
  (13 shorter events, 0.2 us)
Async XLA Ops:
  0.6 25.6 %copy-start = (bf16[2048,128]{1,0:T(8,128)(2,1)S(1)}, bf16[2048,128]{1,0:T(8,128)(2,1)}, u32[]{:S(2)}) copy-start(bf16[2048,128]{1,0:T(8,128)(2,1)} %wn_ref.1) | copy-start | bytes 1572868
  2.7 23.6 %all-to-all-start = ((bf16[16,256,128]{2,1,0:T(8,128)(2,1)}), bf16[16,256,128]{2,1,0:T(8,128)(2,1)S(1)}, u32[]{:S(2)}, u32[]{:S(2)}) async-start(bf16[16,256,128]{2,1,0:T(8,128)(2,1)} %spread_kernel.1), calls=%async_computation | async-start | bytes 2097152 | tf_op jit(solution)/shard_map/all_to_all | solution.py:273
  10.9 45.4 %copy-start.1 = (bf16[2048,128]{1,0:T(8,128)(2,1)S(1)}, bf16[2048,128]{1,0:T(8,128)(2,1)}, u32[]{:S(2)}) copy-start(bf16[2048,128]{1,0:T(8,128)(2,1)} %ws_ref.1) | copy-start | bytes 1572868
  14.3 43.0 %copy-start.2 = (bf16[256,128]{1,0:T(8,128)(2,1)S(1)}, bf16[256,128]{1,0:T(8,128)(2,1)}, u32[]{:S(2)}) copy-start(bf16[256,128]{1,0:T(8,128)(2,1)} %og_ref.1) | copy-start | bytes 196612
  14.4 2.1 %collective-permute-start.1 = (bf16[8,256,128]{2,1,0:T(8,128)(2,1)S(1)}, bf16[8,256,128]{2,1,0:T(8,128)(2,1)}, u32[]{:S(2)}, u32[]{:S(2)}) collective-permute-start(bf16[8,256,128]{2,1,0:T(8,128)(2,1)S(1)} %get-tuple-element.39), channel_id=1, source_target_pairs={{0,16},{16,0},{1,17},{17,1},{2,18},{18,2},{3,19},{19,3},{4,20},{20... | collective-permute-start | bytes 1572872 | tf_op jit(solution)/shard_map/ppermute | solution.py:296
  14.5 1.9 %collective-permute-start = (s32[16]{0:T(128)S(1)}, s32[16]{0:T(128)S(1)}, u32[]{:S(2)}, u32[]{:S(2)}) collective-permute-start(s32[16]{0:T(128)S(1)} %get-tuple-element.37.sel_ref), channel_id=1, source_target_pairs={{0,16},{16,0},{1,17},{17,1},{2,18},{18,2},{3,19},{19,3},{4,20},{20... | collective-permute-start | bytes 200 | tf_op jit(solution)/shard_map/ppermute | solution.py:299
  51.7 5.6 %collective-permute-start.2 = (f32[264,128]{1,0:T(8,128)S(1)}, f32[264,128]{1,0:T(8,128)S(1)}, u32[]{:S(2)}, u32[]{:S(2)}) collective-permute-start(f32[264,128]{1,0:T(8,128)S(1)} %get-tuple-element.45), channel_id=1, source_target_pairs={{0,16},{16,0},{1,17},{17,1},{2,18},{18,2},{3,19},{19,3},{4,20},{20... | collective-permute-start | bytes 405512 | tf_op jit(solution)/shard_map/ppermute | solution.py:314
  79.5 2.0 %collective-permute-start.3 = (bf16[8,256,128]{2,1,0:T(8,128)(2,1)S(1)}, bf16[8,256,128]{2,1,0:T(8,128)(2,1)S(1)}, u32[]{:S(2)}, u32[]{:S(2)}) collective-permute-start(bf16[8,256,128]{2,1,0:T(8,128)(2,1)S(1)} %get-tuple-element.52), channel_id=1, source_target_pairs={{0,16},{16,0},{1,17},{17,1},{2,18},{18,2},{3,19},{19,3},{4,20},{20... | collective-permute-start | bytes 1572872 | tf_op jit(solution)/shard_map/ppermute | solution.py:327
  81.5 21.0 %all-to-all-start.3 = ((bf16[16,128,256]{2,1,0:T(8,128)(2,1)}), bf16[16,128,256]{2,1,0:T(8,128)(2,1)S(1)}, u32[]{:S(2)}, u32[]{:S(2)}) async-start(bf16[16,128,256]{2,1,0:T(8,128)(2,1)} %get-tuple-element.55), calls=%async_computation.3 | async-start | bytes 2097152 | tf_op jit(solution)/shard_map/all_to_all | solution.py:343
  85.8 9.2 %collective-permute-start.4 = (bf16[256,128]{1,0:T(8,128)(2,1)S(1)}, bf16[256,128]{1,0:T(8,128)(2,1)S(1)}, u32[]{:S(2)}, u32[]{:S(2)}) collective-permute-start(bf16[256,128]{1,0:T(8,128)(2,1)S(1)} %get-tuple-element.56), channel_id=1, source_target_pairs={{0,128},{32,160},{64,192},{96,224},{128,0},{160,32},{192,64},{224,... | collective-permute-start | bytes 196616 | tf_op jit(solution)/shard_map/ppermute | solution.py:345
  86.8 10.4 %collective-permute-start.5 = (bf16[256,128]{1,0:T(8,128)(2,1)S(1)}, bf16[256,128]{1,0:T(8,128)(2,1)S(1)}, u32[]{:S(2)}, u32[]{:S(2)}) collective-permute-start(bf16[256,128]{1,0:T(8,128)(2,1)S(1)} %get-tuple-element.57), channel_id=1, source_target_pairs={{0,96},{32,128},{64,160},{96,192},{128,224},{160,0},{192,32},{224,... | collective-permute-start | bytes 196616 | tf_op jit(solution)/shard_map/ppermute | solution.py:345
  87.9 15.5 %collective-permute-start.6 = (bf16[256,128]{1,0:T(8,128)(2,1)S(1)}, bf16[256,128]{1,0:T(8,128)(2,1)S(1)}, u32[]{:S(2)}, u32[]{:S(2)}) collective-permute-start(bf16[256,128]{1,0:T(8,128)(2,1)S(1)} %get-tuple-element.58), channel_id=1, source_target_pairs={{0,160},{32,192},{64,224},{96,0},{128,32},{160,64},{192,96},{224,1... | collective-permute-start | bytes 196616 | tf_op jit(solution)/shard_map/ppermute | solution.py:345
  91.3 12.1 %collective-permute-start.7 = (bf16[256,128]{1,0:T(8,128)(2,1)S(1)}, bf16[256,128]{1,0:T(8,128)(2,1)S(1)}, u32[]{:S(2)}, u32[]{:S(2)}) collective-permute-start(bf16[256,128]{1,0:T(8,128)(2,1)S(1)} %get-tuple-element.59), channel_id=1, source_target_pairs={{0,64},{32,96},{64,128},{96,160},{128,192},{160,224},{192,0},{224,... | collective-permute-start | bytes 196616 | tf_op jit(solution)/shard_map/ppermute | solution.py:345
  92.7 10.7 %collective-permute-start.8 = (bf16[256,128]{1,0:T(8,128)(2,1)S(1)}, bf16[256,128]{1,0:T(8,128)(2,1)S(1)}, u32[]{:S(2)}, u32[]{:S(2)}) collective-permute-start(bf16[256,128]{1,0:T(8,128)(2,1)S(1)} %get-tuple-element.60), channel_id=1, source_target_pairs={{0,192},{32,224},{64,0},{96,32},{128,64},{160,96},{192,128},{224,1... | collective-permute-start | bytes 196616 | tf_op jit(solution)/shard_map/ppermute | solution.py:345
  94.9 8.4 %collective-permute-start.9 = (bf16[256,128]{1,0:T(8,128)(2,1)S(1)}, bf16[256,128]{1,0:T(8,128)(2,1)S(1)}, u32[]{:S(2)}, u32[]{:S(2)}) collective-permute-start(bf16[256,128]{1,0:T(8,128)(2,1)S(1)} %get-tuple-element.61), channel_id=1, source_target_pairs={{0,32},{32,64},{64,96},{96,128},{128,160},{160,192},{192,224},{224... | collective-permute-start | bytes 196616 | tf_op jit(solution)/shard_map/ppermute | solution.py:345
  97.2 6.1 %collective-permute-start.10 = (bf16[256,128]{1,0:T(8,128)(2,1)S(1)}, bf16[256,128]{1,0:T(8,128)(2,1)S(1)}, u32[]{:S(2)}, u32[]{:S(2)}) collective-permute-start(bf16[256,128]{1,0:T(8,128)(2,1)S(1)} %get-tuple-element.62), channel_id=1, source_target_pairs={{0,224},{32,0},{64,32},{96,64},{128,96},{160,128},{192,160},{224,1... | collective-permute-start | bytes 196616 | tf_op jit(solution)/shard_map/ppermute | solution.py:345

commit v10 on v9

--- a/solution.py
+++ b/solution.py
@@ -22,8 +22,15 @@
     return jnp.dot(a, b, preferred_element_type=F32)
 
 
-def far_first(chips):
-    return tuple(sorted(range(1, chips), key=lambda step: abs(step - chips // 2)))
+def owners(here, core, chips):
+    way = 1 - 2 * core
+
+    def chip(step):
+        return lax.rem(here + step + chips, chips)
+
+    far = 2 * chip(chips // 2) + core
+    three, two, one = (2 * chip(step * way) for step in (3, 2, 1))
+    return [three, three + 1, far, two, two + 1, one, one + 1, 2 * here + core]
 
 
 def halves(block):
@@ -106,7 +113,7 @@
     flag_ref[...] = flags.astype(BF16)
 
 
-def neighbour_kernel(sel_ref, x_ref, w_ref, flag_ref, adj_ref, pay_ref, sel_same_ref, adj_same_ref):
+def neighbour_kernel(x_ref, w_ref, flag_ref, sel_ref, adj_ref, pay_ref, sel_same_ref, adj_same_ref):
     rows = x_ref.shape[1]
     total = dot(x_ref[0], w_ref[0:T, :])
     for part in range(1, x_ref.shape[0]):
@@ -116,8 +123,6 @@
     for copy in range(pay_ref.shape[0]):
         pay_ref[copy, 0:rows, :] = product
         pay_ref[copy, rows:, :] = flags
-    for owner in range(sel_ref.shape[0]):
-        sel_same_ref[owner] = sel_ref[owner]
 
 
 def self_kernel(x_ref, w_ref, z_ref):
@@ -191,10 +196,10 @@
     both = halves(jnp.concatenate([low, high], axis=1))
     bt_ref[...] = both[0:T]
     left = jnp.concatenate([gt_ref[...], both], axis=0)
-    for slot, step in enumerate(far_first(chips) + (0,)):
-        chip = lax.rem(here + step, chips)
-        kept = dot(left, x_ref[2 * chip + core])
-        sent = dot(left, x_ref[2 * chip + 1 - core])
+    slots = zip(owners(here, core, chips), owners(here, 1 - core, chips))
+    for slot, (ours, theirs) in enumerate(slots):
+        kept = dot(left, x_ref[ours])
+        sent = dot(left, x_ref[theirs])
         keep_ref[slot, 0:T] = kept[0:T]
         keep_ref[slot, T:] = kept[T : 2 * T] + kept[2 * T :]
         send_ref[slot, 0:T] = sent[0:T].astype(BF16)
@@ -214,16 +219,34 @@
         copy.wait()
 
 
-def pair_kernel(keep_ref, came_ref, payload_ref, *pay_refs):
-    for slot, pay_ref in enumerate(pay_refs[:-1]):
-        pay_ref[...] = (keep_ref[slot] + came_ref[slot].astype(F32)).astype(pay_ref.dtype)
-
-
-def weight_sum_kernel(own_ref, done_ref, *refs):
-    parts, (self_ref, neigh_ref, same_ref) = refs[:-3], refs[-3:]
-    total = own_ref[...]
-    for part in parts:
-        total = total + part[...].astype(F32)
+def pair_kernel(keep_ref, came_ref, payload_ref, three_ref, two_ref, one_ref, own_ref, same_ref):
+    def pair(slot):
+        return keep_ref[slot] + came_ref[slot].astype(F32)
+
+    for place in range(3):
+        three_ref[place] = pair(place).astype(BF16)
+    for place in range(2):
+        two_ref[place] = pair(3 + place).astype(BF16)
+        one_ref[place] = pair(5 + place)
+    own_ref[...] = pair(7)
+
+
+def relay_kernel(part_ref, own_ref, three_ref, two_ref, one_ref, fold_ref):
+    core = lax.axis_index("c")
+    one_ref[core] = (part_ref[core] + three_ref[2].astype(F32)).astype(BF16)
+    one_ref[1 - core] = part_ref[1 - core].astype(BF16)
+    fold_ref[0] = own_ref[...] + three_ref[core].astype(F32) + two_ref[core].astype(F32)
+    fold_ref[1] = three_ref[1 - core].astype(F32) + two_ref[1 - core].astype(F32)
+
+
+def fold_kernel(fold_ref, one_ref, mine_ref, theirs_ref):
+    core = lax.axis_index("c")
+    theirs_ref[...] = fold_ref[1] + one_ref[1 - core].astype(F32)
+    mine_ref[...] = fold_ref[0] + one_ref[core].astype(F32)
+
+
+def last_kernel(mine_ref, came_ref, done_ref, self_ref, neigh_ref, same_ref):
+    total = mine_ref[...] + came_ref[...]
     self_ref[...] = total[0:T].T
     neigh_ref[...] = total[T:].T
 
@@ -254,6 +277,12 @@
         compiler_params=pltpu.CompilerParams(vmem_limit_bytes=limit * MIB),
         name=kernel.__name__,
     )(*ins)
+
+
+def along(value, step, chips):
+    pairs = [(2 * chip, 2 * ((chip + step) % chips)) for chip in range(chips)]
+    pairs += [(2 * chip + 1, 2 * ((chip - step) % chips) + 1) for chip in range(chips)]
+    return lax.ppermute(value, ("z", "c"), pairs)
 
 
 def per_device(features, w_self, w_neigh, out_grad, tile_count, tile_dst, tile_src, tile_weight, chips, parts):
@@ -296,11 +325,11 @@
     adj_pair = lax.ppermute(adj_send, "c", swap)
     y_pay, sel_pair, adj_pair = call(
         neighbour_kernel,
-        (lax.ppermute(sel, "c", swap), x_all, w_neigh, flags, adj_pair),
+        (x_all, w_neigh, flags, lax.ppermute(sel, "c", swap), adj_pair),
         [((chips, rows + groups, T), BF16), ((groups,), jnp.int32), (adj_pair.shape, BF16)],
-        in_specs=[SMEM] + [VMEM] * 3 + [HBM],
-        out_specs=[VMEM, SMEM, HBM],
-        aliases={4: 2},
+        in_specs=[VMEM] * 3 + [ANY, HBM],
+        out_specs=[VMEM, ANY, HBM],
+        aliases={3: 1, 4: 2},
     )
     y_own = lax.all_to_all(y_pay, "z", 0, 0, tiled=True)
     mine, own_mask, theirs, x_late = call(
@@ -332,27 +361,30 @@
         out_specs=[HBM],
         scratch=[pltpu.VMEM((parts, T, rows), BF16), pltpu.SemaphoreType.DMA((parts,))],
     )
-    *w_pay, own, p_pay = call(
+    block = (2 * T, T)
+    three, two, part, own, p_pay = call(
         pair_kernel,
         (keep, came, p_pay),
-        [((2 * T, T), BF16)] * (chips - 1) + [((2 * T, T), F32), (p_pay.shape, BF16)],
+        [((3,) + block, BF16), ((2,) + block, BF16), ((2,) + block, F32), (block, F32), (p_pay.shape, BF16)],
         in_specs=[VMEM, VMEM, HBM],
-        out_specs=[VMEM] * chips + [HBM],
-        aliases={2: chips},
+        out_specs=[VMEM] * 4 + [HBM],
+        aliases={2: 4},
     )
     p_all = lax.all_to_all(p_pay, "f", 0, 0, tiled=True)
-    w_came = [
-        lax.ppermute(block, "z", [(chip, (chip + step) % chips) for chip in range(chips)])
-        for step, block in zip(far_first(chips), w_pay)
-    ]
+    one, fold = call(
+        relay_kernel,
+        (part, own, along(three, 3, chips), along(two, 2, chips)),
+        [((2,) + block, BF16), ((2,) + block, F32)],
+    )
+    mine, theirs = call(fold_kernel, (fold, along(one, 1, chips)), [(block, F32)] * 2)
     (grad_features,) = call(sum_kernel, (p_all,), [((rows, T), BF16)])
     grad_self, grad_neigh, grad_features = call(
-        weight_sum_kernel,
-        (own, grad_features, *w_came),
+        last_kernel,
+        (mine, lax.ppermute(theirs, "c", swap), grad_features),
         [((T, T), F32), ((T, T), F32), ((rows, T), BF16)],
-        in_specs=[VMEM, ANY] + [VMEM] * (chips - 1),
+        in_specs=[VMEM, VMEM, ANY],
         out_specs=[VMEM, VMEM, ANY],
-        aliases={1: 2},
+        aliases={2: 2},
     )
     return output, grad_features, grad_self, grad_neigh
 

time: 105 us -> 106 us (level)
  waiting for transfers between devices: 16 us -> 22.8 us
  starting transfers between devices: 30.1 us -> 27 us
  Pallas kernels: 13.8 us -> 11.9 us
    ppermute x7 -> x4, waiting for transfers between devices: 1.29 us -> 10.1 us  [the longest x3 9.99 us: along(): return lax.ppermute(value, ('z', 'c'), pairs)]
    ppermute x7 -> x4, starting transfers between devices: 13 us -> 9.18 us  [the longest x3 6.09 us: along(): return lax.ppermute(value, ('z', 'c'), pairs)]
    all_to_all x1, waiting for transfers between devices: 2.48 us -> 0.01 us  [per_device(): p_all = lax.all_to_all(p_pay, 'f', 0, 0, tiled=True)]
    pallas_call x11 -> x13, Pallas kernels: 13.8 us -> 11.9 us  [call(): pl.pallas_call(kernel, out_shape=shapes, in_specs=in_specs or [VMEM] * le...]
    ppermute x1, starting transfers between devices: 0.09 us -> 1.2 us  [per_device(): adj_pair = lax.ppermute(adj_send, 'c', swap)]
  transfers between devices with their start and end apart: 13 -> 10, of which waited for: 8 -> 9; matrix products, arithmetic and copies ran while one was open for 0% -> 0% of each run, Pallas kernels for 6% -> 5%
where the time goes in v10:
time: 106 us
  blocking collectives  42.7 us (40%)
  starting transfers between devices  27 us (25%)
  waiting for transfers between devices  22.8 us (22%)
  Pallas kernels  11.9 us (11%)
  between operations  1.41 us (1%)
    all_to_all x1, blocking collectives, per_device(): y_own = lax.all_to_all(y_pay, 'z', 0, 0, tiled=True)  22.6 us
    all_to_all x1, blocking collectives, per_device(): c_all = lax.all_to_all(c_pay, ('z', 'c'), 0, 0, tiled=True)  20.1 us
    pallas_call x13, Pallas kernels, call(): pl.pallas_call(kernel, out_shape=shapes, in_specs=in_specs or [VMEM] * le...  11.9 us
    all_to_all x1, waiting for transfers between devices, per_device(): x_all = lax.all_to_all(x_pay, 'f', 0, 0, tiled=True)  10.1 us
    ppermute x3, waiting for transfers between devices, along(): return lax.ppermute(value, ('z', 'c'), pairs)  9.99 us
    all_to_all x1, starting transfers between devices, per_device(): x_all = lax.all_to_all(x_pay, 'f', 0, 0, tiled=True)  7.6 us
    ppermute x3, starting transfers between devices, along(): return lax.ppermute(value, ('z', 'c'), pairs)  6.09 us
    ppermute x1, starting transfers between devices, per_device(): came = lax.ppermute(theirs, 'c', swap)  4.63 us
  transfers between devices with their start and end apart: 10, of which 9 were waited for; matrix products, arithmetic and copies ran while one was open for 0% of the time, Pallas kernels for 5%

profile of v10, /device:TPU:1, one launch (start us, length us, event | category | flops | bytes accessed | tf_op | source)
XLA Modules:
  0.0 105.8 jit_solution(15892806174519672304)
XLA Ops:
  0.6 2.0 %spread_kernel.1 = bf16[16,256,128]{2,1,0:T(8,128)(2,1)} custom-call(bf16[256,128]{1,0:T(8,128)(2,1)} %x_hbm.1), custom_call_target="tpu_custom_call" | custom-call | tf_op jit(solution)/shard_map/spread_kernel/pallas_call | solution.py:270
  2.7 7.6 %all-to-all-start = ((bf16[16,256,128]{2,1,0:T(8,128)(2,1)}), bf16[16,256,128]{2,1,0:T(8,128)(2,1)S(1)}, u32[]{:S(2)}, u32[]{:S(2)}) async-start(bf16[16,256,128]{2,1,0:T(8,128)(2,1)} %spread_kernel.1), calls=%async_computation | async-start | bytes 2097152 | tf_op jit(solution)/shard_map/all_to_all | solution.py:302
  11.0 2.3 %adjacency_kernel.1 = (bf16[16,256,128]{2,1,0:T(8,128)(2,1)S(1)}, bf16[8,256,128]{2,1,0:T(8,128)(2,1)S(1)}, f32[256,128]{1,0:T(8,128)S(1)}, bf16[16,128]{1,0:T(8,128)(2,1)S(1)}, s32[16]{0:T(128)S(1)}) custom-call(s32[1]{0:T(128)S(6)} %copy.22.count_ref, s32[1,80]{1,0:T(1,128)} %dst_hbm.1, s32[1,80]{1,0:T(1,128)} %src_hbm.1, s32[80,128,128]{2,1,0:T(8,128)} %bitcast.1), custom_call_target="tpu_custom_call" | custom-call | tf_op jit(solution)/shard_map/adjacency_kernel/pallas_call | solution.py:270
  13.3 1.2 %collective-permute-start.1 = (bf16[8,256,128]{2,1,0:T(8,128)(2,1)S(1)}, bf16[8,256,128]{2,1,0:T(8,128)(2,1)}, u32[]{:S(2)}, u32[]{:S(2)}) collective-permute-start(bf16[8,256,128]{2,1,0:T(8,128)(2,1)S(1)} %get-tuple-element.39), channel_id=1, source_target_pairs={{0,16},{16,0},{1,17},{17,1},{2,18},{18,2},{3,19},{19,3},{4,20},{20... | collective-permute-start | bytes 1572872 | tf_op jit(solution)/shard_map/ppermute | solution.py:325
  14.5 0.1 collective-permute-start
  14.6 1.4 %collective-permute-done.sel_ref = s32[16]{0:T(128)S(1)} collective-permute-done((s32[16]{0:T(128)S(1)}, s32[16]{0:T(128)S(1)}, u32[]{:S(2)}, u32[]{:S(2)}) %collective-permute-start) | collective-permute-done | bytes 96 | tf_op jit(solution)/shard_map/ppermute | solution.py:328
  16.0 0.1 collective-permute-done.1.adj_ref
  16.2 10.1 %all-to-all-done.x_ref = bf16[16,256,128]{2,1,0:T(8,128)(2,1)S(1)} async-done(((bf16[16,256,128]{2,1,0:T(8,128)(2,1)}), bf16[16,256,128]{2,1,0:T(8,128)(2,1)S(1)}, u32[]{:S(2)}, u32[]{:S(2)}) %all-to-all-start) | async-done | bytes 1048608 | tf_op jit(solution)/shard_map/all_to_all | solution.py:302
  26.3 0.4 neighbour_kernel.1
  26.7 22.6 %all_to_all.20.y_ref = bf16[8,272,128]{2,1,0:T(8,128)(2,1)S(1)} all-to-all(bf16[8,272,128]{2,1,0:T(8,128)(2,1)S(1)} %get-tuple-element.42), channel_id=1, replica_groups=mesh['z'=8,'c'=2,'f'=16] {'z'}, dimensions={0} | all-to-all | bytes 1114112 | tf_op jit(solution)/shard_map/all_to_all | solution.py:334
  49.3 1.5 %aggregate_kernel.1 = (f32[256,128]{1,0:T(8,128)S(1)}, f32[8,128]{1,0:T(8,128)S(1)}, f32[264,128]{1,0:T(8,128)S(1)}, bf16[16,256,128]{2,1,0:T(8,128)(2,1)S(1)}) custom-call(s32[16]{0:T(128)S(1)} %get-tuple-element.37.sel_ref, s32[16]{0:T(128)S(1)} %get-tuple-element.40.sel_pair_ref, ...), custom_call_target="tpu_custom_call", output_to_operand_aliasing={{3}: (5, {})} | custom-call | tf_op jit(solution)/shard_map/aggregate_kernel/pallas_call | solution.py:270
  50.8 4.6 %collective-permute-start.2 = (f32[264,128]{1,0:T(8,128)S(1)}, f32[264,128]{1,0:T(8,128)S(1)}, u32[]{:S(2)}, u32[]{:S(2)}) collective-permute-start(f32[264,128]{1,0:T(8,128)S(1)} %get-tuple-element.45), channel_id=1, source_target_pairs={{0,16},{16,0},{1,17},{17,1},{2,18},{18,2},{3,19},{19,3},{4,20},{20... | collective-permute-start | bytes 405512 | tf_op jit(solution)/shard_map/ppermute | solution.py:343
  55.4 0.4 self_kernel.1.z_ref
  55.9 0.6 collective-permute-done.2.came_ref
  56.4 0.8 activation_kernel.1
  57.3 20.1 %all_to_all.21.came_ref = bf16[16,128,128]{2,1,0:T(8,128)(2,1)S(1)} all-to-all(bf16[16,128,128]{2,1,0:T(8,128)(2,1)S(1)} %get-tuple-element.48), channel_id=1, replica_groups=mesh['z'=8,'c'=2,'f'=16] {'z','c'}, dimensions={0} | all-to-all | bytes 1048576 | tf_op jit(solution)/shard_map/all_to_all | solution.py:350
  77.4 1.1 %weight_grad_kernel.1 = (bf16[128,256]{1,0:T(8,128)(2,1)S(1)}, f32[8,256,128]{2,1,0:T(8,128)S(1)}, bf16[8,256,128]{2,1,0:T(8,128)(2,1)S(1)}) custom-call(bf16[16,128,128]{2,1,0:T(8,128)(2,1)S(1)} %all_to_all.21.came_ref, f32[16,128]{1,0:T(8,128)S(1)} %get-tuple-element.49.mask_ref, bf16[128,256]{1,0:T(8,128)(2,1)S(1)} %get-tuple-element.50.gt_ref, ...), custom_call_target="tpu_custom_call" | custom-call | tf_op jit(solution)/shard_map/weight_grad_kernel/pallas_call | solution.py:270
  78.5 0.1 collective-permute-start.3
  78.6 1.5 %feature_grad_kernel.1.payload_ref = bf16[16,128,256]{2,1,0:T(8,128)(2,1)} custom-call(bf16[128,256]{1,0:T(8,128)(2,1)S(1)} %get-tuple-element.50.gt_ref, bf16[128,256]{1,0:T(8,128)(2,1)S(1)} %get-tuple-element.53.bt_ref, bf16[2048,128]{1,0:T(8,128)(2,1)S(1)} %copy-done.1, bf16[2048,128]{1,0:T(8,128)(2,1)S(1)} %copy-done), custom_call_target="tpu_custom_call" | custom-call | tf_op jit(solution)/shard_map/feature_grad_kernel/pallas_call | solution.py:270
  80.1 0.4 collective-permute-done.3.came_ref
  80.5 0.1 pair_kernel.1
  80.6 4.2 %all-to-all-start.3 = ((bf16[16,128,256]{2,1,0:T(8,128)(2,1)}), bf16[16,128,256]{2,1,0:T(8,128)(2,1)S(1)}, u32[]{:S(2)}, u32[]{:S(2)}) async-start(bf16[16,128,256]{2,1,0:T(8,128)(2,1)} %get-tuple-element.62), calls=%async_computation.3 | async-start | bytes 2097152 | tf_op jit(solution)/shard_map/all_to_all | solution.py:373
  84.8 1.1 collective-permute-start.4
  85.9 2.3 %collective-permute-start.5 = (bf16[2,256,128]{2,1,0:T(8,128)(2,1)S(1)}, bf16[2,256,128]{2,1,0:T(8,128)(2,1)S(1)}, u32[]{:S(2)}, u32[]{:S(2)}) collective-permute-start(bf16[2,256,128]{2,1,0:T(8,128)(2,1)S(1)} %get-tuple-element.57), channel_id=1, source_target_pairs={{0,64},{32,96},{64,128},{96,160},{128,192},{160,224},{192,0},{224,... | collective-permute-start | bytes 393224 | tf_op jit(solution)/shard_map/ppermute | solution.py:285
  88.2 6.6 %collective-permute-done.5.two_ref = bf16[2,256,128]{2,1,0:T(8,128)(2,1)S(1)} collective-permute-done((bf16[2,256,128]{2,1,0:T(8,128)(2,1)S(1)}, bf16[2,256,128]{2,1,0:T(8,128)(2,1)S(1)}, u32[]{:S(2)}, u32[]{:S(2)}) %collective-permute-start.5) | collective-permute-done | bytes 131104 | tf_op jit(solution)/shard_map/ppermute | solution.py:285
  94.8 1.1 %collective-permute-done.4.three_ref = bf16[3,256,128]{2,1,0:T(8,128)(2,1)S(1)} collective-permute-done((bf16[3,256,128]{2,1,0:T(8,128)(2,1)S(1)}, bf16[3,256,128]{2,1,0:T(8,128)(2,1)S(1)}, u32[]{:S(2)}, u32[]{:S(2)}) %collective-permute-start.4) | collective-permute-done | bytes 196640 | tf_op jit(solution)/shard_map/ppermute | solution.py:285
  95.9 2.8 %collective-permute-start.6 = (bf16[2,256,128]{2,1,0:T(8,128)(2,1)S(1)}, bf16[2,256,128]{2,1,0:T(8,128)(2,1)S(1)}, u32[]{:S(2)}, u32[]{:S(2)}) collective-permute-start(bf16[2,256,128]{2,1,0:T(8,128)(2,1)S(1)} %get-tuple-element.59), channel_id=1, source_target_pairs={{0,32},{32,64},{64,96},{96,128},{128,160},{160,192},{192,224},{224... | collective-permute-start | bytes 393224 | tf_op jit(solution)/shard_map/ppermute | solution.py:285
  98.7 2.3 %collective-permute-done.6.one_ref = bf16[2,256,128]{2,1,0:T(8,128)(2,1)S(1)} collective-permute-done((bf16[2,256,128]{2,1,0:T(8,128)(2,1)S(1)}, bf16[2,256,128]{2,1,0:T(8,128)(2,1)S(1)}, u32[]{:S(2)}, u32[]{:S(2)}) %collective-permute-start.6) | collective-permute-done | bytes 131104 | tf_op jit(solution)/shard_map/ppermute | solution.py:285
  101.0 3.1 %collective-permute-start.7 = (f32[256,128]{1,0:T(8,128)S(1)}, f32[256,128]{1,0:T(8,128)S(1)}, u32[]{:S(2)}, u32[]{:S(2)}) collective-permute-start(f32[256,128]{1,0:T(8,128)S(1)} %get-tuple-element.61), channel_id=1, source_target_pairs={{0,16},{16,0},{1,17},{17,1},{2,18},{18,2},{3,19},{19,3},{4,20},{20... | collective-permute-start | bytes 393224 | tf_op jit(solution)/shard_map/ppermute | solution.py:383
  104.1 0.8 sum_kernel.1.done_ref
  104.9 0.1 collective-permute-done.7.came_ref
  105.1 0.8 last_kernel.1
  (9 shorter events, 0.1 us)
Async XLA Ops:
  0.6 25.7 %copy-start = (bf16[2048,128]{1,0:T(8,128)(2,1)S(1)}, bf16[2048,128]{1,0:T(8,128)(2,1)}, u32[]{:S(2)}) copy-start(bf16[2048,128]{1,0:T(8,128)(2,1)} %wn_ref.1) | copy-start | bytes 1572868
  2.7 23.6 %all-to-all-start = ((bf16[16,256,128]{2,1,0:T(8,128)(2,1)}), bf16[16,256,128]{2,1,0:T(8,128)(2,1)S(1)}, u32[]{:S(2)}, u32[]{:S(2)}) async-start(bf16[16,256,128]{2,1,0:T(8,128)(2,1)} %spread_kernel.1), calls=%async_computation | async-start | bytes 2097152 | tf_op jit(solution)/shard_map/all_to_all | solution.py:302
  10.9 44.5 %copy-start.1 = (bf16[2048,128]{1,0:T(8,128)(2,1)S(1)}, bf16[2048,128]{1,0:T(8,128)(2,1)}, u32[]{:S(2)}) copy-start(bf16[2048,128]{1,0:T(8,128)(2,1)} %ws_ref.1) | copy-start | bytes 1572868
  13.3 43.1 %copy-start.2 = (bf16[256,128]{1,0:T(8,128)(2,1)S(1)}, bf16[256,128]{1,0:T(8,128)(2,1)}, u32[]{:S(2)}) copy-start(bf16[256,128]{1,0:T(8,128)(2,1)} %og_ref.1) | copy-start | bytes 196612
  13.3 2.9 %collective-permute-start.1 = (bf16[8,256,128]{2,1,0:T(8,128)(2,1)S(1)}, bf16[8,256,128]{2,1,0:T(8,128)(2,1)}, u32[]{:S(2)}, u32[]{:S(2)}) collective-permute-start(bf16[8,256,128]{2,1,0:T(8,128)(2,1)S(1)} %get-tuple-element.39), channel_id=1, source_target_pairs={{0,16},{16,0},{1,17},{17,1},{2,18},{18,2},{3,19},{19,3},{4,20},{20... | collective-permute-start | bytes 1572872 | tf_op jit(solution)/shard_map/ppermute | solution.py:325
  14.5 1.5 %collective-permute-start = (s32[16]{0:T(128)S(1)}, s32[16]{0:T(128)S(1)}, u32[]{:S(2)}, u32[]{:S(2)}) collective-permute-start(s32[16]{0:T(128)S(1)} %get-tuple-element.37.sel_ref), channel_id=1, source_target_pairs={{0,16},{16,0},{1,17},{17,1},{2,18},{18,2},{3,19},{19,3},{4,20},{20... | collective-permute-start | bytes 200 | tf_op jit(solution)/shard_map/ppermute | solution.py:328
  50.8 5.6 %collective-permute-start.2 = (f32[264,128]{1,0:T(8,128)S(1)}, f32[264,128]{1,0:T(8,128)S(1)}, u32[]{:S(2)}, u32[]{:S(2)}) collective-permute-start(f32[264,128]{1,0:T(8,128)S(1)} %get-tuple-element.45), channel_id=1, source_target_pairs={{0,16},{16,0},{1,17},{17,1},{2,18},{18,2},{3,19},{19,3},{4,20},{20... | collective-permute-start | bytes 405512 | tf_op jit(solution)/shard_map/ppermute | solution.py:343
  78.5 2.0 %collective-permute-start.3 = (bf16[8,256,128]{2,1,0:T(8,128)(2,1)S(1)}, bf16[8,256,128]{2,1,0:T(8,128)(2,1)S(1)}, u32[]{:S(2)}, u32[]{:S(2)}) collective-permute-start(bf16[8,256,128]{2,1,0:T(8,128)(2,1)S(1)} %get-tuple-element.52), channel_id=1, source_target_pairs={{0,16},{16,0},{1,17},{17,1},{2,18},{18,2},{3,19},{19,3},{4,20},{20... | collective-permute-start | bytes 1572872 | tf_op jit(solution)/shard_map/ppermute | solution.py:356
  80.6 23.5 %all-to-all-start.3 = ((bf16[16,128,256]{2,1,0:T(8,128)(2,1)}), bf16[16,128,256]{2,1,0:T(8,128)(2,1)S(1)}, u32[]{:S(2)}, u32[]{:S(2)}) async-start(bf16[16,128,256]{2,1,0:T(8,128)(2,1)} %get-tuple-element.62), calls=%async_computation.3 | async-start | bytes 2097152 | tf_op jit(solution)/shard_map/all_to_all | solution.py:373
  84.8 11.1 %collective-permute-start.4 = (bf16[3,256,128]{2,1,0:T(8,128)(2,1)S(1)}, bf16[3,256,128]{2,1,0:T(8,128)(2,1)S(1)}, u32[]{:S(2)}, u32[]{:S(2)}) collective-permute-start(bf16[3,256,128]{2,1,0:T(8,128)(2,1)S(1)} %get-tuple-element.56), channel_id=1, source_target_pairs={{0,96},{32,128},{64,160},{96,192},{128,224},{160,0},{192,32},{224,... | collective-permute-start | bytes 589832 | tf_op jit(solution)/shard_map/ppermute | solution.py:285
  85.9 8.9 %collective-permute-start.5 = (bf16[2,256,128]{2,1,0:T(8,128)(2,1)S(1)}, bf16[2,256,128]{2,1,0:T(8,128)(2,1)S(1)}, u32[]{:S(2)}, u32[]{:S(2)}) collective-permute-start(bf16[2,256,128]{2,1,0:T(8,128)(2,1)S(1)} %get-tuple-element.57), channel_id=1, source_target_pairs={{0,64},{32,96},{64,128},{96,160},{128,192},{160,224},{192,0},{224,... | collective-permute-start | bytes 393224 | tf_op jit(solution)/shard_map/ppermute | solution.py:285
  95.9 5.0 %collective-permute-start.6 = (bf16[2,256,128]{2,1,0:T(8,128)(2,1)S(1)}, bf16[2,256,128]{2,1,0:T(8,128)(2,1)S(1)}, u32[]{:S(2)}, u32[]{:S(2)}) collective-permute-start(bf16[2,256,128]{2,1,0:T(8,128)(2,1)S(1)} %get-tuple-element.59), channel_id=1, source_target_pairs={{0,32},{32,64},{64,96},{96,128},{128,160},{160,192},{192,224},{224... | collective-permute-start | bytes 393224 | tf_op jit(solution)/shard_map/ppermute | solution.py:285
  101.0 4.1 %collective-permute-start.7 = (f32[256,128]{1,0:T(8,128)S(1)}, f32[256,128]{1,0:T(8,128)S(1)}, u32[]{:S(2)}, u32[]{:S(2)}) collective-permute-start(f32[256,128]{1,0:T(8,128)S(1)} %get-tuple-element.61), channel_id=1, source_target_pairs={{0,16},{16,0},{1,17},{17,1},{2,18},{18,2},{3,19},{19,3},{4,20},{20... | collective-permute-start | bytes 393224 | tf_op jit(solution)/shard_map/ppermute | solution.py:383

commit v11 on v9

--- a/solution.py
+++ b/solution.py
@@ -45,8 +45,8 @@
 
 
 def adjacency_kernel(
-    count_ref, dst_hbm, src_hbm, weight_ref, adj_ref, send_ref, inv_ref, flag_ref, sel_ref,
-    dst_ref, src_ref, buf, acc, in_sems, sems,
+    count_ref, dst_hbm, src_hbm, weight_ref, adj_ref, send_ref, inv_ref, flag_ref,
+    dst_ref, src_ref, buf, acc, sel_ref, in_sems, sems,
 ):
     count = count_ref[0]
     slots = weight_ref.shape[0]
@@ -103,32 +103,33 @@
     flags = jnp.zeros(flag_ref.shape, F32)
     for owner in range(groups):
         flags = jnp.where(row == owner, sel_ref[owner].astype(F32), flags)
-    flag_ref[...] = flags.astype(BF16)
-
-
-def neighbour_kernel(sel_ref, x_ref, w_ref, flag_ref, adj_ref, pay_ref, sel_same_ref, adj_same_ref):
+    flag_ref[...] = flags
+
+
+def wide_dot(x_ref, w_ref):
+    total = None
+    for part in range(0, x_ref.shape[0], 2):
+        pair = jnp.concatenate([x_ref[part], x_ref[part + 1]], axis=1)
+        product = dot(pair, w_ref[part * T : (part + 2) * T, :])
+        total = product if total is None else total + product
+    return total
+
+
+def neighbour_kernel(x_ref, w_ref, flag_ref, pair_flag_ref, adj_ref, pay_ref, flag_same_ref, adj_same_ref):
     rows = x_ref.shape[1]
-    total = dot(x_ref[0], w_ref[0:T, :])
-    for part in range(1, x_ref.shape[0]):
-        total = total + dot(x_ref[part], w_ref[part * T : (part + 1) * T, :])
-    product = total.astype(BF16)
-    flags = flag_ref[...]
+    product = wide_dot(x_ref, w_ref).astype(BF16)
+    flags = flag_ref[...].astype(BF16)
     for copy in range(pay_ref.shape[0]):
         pay_ref[copy, 0:rows, :] = product
         pay_ref[copy, rows:, :] = flags
-    for owner in range(sel_ref.shape[0]):
-        sel_same_ref[owner] = sel_ref[owner]
 
 
 def self_kernel(x_ref, w_ref, z_ref):
-    total = dot(x_ref[0], w_ref[0:T, :])
-    for part in range(1, x_ref.shape[0]):
-        total = total + dot(x_ref[part], w_ref[part * T : (part + 1) * T, :])
-    z_ref[...] = total
+    z_ref[...] = wide_dot(x_ref, w_ref)
 
 
 def aggregate_kernel(
-    sel_ref, sel_pair_ref, adj_ref, adj_pair_ref, y_ref, x_ref, mine_ref, mask_ref, theirs_ref, x_same_ref
+    flag_ref, flag_pair_ref, adj_ref, adj_pair_ref, y_ref, x_ref, mine_ref, mask_ref, theirs_ref, x_same_ref
 ):
     core = lax.axis_index("c")
     here = 2 * lax.axis_index("z")
@@ -136,16 +137,21 @@
     rows = mine_ref.shape[0]
     row = lax.broadcasted_iota(jnp.int32, (y_ref.shape[1] - rows, T), 0)
 
-    def summed(adj, sel):
+    def summed(adj, flag):
         total = jnp.zeros(mine_ref.shape, F32)
-        for chip in range(chips):
-            owner = 2 * chip + core
-            tile = y_ref[chip, pl.ds(pl.multiple_of(sel[owner] * T, T), T), :]
-            total = total + dot(adj(chip, owner), tile)
+        for first in range(0, chips, 2):
+            blocks, tiles = [], []
+            for chip in (first, first + 1):
+                high = flag[pl.ds(2 * chip + core, 1), :] > 0.5
+                blocks.append(adj(chip))
+                low_tile = y_ref[chip, 0:T, :].astype(F32)
+                high_tile = y_ref[chip, T : 2 * T, :].astype(F32)
+                tiles.append(jnp.where(high, high_tile, low_tile).astype(BF16))
+            total = total + dot(jnp.concatenate(blocks, axis=1), jnp.concatenate(tiles, axis=0))
         return total
 
-    theirs_ref[0:rows] = summed(lambda chip, owner: adj_pair_ref[chip], sel_pair_ref)
-    mine_ref[...] = summed(lambda chip, owner: adj_ref[owner], sel_ref)
+    theirs_ref[0:rows] = summed(lambda chip: adj_pair_ref[chip], flag_pair_ref)
+    mine_ref[...] = summed(lambda chip: adj_ref[2 * chip + core], flag_ref)
     for chip in range(chips):
         flags = y_ref[chip, rows:, :].astype(F32)
         mask_ref[chip : chip + 1, :] = jnp.sum(
@@ -169,9 +175,11 @@
     sig = 1.0 / (1.0 + jnp.exp(-z))
     grad = (og_ref[...].astype(F32) * sig * (1.0 + z * (1.0 - sig))).astype(BF16).astype(F32)
     scaled = halves((grad * inverse).T)
-    for owner in range(pay_ref.shape[0]):
-        spread = dot(scaled, adj_ref[owner])
-        pay_ref[owner] = (spread[0:T] + spread[T:]).astype(BF16)
+    for owner in range(0, pay_ref.shape[0], 2):
+        spread = dot(scaled, jnp.concatenate([adj_ref[owner], adj_ref[owner + 1]], axis=1))
+        spread = (spread[0:T] + spread[T:]).astype(BF16)
+        pay_ref[owner] = spread[:, 0:T]
+        pay_ref[owner + 1] = spread[:, T:]
     out_ref[...] = (z * sig).astype(BF16)
     gt_ref[...] = grad.T.astype(BF16)
 
@@ -193,8 +201,9 @@
     left = jnp.concatenate([gt_ref[...], both], axis=0)
     for slot, step in enumerate(far_first(chips) + (0,)):
         chip = lax.rem(here + step, chips)
-        kept = dot(left, x_ref[2 * chip + core])
-        sent = dot(left, x_ref[2 * chip + 1 - core])
+        pair = jnp.concatenate([x_ref[2 * chip + core], x_ref[2 * chip + 1 - core]], axis=1)
+        total = dot(left, pair)
+        kept, sent = total[:, 0:T], total[:, T:]
         keep_ref[slot, 0:T] = kept[0:T]
         keep_ref[slot, T:] = kept[T : 2 * T] + kept[2 * T :]
         send_ref[slot, 0:T] = sent[0:T].astype(BF16)
@@ -202,12 +211,12 @@
 
 
 def feature_grad_kernel(gt_ref, bt_ref, ws_ref, wn_ref, pay_ref, buf, sems):
-    gt = gt_ref[...]
-    bt = bt_ref[...]
+    right = jnp.concatenate([gt_ref[...], bt_ref[...]], axis=0)
     copies = []
     for part in range(pay_ref.shape[0]):
         span = slice(part * T, (part + 1) * T)
-        buf[part] = (dot(ws_ref[span, :], gt) + dot(wn_ref[span, :], bt)).astype(BF16)
+        left = jnp.concatenate([ws_ref[span, :], wn_ref[span, :]], axis=1)
+        buf[part] = dot(left, right).astype(BF16)
         copies.append(pltpu.make_async_copy(buf.at[part], pay_ref.at[part], sems.at[part]))
         copies[-1].start()
     for copy in copies:
@@ -271,43 +280,42 @@
         scratch=[pltpu.VMEM((rows, T), BF16), pltpu.SemaphoreType.DMA, pltpu.SemaphoreType.DMA((parts,))],
     )
     x_all = lax.all_to_all(x_pay, "f", 0, 0, tiled=True)
-    adj, adj_send, inverse, flags, sel = call(
+    adj, adj_send, inverse, flags = call(
         adjacency_kernel,
         (tile_count, tile_dst, tile_src, tile_weight[0]),
         [
             ((groups, rows, T), BF16),
             ((chips, rows, T), BF16),
             ((rows, T), F32),
-            ((groups, T), BF16),
-            ((groups,), jnp.int32),
+            ((groups, T), F32),
         ],
         in_specs=[SMEM, HBM, HBM, HBM],
-        out_specs=[VMEM, VMEM, VMEM, VMEM, SMEM],
         scratch=[
             pltpu.SMEM(tile_dst.shape, jnp.int32),
             pltpu.SMEM(tile_src.shape, jnp.int32),
             pltpu.VMEM((slots, T, T), jnp.int32),
             pltpu.VMEM((groups, rows, T), jnp.int32),
+            pltpu.SMEM((groups,), jnp.int32),
             pltpu.SemaphoreType.DMA((2,)),
             pltpu.SemaphoreType.DMA((slots // CHUNK,)),
         ],
         limit=20,
     )
     adj_pair = lax.ppermute(adj_send, "c", swap)
-    y_pay, sel_pair, adj_pair = call(
+    y_pay, flags_pair, adj_pair = call(
         neighbour_kernel,
-        (lax.ppermute(sel, "c", swap), x_all, w_neigh, flags, adj_pair),
-        [((chips, rows + groups, T), BF16), ((groups,), jnp.int32), (adj_pair.shape, BF16)],
-        in_specs=[SMEM] + [VMEM] * 3 + [HBM],
-        out_specs=[VMEM, SMEM, HBM],
-        aliases={4: 2},
+        (x_all, w_neigh, flags, lax.ppermute(flags, "c", swap), adj_pair),
+        [((chips, rows + groups, T), BF16), (flags.shape, F32), (adj_pair.shape, BF16)],
+        in_specs=[VMEM] * 3 + [ANY, HBM],
+        out_specs=[VMEM, ANY, HBM],
+        aliases={3: 1, 4: 2},
     )
     y_own = lax.all_to_all(y_pay, "z", 0, 0, tiled=True)
     mine, own_mask, theirs, x_late = call(
         aggregate_kernel,
-        (sel, sel_pair, adj, adj_pair, y_own, x_all),
+        (flags, flags_pair, adj, adj_pair, y_own, x_all),
         [((rows, T), F32), ((chips, T), F32), ((rows + chips, T), F32), (x_all.shape, BF16)],
-        in_specs=[SMEM] * 2 + [VMEM] * 3 + [ANY],
+        in_specs=[VMEM] * 5 + [ANY],
         out_specs=[VMEM] * 3 + [ANY],
         aliases={5: 3},
     )

time: 105 us -> 103 us (0.981)
  Pallas kernels: 13.8 us -> 11.3 us
    pallas_call x11, Pallas kernels: 13.8 us -> 11.3 us  [call(): pl.pallas_call(kernel, out_shape=shapes, in_specs=in_specs or [VMEM] * le...]
  transfers between devices with their start and end apart: 13 -> 13, of which waited for: 8 -> 8; matrix products, arithmetic and copies ran while one was open for 0% -> 0% of each run, Pallas kernels for 6% -> 5%
where the time goes in v11:
time: 103 us
  blocking collectives  42.7 us (41%)
  starting transfers between devices  30.6 us (30%)
  waiting for transfers between devices  16.8 us (16%)
  Pallas kernels  11.3 us (11%)
  between operations  1.41 us (1%)
    all_to_all x1, blocking collectives, per_device(): y_own = lax.all_to_all(y_pay, 'z', 0, 0, tiled=True)  22.6 us
    all_to_all x1, blocking collectives, per_device(): c_all = lax.all_to_all(c_pay, ('z', 'c'), 0, 0, tiled=True)  20.1 us
    ppermute x7, starting transfers between devices, per_device(): lax.ppermute(block, 'z', [(chip, (chip + step) % chips) for chip in range...  13 us
    pallas_call x11, Pallas kernels, call(): pl.pallas_call(kernel, out_shape=shapes, in_specs=in_specs or [VMEM] * le...  11.3 us
    all_to_all x1, waiting for transfers between devices, per_device(): x_all = lax.all_to_all(x_pay, 'f', 0, 0, tiled=True)  10.4 us
    all_to_all x1, starting transfers between devices, per_device(): x_all = lax.all_to_all(x_pay, 'f', 0, 0, tiled=True)  7.6 us
    ppermute x1, starting transfers between devices, per_device(): came = lax.ppermute(theirs, 'c', swap)  4.63 us
    all_to_all x1, starting transfers between devices, per_device(): p_all = lax.all_to_all(p_pay, 'f', 0, 0, tiled=True)  4.21 us
  transfers between devices with their start and end apart: 13, of which 8 were waited for; matrix products, arithmetic and copies ran while one was open for 0% of the time, Pallas kernels for 5%

profile of v11, /device:TPU:1, one launch (start us, length us, event | category | flops | bytes accessed | tf_op | source)
XLA Modules:
  0.0 102.9 jit_solution(14807776269154369032)
XLA Ops:
  0.6 2.0 %spread_kernel.1 = bf16[16,256,128]{2,1,0:T(8,128)(2,1)} custom-call(bf16[256,128]{1,0:T(8,128)(2,1)} %x_hbm.1), custom_call_target="tpu_custom_call" | custom-call | tf_op jit(solution)/shard_map/spread_kernel/pallas_call | solution.py:256
  2.7 7.6 %all-to-all-start = ((bf16[16,256,128]{2,1,0:T(8,128)(2,1)}), bf16[16,256,128]{2,1,0:T(8,128)(2,1)S(1)}, u32[]{:S(2)}, u32[]{:S(2)}) async-start(bf16[16,256,128]{2,1,0:T(8,128)(2,1)} %spread_kernel.1), calls=%async_computation | async-start | bytes 2097152 | tf_op jit(solution)/shard_map/all_to_all | solution.py:282
  10.9 2.3 %adjacency_kernel.1 = (bf16[16,256,128]{2,1,0:T(8,128)(2,1)S(1)}, bf16[8,256,128]{2,1,0:T(8,128)(2,1)S(1)}, f32[256,128]{1,0:T(8,128)S(1)}, f32[16,128]{1,0:T(8,128)S(1)}) custom-call(s32[1]{0:T(128)S(6)} %copy.22.count_ref, s32[1,80]{1,0:T(1,128)} %dst_hbm.1, s32[1,80]{1,0:T(1,128)} %src_hbm.1, s32[80,128,128]{2,1,0:T(8,128)} %bitcast.1), custom_call_target="tpu_custom_call" | custom-call | tf_op jit(solution)/shard_map/adjacency_kernel/pallas_call | solution.py:256
  13.3 1.0 collective-permute-start.1
  14.2 0.1 collective-permute-start
  14.3 1.4 %collective-permute-done.pair_flag_ref = f32[16,128]{1,0:T(8,128)S(1)} collective-permute-done((f32[16,128]{1,0:T(8,128)S(1)}, f32[16,128]{1,0:T(8,128)S(1)}, u32[]{:S(2)}, u32[]{:S(2)}) %collective-permute-start) | collective-permute-done | bytes 8224 | tf_op jit(solution)/shard_map/ppermute | solution.py:307
  15.8 0.1 collective-permute-done.1.adj_ref
  15.9 10.4 %all-to-all-done.x_ref = bf16[16,256,128]{2,1,0:T(8,128)(2,1)S(1)} async-done(((bf16[16,256,128]{2,1,0:T(8,128)(2,1)}), bf16[16,256,128]{2,1,0:T(8,128)(2,1)S(1)}, u32[]{:S(2)}, u32[]{:S(2)}) %all-to-all-start) | async-done | bytes 1048608 | tf_op jit(solution)/shard_map/all_to_all | solution.py:282
  26.3 0.4 neighbour_kernel.1
  26.7 22.6 %all_to_all.20.y_ref = bf16[8,272,128]{2,1,0:T(8,128)(2,1)S(1)} all-to-all(bf16[8,272,128]{2,1,0:T(8,128)(2,1)S(1)} %get-tuple-element.40), channel_id=1, replica_groups=mesh['z'=8,'c'=2,'f'=16] {'z'}, dimensions={0} | all-to-all | bytes 1114112 | tf_op jit(solution)/shard_map/all_to_all | solution.py:313
  49.3 1.5 %aggregate_kernel.1 = (f32[256,128]{1,0:T(8,128)S(1)}, f32[8,128]{1,0:T(8,128)S(1)}, f32[264,128]{1,0:T(8,128)S(1)}, bf16[16,256,128]{2,1,0:T(8,128)(2,1)S(1)}) custom-call(f32[16,128]{1,0:T(8,128)S(1)} %get-tuple-element.36.flag_ref, f32[16,128]{1,0:T(8,128)S(1)} %get-tuple-element.38.flag_pair_ref, ...), custom_call_target="tpu_custom_call", output_to_operand_aliasing={{3}: (5, {})} | custom-call | tf_op jit(solution)/shard_map/aggregate_kernel/pallas_call | solution.py:256
  50.8 4.6 %collective-permute-start.2 = (f32[264,128]{1,0:T(8,128)S(1)}, f32[264,128]{1,0:T(8,128)S(1)}, u32[]{:S(2)}, u32[]{:S(2)}) collective-permute-start(f32[264,128]{1,0:T(8,128)S(1)} %get-tuple-element.43), channel_id=1, source_target_pairs={{0,16},{16,0},{1,17},{17,1},{2,18},{18,2},{3,19},{19,3},{4,20},{20... | collective-permute-start | bytes 405512 | tf_op jit(solution)/shard_map/ppermute | solution.py:322
  55.5 0.4 self_kernel.1.z_ref
  55.9 0.6 collective-permute-done.2.came_ref
  56.5 0.8 activation_kernel.1
  57.3 20.1 %all_to_all.21.came_ref = bf16[16,128,128]{2,1,0:T(8,128)(2,1)S(1)} all-to-all(bf16[16,128,128]{2,1,0:T(8,128)(2,1)S(1)} %get-tuple-element.46), channel_id=1, replica_groups=mesh['z'=8,'c'=2,'f'=16] {'z','c'}, dimensions={0} | all-to-all | bytes 1048576 | tf_op jit(solution)/shard_map/all_to_all | solution.py:329
  77.4 0.7 weight_grad_kernel.1
  78.1 0.1 collective-permute-start.3
  78.2 1.3 %feature_grad_kernel.1.payload_ref = bf16[16,128,256]{2,1,0:T(8,128)(2,1)} custom-call(bf16[128,256]{1,0:T(8,128)(2,1)S(1)} %get-tuple-element.48.gt_ref, bf16[128,256]{1,0:T(8,128)(2,1)S(1)} %get-tuple-element.51.bt_ref, bf16[2048,128]{1,0:T(8,128)(2,1)S(1)} %copy-done, bf16[2048,128]{1,0:T(8,128)(2,1)S(1)} %copy-done.1), custom_call_target="tpu_custom_call" | custom-call | tf_op jit(solution)/shard_map/feature_grad_kernel/pallas_call | solution.py:256
  79.6 0.5 collective-permute-done.3.came_ref
  80.2 4.2 %all-to-all-start.3 = ((bf16[16,128,256]{2,1,0:T(8,128)(2,1)}), bf16[16,128,256]{2,1,0:T(8,128)(2,1)S(1)}, u32[]{:S(2)}, u32[]{:S(2)}) async-start(bf16[16,128,256]{2,1,0:T(8,128)(2,1)} %get-tuple-element.53), calls=%async_computation.3 | async-start | bytes 2097152 | tf_op jit(solution)/shard_map/all_to_all | solution.py:351
  84.4 1.0 %collective-permute-start.4 = (bf16[256,128]{1,0:T(8,128)(2,1)S(1)}, bf16[256,128]{1,0:T(8,128)(2,1)S(1)}, u32[]{:S(2)}, u32[]{:S(2)}) collective-permute-start(bf16[256,128]{1,0:T(8,128)(2,1)S(1)} %get-tuple-element.54), channel_id=1, source_target_pairs={{0,128},{32,160},{64,192},{96,224},{128,0},{160,32},{192,64},{224,... | collective-permute-start | bytes 196616 | tf_op jit(solution)/shard_map/ppermute | solution.py:353
  85.5 1.1 %collective-permute-start.5 = (bf16[256,128]{1,0:T(8,128)(2,1)S(1)}, bf16[256,128]{1,0:T(8,128)(2,1)S(1)}, u32[]{:S(2)}, u32[]{:S(2)}) collective-permute-start(bf16[256,128]{1,0:T(8,128)(2,1)S(1)} %get-tuple-element.55), channel_id=1, source_target_pairs={{0,96},{32,128},{64,160},{96,192},{128,224},{160,0},{192,32},{224,... | collective-permute-start | bytes 196616 | tf_op jit(solution)/shard_map/ppermute | solution.py:353
  86.6 3.4 %collective-permute-start.6 = (bf16[256,128]{1,0:T(8,128)(2,1)S(1)}, bf16[256,128]{1,0:T(8,128)(2,1)S(1)}, u32[]{:S(2)}, u32[]{:S(2)}) collective-permute-start(bf16[256,128]{1,0:T(8,128)(2,1)S(1)} %get-tuple-element.56), channel_id=1, source_target_pairs={{0,160},{32,192},{64,224},{96,0},{128,32},{160,64},{192,96},{224,1... | collective-permute-start | bytes 196616 | tf_op jit(solution)/shard_map/ppermute | solution.py:353
  90.0 1.4 %collective-permute-start.7 = (bf16[256,128]{1,0:T(8,128)(2,1)S(1)}, bf16[256,128]{1,0:T(8,128)(2,1)S(1)}, u32[]{:S(2)}, u32[]{:S(2)}) collective-permute-start(bf16[256,128]{1,0:T(8,128)(2,1)S(1)} %get-tuple-element.57), channel_id=1, source_target_pairs={{0,64},{32,96},{64,128},{96,160},{128,192},{160,224},{192,0},{224,... | collective-permute-start | bytes 196616 | tf_op jit(solution)/shard_map/ppermute | solution.py:353
  91.4 2.2 %collective-permute-start.8 = (bf16[256,128]{1,0:T(8,128)(2,1)S(1)}, bf16[256,128]{1,0:T(8,128)(2,1)S(1)}, u32[]{:S(2)}, u32[]{:S(2)}) collective-permute-start(bf16[256,128]{1,0:T(8,128)(2,1)S(1)} %get-tuple-element.58), channel_id=1, source_target_pairs={{0,192},{32,224},{64,0},{96,32},{128,64},{160,96},{192,128},{224,1... | collective-permute-start | bytes 196616 | tf_op jit(solution)/shard_map/ppermute | solution.py:353
  93.6 1.1 %collective-permute-start.9 = (bf16[256,128]{1,0:T(8,128)(2,1)S(1)}, bf16[256,128]{1,0:T(8,128)(2,1)S(1)}, u32[]{:S(2)}, u32[]{:S(2)}) collective-permute-start(bf16[256,128]{1,0:T(8,128)(2,1)S(1)} %get-tuple-element.59), channel_id=1, source_target_pairs={{0,32},{32,64},{64,96},{96,128},{128,160},{160,192},{192,224},{224... | collective-permute-start | bytes 196616 | tf_op jit(solution)/shard_map/ppermute | solution.py:353
  94.8 1.2 %collective-permute-done.5.refs_1_ = bf16[256,128]{1,0:T(8,128)(2,1)S(1)} collective-permute-done((bf16[256,128]{1,0:T(8,128)(2,1)S(1)}, bf16[256,128]{1,0:T(8,128)(2,1)S(1)}, u32[]{:S(2)}, u32[]{:S(2)}) %collective-permute-start.5) | collective-permute-done | bytes 65568 | tf_op jit(solution)/shard_map/ppermute | solution.py:353
  95.9 2.8 %collective-permute-start.10 = (bf16[256,128]{1,0:T(8,128)(2,1)S(1)}, bf16[256,128]{1,0:T(8,128)(2,1)S(1)}, u32[]{:S(2)}, u32[]{:S(2)}) collective-permute-start(bf16[256,128]{1,0:T(8,128)(2,1)S(1)} %get-tuple-element.60), channel_id=1, source_target_pairs={{0,224},{32,0},{64,32},{96,64},{128,96},{160,128},{192,160},{224,1... | collective-permute-start | bytes 196616 | tf_op jit(solution)/shard_map/ppermute | solution.py:353
  98.7 2.5 %all-to-all-done.3.parts_ref = bf16[16,128,256]{2,1,0:T(8,128)(2,1)S(1)} async-done(((bf16[16,128,256]{2,1,0:T(8,128)(2,1)}), bf16[16,128,256]{2,1,0:T(8,128)(2,1)S(1)}, u32[]{:S(2)}, u32[]{:S(2)}) %all-to-all-start.3) | async-done | bytes 1048608 | tf_op jit(solution)/shard_map/all_to_all | solution.py:351
  101.2 0.8 sum_kernel.1.done_ref
  102.1 0.8 weight_sum_kernel.1
  (13 shorter events, 0.2 us)
Async XLA Ops:
  0.6 25.6 %copy-start.1 = (bf16[2048,128]{1,0:T(8,128)(2,1)S(1)}, bf16[2048,128]{1,0:T(8,128)(2,1)}, u32[]{:S(2)}) copy-start(bf16[2048,128]{1,0:T(8,128)(2,1)} %wn_ref.1) | copy-start | bytes 1572868
  2.7 23.6 %all-to-all-start = ((bf16[16,256,128]{2,1,0:T(8,128)(2,1)}), bf16[16,256,128]{2,1,0:T(8,128)(2,1)S(1)}, u32[]{:S(2)}, u32[]{:S(2)}) async-start(bf16[16,256,128]{2,1,0:T(8,128)(2,1)} %spread_kernel.1), calls=%async_computation | async-start | bytes 2097152 | tf_op jit(solution)/shard_map/all_to_all | solution.py:282
  10.9 44.5 %copy-start = (bf16[2048,128]{1,0:T(8,128)(2,1)S(1)}, bf16[2048,128]{1,0:T(8,128)(2,1)}, u32[]{:S(2)}) copy-start(bf16[2048,128]{1,0:T(8,128)(2,1)} %ws_ref.1) | copy-start | bytes 1572868
  13.3 43.2 %copy-start.2 = (bf16[256,128]{1,0:T(8,128)(2,1)S(1)}, bf16[256,128]{1,0:T(8,128)(2,1)}, u32[]{:S(2)}) copy-start(bf16[256,128]{1,0:T(8,128)(2,1)} %og_ref.1) | copy-start | bytes 196612
  13.3 2.6 %collective-permute-start.1 = (bf16[8,256,128]{2,1,0:T(8,128)(2,1)S(1)}, bf16[8,256,128]{2,1,0:T(8,128)(2,1)}, u32[]{:S(2)}, u32[]{:S(2)}) collective-permute-start(bf16[8,256,128]{2,1,0:T(8,128)(2,1)S(1)} %get-tuple-element.37), channel_id=1, source_target_pairs={{0,16},{16,0},{1,17},{17,1},{2,18},{18,2},{3,19},{19,3},{4,20},{20... | collective-permute-start | bytes 1572872 | tf_op jit(solution)/shard_map/ppermute | solution.py:304
  14.2 1.5 %collective-permute-start = (f32[16,128]{1,0:T(8,128)S(1)}, f32[16,128]{1,0:T(8,128)S(1)}, u32[]{:S(2)}, u32[]{:S(2)}) collective-permute-start(f32[16,128]{1,0:T(8,128)S(1)} %get-tuple-element.36.flag_ref), channel_id=1, source_target_pairs={{0,16},{16,0},{1,17},{17,1},{2,18},{18,2},{3,19},{19,3},{4,20},{20... | collective-permute-start | bytes 24584 | tf_op jit(solution)/shard_map/ppermute | solution.py:307
  50.8 5.6 %collective-permute-start.2 = (f32[264,128]{1,0:T(8,128)S(1)}, f32[264,128]{1,0:T(8,128)S(1)}, u32[]{:S(2)}, u32[]{:S(2)}) collective-permute-start(f32[264,128]{1,0:T(8,128)S(1)} %get-tuple-element.43), channel_id=1, source_target_pairs={{0,16},{16,0},{1,17},{17,1},{2,18},{18,2},{3,19},{19,3},{4,20},{20... | collective-permute-start | bytes 405512 | tf_op jit(solution)/shard_map/ppermute | solution.py:322
  78.1 2.0 %collective-permute-start.3 = (bf16[8,256,128]{2,1,0:T(8,128)(2,1)S(1)}, bf16[8,256,128]{2,1,0:T(8,128)(2,1)S(1)}, u32[]{:S(2)}, u32[]{:S(2)}) collective-permute-start(bf16[8,256,128]{2,1,0:T(8,128)(2,1)S(1)} %get-tuple-element.50), channel_id=1, source_target_pairs={{0,16},{16,0},{1,17},{17,1},{2,18},{18,2},{3,19},{19,3},{4,20},{20... | collective-permute-start | bytes 1572872 | tf_op jit(solution)/shard_map/ppermute | solution.py:335
  80.2 21.0 %all-to-all-start.3 = ((bf16[16,128,256]{2,1,0:T(8,128)(2,1)}), bf16[16,128,256]{2,1,0:T(8,128)(2,1)S(1)}, u32[]{:S(2)}, u32[]{:S(2)}) async-start(bf16[16,128,256]{2,1,0:T(8,128)(2,1)} %get-tuple-element.53), calls=%async_computation.3 | async-start | bytes 2097152 | tf_op jit(solution)/shard_map/all_to_all | solution.py:351
  84.4 9.2 %collective-permute-start.4 = (bf16[256,128]{1,0:T(8,128)(2,1)S(1)}, bf16[256,128]{1,0:T(8,128)(2,1)S(1)}, u32[]{:S(2)}, u32[]{:S(2)}) collective-permute-start(bf16[256,128]{1,0:T(8,128)(2,1)S(1)} %get-tuple-element.54), channel_id=1, source_target_pairs={{0,128},{32,160},{64,192},{96,224},{128,0},{160,32},{192,64},{224,... | collective-permute-start | bytes 196616 | tf_op jit(solution)/shard_map/ppermute | solution.py:353
  85.5 10.4 %collective-permute-start.5 = (bf16[256,128]{1,0:T(8,128)(2,1)S(1)}, bf16[256,128]{1,0:T(8,128)(2,1)S(1)}, u32[]{:S(2)}, u32[]{:S(2)}) collective-permute-start(bf16[256,128]{1,0:T(8,128)(2,1)S(1)} %get-tuple-element.55), channel_id=1, source_target_pairs={{0,96},{32,128},{64,160},{96,192},{128,224},{160,0},{192,32},{224,... | collective-permute-start | bytes 196616 | tf_op jit(solution)/shard_map/ppermute | solution.py:353
  86.6 15.5 %collective-permute-start.6 = (bf16[256,128]{1,0:T(8,128)(2,1)S(1)}, bf16[256,128]{1,0:T(8,128)(2,1)S(1)}, u32[]{:S(2)}, u32[]{:S(2)}) collective-permute-start(bf16[256,128]{1,0:T(8,128)(2,1)S(1)} %get-tuple-element.56), channel_id=1, source_target_pairs={{0,160},{32,192},{64,224},{96,0},{128,32},{160,64},{192,96},{224,1... | collective-permute-start | bytes 196616 | tf_op jit(solution)/shard_map/ppermute | solution.py:353
  90.0 12.1 %collective-permute-start.7 = (bf16[256,128]{1,0:T(8,128)(2,1)S(1)}, bf16[256,128]{1,0:T(8,128)(2,1)S(1)}, u32[]{:S(2)}, u32[]{:S(2)}) collective-permute-start(bf16[256,128]{1,0:T(8,128)(2,1)S(1)} %get-tuple-element.57), channel_id=1, source_target_pairs={{0,64},{32,96},{64,128},{96,160},{128,192},{160,224},{192,0},{224,... | collective-permute-start | bytes 196616 | tf_op jit(solution)/shard_map/ppermute | solution.py:353
  91.4 10.7 %collective-permute-start.8 = (bf16[256,128]{1,0:T(8,128)(2,1)S(1)}, bf16[256,128]{1,0:T(8,128)(2,1)S(1)}, u32[]{:S(2)}, u32[]{:S(2)}) collective-permute-start(bf16[256,128]{1,0:T(8,128)(2,1)S(1)} %get-tuple-element.58), channel_id=1, source_target_pairs={{0,192},{32,224},{64,0},{96,32},{128,64},{160,96},{192,128},{224,1... | collective-permute-start | bytes 196616 | tf_op jit(solution)/shard_map/ppermute | solution.py:353
  93.6 8.4 %collective-permute-start.9 = (bf16[256,128]{1,0:T(8,128)(2,1)S(1)}, bf16[256,128]{1,0:T(8,128)(2,1)S(1)}, u32[]{:S(2)}, u32[]{:S(2)}) collective-permute-start(bf16[256,128]{1,0:T(8,128)(2,1)S(1)} %get-tuple-element.59), channel_id=1, source_target_pairs={{0,32},{32,64},{64,96},{96,128},{128,160},{160,192},{192,224},{224... | collective-permute-start | bytes 196616 | tf_op jit(solution)/shard_map/ppermute | solution.py:353
  95.9 6.1 %collective-permute-start.10 = (bf16[256,128]{1,0:T(8,128)(2,1)S(1)}, bf16[256,128]{1,0:T(8,128)(2,1)S(1)}, u32[]{:S(2)}, u32[]{:S(2)}) collective-permute-start(bf16[256,128]{1,0:T(8,128)(2,1)S(1)} %get-tuple-element.60), channel_id=1, source_target_pairs={{0,224},{32,0},{64,32},{96,64},{128,96},{160,128},{192,160},{224,1... | collective-permute-start | bytes 196616 | tf_op jit(solution)/shard_map/ppermute | solution.py:353

commit v12 on v11

--- a/solution.py
+++ b/solution.py
@@ -22,8 +22,15 @@
     return jnp.dot(a, b, preferred_element_type=F32)
 
 
-def far_first(chips):
-    return tuple(sorted(range(1, chips), key=lambda step: abs(step - chips // 2)))
+def owners(here, core, chips):
+    way = 1 - 2 * core
+
+    def chip(step):
+        return lax.rem(here + step + chips, chips)
+
+    far = 2 * chip(chips // 2) + 1 - core
+    three, two, one = (2 * chip(step * way) for step in (3, 2, 1))
+    return [far, three, three + 1, two, two + 1, one, one + 1, 2 * here + core]
 
 
 def halves(block):
@@ -199,10 +206,9 @@
     both = halves(jnp.concatenate([low, high], axis=1))
     bt_ref[...] = both[0:T]
     left = jnp.concatenate([gt_ref[...], both], axis=0)
-    for slot, step in enumerate(far_first(chips) + (0,)):
-        chip = lax.rem(here + step, chips)
-        pair = jnp.concatenate([x_ref[2 * chip + core], x_ref[2 * chip + 1 - core]], axis=1)
-        total = dot(left, pair)
+    slots = zip(owners(here, core, chips), owners(here, 1 - core, chips))
+    for slot, (ours, theirs) in enumerate(slots):
+        total = dot(left, jnp.concatenate([x_ref[ours], x_ref[theirs]], axis=1))
         kept, sent = total[:, 0:T], total[:, T:]
         keep_ref[slot, 0:T] = kept[0:T]
         keep_ref[slot, T:] = kept[T : 2 * T] + kept[2 * T :]
@@ -223,16 +229,29 @@
         copy.wait()
 
 
-def pair_kernel(keep_ref, came_ref, payload_ref, *pay_refs):
-    for slot, pay_ref in enumerate(pay_refs[:-1]):
-        pay_ref[...] = (keep_ref[slot] + came_ref[slot].astype(F32)).astype(pay_ref.dtype)
-
-
-def weight_sum_kernel(own_ref, done_ref, *refs):
-    parts, (self_ref, neigh_ref, same_ref) = refs[:-3], refs[-3:]
-    total = own_ref[...]
-    for part in parts:
-        total = total + part[...].astype(F32)
+def pair_kernel(keep_ref, came_ref, payload_ref, far_ref, three_ref, two_ref, one_ref, own_ref, same_ref):
+    def pair(slot):
+        return keep_ref[slot] + came_ref[slot].astype(F32)
+
+    far_ref[...] = pair(0).astype(BF16)
+    for index, ref in enumerate((three_ref, two_ref, one_ref)):
+        for place in range(2):
+            ref[place] = pair(1 + 2 * index + place).astype(BF16)
+    own_ref[...] = pair(7)
+
+
+def fold_kernel(own_ref, far_ref, three_ref, two_ref, one_ref, mine_ref, theirs_ref):
+    core = lax.axis_index("c")
+    mine, theirs = own_ref[...] + far_ref[...].astype(F32), jnp.zeros(own_ref.shape, F32)
+    for ref in (three_ref, two_ref, one_ref):
+        mine = mine + ref[core].astype(F32)
+        theirs = theirs + ref[1 - core].astype(F32)
+    theirs_ref[...] = theirs
+    mine_ref[...] = mine
+
+
+def last_kernel(mine_ref, came_ref, done_ref, self_ref, neigh_ref, same_ref):
+    total = mine_ref[...] + came_ref[...]
     self_ref[...] = total[0:T].T
     neigh_ref[...] = total[T:].T
 
@@ -263,6 +282,12 @@
         compiler_params=pltpu.CompilerParams(vmem_limit_bytes=limit * MIB),
         name=kernel.__name__,
     )(*ins)
+
+
+def along(value, step, chips):
+    pairs = [(2 * chip, 2 * ((chip + step) % chips)) for chip in range(chips)]
+    pairs += [(2 * chip + 1, 2 * ((chip - step) % chips) + 1) for chip in range(chips)]
+    return lax.ppermute(value, ("z", "c"), pairs)
 
 
 def per_device(features, w_self, w_neigh, out_grad, tile_count, tile_dst, tile_src, tile_weight, chips, parts):
@@ -340,27 +365,28 @@
         out_specs=[HBM],
         scratch=[pltpu.VMEM((parts, T, rows), BF16), pltpu.SemaphoreType.DMA((parts,))],
     )
-    *w_pay, own, p_pay = call(
+    block = (2 * T, T)
+    far, three, two, one, own, p_pay = call(
         pair_kernel,
         (keep, came, p_pay),
-        [((2 * T, T), BF16)] * (chips - 1) + [((2 * T, T), F32), (p_pay.shape, BF16)],
+        [(block, BF16)] + [((2,) + block, BF16)] * 3 + [(block, F32), (p_pay.shape, BF16)],
         in_specs=[VMEM, VMEM, HBM],
-        out_specs=[VMEM] * chips + [HBM],
-        aliases={2: chips},
+        out_specs=[VMEM] * 5 + [HBM],
+        aliases={2: 5},
     )
     p_all = lax.all_to_all(p_pay, "f", 0, 0, tiled=True)
-    w_came = [
-        lax.ppermute(block, "z", [(chip, (chip + step) % chips) for chip in range(chips)])
-        for step, block in zip(far_first(chips), w_pay)
-    ]
+    across = [(chip, (chip + chips // 2) % chips) for chip in range(chips)]
+    far = lax.ppermute(lax.ppermute(far, "z", across), "c", swap)
+    three, two, one = along(three, 3, chips), along(two, 2, chips), along(one, 1, chips)
+    mine, theirs = call(fold_kernel, (own, far, three, two, one), [(block, F32)] * 2)
     (grad_features,) = call(sum_kernel, (p_all,), [((rows, T), BF16)])
     grad_self, grad_neigh, grad_features = call(
-        weight_sum_kernel,
-        (own, grad_features, *w_came),
+        last_kernel,
+        (mine, lax.ppermute(theirs, "c", swap), grad_features),
         [((T, T), F32), ((T, T), F32), ((rows, T), BF16)],
-        in_specs=[VMEM, ANY] + [VMEM] * (chips - 1),
+        in_specs=[VMEM] * 2 + [ANY],
         out_specs=[VMEM, VMEM, ANY],
-        aliases={1: 2},
+        aliases={2: 2},
     )
     return output, grad_features, grad_self, grad_neigh
 

time: 103 us -> 104 us (level)
  waiting for transfers between devices: 16.8 us -> 19.9 us
  starting transfers between devices: 30.6 us -> 28.5 us
    ppermute x7 -> x6, waiting for transfers between devices: 1.28 us -> 7.89 us  [the longest x3 3.88 us: along(): return lax.ppermute(value, ('z', 'c'), pairs)]
    ppermute x7 -> x6, starting transfers between devices: 13 us -> 9.76 us  [the longest x3 4.99 us: along(): return lax.ppermute(value, ('z', 'c'), pairs)]
    all_to_all x1, waiting for transfers between devices: 2.49 us -> 0.01 us  [per_device(): p_all = lax.all_to_all(p_pay, 'f', 0, 0, tiled=True)]
    ppermute x1, starting transfers between devices: 0.97 us -> 2.12 us  [per_device(): adj_pair = lax.ppermute(adj_send, 'c', swap)]
    pallas_call x11 -> x12, Pallas kernels: 11.3 us -> 11.2 us  [call(): pl.pallas_call(kernel, out_shape=shapes, in_specs=in_specs or [VMEM] * le...]
  transfers between devices with their start and end apart: 13 -> 12, of which waited for: 8 -> 10; matrix products, arithmetic and copies ran while one was open for 0% -> 0% of each run, Pallas kernels for 5% -> 5%
where the time goes in v12:
time: 104 us
  blocking collectives  42.7 us (41%)
  starting transfers between devices  28.5 us (27%)
  waiting for transfers between devices  19.9 us (19%)
  Pallas kernels  11.2 us (11%)
  between operations  1.39 us (1%)
    all_to_all x1, blocking collectives, per_device(): y_own = lax.all_to_all(y_pay, 'z', 0, 0, tiled=True)  22.6 us
    all_to_all x1, blocking collectives, per_device(): c_all = lax.all_to_all(c_pay, ('z', 'c'), 0, 0, tiled=True)  20.1 us
    pallas_call x12, Pallas kernels, call(): pl.pallas_call(kernel, out_shape=shapes, in_specs=in_specs or [VMEM] * le...  11.2 us
    all_to_all x1, waiting for transfers between devices, per_device(): x_all = lax.all_to_all(x_pay, 'f', 0, 0, tiled=True)  9.38 us
    all_to_all x1, starting transfers between devices, per_device(): x_all = lax.all_to_all(x_pay, 'f', 0, 0, tiled=True)  7.6 us
    ppermute x3, starting transfers between devices, along(): return lax.ppermute(value, ('z', 'c'), pairs)  4.99 us
    ppermute x1, starting transfers between devices, per_device(): came = lax.ppermute(theirs, 'c', swap)  4.63 us
    all_to_all x1, starting transfers between devices, per_device(): p_all = lax.all_to_all(p_pay, 'f', 0, 0, tiled=True)  4.21 us
  transfers between devices with their start and end apart: 12, of which 10 were waited for; matrix products, arithmetic and copies ran while one was open for 0% of the time, Pallas kernels for 5%

profile of v12, /device:TPU:1, one launch (start us, length us, event | category | flops | bytes accessed | tf_op | source)
XLA Modules:
  0.0 103.8 jit_solution(17974097372832999902)
XLA Ops:
  0.6 2.0 %spread_kernel.1 = bf16[16,256,128]{2,1,0:T(8,128)(2,1)} custom-call(bf16[256,128]{1,0:T(8,128)(2,1)} %x_hbm.1), custom_call_target="tpu_custom_call" | custom-call | tf_op jit(solution)/shard_map/spread_kernel/pallas_call | solution.py:275
  2.7 7.6 %all-to-all-start = ((bf16[16,256,128]{2,1,0:T(8,128)(2,1)}), bf16[16,256,128]{2,1,0:T(8,128)(2,1)S(1)}, u32[]{:S(2)}, u32[]{:S(2)}) async-start(bf16[16,256,128]{2,1,0:T(8,128)(2,1)} %spread_kernel.1), calls=%async_computation | async-start | bytes 2097152 | tf_op jit(solution)/shard_map/all_to_all | solution.py:307
  10.9 2.1 %adjacency_kernel.1 = (bf16[16,256,128]{2,1,0:T(8,128)(2,1)S(1)}, bf16[8,256,128]{2,1,0:T(8,128)(2,1)S(1)}, f32[256,128]{1,0:T(8,128)S(1)}, f32[16,128]{1,0:T(8,128)S(1)}) custom-call(s32[1]{0:T(128)S(6)} %copy.22.count_ref, s32[1,80]{1,0:T(1,128)} %dst_hbm.1, s32[1,80]{1,0:T(1,128)} %src_hbm.1, s32[80,128,128]{2,1,0:T(8,128)} %bitcast.1), custom_call_target="tpu_custom_call" | custom-call | tf_op jit(solution)/shard_map/adjacency_kernel/pallas_call | solution.py:275
  13.1 2.1 %collective-permute-start.1 = (bf16[8,256,128]{2,1,0:T(8,128)(2,1)S(1)}, bf16[8,256,128]{2,1,0:T(8,128)(2,1)}, u32[]{:S(2)}, u32[]{:S(2)}) collective-permute-start(bf16[8,256,128]{2,1,0:T(8,128)(2,1)S(1)} %get-tuple-element.36), channel_id=1, source_target_pairs={{0,16},{16,0},{1,17},{17,1},{2,18},{18,2},{3,19},{19,3},{4,20},{20... | collective-permute-start | bytes 1572872 | tf_op jit(solution)/shard_map/ppermute | solution.py:329
  15.3 1.4 %collective-permute-done.pair_flag_ref = f32[16,128]{1,0:T(8,128)S(1)} collective-permute-done((f32[16,128]{1,0:T(8,128)S(1)}, f32[16,128]{1,0:T(8,128)S(1)}, u32[]{:S(2)}, u32[]{:S(2)}) %collective-permute-start) | collective-permute-done | bytes 8224 | tf_op jit(solution)/shard_map/ppermute | solution.py:332
  16.8 0.1 collective-permute-done.1.adj_ref
  16.9 9.4 %all-to-all-done.x_ref = bf16[16,256,128]{2,1,0:T(8,128)(2,1)S(1)} async-done(((bf16[16,256,128]{2,1,0:T(8,128)(2,1)}), bf16[16,256,128]{2,1,0:T(8,128)(2,1)S(1)}, u32[]{:S(2)}, u32[]{:S(2)}) %all-to-all-start) | async-done | bytes 1048608 | tf_op jit(solution)/shard_map/all_to_all | solution.py:307
  26.3 0.4 neighbour_kernel.1
  26.7 22.6 %all_to_all.20.y_ref = bf16[8,272,128]{2,1,0:T(8,128)(2,1)S(1)} all-to-all(bf16[8,272,128]{2,1,0:T(8,128)(2,1)S(1)} %get-tuple-element.39), channel_id=1, replica_groups=mesh['z'=8,'c'=2,'f'=16] {'z'}, dimensions={0} | all-to-all | bytes 1114112 | tf_op jit(solution)/shard_map/all_to_all | solution.py:338
  49.3 1.5 %aggregate_kernel.1 = (f32[256,128]{1,0:T(8,128)S(1)}, f32[8,128]{1,0:T(8,128)S(1)}, f32[264,128]{1,0:T(8,128)S(1)}, bf16[16,256,128]{2,1,0:T(8,128)(2,1)S(1)}) custom-call(f32[16,128]{1,0:T(8,128)S(1)} %get-tuple-element.35.flag_ref, f32[16,128]{1,0:T(8,128)S(1)} %get-tuple-element.37.flag_pair_ref, ...), custom_call_target="tpu_custom_call", output_to_operand_aliasing={{3}: (5, {})} | custom-call | tf_op jit(solution)/shard_map/aggregate_kernel/pallas_call | solution.py:275
  50.8 4.6 %collective-permute-start.2 = (f32[264,128]{1,0:T(8,128)S(1)}, f32[264,128]{1,0:T(8,128)S(1)}, u32[]{:S(2)}, u32[]{:S(2)}) collective-permute-start(f32[264,128]{1,0:T(8,128)S(1)} %get-tuple-element.42), channel_id=1, source_target_pairs={{0,16},{16,0},{1,17},{17,1},{2,18},{18,2},{3,19},{19,3},{4,20},{20... | collective-permute-start | bytes 405512 | tf_op jit(solution)/shard_map/ppermute | solution.py:347
  55.5 0.4 self_kernel.1.z_ref
  55.9 0.6 collective-permute-done.2.came_ref
  56.5 0.8 activation_kernel.1
  57.3 20.1 %all_to_all.21.came_ref = bf16[16,128,128]{2,1,0:T(8,128)(2,1)S(1)} all-to-all(bf16[16,128,128]{2,1,0:T(8,128)(2,1)S(1)} %get-tuple-element.45), channel_id=1, replica_groups=mesh['z'=8,'c'=2,'f'=16] {'z','c'}, dimensions={0} | all-to-all | bytes 1048576 | tf_op jit(solution)/shard_map/all_to_all | solution.py:354
  77.4 0.7 weight_grad_kernel.1
  78.2 1.4 %feature_grad_kernel.1.payload_ref = bf16[16,128,256]{2,1,0:T(8,128)(2,1)} custom-call(bf16[128,256]{1,0:T(8,128)(2,1)S(1)} %get-tuple-element.47.gt_ref, bf16[128,256]{1,0:T(8,128)(2,1)S(1)} %get-tuple-element.50.bt_ref, bf16[2048,128]{1,0:T(8,128)(2,1)S(1)} %copy-done, bf16[2048,128]{1,0:T(8,128)(2,1)S(1)} %copy-done.1), custom_call_target="tpu_custom_call" | custom-call | tf_op jit(solution)/shard_map/feature_grad_kernel/pallas_call | solution.py:275
  79.6 0.5 collective-permute-done.3.came_ref
  80.2 4.2 %all-to-all-start.3 = ((bf16[16,128,256]{2,1,0:T(8,128)(2,1)}), bf16[16,128,256]{2,1,0:T(8,128)(2,1)S(1)}, u32[]{:S(2)}, u32[]{:S(2)}) async-start(bf16[16,128,256]{2,1,0:T(8,128)(2,1)} %get-tuple-element.58), calls=%async_computation.3 | async-start | bytes 2097152 | tf_op jit(solution)/shard_map/all_to_all | solution.py:377
  84.4 1.0 %collective-permute-start.4 = (bf16[256,128]{1,0:T(8,128)(2,1)S(1)}, bf16[256,128]{1,0:T(8,128)(2,1)S(1)}, u32[]{:S(2)}, u32[]{:S(2)}) collective-permute-start(bf16[256,128]{1,0:T(8,128)(2,1)S(1)} %get-tuple-element.52), channel_id=1, source_target_pairs={{0,128},{32,160},{64,192},{96,224},{128,0},{160,32},{192,64},{224,... | collective-permute-start | bytes 196616 | tf_op jit(solution)/shard_map/ppermute | solution.py:379
  85.5 1.6 %collective-permute-start.6 = (bf16[2,256,128]{2,1,0:T(8,128)(2,1)S(1)}, bf16[2,256,128]{2,1,0:T(8,128)(2,1)S(1)}, u32[]{:S(2)}, u32[]{:S(2)}) collective-permute-start(bf16[2,256,128]{2,1,0:T(8,128)(2,1)S(1)} %get-tuple-element.53), channel_id=1, source_target_pairs={{0,96},{32,128},{64,160},{96,192},{128,224},{160,0},{192,32},{224,... | collective-permute-start | bytes 393224 | tf_op jit(solution)/shard_map/ppermute | solution.py:290
  87.1 1.9 %collective-permute-start.7 = (bf16[2,256,128]{2,1,0:T(8,128)(2,1)S(1)}, bf16[2,256,128]{2,1,0:T(8,128)(2,1)S(1)}, u32[]{:S(2)}, u32[]{:S(2)}) collective-permute-start(bf16[2,256,128]{2,1,0:T(8,128)(2,1)S(1)} %get-tuple-element.54), channel_id=1, source_target_pairs={{0,64},{32,96},{64,128},{96,160},{128,192},{160,224},{192,0},{224,... | collective-permute-start | bytes 393224 | tf_op jit(solution)/shard_map/ppermute | solution.py:290
  88.9 1.5 %collective-permute-start.8 = (bf16[2,256,128]{2,1,0:T(8,128)(2,1)S(1)}, bf16[2,256,128]{2,1,0:T(8,128)(2,1)S(1)}, u32[]{:S(2)}, u32[]{:S(2)}) collective-permute-start(bf16[2,256,128]{2,1,0:T(8,128)(2,1)S(1)} %get-tuple-element.55), channel_id=1, source_target_pairs={{0,32},{32,64},{64,96},{96,128},{128,160},{160,192},{192,224},{224... | collective-permute-start | bytes 393224 | tf_op jit(solution)/shard_map/ppermute | solution.py:290
  90.5 3.0 %collective-permute-done.4 = bf16[256,128]{1,0:T(8,128)(2,1)S(1)} collective-permute-done((bf16[256,128]{1,0:T(8,128)(2,1)S(1)}, bf16[256,128]{1,0:T(8,128)(2,1)S(1)}, u32[]{:S(2)}, u32[]{:S(2)}) %collective-permute-start.4) | collective-permute-done | bytes 65568 | tf_op jit(solution)/shard_map/ppermute | solution.py:379
  93.4 0.8 collective-permute-start.5
  94.2 0.9 collective-permute-done.5.far_ref
  95.1 2.0 %collective-permute-done.7.two_ref = bf16[2,256,128]{2,1,0:T(8,128)(2,1)S(1)} collective-permute-done((bf16[2,256,128]{2,1,0:T(8,128)(2,1)S(1)}, bf16[2,256,128]{2,1,0:T(8,128)(2,1)S(1)}, u32[]{:S(2)}, u32[]{:S(2)}) %collective-permute-start.7) | collective-permute-done | bytes 131104 | tf_op jit(solution)/shard_map/ppermute | solution.py:290
  97.2 1.9 %collective-permute-done.8.one_ref = bf16[2,256,128]{2,1,0:T(8,128)(2,1)S(1)} collective-permute-done((bf16[2,256,128]{2,1,0:T(8,128)(2,1)S(1)}, bf16[2,256,128]{2,1,0:T(8,128)(2,1)S(1)}, u32[]{:S(2)}, u32[]{:S(2)}) %collective-permute-start.8) | collective-permute-done | bytes 131104 | tf_op jit(solution)/shard_map/ppermute | solution.py:290
  99.1 2.9 %collective-permute-start.9 = (f32[256,128]{1,0:T(8,128)S(1)}, f32[256,128]{1,0:T(8,128)S(1)}, u32[]{:S(2)}, u32[]{:S(2)}) collective-permute-start(f32[256,128]{1,0:T(8,128)S(1)} %get-tuple-element.57), channel_id=1, source_target_pairs={{0,16},{16,0},{1,17},{17,1},{2,18},{18,2},{3,19},{19,3},{4,20},{20... | collective-permute-start | bytes 393224 | tf_op jit(solution)/shard_map/ppermute | solution.py:385
  102.0 0.8 sum_kernel.1.done_ref
  102.9 0.1 collective-permute-done.9.came_ref
  103.0 0.8 last_kernel.1
  (12 shorter events, 0.4 us)
Async XLA Ops:
  0.6 25.6 %copy-start.1 = (bf16[2048,128]{1,0:T(8,128)(2,1)S(1)}, bf16[2048,128]{1,0:T(8,128)(2,1)}, u32[]{:S(2)}) copy-start(bf16[2048,128]{1,0:T(8,128)(2,1)} %wn_ref.1) | copy-start | bytes 1572868
  2.7 23.6 %all-to-all-start = ((bf16[16,256,128]{2,1,0:T(8,128)(2,1)}), bf16[16,256,128]{2,1,0:T(8,128)(2,1)S(1)}, u32[]{:S(2)}, u32[]{:S(2)}) async-start(bf16[16,256,128]{2,1,0:T(8,128)(2,1)} %spread_kernel.1), calls=%async_computation | async-start | bytes 2097152 | tf_op jit(solution)/shard_map/all_to_all | solution.py:307
  10.9 44.5 %copy-start = (bf16[2048,128]{1,0:T(8,128)(2,1)S(1)}, bf16[2048,128]{1,0:T(8,128)(2,1)}, u32[]{:S(2)}) copy-start(bf16[2048,128]{1,0:T(8,128)(2,1)} %ws_ref.1) | copy-start | bytes 1572868
  13.1 43.4 %copy-start.2 = (bf16[256,128]{1,0:T(8,128)(2,1)S(1)}, bf16[256,128]{1,0:T(8,128)(2,1)}, u32[]{:S(2)}) copy-start(bf16[256,128]{1,0:T(8,128)(2,1)} %og_ref.1) | copy-start | bytes 196612
  13.1 3.8 %collective-permute-start.1 = (bf16[8,256,128]{2,1,0:T(8,128)(2,1)S(1)}, bf16[8,256,128]{2,1,0:T(8,128)(2,1)}, u32[]{:S(2)}, u32[]{:S(2)}) collective-permute-start(bf16[8,256,128]{2,1,0:T(8,128)(2,1)S(1)} %get-tuple-element.36), channel_id=1, source_target_pairs={{0,16},{16,0},{1,17},{17,1},{2,18},{18,2},{3,19},{19,3},{4,20},{20... | collective-permute-start | bytes 1572872 | tf_op jit(solution)/shard_map/ppermute | solution.py:329
  15.2 1.5 %collective-permute-start = (f32[16,128]{1,0:T(8,128)S(1)}, f32[16,128]{1,0:T(8,128)S(1)}, u32[]{:S(2)}, u32[]{:S(2)}) collective-permute-start(f32[16,128]{1,0:T(8,128)S(1)} %get-tuple-element.35.flag_ref), channel_id=1, source_target_pairs={{0,16},{16,0},{1,17},{17,1},{2,18},{18,2},{3,19},{19,3},{4,20},{20... | collective-permute-start | bytes 24584 | tf_op jit(solution)/shard_map/ppermute | solution.py:332
  50.8 5.6 %collective-permute-start.2 = (f32[264,128]{1,0:T(8,128)S(1)}, f32[264,128]{1,0:T(8,128)S(1)}, u32[]{:S(2)}, u32[]{:S(2)}) collective-permute-start(f32[264,128]{1,0:T(8,128)S(1)} %get-tuple-element.42), channel_id=1, source_target_pairs={{0,16},{16,0},{1,17},{17,1},{2,18},{18,2},{3,19},{19,3},{4,20},{20... | collective-permute-start | bytes 405512 | tf_op jit(solution)/shard_map/ppermute | solution.py:347
  78.1 2.0 %collective-permute-start.3 = (bf16[8,256,128]{2,1,0:T(8,128)(2,1)S(1)}, bf16[8,256,128]{2,1,0:T(8,128)(2,1)S(1)}, u32[]{:S(2)}, u32[]{:S(2)}) collective-permute-start(bf16[8,256,128]{2,1,0:T(8,128)(2,1)S(1)} %get-tuple-element.49), channel_id=1, source_target_pairs={{0,16},{16,0},{1,17},{17,1},{2,18},{18,2},{3,19},{19,3},{4,20},{20... | collective-permute-start | bytes 1572872 | tf_op jit(solution)/shard_map/ppermute | solution.py:360
  80.2 21.8 %all-to-all-start.3 = ((bf16[16,128,256]{2,1,0:T(8,128)(2,1)}), bf16[16,128,256]{2,1,0:T(8,128)(2,1)S(1)}, u32[]{:S(2)}, u32[]{:S(2)}) async-start(bf16[16,128,256]{2,1,0:T(8,128)(2,1)} %get-tuple-element.58), calls=%async_computation.3 | async-start | bytes 2097152 | tf_op jit(solution)/shard_map/all_to_all | solution.py:377
  84.4 9.0 %collective-permute-start.4 = (bf16[256,128]{1,0:T(8,128)(2,1)S(1)}, bf16[256,128]{1,0:T(8,128)(2,1)S(1)}, u32[]{:S(2)}, u32[]{:S(2)}) collective-permute-start(bf16[256,128]{1,0:T(8,128)(2,1)S(1)} %get-tuple-element.52), channel_id=1, source_target_pairs={{0,128},{32,160},{64,192},{96,224},{128,0},{160,32},{192,64},{224,... | collective-permute-start | bytes 196616 | tf_op jit(solution)/shard_map/ppermute | solution.py:379
  85.5 9.7 %collective-permute-start.6 = (bf16[2,256,128]{2,1,0:T(8,128)(2,1)S(1)}, bf16[2,256,128]{2,1,0:T(8,128)(2,1)S(1)}, u32[]{:S(2)}, u32[]{:S(2)}) collective-permute-start(bf16[2,256,128]{2,1,0:T(8,128)(2,1)S(1)} %get-tuple-element.53), channel_id=1, source_target_pairs={{0,96},{32,128},{64,160},{96,192},{128,224},{160,0},{192,32},{224,... | collective-permute-start | bytes 393224 | tf_op jit(solution)/shard_map/ppermute | solution.py:290
  87.1 10.1 %collective-permute-start.7 = (bf16[2,256,128]{2,1,0:T(8,128)(2,1)S(1)}, bf16[2,256,128]{2,1,0:T(8,128)(2,1)S(1)}, u32[]{:S(2)}, u32[]{:S(2)}) collective-permute-start(bf16[2,256,128]{2,1,0:T(8,128)(2,1)S(1)} %get-tuple-element.54), channel_id=1, source_target_pairs={{0,64},{32,96},{64,128},{96,160},{128,192},{160,224},{192,0},{224,... | collective-permute-start | bytes 393224 | tf_op jit(solution)/shard_map/ppermute | solution.py:290
  88.9 10.1 %collective-permute-start.8 = (bf16[2,256,128]{2,1,0:T(8,128)(2,1)S(1)}, bf16[2,256,128]{2,1,0:T(8,128)(2,1)S(1)}, u32[]{:S(2)}, u32[]{:S(2)}) collective-permute-start(bf16[2,256,128]{2,1,0:T(8,128)(2,1)S(1)} %get-tuple-element.55), channel_id=1, source_target_pairs={{0,32},{32,64},{64,96},{96,128},{128,160},{160,192},{192,224},{224... | collective-permute-start | bytes 393224 | tf_op jit(solution)/shard_map/ppermute | solution.py:290
  93.4 1.7 %collective-permute-start.5 = (bf16[256,128]{1,0:T(8,128)(2,1)S(1)}, bf16[256,128]{1,0:T(8,128)(2,1)S(1)}, u32[]{:S(2)}, u32[]{:S(2)}) collective-permute-start(bf16[256,128]{1,0:T(8,128)(2,1)S(1)} %collective-permute-done.4), channel_id=1, source_target_pairs={{0,16},{16,0},{1,17},{17,1},{2,18},{18,2},{3,19},{19,3},{4,20},{20... | collective-permute-start | bytes 196616 | tf_op jit(solution)/shard_map/ppermute | solution.py:379
  99.1 3.9 %collective-permute-start.9 = (f32[256,128]{1,0:T(8,128)S(1)}, f32[256,128]{1,0:T(8,128)S(1)}, u32[]{:S(2)}, u32[]{:S(2)}) collective-permute-start(f32[256,128]{1,0:T(8,128)S(1)} %get-tuple-element.57), channel_id=1, source_target_pairs={{0,16},{16,0},{1,17},{17,1},{2,18},{18,2},{3,19},{19,3},{4,20},{20... | collective-permute-start | bytes 393224 | tf_op jit(solution)/shard_map/ppermute | solution.py:385

commit v13 on v11

--- a/solution.py
+++ b/solution.py
@@ -24,6 +24,15 @@
 
 def far_first(chips):
     return tuple(sorted(range(1, chips), key=lambda step: abs(step - chips // 2)))
+
+
+def sources(here, core, chips):
+    way = 1 - 2 * core
+    found = []
+    for step in (1, 2, 3):
+        chip = lax.rem(here - step * way + chips, chips)
+        found += [2 * chip, 2 * chip + 1]
+    return found + [2 * lax.rem(here + chips // 2, chips) + core]
 
 
 def halves(block):
@@ -94,9 +103,8 @@
         if owner > 0:
             total = total + acc[owner]
         adj_ref[owner] = acc[owner].astype(F32).astype(BF16)
-    other = 1 - lax.axis_index("c")
-    for chip in range(send_ref.shape[0]):
-        send_ref[chip] = adj_ref[2 * chip + other]
+    for slot, owner in enumerate(sources(lax.axis_index("z"), 1 - lax.axis_index("c"), groups // 2)):
+        send_ref[slot] = adj_ref[owner]
     degree = jnp.sum(total.astype(F32), axis=1, keepdims=True)
     inv_ref[...] = jnp.broadcast_to(1.0 / jnp.maximum(degree, 1.0), inv_ref.shape)
     row = lax.broadcasted_iota(jnp.int32, flag_ref.shape, 0)
@@ -119,9 +127,18 @@
     rows = x_ref.shape[1]
     product = wide_dot(x_ref, w_ref).astype(BF16)
     flags = flag_ref[...].astype(BF16)
-    for copy in range(pay_ref.shape[0]):
-        pay_ref[copy, 0:rows, :] = product
-        pay_ref[copy, rows:, :] = flags
+    pay_ref[0:rows, :] = product
+    pay_ref[rows:, :] = flags
+
+
+def join_kernel(y_ref, y_pair_ref, pair_ref):
+    core = lax.axis_index("c")
+    pair_ref[core] = y_ref[...]
+    pair_ref[1 - core] = y_pair_ref[...]
+
+
+def half_kernel(pair_ref, half_ref):
+    half_ref[...] = pair_ref[lax.axis_index("c")]
 
 
 def self_kernel(x_ref, w_ref, z_ref):
@@ -129,47 +146,49 @@
 
 
 def aggregate_kernel(
-    flag_ref, flag_pair_ref, adj_ref, adj_pair_ref, y_ref, x_ref, mine_ref, mask_ref, theirs_ref, x_same_ref
+    flag_ref, flag_pair_ref, adj_ref, adj_pair_ref, pair_ref, one_ref, two_ref, three_ref, far_ref,
+    mine_ref, mask_ref, theirs_ref,
 ):
     core = lax.axis_index("c")
-    here = 2 * lax.axis_index("z")
-    chips = y_ref.shape[0]
+    here = lax.axis_index("z")
     rows = mine_ref.shape[0]
-    row = lax.broadcasted_iota(jnp.int32, (y_ref.shape[1] - rows, T), 0)
-
-    def summed(adj, flag):
-        total = jnp.zeros(mine_ref.shape, F32)
-        for first in range(0, chips, 2):
-            blocks, tiles = [], []
-            for chip in (first, first + 1):
-                high = flag[pl.ds(2 * chip + core, 1), :] > 0.5
-                blocks.append(adj(chip))
-                low_tile = y_ref[chip, 0:T, :].astype(F32)
-                high_tile = y_ref[chip, T : 2 * T, :].astype(F32)
-                tiles.append(jnp.where(high, high_tile, low_tile).astype(BF16))
-            total = total + dot(jnp.concatenate(blocks, axis=1), jnp.concatenate(tiles, axis=0))
-        return total
-
-    theirs_ref[0:rows] = summed(lambda chip: adj_pair_ref[chip], flag_pair_ref)
-    mine_ref[...] = summed(lambda chip: adj_ref[2 * chip + core], flag_ref)
-    for chip in range(chips):
-        flags = y_ref[chip, rows:, :].astype(F32)
-        mask_ref[chip : chip + 1, :] = jnp.sum(
-            jnp.where(row == here + core, flags, 0.0), axis=0, keepdims=True
-        )
-        theirs_ref[rows + chip : rows + chip + 1, :] = jnp.sum(
-            jnp.where(row == here + 1 - core, flags, 0.0), axis=0, keepdims=True
-        )
+    row = lax.broadcasted_iota(jnp.int32, (far_ref.shape[0] - rows, T), 0)
+    blocks = [ref.at[side] for ref in (one_ref, two_ref, three_ref) for side in range(2)] + [far_ref]
+    found = sources(here, core, flag_ref.shape[0] // 2)
+
+    def summed(adj, flag, blocks, found):
+        tiles = []
+        for block, owner in zip(blocks, found):
+            high = flag[pl.ds(owner, 1), :] > 0.5
+            low_tile = block[0:T, :].astype(F32)
+            high_tile = block[T : 2 * T, :].astype(F32)
+            tiles.append(jnp.where(high, high_tile, low_tile).astype(BF16))
+        return dot(jnp.concatenate(adj, axis=1), jnp.concatenate(tiles, axis=0))
+
+    def mask_row(block, reader):
+        return jnp.sum(jnp.where(row == reader, block[rows:, :].astype(F32), 0.0), axis=0, keepdims=True)
+
+    adj_pair = [adj_pair_ref[slot] for slot in range(len(found))]
+    theirs_ref[0:rows] = summed(adj_pair, flag_pair_ref, blocks, found)
+    theirs_ref[rows:] = jnp.zeros((theirs_ref.shape[0] - rows, T), F32)
+    for slot, block in enumerate(blocks):
+        theirs_ref[rows + slot : rows + slot + 1, :] = mask_row(block, 2 * here + 1 - core)
+    blocks = blocks + [pair_ref.at[0], pair_ref.at[1]]
+    found = found + [2 * here, 2 * here + 1]
+    mine_ref[...] = summed([adj_ref[owner] for owner in found], flag_ref, blocks, found)
+    mask_ref[...] = jnp.zeros_like(mask_ref)
+    for block, owner in zip(blocks, found):
+        mask_ref[pl.ds(owner, 1), :] = mask_row(block, 2 * here + core)
 
 
 def activation_kernel(
     adj_ref, inv_ref, mine_ref, own_mask_ref, came_ref, z_ref, og_ref, out_ref, gt_ref, pay_ref, mask_ref
 ):
-    core = lax.axis_index("c")
     rows = z_ref.shape[0]
-    chips = own_mask_ref.shape[0]
-    mask_ref[pl.ds(pl.multiple_of(core * chips, chips), chips), :] = own_mask_ref[...]
-    mask_ref[pl.ds(pl.multiple_of((1 - core) * chips, chips), chips), :] = came_ref[rows:, :]
+    mask_ref[...] = own_mask_ref[...]
+    found = sources(lax.axis_index("z"), 1 - lax.axis_index("c"), mask_ref.shape[0] // 2)
+    for slot, owner in enumerate(found):
+        mask_ref[pl.ds(owner, 1), :] = came_ref[rows + slot : rows + slot + 1, :]
     inverse = inv_ref[...]
     z = z_ref[...] + inverse * (mine_ref[...] + came_ref[0:rows])
     sig = 1.0 / (1.0 + jnp.exp(-z))
@@ -192,8 +211,7 @@
     high = jnp.zeros((T, T), F32)
     for sender in range(came_ref.shape[0]):
         came = came_ref[sender].astype(F32)
-        place = sender % 2 * chips + sender // 2
-        is_high = mask_ref[place : place + 1, :] > 0.5
+        is_high = mask_ref[sender : sender + 1, :] > 0.5
         low = low + jnp.where(is_high, 0.0, came)
         high = high + jnp.where(is_high, came, 0.0)
     both = halves(jnp.concatenate([low, high], axis=1))
@@ -265,6 +283,12 @@
     )(*ins)
 
 
+def along(value, step, chips):
+    pairs = [(2 * chip, 2 * ((chip + step) % chips)) for chip in range(chips)]
+    pairs += [(2 * chip + 1, 2 * ((chip - step) % chips) + 1) for chip in range(chips)]
+    return lax.ppermute(value, ("z", "c"), pairs)
+
+
 def per_device(features, w_self, w_neigh, out_grad, tile_count, tile_dst, tile_src, tile_weight, chips, parts):
     rows = features.shape[0]
     groups = 2 * chips
@@ -285,7 +309,7 @@
         (tile_count, tile_dst, tile_src, tile_weight[0]),
         [
             ((groups, rows, T), BF16),
-            ((chips, rows, T), BF16),
+            ((chips - 1, rows, T), BF16),
             ((rows, T), F32),
             ((groups, T), F32),
         ],
@@ -302,25 +326,25 @@
         limit=20,
     )
     adj_pair = lax.ppermute(adj_send, "c", swap)
-    y_pay, flags_pair, adj_pair = call(
+    y, flags_pair, adj_pair = call(
         neighbour_kernel,
         (x_all, w_neigh, flags, lax.ppermute(flags, "c", swap), adj_pair),
-        [((chips, rows + groups, T), BF16), (flags.shape, F32), (adj_pair.shape, BF16)],
+        [((rows + groups, T), BF16), (flags.shape, F32), (adj_pair.shape, BF16)],
         in_specs=[VMEM] * 3 + [ANY, HBM],
         out_specs=[VMEM, ANY, HBM],
         aliases={3: 1, 4: 2},
     )
-    y_own = lax.all_to_all(y_pay, "z", 0, 0, tiled=True)
-    mine, own_mask, theirs, x_late = call(
+    (pair,) = call(join_kernel, (y, lax.ppermute(y, "c", swap)), [((2,) + y.shape, BF16)])
+    two, one = along(pair, 2, chips), along(pair, 1, chips)
+    (half,) = call(half_kernel, (two,), [(y.shape, BF16)])
+    three, far = along(two, 1, chips), along(half, 2, chips)
+    mine, own_mask, theirs = call(
         aggregate_kernel,
-        (flags, flags_pair, adj, adj_pair, y_own, x_all),
-        [((rows, T), F32), ((chips, T), F32), ((rows + chips, T), F32), (x_all.shape, BF16)],
-        in_specs=[VMEM] * 5 + [ANY],
-        out_specs=[VMEM] * 3 + [ANY],
-        aliases={5: 3},
+        (flags, flags_pair, adj, adj_pair, pair, one, two, three, far),
+        [((rows, T), F32), ((groups, T), F32), ((rows + chips, T), F32)],
     )
     came = lax.ppermute(theirs, "c", swap)
-    (z_self,) = call(self_kernel, (x_late, w_self), [((rows, T), F32)])
+    (z_self,) = call(self_kernel, (x_all, w_self), [((rows, T), F32)])
     output, gt, c_pay, mask = call(
         activation_kernel,
         (adj, inverse, mine, own_mask, came, z_self, out_grad),
@@ -329,7 +353,7 @@
     c_all = lax.all_to_all(c_pay, ("z", "c"), 0, 0, tiled=True)
     bt, keep, send = call(
         weight_grad_kernel,
-        (c_all, mask, gt, x_late),
+        (c_all, mask, gt, x_all),
         [((T, rows), BF16), ((chips, 2 * T, T), F32), ((chips, 2 * T, T), BF16)],
     )
     came = lax.ppermute(send, "c", swap)

time: 103 us -> 104 us (level)
  blocking collectives: 42.7 us -> 23.4 us
  starting transfers between devices: 30.6 us -> 42.9 us
  waiting for transfers between devices: 16.8 us -> 24.7 us
    all_to_all x1 -> x0, blocking collectives: 22.6 us -> none  [per_device(): y_own = lax.all_to_all(y_pay, 'z', 0, 0, tiled=True)]
    ppermute x0 -> x5, starting transfers between devices: none -> 13.6 us  [the longest x4 10.9 us: along(): return lax.ppermute(value, ('z', 'c'), pairs)]
    ppermute x0 -> x5, waiting for transfers between devices: none -> 6.35 us  [the longest x4 5.44 us: along(): return lax.ppermute(value, ('z', 'c'), pairs)]
    all_to_all x1, blocking collectives: 20.1 us -> 23.4 us  [per_device(): c_all = lax.all_to_all(c_pay, ('z', 'c'), 0, 0, tiled=True)]
    all_to_all x1, waiting for transfers between devices: 2.49 us -> 4.04 us  [per_device(): p_all = lax.all_to_all(p_pay, 'f', 0, 0, tiled=True)]
    ppermute x1, starting transfers between devices: 4.63 us -> 3.43 us  [per_device(): came = lax.ppermute(theirs, 'c', swap)]
    pallas_call x11 -> x13, Pallas kernels: 11.3 us -> 10.9 us  [call(): pl.pallas_call(kernel, out_shape=shapes, in_specs=in_specs or [VMEM] * le...]
  transfers between devices with their start and end apart: 13 -> 18, of which waited for: 8 -> 10; matrix products, arithmetic and copies ran while one was open for 0% -> 0% of each run, Pallas kernels for 5% -> 4%
where the time goes in v13:
time: 104 us; the launch traced here: 103 us
  starting transfers between devices  42.9 us (41%)
  waiting for transfers between devices  24.7 us (24%)
  blocking collectives  23.4 us (22%)
  Pallas kernels  10.9 us (10%)
  between operations  1.47 us (1%)
    all_to_all x1, blocking collectives, per_device(): c_all = lax.all_to_all(c_pay, ('z', 'c'), 0, 0, tiled=True)  23.4 us
    ppermute x7, starting transfers between devices, per_device(): lax.ppermute(block, 'z', [(chip, (chip + step) % chips) for chip in range...  13.2 us
    ppermute x4, starting transfers between devices, along(): return lax.ppermute(value, ('z', 'c'), pairs)  10.9 us
    pallas_call x13, Pallas kernels, call(): pl.pallas_call(kernel, out_shape=shapes, in_specs=in_specs or [VMEM] * le...  10.9 us
    all_to_all x1, waiting for transfers between devices, per_device(): x_all = lax.all_to_all(x_pay, 'f', 0, 0, tiled=True)  10.5 us
    all_to_all x1, starting transfers between devices, per_device(): x_all = lax.all_to_all(x_pay, 'f', 0, 0, tiled=True)  7.6 us
    ppermute x4, waiting for transfers between devices, along(): return lax.ppermute(value, ('z', 'c'), pairs)  5.44 us
    all_to_all x1, waiting for transfers between devices, per_device(): p_all = lax.all_to_all(p_pay, 'f', 0, 0, tiled=True)  4.04 us
  transfers between devices with their start and end apart: 18, of which 10 were waited for; matrix products, arithmetic and copies ran while one was open for 0% of the time, Pallas kernels for 4%

profile of v13, /device:TPU:1, one launch (start us, length us, event | category | flops | bytes accessed | tf_op | source)
XLA Modules:
  0.0 103.4 jit_solution(1040937023746589409)
XLA Ops:
  0.6 2.0 %spread_kernel.1 = bf16[16,256,128]{2,1,0:T(8,128)(2,1)} custom-call(bf16[256,128]{1,0:T(8,128)(2,1)} %x_hbm.1), custom_call_target="tpu_custom_call" | custom-call | tf_op jit(solution)/shard_map/spread_kernel/pallas_call | solution.py:274
  2.7 7.6 %all-to-all-start = ((bf16[16,256,128]{2,1,0:T(8,128)(2,1)}), bf16[16,256,128]{2,1,0:T(8,128)(2,1)S(1)}, u32[]{:S(2)}, u32[]{:S(2)}) async-start(bf16[16,256,128]{2,1,0:T(8,128)(2,1)} %spread_kernel.1), calls=%async_computation | async-start | bytes 2097152 | tf_op jit(solution)/shard_map/all_to_all | solution.py:306
  11.0 1.9 %adjacency_kernel.1 = (bf16[16,256,128]{2,1,0:T(8,128)(2,1)S(1)}, bf16[7,256,128]{2,1,0:T(8,128)(2,1)S(1)}, f32[256,128]{1,0:T(8,128)S(1)}, f32[16,128]{1,0:T(8,128)S(1)}) custom-call(s32[1]{0:T(128)S(6)} %copy.20.count_ref, s32[1,80]{1,0:T(1,128)} %dst_hbm.1, s32[1,80]{1,0:T(1,128)} %src_hbm.1, s32[80,128,128]{2,1,0:T(8,128)} %bitcast.1), custom_call_target="tpu_custom_call" | custom-call | tf_op jit(solution)/shard_map/adjacency_kernel/pallas_call | solution.py:274
  13.0 1.3 %collective-permute-start.1 = (bf16[7,256,128]{2,1,0:T(8,128)(2,1)S(1)}, bf16[7,256,128]{2,1,0:T(8,128)(2,1)}, u32[]{:S(2)}, u32[]{:S(2)}) collective-permute-start(bf16[7,256,128]{2,1,0:T(8,128)(2,1)S(1)} %get-tuple-element.36), channel_id=1, source_target_pairs={{0,16},{16,0},{1,17},{17,1},{2,18},{18,2},{3,19},{19,3},{4,20},{20... | collective-permute-start | bytes 1376264 | tf_op jit(solution)/shard_map/ppermute | solution.py:328
  14.3 1.4 %collective-permute-done.pair_flag_ref = f32[16,128]{1,0:T(8,128)S(1)} collective-permute-done((f32[16,128]{1,0:T(8,128)S(1)}, f32[16,128]{1,0:T(8,128)S(1)}, u32[]{:S(2)}, u32[]{:S(2)}) %collective-permute-start) | collective-permute-done | bytes 8224 | tf_op jit(solution)/shard_map/ppermute | solution.py:331
  15.8 10.5 %all-to-all-done.x_ref = bf16[16,256,128]{2,1,0:T(8,128)(2,1)S(1)} async-done(((bf16[16,256,128]{2,1,0:T(8,128)(2,1)}), bf16[16,256,128]{2,1,0:T(8,128)(2,1)S(1)}, u32[]{:S(2)}, u32[]{:S(2)}) %all-to-all-start) | async-done | bytes 1048608 | tf_op jit(solution)/shard_map/all_to_all | solution.py:306
  26.7 2.7 %collective-permute-start.2 = (bf16[272,128]{1,0:T(8,128)(2,1)S(1)}, bf16[272,128]{1,0:T(8,128)(2,1)S(1)}, u32[]{:S(2)}, u32[]{:S(2)}) collective-permute-start(bf16[272,128]{1,0:T(8,128)(2,1)S(1)} %get-tuple-element.39.y_ref), channel_id=1, source_target_pairs={{0,16},{16,0},{1,17},{17,1},{2,18},{18,2},{3,19},{19,3},{4,20},{20... | collective-permute-start | bytes 208904 | tf_op jit(solution)/shard_map/ppermute | solution.py:337
  29.4 0.9 collective-permute-done.2.y_pair_ref
  30.3 6.1 %collective-permute-start.4 = (bf16[2,272,128]{2,1,0:T(8,128)(2,1)S(1)}, bf16[2,272,128]{2,1,0:T(8,128)(2,1)S(1)}, u32[]{:S(2)}, u32[]{:S(2)}) collective-permute-start(bf16[2,272,128]{2,1,0:T(8,128)(2,1)S(1)} %join_kernel.1.pair_ref), channel_id=1, source_target_pairs={{0,64},{32,96},{64,128},{96,160},{128,192},{160,224},{192,0},{224,... | collective-permute-start | bytes 417800 | tf_op jit(solution)/shard_map/ppermute | solution.py:289
  36.4 0.7 collective-permute-start.3
  37.2 2.8 %collective-permute-done.4.pair_ref.two_ref = bf16[2,272,128]{2,1,0:T(8,128)(2,1)S(1)} collective-permute-done((bf16[2,272,128]{2,1,0:T(8,128)(2,1)S(1)}, bf16[2,272,128]{2,1,0:T(8,128)(2,1)S(1)}, u32[]{:S(2)}, u32[]{:S(2)}) %collective-permute-start.4) | collective-permute-done | bytes 139296 | tf_op jit(solution)/shard_map/ppermute | solution.py:289
  39.9 2.2 %collective-permute-start.5 = (bf16[2,272,128]{2,1,0:T(8,128)(2,1)S(1)}, bf16[2,272,128]{2,1,0:T(8,128)(2,1)S(1)}, u32[]{:S(2)}, u32[]{:S(2)}) collective-permute-start(bf16[2,272,128]{2,1,0:T(8,128)(2,1)S(1)} %collective-permute-done.4.pair_ref.two_ref), channel_id=1, source_target_pairs={{0,32},{32,64},{64,96},{96,128},{128,160},{160,192},{192,224},{224... | collective-permute-start | bytes 417800 | tf_op jit(solution)/shard_map/ppermute | solution.py:289
  42.1 1.9 %collective-permute-start.6 = (bf16[272,128]{1,0:T(8,128)(2,1)S(1)}, bf16[272,128]{1,0:T(8,128)(2,1)S(1)}, u32[]{:S(2)}, u32[]{:S(2)}) collective-permute-start(bf16[272,128]{1,0:T(8,128)(2,1)S(1)} %half_kernel.1), channel_id=1, source_target_pairs={{0,64},{32,96},{64,128},{96,160},{128,192},{160,224},{192,0},{224,... | collective-permute-start | bytes 208904 | tf_op jit(solution)/shard_map/ppermute | solution.py:289
  44.0 2.7 %collective-permute-done.6.far_ref = bf16[272,128]{1,0:T(8,128)(2,1)S(1)} collective-permute-done((bf16[272,128]{1,0:T(8,128)(2,1)S(1)}, bf16[272,128]{1,0:T(8,128)(2,1)S(1)}, u32[]{:S(2)}, u32[]{:S(2)}) %collective-permute-start.6) | collective-permute-done | bytes 69664 | tf_op jit(solution)/shard_map/ppermute | solution.py:289
  46.7 1.5 %aggregate_kernel.1 = (f32[256,128]{1,0:T(8,128)S(1)}, f32[16,128]{1,0:T(8,128)S(1)}, f32[264,128]{1,0:T(8,128)S(1)}) custom-call(f32[16,128]{1,0:T(8,128)S(1)} %get-tuple-element.35.flag_ref, f32[16,128]{1,0:T(8,128)S(1)} %get-tuple-element.37.flag_pair_ref, bf16[16,256,128]{2,1,0:T(8,128)(2,1)S(1)} %get-tuple-element.33.adj_ref, ...), custom_call_target="tpu_custom_call" | custom-call | tf_op jit(solution)/shard_map/aggregate_kernel/pallas_call | solution.py:274
  48.2 3.4 %collective-permute-start.7 = (f32[264,128]{1,0:T(8,128)S(1)}, f32[264,128]{1,0:T(8,128)S(1)}, u32[]{:S(2)}, u32[]{:S(2)}) collective-permute-start(f32[264,128]{1,0:T(8,128)S(1)} %get-tuple-element.42), channel_id=1, source_target_pairs={{0,16},{16,0},{1,17},{17,1},{2,18},{18,2},{3,19},{19,3},{4,20},{20... | collective-permute-start | bytes 405512 | tf_op jit(solution)/shard_map/ppermute | solution.py:346
  52.6 0.8 activation_kernel.1
  53.4 23.4 %all_to_all.15.came_ref = bf16[16,128,128]{2,1,0:T(8,128)(2,1)S(1)} all-to-all(bf16[16,128,128]{2,1,0:T(8,128)(2,1)S(1)} %get-tuple-element.44), channel_id=1, replica_groups=mesh['z'=8,'c'=2,'f'=16] {'z','c'}, dimensions={0} | all-to-all | bytes 1048576 | tf_op jit(solution)/shard_map/all_to_all | solution.py:353
  76.8 0.7 weight_grad_kernel.1
  77.7 1.3 %feature_grad_kernel.1.payload_ref = bf16[16,128,256]{2,1,0:T(8,128)(2,1)} custom-call(bf16[128,256]{1,0:T(8,128)(2,1)S(1)} %get-tuple-element.46.gt_ref, bf16[128,256]{1,0:T(8,128)(2,1)S(1)} %get-tuple-element.49.bt_ref, bf16[2048,128]{1,0:T(8,128)(2,1)S(1)} %copy-done, bf16[2048,128]{1,0:T(8,128)(2,1)S(1)} %copy-done.1), custom_call_target="tpu_custom_call" | custom-call | tf_op jit(solution)/shard_map/feature_grad_kernel/pallas_call | solution.py:274
  79.7 3.7 %all-to-all-start.2 = ((bf16[16,128,256]{2,1,0:T(8,128)(2,1)}), bf16[16,128,256]{2,1,0:T(8,128)(2,1)S(1)}, u32[]{:S(2)}, u32[]{:S(2)}) async-start(bf16[16,128,256]{2,1,0:T(8,128)(2,1)} %get-tuple-element.51), calls=%async_computation.2 | async-start | bytes 2097152 | tf_op jit(solution)/shard_map/all_to_all | solution.py:375
  83.3 1.0 %collective-permute-start.9 = (bf16[256,128]{1,0:T(8,128)(2,1)S(1)}, bf16[256,128]{1,0:T(8,128)(2,1)S(1)}, u32[]{:S(2)}, u32[]{:S(2)}) collective-permute-start(bf16[256,128]{1,0:T(8,128)(2,1)S(1)} %get-tuple-element.52), channel_id=1, source_target_pairs={{0,128},{32,160},{64,192},{96,224},{128,0},{160,32},{192,64},{224,... | collective-permute-start | bytes 196616 | tf_op jit(solution)/shard_map/ppermute | solution.py:377
  84.4 0.9 collective-permute-start.10
  85.3 3.5 %collective-permute-start.11 = (bf16[256,128]{1,0:T(8,128)(2,1)S(1)}, bf16[256,128]{1,0:T(8,128)(2,1)S(1)}, u32[]{:S(2)}, u32[]{:S(2)}) collective-permute-start(bf16[256,128]{1,0:T(8,128)(2,1)S(1)} %get-tuple-element.54), channel_id=1, source_target_pairs={{0,160},{32,192},{64,224},{96,0},{128,32},{160,64},{192,96},{224,1... | collective-permute-start | bytes 196616 | tf_op jit(solution)/shard_map/ppermute | solution.py:377
  88.9 1.4 %collective-permute-start.12 = (bf16[256,128]{1,0:T(8,128)(2,1)S(1)}, bf16[256,128]{1,0:T(8,128)(2,1)S(1)}, u32[]{:S(2)}, u32[]{:S(2)}) collective-permute-start(bf16[256,128]{1,0:T(8,128)(2,1)S(1)} %get-tuple-element.55), channel_id=1, source_target_pairs={{0,64},{32,96},{64,128},{96,160},{128,192},{160,224},{192,0},{224,... | collective-permute-start | bytes 196616 | tf_op jit(solution)/shard_map/ppermute | solution.py:377
  90.3 2.2 %collective-permute-start.13 = (bf16[256,128]{1,0:T(8,128)(2,1)S(1)}, bf16[256,128]{1,0:T(8,128)(2,1)S(1)}, u32[]{:S(2)}, u32[]{:S(2)}) collective-permute-start(bf16[256,128]{1,0:T(8,128)(2,1)S(1)} %get-tuple-element.56), channel_id=1, source_target_pairs={{0,192},{32,224},{64,0},{96,32},{128,64},{160,96},{192,128},{224,1... | collective-permute-start | bytes 196616 | tf_op jit(solution)/shard_map/ppermute | solution.py:377
  92.4 1.2 %collective-permute-start.14 = (bf16[256,128]{1,0:T(8,128)(2,1)S(1)}, bf16[256,128]{1,0:T(8,128)(2,1)S(1)}, u32[]{:S(2)}, u32[]{:S(2)}) collective-permute-start(bf16[256,128]{1,0:T(8,128)(2,1)S(1)} %get-tuple-element.57), channel_id=1, source_target_pairs={{0,32},{32,64},{64,96},{96,128},{128,160},{160,192},{192,224},{224... | collective-permute-start | bytes 196616 | tf_op jit(solution)/shard_map/ppermute | solution.py:377
  93.6 1.2 %collective-permute-done.10.refs_1_ = bf16[256,128]{1,0:T(8,128)(2,1)S(1)} collective-permute-done((bf16[256,128]{1,0:T(8,128)(2,1)S(1)}, bf16[256,128]{1,0:T(8,128)(2,1)S(1)}, u32[]{:S(2)}, u32[]{:S(2)}) %collective-permute-start.10) | collective-permute-done | bytes 65568 | tf_op jit(solution)/shard_map/ppermute | solution.py:377
  94.8 2.9 %collective-permute-start.15 = (bf16[256,128]{1,0:T(8,128)(2,1)S(1)}, bf16[256,128]{1,0:T(8,128)(2,1)S(1)}, u32[]{:S(2)}, u32[]{:S(2)}) collective-permute-start(bf16[256,128]{1,0:T(8,128)(2,1)S(1)} %get-tuple-element.58), channel_id=1, source_target_pairs={{0,224},{32,0},{64,32},{96,64},{128,96},{160,128},{192,160},{224,1... | collective-permute-start | bytes 196616 | tf_op jit(solution)/shard_map/ppermute | solution.py:377
  97.7 4.0 %all-to-all-done.2.parts_ref = bf16[16,128,256]{2,1,0:T(8,128)(2,1)S(1)} async-done(((bf16[16,128,256]{2,1,0:T(8,128)(2,1)}), bf16[16,128,256]{2,1,0:T(8,128)(2,1)S(1)}, u32[]{:S(2)}, u32[]{:S(2)}) %all-to-all-start.2) | async-done | bytes 1048608 | tf_op jit(solution)/shard_map/all_to_all | solution.py:375
  101.8 0.8 sum_kernel.1.done_ref
  102.7 0.8 weight_sum_kernel.1
  (24 shorter events, 2.4 us)
Async XLA Ops:
  0.6 25.6 %copy-start.1 = (bf16[2048,128]{1,0:T(8,128)(2,1)S(1)}, bf16[2048,128]{1,0:T(8,128)(2,1)}, u32[]{:S(2)}) copy-start(bf16[2048,128]{1,0:T(8,128)(2,1)} %wn_ref.1) | copy-start | bytes 1572868
  2.7 23.6 %all-to-all-start = ((bf16[16,256,128]{2,1,0:T(8,128)(2,1)}), bf16[16,256,128]{2,1,0:T(8,128)(2,1)S(1)}, u32[]{:S(2)}, u32[]{:S(2)}) async-start(bf16[16,256,128]{2,1,0:T(8,128)(2,1)} %spread_kernel.1), calls=%async_computation | async-start | bytes 2097152 | tf_op jit(solution)/shard_map/all_to_all | solution.py:306
  10.3 41.3 %copy-start = (bf16[2048,128]{1,0:T(8,128)(2,1)S(1)}, bf16[2048,128]{1,0:T(8,128)(2,1)}, u32[]{:S(2)}) copy-start(bf16[2048,128]{1,0:T(8,128)(2,1)} %ws_ref.1) | copy-start | bytes 1572868
  11.0 41.6 %copy-start.2 = (bf16[256,128]{1,0:T(8,128)(2,1)S(1)}, bf16[256,128]{1,0:T(8,128)(2,1)}, u32[]{:S(2)}) copy-start(bf16[256,128]{1,0:T(8,128)(2,1)} %og_ref.1) | copy-start | bytes 196612
  13.0 2.8 %collective-permute-start.1 = (bf16[7,256,128]{2,1,0:T(8,128)(2,1)S(1)}, bf16[7,256,128]{2,1,0:T(8,128)(2,1)}, u32[]{:S(2)}, u32[]{:S(2)}) collective-permute-start(bf16[7,256,128]{2,1,0:T(8,128)(2,1)S(1)} %get-tuple-element.36), channel_id=1, source_target_pairs={{0,16},{16,0},{1,17},{17,1},{2,18},{18,2},{3,19},{19,3},{4,20},{20... | collective-permute-start | bytes 1376264 | tf_op jit(solution)/shard_map/ppermute | solution.py:328
  14.2 1.5 %collective-permute-start = (f32[16,128]{1,0:T(8,128)S(1)}, f32[16,128]{1,0:T(8,128)S(1)}, u32[]{:S(2)}, u32[]{:S(2)}) collective-permute-start(f32[16,128]{1,0:T(8,128)S(1)} %get-tuple-element.35.flag_ref), channel_id=1, source_target_pairs={{0,16},{16,0},{1,17},{17,1},{2,18},{18,2},{3,19},{19,3},{4,20},{20... | collective-permute-start | bytes 24584 | tf_op jit(solution)/shard_map/ppermute | solution.py:331
  26.7 3.6 %collective-permute-start.2 = (bf16[272,128]{1,0:T(8,128)(2,1)S(1)}, bf16[272,128]{1,0:T(8,128)(2,1)S(1)}, u32[]{:S(2)}, u32[]{:S(2)}) collective-permute-start(bf16[272,128]{1,0:T(8,128)(2,1)S(1)} %get-tuple-element.39.y_ref), channel_id=1, source_target_pairs={{0,16},{16,0},{1,17},{17,1},{2,18},{18,2},{3,19},{19,3},{4,20},{20... | collective-permute-start | bytes 208904 | tf_op jit(solution)/shard_map/ppermute | solution.py:337
  30.3 9.6 %collective-permute-start.4 = (bf16[2,272,128]{2,1,0:T(8,128)(2,1)S(1)}, bf16[2,272,128]{2,1,0:T(8,128)(2,1)S(1)}, u32[]{:S(2)}, u32[]{:S(2)}) collective-permute-start(bf16[2,272,128]{2,1,0:T(8,128)(2,1)S(1)} %join_kernel.1.pair_ref), channel_id=1, source_target_pairs={{0,64},{32,96},{64,128},{96,160},{128,192},{160,224},{192,0},{224,... | collective-permute-start | bytes 417800 | tf_op jit(solution)/shard_map/ppermute | solution.py:289
  36.4 7.6 %collective-permute-start.3 = (bf16[2,272,128]{2,1,0:T(8,128)(2,1)S(1)}, bf16[2,272,128]{2,1,0:T(8,128)(2,1)S(1)}, u32[]{:S(2)}, u32[]{:S(2)}) collective-permute-start(bf16[2,272,128]{2,1,0:T(8,128)(2,1)S(1)} %join_kernel.1.pair_ref), channel_id=1, source_target_pairs={{0,32},{32,64},{64,96},{96,128},{128,160},{160,192},{192,224},{224... | collective-permute-start | bytes 417800 | tf_op jit(solution)/shard_map/ppermute | solution.py:289
  39.9 6.8 %collective-permute-start.5 = (bf16[2,272,128]{2,1,0:T(8,128)(2,1)S(1)}, bf16[2,272,128]{2,1,0:T(8,128)(2,1)S(1)}, u32[]{:S(2)}, u32[]{:S(2)}) collective-permute-start(bf16[2,272,128]{2,1,0:T(8,128)(2,1)S(1)} %collective-permute-done.4.pair_ref.two_ref), channel_id=1, source_target_pairs={{0,32},{32,64},{64,96},{96,128},{128,160},{160,192},{192,224},{224... | collective-permute-start | bytes 417800 | tf_op jit(solution)/shard_map/ppermute | solution.py:289
  42.1 4.6 %collective-permute-start.6 = (bf16[272,128]{1,0:T(8,128)(2,1)S(1)}, bf16[272,128]{1,0:T(8,128)(2,1)S(1)}, u32[]{:S(2)}, u32[]{:S(2)}) collective-permute-start(bf16[272,128]{1,0:T(8,128)(2,1)S(1)} %half_kernel.1), channel_id=1, source_target_pairs={{0,64},{32,96},{64,128},{96,160},{128,192},{160,224},{192,0},{224,... | collective-permute-start | bytes 208904 | tf_op jit(solution)/shard_map/ppermute | solution.py:289
  48.2 4.4 %collective-permute-start.7 = (f32[264,128]{1,0:T(8,128)S(1)}, f32[264,128]{1,0:T(8,128)S(1)}, u32[]{:S(2)}, u32[]{:S(2)}) collective-permute-start(f32[264,128]{1,0:T(8,128)S(1)} %get-tuple-element.42), channel_id=1, source_target_pairs={{0,16},{16,0},{1,17},{17,1},{2,18},{18,2},{3,19},{19,3},{4,20},{20... | collective-permute-start | bytes 405512 | tf_op jit(solution)/shard_map/ppermute | solution.py:346
  77.6 2.0 %collective-permute-start.8 = (bf16[8,256,128]{2,1,0:T(8,128)(2,1)S(1)}, bf16[8,256,128]{2,1,0:T(8,128)(2,1)S(1)}, u32[]{:S(2)}, u32[]{:S(2)}) collective-permute-start(bf16[8,256,128]{2,1,0:T(8,128)(2,1)S(1)} %get-tuple-element.48), channel_id=1, source_target_pairs={{0,16},{16,0},{1,17},{17,1},{2,18},{18,2},{3,19},{19,3},{4,20},{20... | collective-permute-start | bytes 1572872 | tf_op jit(solution)/shard_map/ppermute | solution.py:359
  79.7 22.1 %all-to-all-start.2 = ((bf16[16,128,256]{2,1,0:T(8,128)(2,1)}), bf16[16,128,256]{2,1,0:T(8,128)(2,1)S(1)}, u32[]{:S(2)}, u32[]{:S(2)}) async-start(bf16[16,128,256]{2,1,0:T(8,128)(2,1)} %get-tuple-element.51), calls=%async_computation.2 | async-start | bytes 2097152 | tf_op jit(solution)/shard_map/all_to_all | solution.py:375
  83.3 9.1 %collective-permute-start.9 = (bf16[256,128]{1,0:T(8,128)(2,1)S(1)}, bf16[256,128]{1,0:T(8,128)(2,1)S(1)}, u32[]{:S(2)}, u32[]{:S(2)}) collective-permute-start(bf16[256,128]{1,0:T(8,128)(2,1)S(1)} %get-tuple-element.52), channel_id=1, source_target_pairs={{0,128},{32,160},{64,192},{96,224},{128,0},{160,32},{192,64},{224,... | collective-permute-start | bytes 196616 | tf_op jit(solution)/shard_map/ppermute | solution.py:377
  84.4 10.5 %collective-permute-start.10 = (bf16[256,128]{1,0:T(8,128)(2,1)S(1)}, bf16[256,128]{1,0:T(8,128)(2,1)S(1)}, u32[]{:S(2)}, u32[]{:S(2)}) collective-permute-start(bf16[256,128]{1,0:T(8,128)(2,1)S(1)} %get-tuple-element.53), channel_id=1, source_target_pairs={{0,96},{32,128},{64,160},{96,192},{128,224},{160,0},{192,32},{224,... | collective-permute-start | bytes 196616 | tf_op jit(solution)/shard_map/ppermute | solution.py:377
  85.3 17.3 %collective-permute-start.11 = (bf16[256,128]{1,0:T(8,128)(2,1)S(1)}, bf16[256,128]{1,0:T(8,128)(2,1)S(1)}, u32[]{:S(2)}, u32[]{:S(2)}) collective-permute-start(bf16[256,128]{1,0:T(8,128)(2,1)S(1)} %get-tuple-element.54), channel_id=1, source_target_pairs={{0,160},{32,192},{64,224},{96,0},{128,32},{160,64},{192,96},{224,1... | collective-permute-start | bytes 196616 | tf_op jit(solution)/shard_map/ppermute | solution.py:377
  88.9 13.8 %collective-permute-start.12 = (bf16[256,128]{1,0:T(8,128)(2,1)S(1)}, bf16[256,128]{1,0:T(8,128)(2,1)S(1)}, u32[]{:S(2)}, u32[]{:S(2)}) collective-permute-start(bf16[256,128]{1,0:T(8,128)(2,1)S(1)} %get-tuple-element.55), channel_id=1, source_target_pairs={{0,64},{32,96},{64,128},{96,160},{128,192},{160,224},{192,0},{224,... | collective-permute-start | bytes 196616 | tf_op jit(solution)/shard_map/ppermute | solution.py:377
  90.3 12.3 %collective-permute-start.13 = (bf16[256,128]{1,0:T(8,128)(2,1)S(1)}, bf16[256,128]{1,0:T(8,128)(2,1)S(1)}, u32[]{:S(2)}, u32[]{:S(2)}) collective-permute-start(bf16[256,128]{1,0:T(8,128)(2,1)S(1)} %get-tuple-element.56), channel_id=1, source_target_pairs={{0,192},{32,224},{64,0},{96,32},{128,64},{160,96},{192,128},{224,1... | collective-permute-start | bytes 196616 | tf_op jit(solution)/shard_map/ppermute | solution.py:377
  92.4 10.2 %collective-permute-start.14 = (bf16[256,128]{1,0:T(8,128)(2,1)S(1)}, bf16[256,128]{1,0:T(8,128)(2,1)S(1)}, u32[]{:S(2)}, u32[]{:S(2)}) collective-permute-start(bf16[256,128]{1,0:T(8,128)(2,1)S(1)} %get-tuple-element.57), channel_id=1, source_target_pairs={{0,32},{32,64},{64,96},{96,128},{128,160},{160,192},{192,224},{224... | collective-permute-start | bytes 196616 | tf_op jit(solution)/shard_map/ppermute | solution.py:377
  94.8 7.8 %collective-permute-start.15 = (bf16[256,128]{1,0:T(8,128)(2,1)S(1)}, bf16[256,128]{1,0:T(8,128)(2,1)S(1)}, u32[]{:S(2)}, u32[]{:S(2)}) collective-permute-start(bf16[256,128]{1,0:T(8,128)(2,1)S(1)} %get-tuple-element.58), channel_id=1, source_target_pairs={{0,224},{32,0},{64,32},{96,64},{128,96},{160,128},{192,160},{224,1... | collective-permute-start | bytes 196616 | tf_op jit(solution)/shard_map/ppermute | solution.py:377

commit v14 on v13

--- a/solution.py
+++ b/solution.py
@@ -22,8 +22,15 @@
     return jnp.dot(a, b, preferred_element_type=F32)
 
 
-def far_first(chips):
-    return tuple(sorted(range(1, chips), key=lambda step: abs(step - chips // 2)))
+def owners(here, core, chips):
+    way = 1 - 2 * core
+
+    def chip(step):
+        return lax.rem(here + step + chips, chips)
+
+    far = 2 * chip(chips // 2) + core
+    three, two, one = (2 * chip(step * way) for step in (3, 2, 1))
+    return [far, three, three + 1, two, two + 1, one, one + 1, 2 * here + core]
 
 
 def sources(here, core, chips):
@@ -217,10 +224,9 @@
     both = halves(jnp.concatenate([low, high], axis=1))
     bt_ref[...] = both[0:T]
     left = jnp.concatenate([gt_ref[...], both], axis=0)
-    for slot, step in enumerate(far_first(chips) + (0,)):
-        chip = lax.rem(here + step, chips)
-        pair = jnp.concatenate([x_ref[2 * chip + core], x_ref[2 * chip + 1 - core]], axis=1)
-        total = dot(left, pair)
+    slots = zip(owners(here, core, chips), owners(here, 1 - core, chips))
+    for slot, (ours, theirs) in enumerate(slots):
+        total = dot(left, jnp.concatenate([x_ref[ours], x_ref[theirs]], axis=1))
         kept, sent = total[:, 0:T], total[:, T:]
         keep_ref[slot, 0:T] = kept[0:T]
         keep_ref[slot, T:] = kept[T : 2 * T] + kept[2 * T :]
@@ -241,16 +247,33 @@
         copy.wait()
 
 
-def pair_kernel(keep_ref, came_ref, payload_ref, *pay_refs):
-    for slot, pay_ref in enumerate(pay_refs[:-1]):
-        pay_ref[...] = (keep_ref[slot] + came_ref[slot].astype(F32)).astype(pay_ref.dtype)
-
-
-def weight_sum_kernel(own_ref, done_ref, *refs):
-    parts, (self_ref, neigh_ref, same_ref) = refs[:-3], refs[-3:]
-    total = own_ref[...]
-    for part in parts:
-        total = total + part[...].astype(F32)
+def pair_kernel(keep_ref, came_ref, payload_ref, far_ref, three_ref, one_ref, two_ref, own_ref, same_ref):
+    def pair(slot):
+        return keep_ref[slot] + came_ref[slot].astype(F32)
+
+    far_ref[...] = pair(0).astype(BF16)
+    for place in range(2):
+        three_ref[place] = pair(1 + place).astype(BF16)
+        two_ref[place] = pair(3 + place)
+        one_ref[place] = pair(5 + place).astype(BF16)
+    own_ref[...] = pair(7)
+
+
+def relay_kernel(two_ref, three_ref, far_ref, out_ref):
+    core = lax.axis_index("c")
+    far = far_ref[...].astype(F32)
+    out_ref[core] = (two_ref[core] + three_ref[core].astype(F32) + far).astype(BF16)
+    out_ref[1 - core] = (two_ref[1 - core] + three_ref[1 - core].astype(F32)).astype(BF16)
+
+
+def fold_kernel(own_ref, two_ref, one_ref, mine_ref, theirs_ref):
+    core = lax.axis_index("c")
+    theirs_ref[...] = two_ref[1 - core].astype(F32) + one_ref[1 - core].astype(F32)
+    mine_ref[...] = own_ref[...] + two_ref[core].astype(F32) + one_ref[core].astype(F32)
+
+
+def last_kernel(mine_ref, came_ref, done_ref, self_ref, neigh_ref, same_ref):
+    total = mine_ref[...] + came_ref[...]
     self_ref[...] = total[0:T].T
     neigh_ref[...] = total[T:].T
 
@@ -364,27 +387,36 @@
         out_specs=[HBM],
         scratch=[pltpu.VMEM((parts, T, rows), BF16), pltpu.SemaphoreType.DMA((parts,))],
     )
-    *w_pay, own, p_pay = call(
+    block = (2 * T, T)
+    far, three, one, two, own, p_pay = call(
         pair_kernel,
         (keep, came, p_pay),
-        [((2 * T, T), BF16)] * (chips - 1) + [((2 * T, T), F32), (p_pay.shape, BF16)],
+        [
+            (block, BF16),
+            ((2,) + block, BF16),
+            ((2,) + block, BF16),
+            ((2,) + block, F32),
+            (block, F32),
+            (p_pay.shape, BF16),
+        ],
         in_specs=[VMEM, VMEM, HBM],
-        out_specs=[VMEM] * chips + [HBM],
-        aliases={2: chips},
+        out_specs=[VMEM] * 5 + [HBM],
+        aliases={2: 5},
     )
     p_all = lax.all_to_all(p_pay, "f", 0, 0, tiled=True)
-    w_came = [
-        lax.ppermute(block, "z", [(chip, (chip + step) % chips) for chip in range(chips)])
-        for step, block in zip(far_first(chips), w_pay)
-    ]
+    (two,) = call(
+        relay_kernel, (two, along(three, 1, chips), along(far, 2, chips)), [((2,) + block, BF16)]
+    )
+    two, one = along(two, 2, chips), along(one, 1, chips)
+    mine, theirs = call(fold_kernel, (own, two, one), [(block, F32)] * 2)
     (grad_features,) = call(sum_kernel, (p_all,), [((rows, T), BF16)])
     grad_self, grad_neigh, grad_features = call(
-        weight_sum_kernel,
-        (own, grad_features, *w_came),
+        last_kernel,
+        (mine, lax.ppermute(theirs, "c", swap), grad_features),
         [((T, T), F32), ((T, T), F32), ((rows, T), BF16)],
-        in_specs=[VMEM, ANY] + [VMEM] * (chips - 1),
+        in_specs=[VMEM] * 2 + [ANY],
         out_specs=[VMEM, VMEM, ANY],
-        aliases={1: 2},
+        aliases={2: 2},
     )
     return output, grad_features, grad_self, grad_neigh
 

time: 104 us -> 104 us (level)
  starting transfers between devices: 42.9 us -> 36.3 us
  waiting for transfers between devices: 24.7 us -> 30.3 us
    ppermute x7 -> x1, starting transfers between devices: 13.2 us -> 3.96 us  [per_device(): lax.ppermute(theirs, 'c', swap)]
    ppermute x4 -> x8, waiting for transfers between devices: 5.44 us -> 13.5 us  [along(): return lax.ppermute(value, ('z', 'c'), pairs)]
    ppermute x4 -> x8, starting transfers between devices: 10.9 us -> 14.7 us  [along(): return lax.ppermute(value, ('z', 'c'), pairs)]
    all_to_all x1, waiting for transfers between devices: 4.04 us -> 2.55 us  [per_device(): p_all = lax.all_to_all(p_pay, 'f', 0, 0, tiled=True)]
    ppermute x7 -> x1, waiting for transfers between devices: 1.22 us -> 0.01 us  [per_device(): lax.ppermute(theirs, 'c', swap)]
    pallas_call x13 -> x15, Pallas kernels: 10.9 us -> 11.2 us  [call(): pl.pallas_call(kernel, out_shape=shapes, in_specs=in_specs or [VMEM] * le...]
  transfers between devices with their start and end apart: 18 -> 16, of which waited for: 10 -> 12; matrix products, arithmetic and copies ran while one was open for 0% -> 0% of each run, Pallas kernels for 4% -> 5%
where the time goes in v14:
time: 104 us; the launch traced here: 103 us
  starting transfers between devices  36.3 us (35%)
  waiting for transfers between devices  30.3 us (29%)
  blocking collectives  24.2 us (23%)
  Pallas kernels  11.2 us (11%)
  between operations  1.47 us (1%)
    all_to_all x1, blocking collectives, per_device(): c_all = lax.all_to_all(c_pay, ('z', 'c'), 0, 0, tiled=True)  24.2 us
    ppermute x8, starting transfers between devices, along(): return lax.ppermute(value, ('z', 'c'), pairs)  14.7 us
    ppermute x8, waiting for transfers between devices, along(): return lax.ppermute(value, ('z', 'c'), pairs)  13.5 us
    pallas_call x15, Pallas kernels, call(): pl.pallas_call(kernel, out_shape=shapes, in_specs=in_specs or [VMEM] * le...  11.2 us
    all_to_all x1, waiting for transfers between devices, per_device(): x_all = lax.all_to_all(x_pay, 'f', 0, 0, tiled=True)  10.8 us
    all_to_all x1, starting transfers between devices, per_device(): x_all = lax.all_to_all(x_pay, 'f', 0, 0, tiled=True)  7.6 us
    ppermute x1, starting transfers between devices, per_device(): lax.ppermute(theirs, 'c', swap)  3.96 us
    all_to_all x1, starting transfers between devices, per_device(): p_all = lax.all_to_all(p_pay, 'f', 0, 0, tiled=True)  3.66 us
  transfers between devices with their start and end apart: 16, of which 12 were waited for; matrix products, arithmetic and copies ran while one was open for 0% of the time, Pallas kernels for 5%

profile of v14, /device:TPU:1, one launch (start us, length us, event | category | flops | bytes accessed | tf_op | source)
XLA Modules:
  0.0 103.4 jit_solution(18397774456897772363)
XLA Ops:
  0.6 2.1 %spread_kernel.1 = bf16[16,256,128]{2,1,0:T(8,128)(2,1)} custom-call(bf16[256,128]{1,0:T(8,128)(2,1)} %x_hbm.1), custom_call_target="tpu_custom_call" | custom-call | tf_op jit(solution)/shard_map/spread_kernel/pallas_call | solution.py:297
  2.7 7.6 %all-to-all-start = ((bf16[16,256,128]{2,1,0:T(8,128)(2,1)}), bf16[16,256,128]{2,1,0:T(8,128)(2,1)S(1)}, u32[]{:S(2)}, u32[]{:S(2)}) async-start(bf16[16,256,128]{2,1,0:T(8,128)(2,1)} %spread_kernel.1), calls=%async_computation | async-start | bytes 2097152 | tf_op jit(solution)/shard_map/all_to_all | solution.py:329
  11.0 2.2 %adjacency_kernel.1 = (bf16[16,256,128]{2,1,0:T(8,128)(2,1)S(1)}, bf16[7,256,128]{2,1,0:T(8,128)(2,1)S(1)}, f32[256,128]{1,0:T(8,128)S(1)}, f32[16,128]{1,0:T(8,128)S(1)}) custom-call(s32[1]{0:T(128)S(6)} %copy.20.count_ref, s32[1,80]{1,0:T(1,128)} %dst_hbm.1, s32[1,80]{1,0:T(1,128)} %src_hbm.1, s32[80,128,128]{2,1,0:T(8,128)} %bitcast.1), custom_call_target="tpu_custom_call" | custom-call | tf_op jit(solution)/shard_map/adjacency_kernel/pallas_call | solution.py:297
  13.2 0.8 collective-permute-start.1
  14.1 1.4 %collective-permute-done.pair_flag_ref = f32[16,128]{1,0:T(8,128)S(1)} collective-permute-done((f32[16,128]{1,0:T(8,128)S(1)}, f32[16,128]{1,0:T(8,128)S(1)}, u32[]{:S(2)}, u32[]{:S(2)}) %collective-permute-start) | collective-permute-done | bytes 8224 | tf_op jit(solution)/shard_map/ppermute | solution.py:354
  15.5 10.8 %all-to-all-done.x_ref = bf16[16,256,128]{2,1,0:T(8,128)(2,1)S(1)} async-done(((bf16[16,256,128]{2,1,0:T(8,128)(2,1)}), bf16[16,256,128]{2,1,0:T(8,128)(2,1)S(1)}, u32[]{:S(2)}, u32[]{:S(2)}) %all-to-all-start) | async-done | bytes 1048608 | tf_op jit(solution)/shard_map/all_to_all | solution.py:329
  26.7 2.7 %collective-permute-start.2 = (bf16[272,128]{1,0:T(8,128)(2,1)S(1)}, bf16[272,128]{1,0:T(8,128)(2,1)S(1)}, u32[]{:S(2)}, u32[]{:S(2)}) collective-permute-start(bf16[272,128]{1,0:T(8,128)(2,1)S(1)} %get-tuple-element.38.y_ref), channel_id=1, source_target_pairs={{0,16},{16,0},{1,17},{17,1},{2,18},{18,2},{3,19},{19,3},{4,20},{20... | collective-permute-start | bytes 208904 | tf_op jit(solution)/shard_map/ppermute | solution.py:360
  29.4 0.9 collective-permute-done.2.y_pair_ref
  30.4 6.1 %collective-permute-start.4 = (bf16[2,272,128]{2,1,0:T(8,128)(2,1)S(1)}, bf16[2,272,128]{2,1,0:T(8,128)(2,1)S(1)}, u32[]{:S(2)}, u32[]{:S(2)}) collective-permute-start(bf16[2,272,128]{2,1,0:T(8,128)(2,1)S(1)} %join_kernel.1.pair_ref), channel_id=1, source_target_pairs={{0,64},{32,96},{64,128},{96,160},{128,192},{160,224},{192,0},{224,... | collective-permute-start | bytes 417800 | tf_op jit(solution)/shard_map/ppermute | solution.py:312
  36.5 0.7 collective-permute-start.3
  37.2 2.8 %collective-permute-done.4.pair_ref.two_ref = bf16[2,272,128]{2,1,0:T(8,128)(2,1)S(1)} collective-permute-done((bf16[2,272,128]{2,1,0:T(8,128)(2,1)S(1)}, bf16[2,272,128]{2,1,0:T(8,128)(2,1)S(1)}, u32[]{:S(2)}, u32[]{:S(2)}) %collective-permute-start.4) | collective-permute-done | bytes 139296 | tf_op jit(solution)/shard_map/ppermute | solution.py:312
  39.9 2.2 %collective-permute-start.5 = (bf16[2,272,128]{2,1,0:T(8,128)(2,1)S(1)}, bf16[2,272,128]{2,1,0:T(8,128)(2,1)S(1)}, u32[]{:S(2)}, u32[]{:S(2)}) collective-permute-start(bf16[2,272,128]{2,1,0:T(8,128)(2,1)S(1)} %collective-permute-done.4.pair_ref.two_ref), channel_id=1, source_target_pairs={{0,32},{32,64},{64,96},{96,128},{128,160},{160,192},{192,224},{224... | collective-permute-start | bytes 417800 | tf_op jit(solution)/shard_map/ppermute | solution.py:312
  42.1 1.9 %collective-permute-start.6 = (bf16[272,128]{1,0:T(8,128)(2,1)S(1)}, bf16[272,128]{1,0:T(8,128)(2,1)S(1)}, u32[]{:S(2)}, u32[]{:S(2)}) collective-permute-start(bf16[272,128]{1,0:T(8,128)(2,1)S(1)} %half_kernel.1), channel_id=1, source_target_pairs={{0,64},{32,96},{64,128},{96,160},{128,192},{160,224},{192,0},{224,... | collective-permute-start | bytes 208904 | tf_op jit(solution)/shard_map/ppermute | solution.py:312
  44.1 2.7 %collective-permute-done.6.far_ref = bf16[272,128]{1,0:T(8,128)(2,1)S(1)} collective-permute-done((bf16[272,128]{1,0:T(8,128)(2,1)S(1)}, bf16[272,128]{1,0:T(8,128)(2,1)S(1)}, u32[]{:S(2)}, u32[]{:S(2)}) %collective-permute-start.6) | collective-permute-done | bytes 69664 | tf_op jit(solution)/shard_map/ppermute | solution.py:312
  46.7 1.5 %aggregate_kernel.1 = (f32[256,128]{1,0:T(8,128)S(1)}, f32[16,128]{1,0:T(8,128)S(1)}, f32[264,128]{1,0:T(8,128)S(1)}) custom-call(f32[16,128]{1,0:T(8,128)S(1)} %get-tuple-element.34.flag_ref, f32[16,128]{1,0:T(8,128)S(1)} %get-tuple-element.36.flag_pair_ref, bf16[16,256,128]{2,1,0:T(8,128)(2,1)S(1)} %get-tuple-element.32.adj_ref, ...), custom_call_target="tpu_custom_call" | custom-call | tf_op jit(solution)/shard_map/aggregate_kernel/pallas_call | solution.py:297
  48.2 2.7 %collective-permute-start.7 = (f32[264,128]{1,0:T(8,128)S(1)}, f32[264,128]{1,0:T(8,128)S(1)}, u32[]{:S(2)}, u32[]{:S(2)}) collective-permute-start(f32[264,128]{1,0:T(8,128)S(1)} %get-tuple-element.41), channel_id=1, source_target_pairs={{0,16},{16,0},{1,17},{17,1},{2,18},{18,2},{3,19},{19,3},{4,20},{20... | collective-permute-start | bytes 405512 | tf_op jit(solution)/shard_map/ppermute | solution.py:369
  51.3 0.6 collective-permute-done.7.came_ref
  51.9 0.8 activation_kernel.1
  52.7 24.2 %all_to_all.15.came_ref = bf16[16,128,128]{2,1,0:T(8,128)(2,1)S(1)} all-to-all(bf16[16,128,128]{2,1,0:T(8,128)(2,1)S(1)} %get-tuple-element.43), channel_id=1, replica_groups=mesh['z'=8,'c'=2,'f'=16] {'z','c'}, dimensions={0} | all-to-all | bytes 1048576 | tf_op jit(solution)/shard_map/all_to_all | solution.py:376
  76.9 0.7 weight_grad_kernel.1
  77.7 1.4 %feature_grad_kernel.1.payload_ref = bf16[16,128,256]{2,1,0:T(8,128)(2,1)} custom-call(bf16[128,256]{1,0:T(8,128)(2,1)S(1)} %get-tuple-element.45.gt_ref, bf16[128,256]{1,0:T(8,128)(2,1)S(1)} %get-tuple-element.48.bt_ref, bf16[2048,128]{1,0:T(8,128)(2,1)S(1)} %copy-done, bf16[2048,128]{1,0:T(8,128)(2,1)S(1)} %copy-done.1), custom_call_target="tpu_custom_call" | custom-call | tf_op jit(solution)/shard_map/feature_grad_kernel/pallas_call | solution.py:297
  79.1 0.5 collective-permute-done.8.came_ref
  79.7 3.7 %all-to-all-start.2 = ((bf16[16,128,256]{2,1,0:T(8,128)(2,1)}), bf16[16,128,256]{2,1,0:T(8,128)(2,1)S(1)}, u32[]{:S(2)}, u32[]{:S(2)}) async-start(bf16[16,128,256]{2,1,0:T(8,128)(2,1)} %get-tuple-element.56), calls=%async_computation.2 | async-start | bytes 2097152 | tf_op jit(solution)/shard_map/all_to_all | solution.py:406
  83.4 1.2 %collective-permute-start.10 = (bf16[256,128]{1,0:T(8,128)(2,1)S(1)}, bf16[256,128]{1,0:T(8,128)(2,1)S(1)}, u32[]{:S(2)}, u32[]{:S(2)}) collective-permute-start(bf16[256,128]{1,0:T(8,128)(2,1)S(1)} %get-tuple-element.52), channel_id=1, source_target_pairs={{0,64},{32,96},{64,128},{96,160},{128,192},{160,224},{192,0},{224,... | collective-permute-start | bytes 196616 | tf_op jit(solution)/shard_map/ppermute | solution.py:312
  85.0 2.7 %collective-permute-done.10.far_ref = bf16[256,128]{1,0:T(8,128)(2,1)S(1)} collective-permute-done((bf16[256,128]{1,0:T(8,128)(2,1)S(1)}, bf16[256,128]{1,0:T(8,128)(2,1)S(1)}, u32[]{:S(2)}, u32[]{:S(2)}) %collective-permute-start.10) | collective-permute-done | bytes 65568 | tf_op jit(solution)/shard_map/ppermute | solution.py:312
  87.6 0.6 collective-permute-done.9.three_ref
  88.3 2.2 %collective-permute-start.11 = (bf16[2,256,128]{2,1,0:T(8,128)(2,1)S(1)}, bf16[2,256,128]{2,1,0:T(8,128)(2,1)S(1)}, u32[]{:S(2)}, u32[]{:S(2)}) collective-permute-start(bf16[2,256,128]{2,1,0:T(8,128)(2,1)S(1)} %relay_kernel.1), channel_id=1, source_target_pairs={{0,64},{32,96},{64,128},{96,160},{128,192},{160,224},{192,0},{224,... | collective-permute-start | bytes 393224 | tf_op jit(solution)/shard_map/ppermute | solution.py:312
  90.5 4.8 %collective-permute-done.11.two_ref = bf16[2,256,128]{2,1,0:T(8,128)(2,1)S(1)} collective-permute-done((bf16[2,256,128]{2,1,0:T(8,128)(2,1)S(1)}, bf16[2,256,128]{2,1,0:T(8,128)(2,1)S(1)}, u32[]{:S(2)}, u32[]{:S(2)}) %collective-permute-start.11) | collective-permute-done | bytes 131104 | tf_op jit(solution)/shard_map/ppermute | solution.py:312
  95.3 4.0 %collective-permute-start.13 = (f32[256,128]{1,0:T(8,128)S(1)}, f32[256,128]{1,0:T(8,128)S(1)}, u32[]{:S(2)}, u32[]{:S(2)}) collective-permute-start(f32[256,128]{1,0:T(8,128)S(1)} %get-tuple-element.55), channel_id=1, source_target_pairs={{0,16},{16,0},{1,17},{17,1},{2,18},{18,2},{3,19},{19,3},{4,20},{20... | collective-permute-start | bytes 393224 | tf_op jit(solution)/shard_map/ppermute | solution.py:415
  99.2 2.5 %all-to-all-done.2.parts_ref = bf16[16,128,256]{2,1,0:T(8,128)(2,1)S(1)} async-done(((bf16[16,128,256]{2,1,0:T(8,128)(2,1)}), bf16[16,128,256]{2,1,0:T(8,128)(2,1)S(1)}, u32[]{:S(2)}, u32[]{:S(2)}) %all-to-all-start.2) | async-done | bytes 1048608 | tf_op jit(solution)/shard_map/all_to_all | solution.py:406
  101.8 0.8 sum_kernel.1.done_ref
  102.6 0.8 last_kernel.1
  (22 shorter events, 1.7 us)
Async XLA Ops:
  0.6 25.7 %copy-start.1 = (bf16[2048,128]{1,0:T(8,128)(2,1)S(1)}, bf16[2048,128]{1,0:T(8,128)(2,1)}, u32[]{:S(2)}) copy-start(bf16[2048,128]{1,0:T(8,128)(2,1)} %wn_ref.1) | copy-start | bytes 1572868
  2.7 23.6 %all-to-all-start = ((bf16[16,256,128]{2,1,0:T(8,128)(2,1)}), bf16[16,256,128]{2,1,0:T(8,128)(2,1)S(1)}, u32[]{:S(2)}, u32[]{:S(2)}) async-start(bf16[16,256,128]{2,1,0:T(8,128)(2,1)} %spread_kernel.1), calls=%async_computation | async-start | bytes 2097152 | tf_op jit(solution)/shard_map/all_to_all | solution.py:329
  10.3 40.6 %copy-start = (bf16[2048,128]{1,0:T(8,128)(2,1)S(1)}, bf16[2048,128]{1,0:T(8,128)(2,1)}, u32[]{:S(2)}) copy-start(bf16[2048,128]{1,0:T(8,128)(2,1)} %ws_ref.1) | copy-start | bytes 1572868
  11.0 40.9 %copy-start.2 = (bf16[256,128]{1,0:T(8,128)(2,1)S(1)}, bf16[256,128]{1,0:T(8,128)(2,1)}, u32[]{:S(2)}) copy-start(bf16[256,128]{1,0:T(8,128)(2,1)} %og_ref.1) | copy-start | bytes 196612
  13.2 2.3 %collective-permute-start.1 = (bf16[7,256,128]{2,1,0:T(8,128)(2,1)S(1)}, bf16[7,256,128]{2,1,0:T(8,128)(2,1)}, u32[]{:S(2)}, u32[]{:S(2)}) collective-permute-start(bf16[7,256,128]{2,1,0:T(8,128)(2,1)S(1)} %get-tuple-element.35), channel_id=1, source_target_pairs={{0,16},{16,0},{1,17},{17,1},{2,18},{18,2},{3,19},{19,3},{4,20},{20... | collective-permute-start | bytes 1376264 | tf_op jit(solution)/shard_map/ppermute | solution.py:351
  14.0 1.5 %collective-permute-start = (f32[16,128]{1,0:T(8,128)S(1)}, f32[16,128]{1,0:T(8,128)S(1)}, u32[]{:S(2)}, u32[]{:S(2)}) collective-permute-start(f32[16,128]{1,0:T(8,128)S(1)} %get-tuple-element.34.flag_ref), channel_id=1, source_target_pairs={{0,16},{16,0},{1,17},{17,1},{2,18},{18,2},{3,19},{19,3},{4,20},{20... | collective-permute-start | bytes 24584 | tf_op jit(solution)/shard_map/ppermute | solution.py:354
  26.7 3.6 %collective-permute-start.2 = (bf16[272,128]{1,0:T(8,128)(2,1)S(1)}, bf16[272,128]{1,0:T(8,128)(2,1)S(1)}, u32[]{:S(2)}, u32[]{:S(2)}) collective-permute-start(bf16[272,128]{1,0:T(8,128)(2,1)S(1)} %get-tuple-element.38.y_ref), channel_id=1, source_target_pairs={{0,16},{16,0},{1,17},{17,1},{2,18},{18,2},{3,19},{19,3},{4,20},{20... | collective-permute-start | bytes 208904 | tf_op jit(solution)/shard_map/ppermute | solution.py:360
  30.4 9.6 %collective-permute-start.4 = (bf16[2,272,128]{2,1,0:T(8,128)(2,1)S(1)}, bf16[2,272,128]{2,1,0:T(8,128)(2,1)S(1)}, u32[]{:S(2)}, u32[]{:S(2)}) collective-permute-start(bf16[2,272,128]{2,1,0:T(8,128)(2,1)S(1)} %join_kernel.1.pair_ref), channel_id=1, source_target_pairs={{0,64},{32,96},{64,128},{96,160},{128,192},{160,224},{192,0},{224,... | collective-permute-start | bytes 417800 | tf_op jit(solution)/shard_map/ppermute | solution.py:312
  36.5 7.6 %collective-permute-start.3 = (bf16[2,272,128]{2,1,0:T(8,128)(2,1)S(1)}, bf16[2,272,128]{2,1,0:T(8,128)(2,1)S(1)}, u32[]{:S(2)}, u32[]{:S(2)}) collective-permute-start(bf16[2,272,128]{2,1,0:T(8,128)(2,1)S(1)} %join_kernel.1.pair_ref), channel_id=1, source_target_pairs={{0,32},{32,64},{64,96},{96,128},{128,160},{160,192},{192,224},{224... | collective-permute-start | bytes 417800 | tf_op jit(solution)/shard_map/ppermute | solution.py:312
  39.9 6.8 %collective-permute-start.5 = (bf16[2,272,128]{2,1,0:T(8,128)(2,1)S(1)}, bf16[2,272,128]{2,1,0:T(8,128)(2,1)S(1)}, u32[]{:S(2)}, u32[]{:S(2)}) collective-permute-start(bf16[2,272,128]{2,1,0:T(8,128)(2,1)S(1)} %collective-permute-done.4.pair_ref.two_ref), channel_id=1, source_target_pairs={{0,32},{32,64},{64,96},{96,128},{128,160},{160,192},{192,224},{224... | collective-permute-start | bytes 417800 | tf_op jit(solution)/shard_map/ppermute | solution.py:312
  42.1 4.6 %collective-permute-start.6 = (bf16[272,128]{1,0:T(8,128)(2,1)S(1)}, bf16[272,128]{1,0:T(8,128)(2,1)S(1)}, u32[]{:S(2)}, u32[]{:S(2)}) collective-permute-start(bf16[272,128]{1,0:T(8,128)(2,1)S(1)} %half_kernel.1), channel_id=1, source_target_pairs={{0,64},{32,96},{64,128},{96,160},{128,192},{160,224},{192,0},{224,... | collective-permute-start | bytes 208904 | tf_op jit(solution)/shard_map/ppermute | solution.py:312
  48.2 3.7 %collective-permute-start.7 = (f32[264,128]{1,0:T(8,128)S(1)}, f32[264,128]{1,0:T(8,128)S(1)}, u32[]{:S(2)}, u32[]{:S(2)}) collective-permute-start(f32[264,128]{1,0:T(8,128)S(1)} %get-tuple-element.41), channel_id=1, source_target_pairs={{0,16},{16,0},{1,17},{17,1},{2,18},{18,2},{3,19},{19,3},{4,20},{20... | collective-permute-start | bytes 405512 | tf_op jit(solution)/shard_map/ppermute | solution.py:369
  77.6 2.0 %collective-permute-start.8 = (bf16[8,256,128]{2,1,0:T(8,128)(2,1)S(1)}, bf16[8,256,128]{2,1,0:T(8,128)(2,1)S(1)}, u32[]{:S(2)}, u32[]{:S(2)}) collective-permute-start(bf16[8,256,128]{2,1,0:T(8,128)(2,1)S(1)} %get-tuple-element.47), channel_id=1, source_target_pairs={{0,16},{16,0},{1,17},{17,1},{2,18},{18,2},{3,19},{19,3},{4,20},{20... | collective-permute-start | bytes 1572872 | tf_op jit(solution)/shard_map/ppermute | solution.py:382
  79.7 22.1 %all-to-all-start.2 = ((bf16[16,128,256]{2,1,0:T(8,128)(2,1)}), bf16[16,128,256]{2,1,0:T(8,128)(2,1)S(1)}, u32[]{:S(2)}, u32[]{:S(2)}) async-start(bf16[16,128,256]{2,1,0:T(8,128)(2,1)} %get-tuple-element.56), calls=%async_computation.2 | async-start | bytes 2097152 | tf_op jit(solution)/shard_map/all_to_all | solution.py:406
  83.3 4.9 %collective-permute-start.9 = (bf16[2,256,128]{2,1,0:T(8,128)(2,1)S(1)}, bf16[2,256,128]{2,1,0:T(8,128)(2,1)S(1)}, u32[]{:S(2)}, u32[]{:S(2)}) collective-permute-start(bf16[2,256,128]{2,1,0:T(8,128)(2,1)S(1)} %get-tuple-element.51), channel_id=1, source_target_pairs={{0,32},{32,64},{64,96},{96,128},{128,160},{160,192},{192,224},{224... | collective-permute-start | bytes 393224 | tf_op jit(solution)/shard_map/ppermute | solution.py:312
  83.4 4.2 %collective-permute-start.10 = (bf16[256,128]{1,0:T(8,128)(2,1)S(1)}, bf16[256,128]{1,0:T(8,128)(2,1)S(1)}, u32[]{:S(2)}, u32[]{:S(2)}) collective-permute-start(bf16[256,128]{1,0:T(8,128)(2,1)S(1)} %get-tuple-element.52), channel_id=1, source_target_pairs={{0,64},{32,96},{64,128},{96,160},{128,192},{160,224},{192,0},{224,... | collective-permute-start | bytes 196616 | tf_op jit(solution)/shard_map/ppermute | solution.py:312
  84.7 5.8 %collective-permute-start.12 = (bf16[2,256,128]{2,1,0:T(8,128)(2,1)S(1)}, bf16[2,256,128]{2,1,0:T(8,128)(2,1)S(1)}, u32[]{:S(2)}, u32[]{:S(2)}) collective-permute-start(bf16[2,256,128]{2,1,0:T(8,128)(2,1)S(1)} %get-tuple-element.53), channel_id=1, source_target_pairs={{0,32},{32,64},{64,96},{96,128},{128,160},{160,192},{192,224},{224... | collective-permute-start | bytes 393224 | tf_op jit(solution)/shard_map/ppermute | solution.py:312
  88.3 7.0 %collective-permute-start.11 = (bf16[2,256,128]{2,1,0:T(8,128)(2,1)S(1)}, bf16[2,256,128]{2,1,0:T(8,128)(2,1)S(1)}, u32[]{:S(2)}, u32[]{:S(2)}) collective-permute-start(bf16[2,256,128]{2,1,0:T(8,128)(2,1)S(1)} %relay_kernel.1), channel_id=1, source_target_pairs={{0,64},{32,96},{64,128},{96,160},{128,192},{160,224},{192,0},{224,... | collective-permute-start | bytes 393224 | tf_op jit(solution)/shard_map/ppermute | solution.py:312
  95.3 7.3 %collective-permute-start.13 = (f32[256,128]{1,0:T(8,128)S(1)}, f32[256,128]{1,0:T(8,128)S(1)}, u32[]{:S(2)}, u32[]{:S(2)}) collective-permute-start(f32[256,128]{1,0:T(8,128)S(1)} %get-tuple-element.55), channel_id=1, source_target_pairs={{0,16},{16,0},{1,17},{17,1},{2,18},{18,2},{3,19},{19,3},{4,20},{20... | collective-permute-start | bytes 393224 | tf_op jit(solution)/shard_map/ppermute | solution.py:415

commit v15 on v14

--- a/solution.py
+++ b/solution.py
@@ -61,7 +61,7 @@
 
 
 def adjacency_kernel(
-    count_ref, dst_hbm, src_hbm, weight_ref, adj_ref, send_ref, inv_ref, flag_ref,
+    count_ref, dst_hbm, src_hbm, weight_ref, adj_ref, send_ref, back_ref, inv_ref, flag_ref,
     dst_ref, src_ref, buf, acc, sel_ref, in_sems, sems,
 ):
     count = count_ref[0]
@@ -112,6 +112,8 @@
         adj_ref[owner] = acc[owner].astype(F32).astype(BF16)
     for slot, owner in enumerate(sources(lax.axis_index("z"), 1 - lax.axis_index("c"), groups // 2)):
         send_ref[slot] = adj_ref[owner]
+    for slot, owner in enumerate(owners(lax.axis_index("z"), 1 - lax.axis_index("c"), groups // 2)[1:]):
+        back_ref[slot] = adj_ref[owner]
     degree = jnp.sum(total.astype(F32), axis=1, keepdims=True)
     inv_ref[...] = jnp.broadcast_to(1.0 / jnp.maximum(degree, 1.0), inv_ref.shape)
     row = lax.broadcasted_iota(jnp.int32, flag_ref.shape, 0)
@@ -130,12 +132,8 @@
     return total
 
 
-def neighbour_kernel(x_ref, w_ref, flag_ref, pair_flag_ref, adj_ref, pay_ref, flag_same_ref, adj_same_ref):
-    rows = x_ref.shape[1]
-    product = wide_dot(x_ref, w_ref).astype(BF16)
-    flags = flag_ref[...].astype(BF16)
-    pay_ref[0:rows, :] = product
-    pay_ref[rows:, :] = flags
+def neighbour_kernel(x_ref, w_ref, pair_flag_ref, adj_ref, pay_ref, flag_same_ref, adj_same_ref):
+    pay_ref[...] = wide_dot(x_ref, w_ref).astype(BF16)
 
 
 def join_kernel(y_ref, y_pair_ref, pair_ref):
@@ -154,12 +152,10 @@
 
 def aggregate_kernel(
     flag_ref, flag_pair_ref, adj_ref, adj_pair_ref, pair_ref, one_ref, two_ref, three_ref, far_ref,
-    mine_ref, mask_ref, theirs_ref,
+    mine_ref, theirs_ref,
 ):
     core = lax.axis_index("c")
     here = lax.axis_index("z")
-    rows = mine_ref.shape[0]
-    row = lax.broadcasted_iota(jnp.int32, (far_ref.shape[0] - rows, T), 0)
     blocks = [ref.at[side] for ref in (one_ref, two_ref, three_ref) for side in range(2)] + [far_ref]
     found = sources(here, core, flag_ref.shape[0] // 2)
 
@@ -172,58 +168,54 @@
             tiles.append(jnp.where(high, high_tile, low_tile).astype(BF16))
         return dot(jnp.concatenate(adj, axis=1), jnp.concatenate(tiles, axis=0))
 
-    def mask_row(block, reader):
-        return jnp.sum(jnp.where(row == reader, block[rows:, :].astype(F32), 0.0), axis=0, keepdims=True)
-
     adj_pair = [adj_pair_ref[slot] for slot in range(len(found))]
-    theirs_ref[0:rows] = summed(adj_pair, flag_pair_ref, blocks, found)
-    theirs_ref[rows:] = jnp.zeros((theirs_ref.shape[0] - rows, T), F32)
-    for slot, block in enumerate(blocks):
-        theirs_ref[rows + slot : rows + slot + 1, :] = mask_row(block, 2 * here + 1 - core)
+    theirs_ref[...] = summed(adj_pair, flag_pair_ref, blocks, found)
     blocks = blocks + [pair_ref.at[0], pair_ref.at[1]]
     found = found + [2 * here, 2 * here + 1]
     mine_ref[...] = summed([adj_ref[owner] for owner in found], flag_ref, blocks, found)
-    mask_ref[...] = jnp.zeros_like(mask_ref)
-    for block, owner in zip(blocks, found):
-        mask_ref[pl.ds(owner, 1), :] = mask_row(block, 2 * here + core)
-
-
-def activation_kernel(
-    adj_ref, inv_ref, mine_ref, own_mask_ref, came_ref, z_ref, og_ref, out_ref, gt_ref, pay_ref, mask_ref
-):
-    rows = z_ref.shape[0]
-    mask_ref[...] = own_mask_ref[...]
-    found = sources(lax.axis_index("z"), 1 - lax.axis_index("c"), mask_ref.shape[0] // 2)
-    for slot, owner in enumerate(found):
-        mask_ref[pl.ds(owner, 1), :] = came_ref[rows + slot : rows + slot + 1, :]
+
+
+def activation_kernel(inv_ref, mine_ref, came_ref, z_ref, og_ref, out_ref, both_ref):
     inverse = inv_ref[...]
-    z = z_ref[...] + inverse * (mine_ref[...] + came_ref[0:rows])
+    z = z_ref[...] + inverse * (mine_ref[...] + came_ref[...])
     sig = 1.0 / (1.0 + jnp.exp(-z))
     grad = (og_ref[...].astype(F32) * sig * (1.0 + z * (1.0 - sig))).astype(BF16).astype(F32)
-    scaled = halves((grad * inverse).T)
-    for owner in range(0, pay_ref.shape[0], 2):
-        spread = dot(scaled, jnp.concatenate([adj_ref[owner], adj_ref[owner + 1]], axis=1))
-        spread = (spread[0:T] + spread[T:]).astype(BF16)
-        pay_ref[owner] = spread[:, 0:T]
-        pay_ref[owner + 1] = spread[:, T:]
+    both_ref[0:T, :] = grad.T.astype(BF16)
+    both_ref[T:, :] = halves((grad * inverse).T)
     out_ref[...] = (z * sig).astype(BF16)
-    gt_ref[...] = grad.T.astype(BF16)
-
-
-def weight_grad_kernel(came_ref, mask_ref, gt_ref, x_ref, bt_ref, keep_ref, send_ref):
+
+
+def transpose_kernel(
+    flag_ref, flag_pair_ref, adj_ref, adj_pair_ref, adj_back_ref, both_ref, both_pair_ref,
+    far_ref, three_ref, one_ref, two_ref, own_ref,
+):
+    found = owners(lax.axis_index("z"), lax.axis_index("c"), flag_ref.shape[0] // 2)
+    adj_pair = [adj_pair_ref[len(found) - 2]] + [adj_back_ref[slot] for slot in range(len(found) - 1)]
+    left = jnp.concatenate([both_ref[T:, :], both_pair_ref[T:, :]], axis=1)
+
+    def block(slot):
+        parts = []
+        for adj, flag in ((adj_ref[found[slot]], flag_ref), (adj_pair[slot], flag_pair_ref)):
+            high = flag[pl.ds(found[slot], 1), :]
+            parts.append(jnp.concatenate([adj * (1.0 - high).astype(BF16), adj * high.astype(BF16)], axis=1))
+        product = dot(left, jnp.concatenate(parts, axis=0))
+        return product[0:T] + product[T:]
+
+    far_ref[...] = block(0).astype(BF16)
+    for place in range(2):
+        three_ref[place] = block(1 + place).astype(BF16)
+        two_ref[place] = block(3 + place)
+        one_ref[place] = block(5 + place).astype(BF16)
+    own_ref[...] = block(7)
+
+
+def weight_grad_kernel(mine_ref, came_ref, both_ref, x_ref, bt_ref, keep_ref, send_ref):
     core = lax.axis_index("c")
     here = lax.axis_index("z")
     chips = keep_ref.shape[0]
-    low = jnp.zeros((T, T), F32)
-    high = jnp.zeros((T, T), F32)
-    for sender in range(came_ref.shape[0]):
-        came = came_ref[sender].astype(F32)
-        is_high = mask_ref[sender : sender + 1, :] > 0.5
-        low = low + jnp.where(is_high, 0.0, came)
-        high = high + jnp.where(is_high, came, 0.0)
-    both = halves(jnp.concatenate([low, high], axis=1))
-    bt_ref[...] = both[0:T]
-    left = jnp.concatenate([gt_ref[...], both], axis=0)
+    split = halves(mine_ref[...] + came_ref[...])
+    bt_ref[...] = split[0:T]
+    left = jnp.concatenate([both_ref[0:T, :], split], axis=0)
     slots = zip(owners(here, core, chips), owners(here, 1 - core, chips))
     for slot, (ours, theirs) in enumerate(slots):
         total = dot(left, jnp.concatenate([x_ref[ours], x_ref[theirs]], axis=1))
@@ -234,8 +226,8 @@
         send_ref[slot, T:] = (sent[T : 2 * T] + sent[2 * T :]).astype(BF16)
 
 
-def feature_grad_kernel(gt_ref, bt_ref, ws_ref, wn_ref, pay_ref, buf, sems):
-    right = jnp.concatenate([gt_ref[...], bt_ref[...]], axis=0)
+def feature_grad_kernel(both_ref, bt_ref, ws_ref, wn_ref, pay_ref, buf, sems):
+    right = jnp.concatenate([both_ref[0:T, :], bt_ref[...]], axis=0)
     copies = []
     for part in range(pay_ref.shape[0]):
         span = slice(part * T, (part + 1) * T)
@@ -327,11 +319,12 @@
         scratch=[pltpu.VMEM((rows, T), BF16), pltpu.SemaphoreType.DMA, pltpu.SemaphoreType.DMA((parts,))],
     )
     x_all = lax.all_to_all(x_pay, "f", 0, 0, tiled=True)
-    adj, adj_send, inverse, flags = call(
+    adj, adj_send, adj_back, inverse, flags = call(
         adjacency_kernel,
         (tile_count, tile_dst, tile_src, tile_weight[0]),
         [
             ((groups, rows, T), BF16),
+            ((chips - 1, rows, T), BF16),
             ((chips - 1, rows, T), BF16),
             ((rows, T), F32),
             ((groups, T), F32),
@@ -348,71 +341,78 @@
         ],
         limit=20,
     )
-    adj_pair = lax.ppermute(adj_send, "c", swap)
+    adj_pair, adj_back = lax.ppermute(adj_send, "c", swap), lax.ppermute(adj_back, "c", swap)
     y, flags_pair, adj_pair = call(
         neighbour_kernel,
-        (x_all, w_neigh, flags, lax.ppermute(flags, "c", swap), adj_pair),
-        [((rows + groups, T), BF16), (flags.shape, F32), (adj_pair.shape, BF16)],
-        in_specs=[VMEM] * 3 + [ANY, HBM],
+        (x_all, w_neigh, lax.ppermute(flags, "c", swap), adj_pair),
+        [((rows, T), BF16), (flags.shape, F32), (adj_pair.shape, BF16)],
+        in_specs=[VMEM] * 2 + [ANY, HBM],
         out_specs=[VMEM, ANY, HBM],
-        aliases={3: 1, 4: 2},
+        aliases={2: 1, 3: 2},
     )
     (pair,) = call(join_kernel, (y, lax.ppermute(y, "c", swap)), [((2,) + y.shape, BF16)])
     two, one = along(pair, 2, chips), along(pair, 1, chips)
     (half,) = call(half_kernel, (two,), [(y.shape, BF16)])
     three, far = along(two, 1, chips), along(half, 2, chips)
-    mine, own_mask, theirs = call(
+    mine, theirs = call(
         aggregate_kernel,
         (flags, flags_pair, adj, adj_pair, pair, one, two, three, far),
-        [((rows, T), F32), ((groups, T), F32), ((rows + chips, T), F32)],
+        [((rows, T), F32)] * 2,
     )
     came = lax.ppermute(theirs, "c", swap)
     (z_self,) = call(self_kernel, (x_all, w_self), [((rows, T), F32)])
-    output, gt, c_pay, mask = call(
+    output, both = call(
         activation_kernel,
-        (adj, inverse, mine, own_mask, came, z_self, out_grad),
-        [((rows, T), BF16), ((T, rows), BF16), ((groups, T, T), BF16), ((groups, T), F32)],
-    )
-    c_all = lax.all_to_all(c_pay, ("z", "c"), 0, 0, tiled=True)
+        (inverse, mine, came, z_self, out_grad),
+        [((rows, T), BF16), ((3 * T, rows), BF16)],
+    )
+
+    def sends(block):
+        pair = (2,) + block
+        return [(block, BF16), (pair, BF16), (pair, BF16), (pair, F32), (block, F32)]
+
+    def reduce(far, three, one, two, own):
+        block = own.shape
+        (two,) = call(
+            relay_kernel, (two, along(three, 1, chips), along(far, 2, chips)), [((2,) + block, BF16)]
+        )
+        two, one = along(two, 2, chips), along(one, 1, chips)
+        mine, theirs = call(fold_kernel, (own, two, one), [(block, F32)] * 2)
+        return mine, lax.ppermute(theirs, "c", swap)
+
+    parts_sent = call(
+        transpose_kernel,
+        (flags, flags_pair, adj, adj_pair, adj_back, both, lax.ppermute(both, "c", swap)),
+        sends((T, rows)),
+    )
+    mine, came = reduce(*parts_sent)
     bt, keep, send = call(
         weight_grad_kernel,
-        (c_all, mask, gt, x_all),
+        (mine, came, both, x_all),
         [((T, rows), BF16), ((chips, 2 * T, T), F32), ((chips, 2 * T, T), BF16)],
     )
     came = lax.ppermute(send, "c", swap)
     (p_pay,) = call(
         feature_grad_kernel,
-        (gt, bt, w_self, w_neigh),
+        (both, bt, w_self, w_neigh),
         [((parts, T, rows), BF16)],
         out_specs=[HBM],
         scratch=[pltpu.VMEM((parts, T, rows), BF16), pltpu.SemaphoreType.DMA((parts,))],
     )
-    block = (2 * T, T)
-    far, three, one, two, own, p_pay = call(
+    *parts_sent, p_pay = call(
         pair_kernel,
         (keep, came, p_pay),
-        [
-            (block, BF16),
-            ((2,) + block, BF16),
-            ((2,) + block, BF16),
-            ((2,) + block, F32),
-            (block, F32),
-            (p_pay.shape, BF16),
-        ],
+        sends((2 * T, T)) + [(p_pay.shape, BF16)],
         in_specs=[VMEM, VMEM, HBM],
         out_specs=[VMEM] * 5 + [HBM],
         aliases={2: 5},
     )
     p_all = lax.all_to_all(p_pay, "f", 0, 0, tiled=True)
-    (two,) = call(
-        relay_kernel, (two, along(three, 1, chips), along(far, 2, chips)), [((2,) + block, BF16)]
-    )
-    two, one = along(two, 2, chips), along(one, 1, chips)
-    mine, theirs = call(fold_kernel, (own, two, one), [(block, F32)] * 2)
+    mine, came = reduce(*parts_sent)
     (grad_features,) = call(sum_kernel, (p_all,), [((rows, T), BF16)])
     grad_self, grad_neigh, grad_features = call(
         last_kernel,
-        (mine, lax.ppermute(theirs, "c", swap), grad_features),
+        (mine, came, grad_features),
         [((T, T), F32), ((T, T), F32), ((rows, T), BF16)],
         in_specs=[VMEM] * 2 + [ANY],
         out_specs=[VMEM, VMEM, ANY],

time: 104 us -> 99.2 us (0.954)
  blocking collectives: 24.2 us -> 0 us
  starting transfers between devices: 36.3 us -> 55.4 us
  waiting for transfers between devices: 30.3 us -> 26.4 us
  local copies, waits for them, and re-layouts: 0.02 us -> 3.87 us
    all_to_all x1 -> x0, blocking collectives: 24.2 us -> none  [per_device(): c_all = lax.all_to_all(c_pay, ('z', 'c'), 0, 0, tiled=True)]
    ppermute x8 -> x12, starting transfers between devices: 14.7 us -> 33.5 us  [along(): return lax.ppermute(value, ('z', 'c'), pairs)]
    unnamed x6 -> x16, local copies, waits for them, and re-layouts: 0.02 us -> 3.87 us
    all_to_all x1, waiting for transfers between devices: 2.55 us -> 0.01 us  [per_device(): p_all = lax.all_to_all(p_pay, 'f', 0, 0, tiled=True)]
    ppermute x2 -> x5, waiting for transfers between devices: 0.12 us -> 2.21 us  [the longest x2 1.13 us: reduce(): return (mine, lax.ppermute(theirs, 'c', swap))]
    ppermute x8 -> x12, waiting for transfers between devices: 13.5 us -> 11.6 us  [along(): return lax.ppermute(value, ('z', 'c'), pairs)]
    all_to_all x1, waiting for transfers between devices: 10.8 us -> 9.6 us  [per_device(): x_all = lax.all_to_all(x_pay, 'f', 0, 0, tiled=True)]
    pallas_call x15 -> x18, Pallas kernels: 11.2 us -> 11.5 us  [call(): pl.pallas_call(kernel, out_shape=shapes, in_specs=in_specs or [VMEM] * le...]
  transfers between devices with their start and end apart: 16 -> 23, of which waited for: 12 -> 13; matrix products, arithmetic and copies ran while one was open for 0% -> 0% of each run, Pallas kernels for 5% -> 7%
where the time goes in v15:
time: 99.2 us; the launch traced here: 98.8 us
  starting transfers between devices  55.4 us (56%)
  waiting for transfers between devices  26.4 us (27%)
  Pallas kernels  11.5 us (12%)
  local copies, waits for them, and re-layouts  3.87 us (4%)
  between operations  1.49 us (2%)
    ppermute x12, starting transfers between devices, along(): return lax.ppermute(value, ('z', 'c'), pairs)  33.5 us
    ppermute x12, waiting for transfers between devices, along(): return lax.ppermute(value, ('z', 'c'), pairs)  11.6 us
    pallas_call x18, Pallas kernels, call(): pl.pallas_call(kernel, out_shape=shapes, in_specs=in_specs or [VMEM] * le...  11.5 us
    all_to_all x1, waiting for transfers between devices, per_device(): x_all = lax.all_to_all(x_pay, 'f', 0, 0, tiled=True)  9.6 us
    all_to_all x1, starting transfers between devices, per_device(): x_all = lax.all_to_all(x_pay, 'f', 0, 0, tiled=True)  7.6 us
    ppermute x2, starting transfers between devices, reduce(): return (mine, lax.ppermute(theirs, 'c', swap))  4.12 us
    unnamed x16, local copies, waits for them, and re-layouts  3.87 us
    all_to_all x1, starting transfers between devices, per_device(): p_all = lax.all_to_all(p_pay, 'f', 0, 0, tiled=True)  3.66 us
  transfers between devices with their start and end apart: 23, of which 13 were waited for; matrix products, arithmetic and copies ran while one was open for 0% of the time, Pallas kernels for 7%

profile of v15, /device:TPU:1, one launch (start us, length us, event | category | flops | bytes accessed | tf_op | source)
XLA Modules:
  0.0 98.8 jit_solution(9719824391492091149)
XLA Ops:
  0.6 2.0 %spread_kernel.1 = bf16[16,256,128]{2,1,0:T(8,128)(2,1)} custom-call(bf16[256,128]{1,0:T(8,128)(2,1)} %x_hbm.1), custom_call_target="tpu_custom_call" | custom-call | tf_op jit(solution)/shard_map/spread_kernel/pallas_call | solution.py:289
  2.6 7.6 %all-to-all-start = ((bf16[16,256,128]{2,1,0:T(8,128)(2,1)}), bf16[16,256,128]{2,1,0:T(8,128)(2,1)S(1)}, u32[]{:S(2)}, u32[]{:S(2)}) async-start(bf16[16,256,128]{2,1,0:T(8,128)(2,1)} %spread_kernel.1), calls=%async_computation | async-start | bytes 2097152 | tf_op jit(solution)/shard_map/all_to_all | solution.py:321
  11.0 3.0 %adjacency_kernel.1 = (bf16[16,256,128]{2,1,0:T(8,128)(2,1)S(1)}, bf16[7,256,128]{2,1,0:T(8,128)(2,1)S(1)}, bf16[7,256,128]{2,1,0:T(8,128)(2,1)S(1)}, f32[256,128]{1,0:T(8,128)S(1)}, f32[16,128]{1,0:T(8,128)S(1)}) custom-call(s32[1]{0:T(128)S(6)} %copy.20.count_ref, s32[1,80]{1,0:T(1,128)} %dst_hbm.1, s32[1,80]{1,0:T(1,128)} %src_hbm.1, s32[80,128,128]{2,1,0:T(8,128)} %bitcast.1), custom_call_target="tpu_custom_call" | custom-call | tf_op jit(solution)/shard_map/adjacency_kernel/pallas_call | solution.py:289
  15.3 1.3 %collective-permute-done.pair_flag_ref = f32[16,128]{1,0:T(8,128)S(1)} collective-permute-done((f32[16,128]{1,0:T(8,128)S(1)}, f32[16,128]{1,0:T(8,128)S(1)}, u32[]{:S(2)}, u32[]{:S(2)}) %collective-permute-start) | collective-permute-done | bytes 8224 | tf_op jit(solution)/shard_map/ppermute | solution.py:347
  16.6 9.6 %all-to-all-done.x_ref = bf16[16,256,128]{2,1,0:T(8,128)(2,1)S(1)} async-done(((bf16[16,256,128]{2,1,0:T(8,128)(2,1)}), bf16[16,256,128]{2,1,0:T(8,128)(2,1)S(1)}, u32[]{:S(2)}, u32[]{:S(2)}) %all-to-all-start) | async-done | bytes 1048608 | tf_op jit(solution)/shard_map/all_to_all | solution.py:321
  26.2 1.0 %copy-done.4 = bf16[2048,128]{1,0:T(8,128)(2,1)S(1)} copy-done((bf16[2048,128]{1,0:T(8,128)(2,1)S(1)}, bf16[2048,128]{1,0:T(8,128)(2,1)}, u32[]{:S(2)}) %copy-start.4) | copy-done | bytes 524312
  27.7 2.7 %collective-permute-start.2 = (bf16[256,128]{1,0:T(8,128)(2,1)S(1)}, bf16[256,128]{1,0:T(8,128)(2,1)S(1)}, u32[]{:S(2)}, u32[]{:S(2)}) collective-permute-start(bf16[256,128]{1,0:T(8,128)(2,1)S(1)} %get-tuple-element.43.y_ref), channel_id=1, source_target_pairs={{0,16},{16,0},{1,17},{17,1},{2,18},{18,2},{3,19},{19,3},{4,20},{20... | collective-permute-start | bytes 196616 | tf_op jit(solution)/shard_map/ppermute | solution.py:353
  30.4 0.9 collective-permute-done.2.y_pair_ref
  31.3 6.1 %collective-permute-start.4 = (bf16[2,256,128]{2,1,0:T(8,128)(2,1)S(1)}, bf16[2,256,128]{2,1,0:T(8,128)(2,1)S(1)}, u32[]{:S(2)}, u32[]{:S(2)}) collective-permute-start(bf16[2,256,128]{2,1,0:T(8,128)(2,1)S(1)} %join_kernel.1.pair_ref), channel_id=1, source_target_pairs={{0,64},{32,96},{64,128},{96,160},{128,192},{160,224},{192,0},{224,... | collective-permute-start | bytes 393224 | tf_op jit(solution)/shard_map/ppermute | solution.py:304
  38.1 2.6 %collective-permute-done.4.pair_ref.two_ref = bf16[2,256,128]{2,1,0:T(8,128)(2,1)S(1)} collective-permute-done((bf16[2,256,128]{2,1,0:T(8,128)(2,1)S(1)}, bf16[2,256,128]{2,1,0:T(8,128)(2,1)S(1)}, u32[]{:S(2)}, u32[]{:S(2)}) %collective-permute-start.4) | collective-permute-done | bytes 131104 | tf_op jit(solution)/shard_map/ppermute | solution.py:304
  40.7 2.3 %collective-permute-start.5 = (bf16[2,256,128]{2,1,0:T(8,128)(2,1)S(1)}, bf16[2,256,128]{2,1,0:T(8,128)(2,1)S(1)}, u32[]{:S(2)}, u32[]{:S(2)}) collective-permute-start(bf16[2,256,128]{2,1,0:T(8,128)(2,1)S(1)} %collective-permute-done.4.pair_ref.two_ref), channel_id=1, source_target_pairs={{0,32},{32,64},{64,96},{96,128},{128,160},{160,192},{192,224},{224... | collective-permute-start | bytes 393224 | tf_op jit(solution)/shard_map/ppermute | solution.py:304
  43.4 2.6 %collective-permute-start.6 = (bf16[256,128]{1,0:T(8,128)(2,1)S(1)}, bf16[256,128]{1,0:T(8,128)(2,1)S(1)}, u32[]{:S(2)}, u32[]{:S(2)}) collective-permute-start(bf16[256,128]{1,0:T(8,128)(2,1)S(1)} %half_kernel.1), channel_id=1, source_target_pairs={{0,64},{32,96},{64,128},{96,160},{128,192},{160,224},{192,0},{224,... | collective-permute-start | bytes 196616 | tf_op jit(solution)/shard_map/ppermute | solution.py:304
  46.1 1.9 %collective-permute-done.6.far_ref = bf16[256,128]{1,0:T(8,128)(2,1)S(1)} collective-permute-done((bf16[256,128]{1,0:T(8,128)(2,1)S(1)}, bf16[256,128]{1,0:T(8,128)(2,1)S(1)}, u32[]{:S(2)}, u32[]{:S(2)}) %collective-permute-start.6) | collective-permute-done | bytes 65568 | tf_op jit(solution)/shard_map/ppermute | solution.py:304
  48.0 1.0 %copy-done.1 = bf16[7,256,128]{2,1,0:T(8,128)(2,1)S(1)} copy-done((bf16[7,256,128]{2,1,0:T(8,128)(2,1)S(1)}, bf16[7,256,128]{2,1,0:T(8,128)(2,1)}, u32[]{:S(2)}) %copy-start.1) | copy-done | bytes 458776
  49.5 2.1 %collective-permute-start.7 = (f32[256,128]{1,0:T(8,128)S(1)}, f32[256,128]{1,0:T(8,128)S(1)}, u32[]{:S(2)}, u32[]{:S(2)}) collective-permute-start(f32[256,128]{1,0:T(8,128)S(1)} %get-tuple-element.45), channel_id=1, source_target_pairs={{0,16},{16,0},{1,17},{17,1},{2,18},{18,2},{3,19},{19,3},{4,20},{20... | collective-permute-start | bytes 393224 | tf_op jit(solution)/shard_map/ppermute | solution.py:362
  53.6 1.1 %collective-permute-done.9.both_pair_ref = bf16[384,256]{1,0:T(8,128)(2,1)S(1)} collective-permute-done((bf16[384,256]{1,0:T(8,128)(2,1)S(1)}, bf16[384,256]{1,0:T(8,128)(2,1)S(1)}, u32[]{:S(2)}, u32[]{:S(2)}) %collective-permute-start.9) | collective-permute-done | bytes 196640 | tf_op jit(solution)/shard_map/ppermute | solution.py:385
  54.7 1.0 %copy-done.2 = bf16[7,256,128]{2,1,0:T(8,128)(2,1)S(1)} copy-done((bf16[7,256,128]{2,1,0:T(8,128)(2,1)S(1)}, bf16[7,256,128]{2,1,0:T(8,128)(2,1)}, u32[]{:S(2)}) %copy-start.2) | copy-done | bytes 458776
  56.5 1.1 %collective-permute-start.10 = (bf16[2,128,256]{2,1,0:T(8,128)(2,1)S(1)}, bf16[2,128,256]{2,1,0:T(8,128)(2,1)S(1)}, u32[]{:S(2)}, u32[]{:S(2)}) collective-permute-start(bf16[2,128,256]{2,1,0:T(8,128)(2,1)S(1)} %get-tuple-element.51), channel_id=1, source_target_pairs={{0,32},{32,64},{64,96},{96,128},{128,160},{160,192},{192,224},{224... | collective-permute-start | bytes 393224 | tf_op jit(solution)/shard_map/ppermute | solution.py:304
  57.5 2.7 %collective-permute-start.11 = (bf16[128,256]{1,0:T(8,128)(2,1)S(1)}, bf16[128,256]{1,0:T(8,128)(2,1)S(1)}, u32[]{:S(2)}, u32[]{:S(2)}) collective-permute-start(bf16[128,256]{1,0:T(8,128)(2,1)S(1)} %get-tuple-element.52), channel_id=1, source_target_pairs={{0,64},{32,96},{64,128},{96,160},{128,192},{160,224},{192,0},{224,... | collective-permute-start | bytes 196616 | tf_op jit(solution)/shard_map/ppermute | solution.py:304
  60.2 2.0 %collective-permute-start.13 = (bf16[2,128,256]{2,1,0:T(8,128)(2,1)S(1)}, bf16[2,128,256]{2,1,0:T(8,128)(2,1)S(1)}, u32[]{:S(2)}, u32[]{:S(2)}) collective-permute-start(bf16[2,128,256]{2,1,0:T(8,128)(2,1)S(1)} %get-tuple-element.53), channel_id=1, source_target_pairs={{0,32},{32,64},{64,96},{96,128},{128,160},{160,192},{192,224},{224... | collective-permute-start | bytes 393224 | tf_op jit(solution)/shard_map/ppermute | solution.py:304
  62.3 4.2 %collective-permute-start.12 = (bf16[2,128,256]{2,1,0:T(8,128)(2,1)S(1)}, bf16[2,128,256]{2,1,0:T(8,128)(2,1)S(1)}, u32[]{:S(2)}, u32[]{:S(2)}) collective-permute-start(bf16[2,128,256]{2,1,0:T(8,128)(2,1)S(1)} %relay_kernel.2), channel_id=1, source_target_pairs={{0,64},{32,96},{64,128},{96,160},{128,192},{160,224},{192,0},{224,... | collective-permute-start | bytes 393224 | tf_op jit(solution)/shard_map/ppermute | solution.py:304
  66.6 3.7 %collective-permute-done.12.two_ref = bf16[2,128,256]{2,1,0:T(8,128)(2,1)S(1)} collective-permute-done((bf16[2,128,256]{2,1,0:T(8,128)(2,1)S(1)}, bf16[2,128,256]{2,1,0:T(8,128)(2,1)S(1)}, u32[]{:S(2)}, u32[]{:S(2)}) %collective-permute-start.12) | collective-permute-done | bytes 131104 | tf_op jit(solution)/shard_map/ppermute | solution.py:304
  70.3 1.1 %collective-permute-start.14 = (f32[128,256]{1,0:T(8,128)S(1)}, f32[128,256]{1,0:T(8,128)S(1)}, u32[]{:S(2)}, u32[]{:S(2)}) collective-permute-start(f32[128,256]{1,0:T(8,128)S(1)} %get-tuple-element.55), channel_id=1, source_target_pairs={{0,16},{16,0},{1,17},{17,1},{2,18},{18,2},{3,19},{19,3},{4,20},{20... | collective-permute-start | bytes 393224 | tf_op jit(solution)/shard_map/ppermute | solution.py:381
  71.3 1.0 collective-permute-done.14.came_ref
  73.4 1.3 %feature_grad_kernel.1.payload_ref = bf16[16,128,256]{2,1,0:T(8,128)(2,1)} custom-call(bf16[384,256]{1,0:T(8,128)(2,1)S(1)} %get-tuple-element.48.both_ref, bf16[128,256]{1,0:T(8,128)(2,1)S(1)} %get-tuple-element.58.bt_ref, bf16[2048,128]{1,0:T(8,128)(2,1)S(1)} %copy-done.3, bf16[2048,128]{1,0:T(8,128)(2,1)S(1)} %copy-done.5), custom_call_target="tpu_custom_call" | custom-call | tf_op jit(solution)/shard_map/feature_grad_kernel/pallas_call | solution.py:289
  75.0 3.7 %all-to-all-start.1 = ((bf16[16,128,256]{2,1,0:T(8,128)(2,1)}), bf16[16,128,256]{2,1,0:T(8,128)(2,1)S(1)}, u32[]{:S(2)}, u32[]{:S(2)}) async-start(bf16[16,128,256]{2,1,0:T(8,128)(2,1)} %get-tuple-element.66), calls=%async_computation.1 | async-start | bytes 2097152 | tf_op jit(solution)/shard_map/all_to_all | solution.py:410
  78.7 3.0 %collective-permute-start.16 = (bf16[2,256,128]{2,1,0:T(8,128)(2,1)S(1)}, bf16[2,256,128]{2,1,0:T(8,128)(2,1)S(1)}, u32[]{:S(2)}, u32[]{:S(2)}) collective-permute-start(bf16[2,256,128]{2,1,0:T(8,128)(2,1)S(1)} %get-tuple-element.61), channel_id=1, source_target_pairs={{0,32},{32,64},{64,96},{96,128},{128,160},{160,192},{192,224},{224... | collective-permute-start | bytes 393224 | tf_op jit(solution)/shard_map/ppermute | solution.py:304
  81.7 4.4 %collective-permute-start.17 = (bf16[256,128]{1,0:T(8,128)(2,1)S(1)}, bf16[256,128]{1,0:T(8,128)(2,1)S(1)}, u32[]{:S(2)}, u32[]{:S(2)}) collective-permute-start(bf16[256,128]{1,0:T(8,128)(2,1)S(1)} %get-tuple-element.62), channel_id=1, source_target_pairs={{0,64},{32,96},{64,128},{96,160},{128,192},{160,224},{192,0},{224,... | collective-permute-start | bytes 196616 | tf_op jit(solution)/shard_map/ppermute | solution.py:304
  86.2 1.2 %collective-permute-done.17.far_ref = bf16[256,128]{1,0:T(8,128)(2,1)S(1)} collective-permute-done((bf16[256,128]{1,0:T(8,128)(2,1)S(1)}, bf16[256,128]{1,0:T(8,128)(2,1)S(1)}, u32[]{:S(2)}, u32[]{:S(2)}) %collective-permute-start.17) | collective-permute-done | bytes 65568 | tf_op jit(solution)/shard_map/ppermute | solution.py:304
  87.4 4.3 %collective-permute-start.18 = (bf16[2,256,128]{2,1,0:T(8,128)(2,1)S(1)}, bf16[2,256,128]{2,1,0:T(8,128)(2,1)S(1)}, u32[]{:S(2)}, u32[]{:S(2)}) collective-permute-start(bf16[2,256,128]{2,1,0:T(8,128)(2,1)S(1)} %relay_kernel.3), channel_id=1, source_target_pairs={{0,64},{32,96},{64,128},{96,160},{128,192},{160,224},{192,0},{224,... | collective-permute-start | bytes 393224 | tf_op jit(solution)/shard_map/ppermute | solution.py:304
  91.7 2.2 %collective-permute-done.18.two_ref = bf16[2,256,128]{2,1,0:T(8,128)(2,1)S(1)} collective-permute-done((bf16[2,256,128]{2,1,0:T(8,128)(2,1)S(1)}, bf16[2,256,128]{2,1,0:T(8,128)(2,1)S(1)}, u32[]{:S(2)}, u32[]{:S(2)}) %collective-permute-start.18) | collective-permute-done | bytes 131104 | tf_op jit(solution)/shard_map/ppermute | solution.py:304
  94.0 3.0 %collective-permute-start.20 = (f32[256,128]{1,0:T(8,128)S(1)}, f32[256,128]{1,0:T(8,128)S(1)}, u32[]{:S(2)}, u32[]{:S(2)}) collective-permute-start(f32[256,128]{1,0:T(8,128)S(1)} %get-tuple-element.65), channel_id=1, source_target_pairs={{0,16},{16,0},{1,17},{17,1},{2,18},{18,2},{3,19},{19,3},{4,20},{20... | collective-permute-start | bytes 393224 | tf_op jit(solution)/shard_map/ppermute | solution.py:381
  (48 shorter events, 9.4 us)
Async XLA Ops:
  2.6 23.6 %all-to-all-start = ((bf16[16,256,128]{2,1,0:T(8,128)(2,1)}), bf16[16,256,128]{2,1,0:T(8,128)(2,1)S(1)}, u32[]{:S(2)}, u32[]{:S(2)}) async-start(bf16[16,256,128]{2,1,0:T(8,128)(2,1)} %spread_kernel.1), calls=%async_computation | async-start | bytes 2097152 | tf_op jit(solution)/shard_map/all_to_all | solution.py:321
  10.2 41.3 %copy-start.3 = (bf16[2048,128]{1,0:T(8,128)(2,1)S(1)}, bf16[2048,128]{1,0:T(8,128)(2,1)}, u32[]{:S(2)}) copy-start(bf16[2048,128]{1,0:T(8,128)(2,1)} %ws_ref.1) | copy-start | bytes 1572868
  10.9 41.6 %copy-start.6 = (bf16[256,128]{1,0:T(8,128)(2,1)S(1)}, bf16[256,128]{1,0:T(8,128)(2,1)}, u32[]{:S(2)}) copy-start(bf16[256,128]{1,0:T(8,128)(2,1)} %og_ref.1) | copy-start | bytes 196612
  14.0 0.8 copy-start.7
  14.8 1.8 %collective-permute-start.1 = (bf16[7,256,128]{2,1,0:T(8,128)(2,1)S(1)}, bf16[7,256,128]{2,1,0:T(8,128)(2,1)S(1)}, u32[]{:S(2)}, u32[]{:S(2)}) collective-permute-start(bf16[7,256,128]{2,1,0:T(8,128)(2,1)S(1)} %get-tuple-element.39), channel_id=1, source_target_pairs={{0,16},{16,0},{1,17},{17,1},{2,18},{18,2},{3,19},{19,3},{4,20},{20... | collective-permute-start | bytes 1376264 | tf_op jit(solution)/shard_map/ppermute | solution.py:344
  14.8 1.8 %collective-permute-start = (f32[16,128]{1,0:T(8,128)S(1)}, f32[16,128]{1,0:T(8,128)S(1)}, u32[]{:S(2)}, u32[]{:S(2)}) collective-permute-start(f32[16,128]{1,0:T(8,128)S(1)} %get-tuple-element.38.flag_ref), channel_id=1, source_target_pairs={{0,16},{16,0},{1,17},{17,1},{2,18},{18,2},{3,19},{19,3},{4,20},{20... | collective-permute-start | bytes 24584 | tf_op jit(solution)/shard_map/ppermute | solution.py:347
  16.6 9.6 %copy-start = (bf16[7,256,128]{2,1,0:T(8,128)(2,1)}, bf16[7,256,128]{2,1,0:T(8,128)(2,1)S(1)}, u32[]{:S(2)}) copy-start(bf16[7,256,128]{2,1,0:T(8,128)(2,1)S(1)} %collective-permute-done.1.adj_ref) | copy-start | bytes 1376260
  26.2 1.0 %copy-start.4 = (bf16[2048,128]{1,0:T(8,128)(2,1)S(1)}, bf16[2048,128]{1,0:T(8,128)(2,1)}, u32[]{:S(2)}) copy-start(bf16[2048,128]{1,0:T(8,128)(2,1)} %wn_ref.1) | copy-start | bytes 1572868
  27.3 46.1 %copy-start.5 = (bf16[2048,128]{1,0:T(8,128)(2,1)S(1)}, bf16[2048,128]{1,0:T(8,128)(2,1)}, u32[]{:S(2)}) copy-start(bf16[2048,128]{1,0:T(8,128)(2,1)} %wn_ref.1) | copy-start | bytes 1572868
  27.7 3.6 %collective-permute-start.2 = (bf16[256,128]{1,0:T(8,128)(2,1)S(1)}, bf16[256,128]{1,0:T(8,128)(2,1)S(1)}, u32[]{:S(2)}, u32[]{:S(2)}) collective-permute-start(bf16[256,128]{1,0:T(8,128)(2,1)S(1)} %get-tuple-element.43.y_ref), channel_id=1, source_target_pairs={{0,16},{16,0},{1,17},{17,1},{2,18},{18,2},{3,19},{19,3},{4,20},{20... | collective-permute-start | bytes 196616 | tf_op jit(solution)/shard_map/ppermute | solution.py:353
  31.3 9.4 %collective-permute-start.4 = (bf16[2,256,128]{2,1,0:T(8,128)(2,1)S(1)}, bf16[2,256,128]{2,1,0:T(8,128)(2,1)S(1)}, u32[]{:S(2)}, u32[]{:S(2)}) collective-permute-start(bf16[2,256,128]{2,1,0:T(8,128)(2,1)S(1)} %join_kernel.1.pair_ref), channel_id=1, source_target_pairs={{0,64},{32,96},{64,128},{96,160},{128,192},{160,224},{192,0},{224,... | collective-permute-start | bytes 393224 | tf_op jit(solution)/shard_map/ppermute | solution.py:304
  37.4 8.6 %collective-permute-start.3 = (bf16[2,256,128]{2,1,0:T(8,128)(2,1)S(1)}, bf16[2,256,128]{2,1,0:T(8,128)(2,1)S(1)}, u32[]{:S(2)}, u32[]{:S(2)}) collective-permute-start(bf16[2,256,128]{2,1,0:T(8,128)(2,1)S(1)} %join_kernel.1.pair_ref), channel_id=1, source_target_pairs={{0,32},{32,64},{64,96},{96,128},{128,160},{160,192},{192,224},{224... | collective-permute-start | bytes 393224 | tf_op jit(solution)/shard_map/ppermute | solution.py:304
  40.7 7.2 %collective-permute-start.5 = (bf16[2,256,128]{2,1,0:T(8,128)(2,1)S(1)}, bf16[2,256,128]{2,1,0:T(8,128)(2,1)S(1)}, u32[]{:S(2)}, u32[]{:S(2)}) collective-permute-start(bf16[2,256,128]{2,1,0:T(8,128)(2,1)S(1)} %collective-permute-done.4.pair_ref.two_ref), channel_id=1, source_target_pairs={{0,32},{32,64},{64,96},{96,128},{128,160},{160,192},{192,224},{224... | collective-permute-start | bytes 393224 | tf_op jit(solution)/shard_map/ppermute | solution.py:304
  43.0 10.6 %collective-permute-start.8 = (bf16[7,256,128]{2,1,0:T(8,128)(2,1)}, bf16[7,256,128]{2,1,0:T(8,128)(2,1)S(1)}, u32[]{:S(2)}, u32[]{:S(2)}) collective-permute-start(bf16[7,256,128]{2,1,0:T(8,128)(2,1)} %copy-done.7), channel_id=1, source_target_pairs={{0,16},{16,0},{1,17},{17,1},{2,18},{18,2},{3,19},{19,3},{4,20},{20... | collective-permute-start | bytes 1376264 | tf_op jit(solution)/shard_map/ppermute | solution.py:344
  43.4 4.6 %collective-permute-start.6 = (bf16[256,128]{1,0:T(8,128)(2,1)S(1)}, bf16[256,128]{1,0:T(8,128)(2,1)S(1)}, u32[]{:S(2)}, u32[]{:S(2)}) collective-permute-start(bf16[256,128]{1,0:T(8,128)(2,1)S(1)} %half_kernel.1), channel_id=1, source_target_pairs={{0,64},{32,96},{64,128},{96,160},{128,192},{160,224},{192,0},{224,... | collective-permute-start | bytes 196616 | tf_op jit(solution)/shard_map/ppermute | solution.py:304
  48.0 1.0 %copy-start.1 = (bf16[7,256,128]{2,1,0:T(8,128)(2,1)S(1)}, bf16[7,256,128]{2,1,0:T(8,128)(2,1)}, u32[]{:S(2)}) copy-start(bf16[7,256,128]{2,1,0:T(8,128)(2,1)} %get-tuple-element.42.adj_pair_ref) | copy-start | bytes 1376260
  49.5 3.1 %collective-permute-start.7 = (f32[256,128]{1,0:T(8,128)S(1)}, f32[256,128]{1,0:T(8,128)S(1)}, u32[]{:S(2)}, u32[]{:S(2)}) collective-permute-start(f32[256,128]{1,0:T(8,128)S(1)} %get-tuple-element.45), channel_id=1, source_target_pairs={{0,16},{16,0},{1,17},{17,1},{2,18},{18,2},{3,19},{19,3},{4,20},{20... | collective-permute-start | bytes 393224 | tf_op jit(solution)/shard_map/ppermute | solution.py:362
  53.3 1.4 %collective-permute-start.9 = (bf16[384,256]{1,0:T(8,128)(2,1)S(1)}, bf16[384,256]{1,0:T(8,128)(2,1)S(1)}, u32[]{:S(2)}, u32[]{:S(2)}) collective-permute-start(bf16[384,256]{1,0:T(8,128)(2,1)S(1)} %get-tuple-element.48.both_ref), channel_id=1, source_target_pairs={{0,16},{16,0},{1,17},{17,1},{2,18},{18,2},{3,19},{19,3},{4,20},{20... | collective-permute-start | bytes 589832 | tf_op jit(solution)/shard_map/ppermute | solution.py:385
  54.7 1.0 %copy-start.2 = (bf16[7,256,128]{2,1,0:T(8,128)(2,1)S(1)}, bf16[7,256,128]{2,1,0:T(8,128)(2,1)}, u32[]{:S(2)}) copy-start(bf16[7,256,128]{2,1,0:T(8,128)(2,1)} %get-tuple-element.42.adj_pair_ref) | copy-start | bytes 1376260
  56.5 5.8 %collective-permute-start.10 = (bf16[2,128,256]{2,1,0:T(8,128)(2,1)S(1)}, bf16[2,128,256]{2,1,0:T(8,128)(2,1)S(1)}, u32[]{:S(2)}, u32[]{:S(2)}) collective-permute-start(bf16[2,128,256]{2,1,0:T(8,128)(2,1)S(1)} %get-tuple-element.51), channel_id=1, source_target_pairs={{0,32},{32,64},{64,96},{96,128},{128,160},{160,192},{192,224},{224... | collective-permute-start | bytes 393224 | tf_op jit(solution)/shard_map/ppermute | solution.py:304
  57.5 4.7 %collective-permute-start.11 = (bf16[128,256]{1,0:T(8,128)(2,1)S(1)}, bf16[128,256]{1,0:T(8,128)(2,1)S(1)}, u32[]{:S(2)}, u32[]{:S(2)}) collective-permute-start(bf16[128,256]{1,0:T(8,128)(2,1)S(1)} %get-tuple-element.52), channel_id=1, source_target_pairs={{0,64},{32,96},{64,128},{96,160},{128,192},{160,224},{192,0},{224,... | collective-permute-start | bytes 196616 | tf_op jit(solution)/shard_map/ppermute | solution.py:304
  60.2 6.3 %collective-permute-start.13 = (bf16[2,128,256]{2,1,0:T(8,128)(2,1)S(1)}, bf16[2,128,256]{2,1,0:T(8,128)(2,1)S(1)}, u32[]{:S(2)}, u32[]{:S(2)}) collective-permute-start(bf16[2,128,256]{2,1,0:T(8,128)(2,1)S(1)} %get-tuple-element.53), channel_id=1, source_target_pairs={{0,32},{32,64},{64,96},{96,128},{128,160},{160,192},{192,224},{224... | collective-permute-start | bytes 393224 | tf_op jit(solution)/shard_map/ppermute | solution.py:304
  62.3 7.9 %collective-permute-start.12 = (bf16[2,128,256]{2,1,0:T(8,128)(2,1)S(1)}, bf16[2,128,256]{2,1,0:T(8,128)(2,1)S(1)}, u32[]{:S(2)}, u32[]{:S(2)}) collective-permute-start(bf16[2,128,256]{2,1,0:T(8,128)(2,1)S(1)} %relay_kernel.2), channel_id=1, source_target_pairs={{0,64},{32,96},{64,128},{96,160},{128,192},{160,224},{192,0},{224,... | collective-permute-start | bytes 393224 | tf_op jit(solution)/shard_map/ppermute | solution.py:304
  70.3 2.1 %collective-permute-start.14 = (f32[128,256]{1,0:T(8,128)S(1)}, f32[128,256]{1,0:T(8,128)S(1)}, u32[]{:S(2)}, u32[]{:S(2)}) collective-permute-start(f32[128,256]{1,0:T(8,128)S(1)} %get-tuple-element.55), channel_id=1, source_target_pairs={{0,16},{16,0},{1,17},{17,1},{2,18},{18,2},{3,19},{19,3},{4,20},{20... | collective-permute-start | bytes 393224 | tf_op jit(solution)/shard_map/ppermute | solution.py:381
  72.9 2.0 %collective-permute-start.15 = (bf16[8,256,128]{2,1,0:T(8,128)(2,1)S(1)}, bf16[8,256,128]{2,1,0:T(8,128)(2,1)S(1)}, u32[]{:S(2)}, u32[]{:S(2)}) collective-permute-start(bf16[8,256,128]{2,1,0:T(8,128)(2,1)S(1)} %get-tuple-element.57), channel_id=1, source_target_pairs={{0,16},{16,0},{1,17},{17,1},{2,18},{18,2},{3,19},{19,3},{4,20},{20... | collective-permute-start | bytes 1572872 | tf_op jit(solution)/shard_map/ppermute | solution.py:394
  75.0 22.0 %all-to-all-start.1 = ((bf16[16,128,256]{2,1,0:T(8,128)(2,1)}), bf16[16,128,256]{2,1,0:T(8,128)(2,1)S(1)}, u32[]{:S(2)}, u32[]{:S(2)}) async-start(bf16[16,128,256]{2,1,0:T(8,128)(2,1)} %get-tuple-element.66), calls=%async_computation.1 | async-start | bytes 2097152 | tf_op jit(solution)/shard_map/all_to_all | solution.py:410
  78.7 8.7 %collective-permute-start.16 = (bf16[2,256,128]{2,1,0:T(8,128)(2,1)S(1)}, bf16[2,256,128]{2,1,0:T(8,128)(2,1)S(1)}, u32[]{:S(2)}, u32[]{:S(2)}) collective-permute-start(bf16[2,256,128]{2,1,0:T(8,128)(2,1)S(1)} %get-tuple-element.61), channel_id=1, source_target_pairs={{0,32},{32,64},{64,96},{96,128},{128,160},{160,192},{192,224},{224... | collective-permute-start | bytes 393224 | tf_op jit(solution)/shard_map/ppermute | solution.py:304
  81.7 5.7 %collective-permute-start.17 = (bf16[256,128]{1,0:T(8,128)(2,1)S(1)}, bf16[256,128]{1,0:T(8,128)(2,1)S(1)}, u32[]{:S(2)}, u32[]{:S(2)}) collective-permute-start(bf16[256,128]{1,0:T(8,128)(2,1)S(1)} %get-tuple-element.62), channel_id=1, source_target_pairs={{0,64},{32,96},{64,128},{96,160},{128,192},{160,224},{192,0},{224,... | collective-permute-start | bytes 196616 | tf_op jit(solution)/shard_map/ppermute | solution.py:304
  86.1 5.6 %collective-permute-start.19 = (bf16[2,256,128]{2,1,0:T(8,128)(2,1)S(1)}, bf16[2,256,128]{2,1,0:T(8,128)(2,1)S(1)}, u32[]{:S(2)}, u32[]{:S(2)}) collective-permute-start(bf16[2,256,128]{2,1,0:T(8,128)(2,1)S(1)} %get-tuple-element.63), channel_id=1, source_target_pairs={{0,32},{32,64},{64,96},{96,128},{128,160},{160,192},{192,224},{224... | collective-permute-start | bytes 393224 | tf_op jit(solution)/shard_map/ppermute | solution.py:304
  87.4 6.5 %collective-permute-start.18 = (bf16[2,256,128]{2,1,0:T(8,128)(2,1)S(1)}, bf16[2,256,128]{2,1,0:T(8,128)(2,1)S(1)}, u32[]{:S(2)}, u32[]{:S(2)}) collective-permute-start(bf16[2,256,128]{2,1,0:T(8,128)(2,1)S(1)} %relay_kernel.3), channel_id=1, source_target_pairs={{0,64},{32,96},{64,128},{96,160},{128,192},{160,224},{192,0},{224,... | collective-permute-start | bytes 393224 | tf_op jit(solution)/shard_map/ppermute | solution.py:304
  94.0 4.0 %collective-permute-start.20 = (f32[256,128]{1,0:T(8,128)S(1)}, f32[256,128]{1,0:T(8,128)S(1)}, u32[]{:S(2)}, u32[]{:S(2)}) collective-permute-start(f32[256,128]{1,0:T(8,128)S(1)} %get-tuple-element.65), channel_id=1, source_target_pairs={{0,16},{16,0},{1,17},{17,1},{2,18},{18,2},{3,19},{19,3},{4,20},{20... | collective-permute-start | bytes 393224 | tf_op jit(solution)/shard_map/ppermute | solution.py:381

commit v16 on v15

--- a/solution.py
+++ b/solution.py
@@ -62,7 +62,7 @@
 
 def adjacency_kernel(
     count_ref, dst_hbm, src_hbm, weight_ref, adj_ref, send_ref, back_ref, inv_ref, flag_ref,
-    dst_ref, src_ref, buf, acc, sel_ref, in_sems, sems,
+    dst_ref, src_ref, buf, acc, sel_ref, send_buf, back_buf, in_sems, out_sems, sems,
 ):
     count = count_ref[0]
     slots = weight_ref.shape[0]
@@ -111,9 +111,15 @@
             total = total + acc[owner]
         adj_ref[owner] = acc[owner].astype(F32).astype(BF16)
     for slot, owner in enumerate(sources(lax.axis_index("z"), 1 - lax.axis_index("c"), groups // 2)):
-        send_ref[slot] = adj_ref[owner]
+        send_buf[slot] = adj_ref[owner]
     for slot, owner in enumerate(owners(lax.axis_index("z"), 1 - lax.axis_index("c"), groups // 2)[1:]):
-        back_ref[slot] = adj_ref[owner]
+        back_buf[slot] = adj_ref[owner]
+    outs = [
+        pltpu.make_async_copy(send_buf, send_ref, out_sems.at[0]),
+        pltpu.make_async_copy(back_buf, back_ref, out_sems.at[1]),
+    ]
+    for copy in outs:
+        copy.start()
     degree = jnp.sum(total.astype(F32), axis=1, keepdims=True)
     inv_ref[...] = jnp.broadcast_to(1.0 / jnp.maximum(degree, 1.0), inv_ref.shape)
     row = lax.broadcasted_iota(jnp.int32, flag_ref.shape, 0)
@@ -121,6 +127,8 @@
     for owner in range(groups):
         flags = jnp.where(row == owner, sel_ref[owner].astype(F32), flags)
     flag_ref[...] = flags
+    for copy in outs:
+        copy.wait()
 
 
 def wide_dot(x_ref, w_ref):
@@ -144,6 +152,17 @@
 
 def half_kernel(pair_ref, half_ref):
     half_ref[...] = pair_ref[lax.axis_index("c")]
+
+
+def fetch_kernel(one_ref, pair_hbm, back_hbm, one_same_ref, pair_ref, back_ref, sems):
+    copies = [
+        pltpu.make_async_copy(pair_hbm, pair_ref, sems.at[0]),
+        pltpu.make_async_copy(back_hbm, back_ref, sems.at[1]),
+    ]
+    for copy in copies:
+        copy.start()
+    for copy in copies:
+        copy.wait()
 
 
 def self_kernel(x_ref, w_ref, z_ref):
@@ -330,12 +349,16 @@
             ((groups, T), F32),
         ],
         in_specs=[SMEM, HBM, HBM, HBM],
+        out_specs=[VMEM, HBM, HBM, VMEM, VMEM],
         scratch=[
             pltpu.SMEM(tile_dst.shape, jnp.int32),
             pltpu.SMEM(tile_src.shape, jnp.int32),
             pltpu.VMEM((slots, T, T), jnp.int32),
             pltpu.VMEM((groups, rows, T), jnp.int32),
             pltpu.SMEM((groups,), jnp.int32),
+            pltpu.VMEM((chips - 1, rows, T), BF16),
+            pltpu.VMEM((chips - 1, rows, T), BF16),
+            pltpu.SemaphoreType.DMA((2,)),
             pltpu.SemaphoreType.DMA((2,)),
             pltpu.SemaphoreType.DMA((slots // CHUNK,)),
         ],
@@ -354,6 +377,15 @@
     two, one = along(pair, 2, chips), along(pair, 1, chips)
     (half,) = call(half_kernel, (two,), [(y.shape, BF16)])
     three, far = along(two, 1, chips), along(half, 2, chips)
+    one, adj_pair, adj_back = call(
+        fetch_kernel,
+        (one, adj_pair, adj_back),
+        [(one.shape, BF16), (adj_pair.shape, BF16), (adj_back.shape, BF16)],
+        in_specs=[ANY, HBM, HBM],
+        out_specs=[ANY, VMEM, VMEM],
+        scratch=[pltpu.SemaphoreType.DMA((2,))],
+        aliases={0: 0},
+    )
     mine, theirs = call(
         aggregate_kernel,
         (flags, flags_pair, adj, adj_pair, pair, one, two, three, far),

time: 99.2 us -> 96 us (0.968)
  local copies, waits for them, and re-layouts: 3.87 us -> 0.02 us
  Pallas kernels: 11.5 us -> 12.7 us
    unnamed x16 -> x6, local copies, waits for them, and re-layouts: 3.87 us -> 0.02 us
    ppermute x12, starting transfers between devices: 33.5 us -> 32.3 us  [along(): return lax.ppermute(value, ('z', 'c'), pairs)]
    pallas_call x18 -> x19, Pallas kernels: 11.5 us -> 12.7 us  [call(): pl.pallas_call(kernel, out_shape=shapes, in_specs=in_specs or [VMEM] * le...]
    ppermute x1, starting transfers between devices: 0.01 us -> 1.13 us  [per_device(): lax.ppermute(adj_send, 'c', swap)]
  transfers between devices with their start and end apart: 23 -> 23, of which waited for: 13 -> 15; matrix products, arithmetic and copies ran while one was open for 0% -> 0% of each run, Pallas kernels for 7% -> 8%
where the time goes in v16:
time: 96 us; the launch traced here: 95.7 us
  starting transfers between devices  56 us (58%)
  waiting for transfers between devices  25.6 us (27%)
  Pallas kernels  12.7 us (13%)
  between operations  1.43 us (1%)
    ppermute x12, starting transfers between devices, along(): return lax.ppermute(value, ('z', 'c'), pairs)  32.3 us
    pallas_call x19, Pallas kernels, call(): pl.pallas_call(kernel, out_shape=shapes, in_specs=in_specs or [VMEM] * le...  12.7 us
    ppermute x12, waiting for transfers between devices, along(): return lax.ppermute(value, ('z', 'c'), pairs)  11.1 us
    all_to_all x1, waiting for transfers between devices, per_device(): x_all = lax.all_to_all(x_pay, 'f', 0, 0, tiled=True)  9.36 us
    all_to_all x1, starting transfers between devices, per_device(): x_all = lax.all_to_all(x_pay, 'f', 0, 0, tiled=True)  7.6 us
    ppermute x2, starting transfers between devices, reduce(): return (mine, lax.ppermute(theirs, 'c', swap))  4.66 us
    all_to_all x1, starting transfers between devices, per_device(): p_all = lax.all_to_all(p_pay, 'f', 0, 0, tiled=True)  3.66 us
    ppermute x1, starting transfers between devices, per_device(): lax.ppermute(y, 'c', swap)  2.7 us
  transfers between devices with their start and end apart: 23, of which 15 were waited for; matrix products, arithmetic and copies ran while one was open for 0% of the time, Pallas kernels for 8%

profile of v16, /device:TPU:1, one launch (start us, length us, event | category | flops | bytes accessed | tf_op | source)
XLA Modules:
  0.0 95.7 jit_solution(5765455751751177647)
XLA Ops:
  0.6 2.0 %spread_kernel.1 = bf16[16,256,128]{2,1,0:T(8,128)(2,1)} custom-call(bf16[256,128]{1,0:T(8,128)(2,1)} %x_hbm.1), custom_call_target="tpu_custom_call" | custom-call | tf_op jit(solution)/shard_map/spread_kernel/pallas_call | solution.py:308
  2.7 7.6 %all-to-all-start = ((bf16[16,256,128]{2,1,0:T(8,128)(2,1)}), bf16[16,256,128]{2,1,0:T(8,128)(2,1)S(1)}, u32[]{:S(2)}, u32[]{:S(2)}) async-start(bf16[16,256,128]{2,1,0:T(8,128)(2,1)} %spread_kernel.1), calls=%async_computation | async-start | bytes 2097152 | tf_op jit(solution)/shard_map/all_to_all | solution.py:340
  10.9 3.0 %adjacency_kernel.1 = (bf16[16,256,128]{2,1,0:T(8,128)(2,1)S(1)}, bf16[7,256,128]{2,1,0:T(8,128)(2,1)}, bf16[7,256,128]{2,1,0:T(8,128)(2,1)}, f32[256,128]{1,0:T(8,128)S(1)}, f32[16,128]{1,0:T(8,128)S(1)}) custom-call(s32[1]{0:T(128)S(6)} %copy.22.count_ref, s32[1,80]{1,0:T(1,128)} %dst_hbm.1, s32[1,80]{1,0:T(1,128)} %src_hbm.1, s32[80,128,128]{2,1,0:T(8,128)} %bitcast.1), custom_call_target="tpu_custom_call" | custom-call | tf_op jit(solution)/shard_map/adjacency_kernel/pallas_call | solution.py:308
  14.0 1.1 %collective-permute-start.1 = (bf16[7,256,128]{2,1,0:T(8,128)(2,1)}, bf16[7,256,128]{2,1,0:T(8,128)(2,1)}, u32[]{:S(2)}, u32[]{:S(2)}) collective-permute-start(bf16[7,256,128]{2,1,0:T(8,128)(2,1)} %get-tuple-element.42), channel_id=1, source_target_pairs={{0,16},{16,0},{1,17},{17,1},{2,18},{18,2},{3,19},{19,3},{4,20},{20... | collective-permute-start | bytes 1376264 | tf_op jit(solution)/shard_map/ppermute | solution.py:367
  15.6 1.0 collective-permute-done.pair_flag_ref
  16.9 9.4 %all-to-all-done.x_ref = bf16[16,256,128]{2,1,0:T(8,128)(2,1)S(1)} async-done(((bf16[16,256,128]{2,1,0:T(8,128)(2,1)}), bf16[16,256,128]{2,1,0:T(8,128)(2,1)S(1)}, u32[]{:S(2)}, u32[]{:S(2)}) %all-to-all-start) | async-done | bytes 1048608 | tf_op jit(solution)/shard_map/all_to_all | solution.py:340
  26.7 2.7 %collective-permute-start.2 = (bf16[256,128]{1,0:T(8,128)(2,1)S(1)}, bf16[256,128]{1,0:T(8,128)(2,1)S(1)}, u32[]{:S(2)}, u32[]{:S(2)}) collective-permute-start(bf16[256,128]{1,0:T(8,128)(2,1)S(1)} %get-tuple-element.45.y_ref), channel_id=1, source_target_pairs={{0,16},{16,0},{1,17},{17,1},{2,18},{18,2},{3,19},{19,3},{4,20},{20... | collective-permute-start | bytes 196616 | tf_op jit(solution)/shard_map/ppermute | solution.py:376
  29.4 0.9 collective-permute-done.2.y_pair_ref
  30.3 6.1 %collective-permute-start.5 = (bf16[2,256,128]{2,1,0:T(8,128)(2,1)S(1)}, bf16[2,256,128]{2,1,0:T(8,128)(2,1)S(1)}, u32[]{:S(2)}, u32[]{:S(2)}) collective-permute-start(bf16[2,256,128]{2,1,0:T(8,128)(2,1)S(1)} %join_kernel.1.pair_ref), channel_id=1, source_target_pairs={{0,64},{32,96},{64,128},{96,160},{128,192},{160,224},{192,0},{224,... | collective-permute-start | bytes 393224 | tf_op jit(solution)/shard_map/ppermute | solution.py:323
  37.1 2.6 %collective-permute-done.5.pair_ref.two_ref = bf16[2,256,128]{2,1,0:T(8,128)(2,1)S(1)} collective-permute-done((bf16[2,256,128]{2,1,0:T(8,128)(2,1)S(1)}, bf16[2,256,128]{2,1,0:T(8,128)(2,1)S(1)}, u32[]{:S(2)}, u32[]{:S(2)}) %collective-permute-start.5) | collective-permute-done | bytes 131104 | tf_op jit(solution)/shard_map/ppermute | solution.py:323
  39.7 2.3 %collective-permute-start.6 = (bf16[2,256,128]{2,1,0:T(8,128)(2,1)S(1)}, bf16[2,256,128]{2,1,0:T(8,128)(2,1)S(1)}, u32[]{:S(2)}, u32[]{:S(2)}) collective-permute-start(bf16[2,256,128]{2,1,0:T(8,128)(2,1)S(1)} %collective-permute-done.5.pair_ref.two_ref), channel_id=1, source_target_pairs={{0,32},{32,64},{64,96},{96,128},{128,160},{160,192},{192,224},{224... | collective-permute-start | bytes 393224 | tf_op jit(solution)/shard_map/ppermute | solution.py:323
  42.0 1.8 %collective-permute-start.7 = (bf16[256,128]{1,0:T(8,128)(2,1)S(1)}, bf16[256,128]{1,0:T(8,128)(2,1)S(1)}, u32[]{:S(2)}, u32[]{:S(2)}) collective-permute-start(bf16[256,128]{1,0:T(8,128)(2,1)S(1)} %half_kernel.1), channel_id=1, source_target_pairs={{0,64},{32,96},{64,128},{96,160},{128,192},{160,224},{192,0},{224,... | collective-permute-start | bytes 196616 | tf_op jit(solution)/shard_map/ppermute | solution.py:323
  43.8 1.2 %fetch_kernel.1 = (bf16[2,256,128]{2,1,0:T(8,128)(2,1)S(1)}, bf16[7,256,128]{2,1,0:T(8,128)(2,1)S(1)}, bf16[7,256,128]{2,1,0:T(8,128)(2,1)S(1)}) custom-call(bf16[2,256,128]{2,1,0:T(8,128)(2,1)S(1)} %collective-permute-done.3.one_ref, bf16[7,256,128]{2,1,0:T(8,128)(2,1)} %get-tuple-element.46.pair_hbm, ...), custom_call_target="tpu_custom_call", output_to_operand_aliasing={{0}: (0, {})} | custom-call | tf_op jit(solution)/shard_map/fetch_kernel/pallas_call | solution.py:308
  45.0 1.4 %collective-permute-done.7.far_ref = bf16[256,128]{1,0:T(8,128)(2,1)S(1)} collective-permute-done((bf16[256,128]{1,0:T(8,128)(2,1)S(1)}, bf16[256,128]{1,0:T(8,128)(2,1)S(1)}, u32[]{:S(2)}, u32[]{:S(2)}) %collective-permute-start.7) | collective-permute-done | bytes 65568 | tf_op jit(solution)/shard_map/ppermute | solution.py:323
  46.9 2.7 %collective-permute-start.8 = (f32[256,128]{1,0:T(8,128)S(1)}, f32[256,128]{1,0:T(8,128)S(1)}, u32[]{:S(2)}, u32[]{:S(2)}) collective-permute-start(f32[256,128]{1,0:T(8,128)S(1)} %get-tuple-element.51), channel_id=1, source_target_pairs={{0,16},{16,0},{1,17},{17,1},{2,18},{18,2},{3,19},{19,3},{4,20},{20... | collective-permute-start | bytes 393224 | tf_op jit(solution)/shard_map/ppermute | solution.py:394
  51.6 1.1 %collective-permute-done.9.both_pair_ref = bf16[384,256]{1,0:T(8,128)(2,1)S(1)} collective-permute-done((bf16[384,256]{1,0:T(8,128)(2,1)S(1)}, bf16[384,256]{1,0:T(8,128)(2,1)S(1)}, u32[]{:S(2)}, u32[]{:S(2)}) %collective-permute-start.9) | collective-permute-done | bytes 196640 | tf_op jit(solution)/shard_map/ppermute | solution.py:417
  53.4 1.1 %collective-permute-start.10 = (bf16[2,128,256]{2,1,0:T(8,128)(2,1)S(1)}, bf16[2,128,256]{2,1,0:T(8,128)(2,1)S(1)}, u32[]{:S(2)}, u32[]{:S(2)}) collective-permute-start(bf16[2,128,256]{2,1,0:T(8,128)(2,1)S(1)} %get-tuple-element.57), channel_id=1, source_target_pairs={{0,32},{32,64},{64,96},{96,128},{128,160},{160,192},{192,224},{224... | collective-permute-start | bytes 393224 | tf_op jit(solution)/shard_map/ppermute | solution.py:323
  54.5 2.7 %collective-permute-start.11 = (bf16[128,256]{1,0:T(8,128)(2,1)S(1)}, bf16[128,256]{1,0:T(8,128)(2,1)S(1)}, u32[]{:S(2)}, u32[]{:S(2)}) collective-permute-start(bf16[128,256]{1,0:T(8,128)(2,1)S(1)} %get-tuple-element.58), channel_id=1, source_target_pairs={{0,64},{32,96},{64,128},{96,160},{128,192},{160,224},{192,0},{224,... | collective-permute-start | bytes 196616 | tf_op jit(solution)/shard_map/ppermute | solution.py:323
  57.2 1.9 %collective-permute-start.13 = (bf16[2,128,256]{2,1,0:T(8,128)(2,1)S(1)}, bf16[2,128,256]{2,1,0:T(8,128)(2,1)S(1)}, u32[]{:S(2)}, u32[]{:S(2)}) collective-permute-start(bf16[2,128,256]{2,1,0:T(8,128)(2,1)S(1)} %get-tuple-element.59), channel_id=1, source_target_pairs={{0,32},{32,64},{64,96},{96,128},{128,160},{160,192},{192,224},{224... | collective-permute-start | bytes 393224 | tf_op jit(solution)/shard_map/ppermute | solution.py:323
  59.5 3.9 %collective-permute-start.12 = (bf16[2,128,256]{2,1,0:T(8,128)(2,1)S(1)}, bf16[2,128,256]{2,1,0:T(8,128)(2,1)S(1)}, u32[]{:S(2)}, u32[]{:S(2)}) collective-permute-start(bf16[2,128,256]{2,1,0:T(8,128)(2,1)S(1)} %relay_kernel.2), channel_id=1, source_target_pairs={{0,64},{32,96},{64,128},{96,160},{128,192},{160,224},{192,0},{224,... | collective-permute-start | bytes 393224 | tf_op jit(solution)/shard_map/ppermute | solution.py:323
  63.4 3.2 %collective-permute-done.12.two_ref = bf16[2,128,256]{2,1,0:T(8,128)(2,1)S(1)} collective-permute-done((bf16[2,128,256]{2,1,0:T(8,128)(2,1)S(1)}, bf16[2,128,256]{2,1,0:T(8,128)(2,1)S(1)}, u32[]{:S(2)}, u32[]{:S(2)}) %collective-permute-start.12) | collective-permute-done | bytes 131104 | tf_op jit(solution)/shard_map/ppermute | solution.py:323
  66.7 1.6 %collective-permute-start.14 = (f32[128,256]{1,0:T(8,128)S(1)}, f32[128,256]{1,0:T(8,128)S(1)}, u32[]{:S(2)}, u32[]{:S(2)}) collective-permute-start(f32[128,256]{1,0:T(8,128)S(1)} %get-tuple-element.61), channel_id=1, source_target_pairs={{0,16},{16,0},{1,17},{17,1},{2,18},{18,2},{3,19},{19,3},{4,20},{20... | collective-permute-start | bytes 393224 | tf_op jit(solution)/shard_map/ppermute | solution.py:413
  68.3 1.0 %collective-permute-done.14.came_ref = f32[128,256]{1,0:T(8,128)S(1)} collective-permute-done((f32[128,256]{1,0:T(8,128)S(1)}, f32[128,256]{1,0:T(8,128)S(1)}, u32[]{:S(2)}, u32[]{:S(2)}) %collective-permute-start.14) | collective-permute-done | bytes 131104 | tf_op jit(solution)/shard_map/ppermute | solution.py:413
  70.3 1.3 %feature_grad_kernel.1.payload_ref = bf16[16,128,256]{2,1,0:T(8,128)(2,1)} custom-call(bf16[384,256]{1,0:T(8,128)(2,1)S(1)} %get-tuple-element.54.both_ref, bf16[128,256]{1,0:T(8,128)(2,1)S(1)} %get-tuple-element.64.bt_ref, bf16[2048,128]{1,0:T(8,128)(2,1)S(1)} %copy-done, bf16[2048,128]{1,0:T(8,128)(2,1)S(1)} %copy-done.1), custom_call_target="tpu_custom_call" | custom-call | tf_op jit(solution)/shard_map/feature_grad_kernel/pallas_call | solution.py:308
  72.0 3.7 %all-to-all-start.1 = ((bf16[16,128,256]{2,1,0:T(8,128)(2,1)}), bf16[16,128,256]{2,1,0:T(8,128)(2,1)S(1)}, u32[]{:S(2)}, u32[]{:S(2)}) async-start(bf16[16,128,256]{2,1,0:T(8,128)(2,1)} %get-tuple-element.72), calls=%async_computation.1 | async-start | bytes 2097152 | tf_op jit(solution)/shard_map/all_to_all | solution.py:442
  75.6 2.9 %collective-permute-start.16 = (bf16[2,256,128]{2,1,0:T(8,128)(2,1)S(1)}, bf16[2,256,128]{2,1,0:T(8,128)(2,1)S(1)}, u32[]{:S(2)}, u32[]{:S(2)}) collective-permute-start(bf16[2,256,128]{2,1,0:T(8,128)(2,1)S(1)} %get-tuple-element.67), channel_id=1, source_target_pairs={{0,32},{32,64},{64,96},{96,128},{128,160},{160,192},{192,224},{224... | collective-permute-start | bytes 393224 | tf_op jit(solution)/shard_map/ppermute | solution.py:323
  78.6 4.5 %collective-permute-start.17 = (bf16[256,128]{1,0:T(8,128)(2,1)S(1)}, bf16[256,128]{1,0:T(8,128)(2,1)S(1)}, u32[]{:S(2)}, u32[]{:S(2)}) collective-permute-start(bf16[256,128]{1,0:T(8,128)(2,1)S(1)} %get-tuple-element.68), channel_id=1, source_target_pairs={{0,64},{32,96},{64,128},{96,160},{128,192},{160,224},{192,0},{224,... | collective-permute-start | bytes 196616 | tf_op jit(solution)/shard_map/ppermute | solution.py:323
  83.1 1.2 %collective-permute-done.17.far_ref = bf16[256,128]{1,0:T(8,128)(2,1)S(1)} collective-permute-done((bf16[256,128]{1,0:T(8,128)(2,1)S(1)}, bf16[256,128]{1,0:T(8,128)(2,1)S(1)}, u32[]{:S(2)}, u32[]{:S(2)}) %collective-permute-start.17) | collective-permute-done | bytes 65568 | tf_op jit(solution)/shard_map/ppermute | solution.py:323
  84.4 4.3 %collective-permute-start.18 = (bf16[2,256,128]{2,1,0:T(8,128)(2,1)S(1)}, bf16[2,256,128]{2,1,0:T(8,128)(2,1)S(1)}, u32[]{:S(2)}, u32[]{:S(2)}) collective-permute-start(bf16[2,256,128]{2,1,0:T(8,128)(2,1)S(1)} %relay_kernel.3), channel_id=1, source_target_pairs={{0,64},{32,96},{64,128},{96,160},{128,192},{160,224},{192,0},{224,... | collective-permute-start | bytes 393224 | tf_op jit(solution)/shard_map/ppermute | solution.py:323
  88.7 2.2 %collective-permute-done.18.two_ref = bf16[2,256,128]{2,1,0:T(8,128)(2,1)S(1)} collective-permute-done((bf16[2,256,128]{2,1,0:T(8,128)(2,1)S(1)}, bf16[2,256,128]{2,1,0:T(8,128)(2,1)S(1)}, u32[]{:S(2)}, u32[]{:S(2)}) %collective-permute-start.18) | collective-permute-done | bytes 131104 | tf_op jit(solution)/shard_map/ppermute | solution.py:323
  91.0 3.0 %collective-permute-start.20 = (f32[256,128]{1,0:T(8,128)S(1)}, f32[256,128]{1,0:T(8,128)S(1)}, u32[]{:S(2)}, u32[]{:S(2)}) collective-permute-start(f32[256,128]{1,0:T(8,128)S(1)} %get-tuple-element.71), channel_id=1, source_target_pairs={{0,16},{16,0},{1,17},{17,1},{2,18},{18,2},{3,19},{19,3},{4,20},{20... | collective-permute-start | bytes 393224 | tf_op jit(solution)/shard_map/ppermute | solution.py:413
  94.0 0.8 sum_kernel.1.done_ref
  (39 shorter events, 8.1 us)
Async XLA Ops:
  0.6 25.6 %copy-start.1 = (bf16[2048,128]{1,0:T(8,128)(2,1)S(1)}, bf16[2048,128]{1,0:T(8,128)(2,1)}, u32[]{:S(2)}) copy-start(bf16[2048,128]{1,0:T(8,128)(2,1)} %wn_ref.1) | copy-start | bytes 1572868
  2.7 23.6 %all-to-all-start = ((bf16[16,256,128]{2,1,0:T(8,128)(2,1)}), bf16[16,256,128]{2,1,0:T(8,128)(2,1)S(1)}, u32[]{:S(2)}, u32[]{:S(2)}) async-start(bf16[16,256,128]{2,1,0:T(8,128)(2,1)} %spread_kernel.1), calls=%async_computation | async-start | bytes 2097152 | tf_op jit(solution)/shard_map/all_to_all | solution.py:340
  10.9 38.6 %copy-start = (bf16[2048,128]{1,0:T(8,128)(2,1)S(1)}, bf16[2048,128]{1,0:T(8,128)(2,1)}, u32[]{:S(2)}) copy-start(bf16[2048,128]{1,0:T(8,128)(2,1)} %ws_ref.1) | copy-start | bytes 1572868
  10.9 39.6 %copy-start.2 = (bf16[256,128]{1,0:T(8,128)(2,1)S(1)}, bf16[256,128]{1,0:T(8,128)(2,1)}, u32[]{:S(2)}) copy-start(bf16[256,128]{1,0:T(8,128)(2,1)} %og_ref.1) | copy-start | bytes 196612
  14.0 2.9 %collective-permute-start.1 = (bf16[7,256,128]{2,1,0:T(8,128)(2,1)}, bf16[7,256,128]{2,1,0:T(8,128)(2,1)}, u32[]{:S(2)}, u32[]{:S(2)}) collective-permute-start(bf16[7,256,128]{2,1,0:T(8,128)(2,1)} %get-tuple-element.42), channel_id=1, source_target_pairs={{0,16},{16,0},{1,17},{17,1},{2,18},{18,2},{3,19},{19,3},{4,20},{20... | collective-permute-start | bytes 1376264 | tf_op jit(solution)/shard_map/ppermute | solution.py:367
  15.1 28.7 %collective-permute-start.4 = (bf16[7,256,128]{2,1,0:T(8,128)(2,1)}, bf16[7,256,128]{2,1,0:T(8,128)(2,1)}, u32[]{:S(2)}, u32[]{:S(2)}) collective-permute-start(bf16[7,256,128]{2,1,0:T(8,128)(2,1)} %get-tuple-element.47), channel_id=1, source_target_pairs={{0,16},{16,0},{1,17},{17,1},{2,18},{18,2},{3,19},{19,3},{4,20},{20... | collective-permute-start | bytes 1376264 | tf_op jit(solution)/shard_map/ppermute | solution.py:367
  15.2 1.4 %collective-permute-start = (f32[16,128]{1,0:T(8,128)S(1)}, f32[16,128]{1,0:T(8,128)S(1)}, u32[]{:S(2)}, u32[]{:S(2)}) collective-permute-start(f32[16,128]{1,0:T(8,128)S(1)} %get-tuple-element.41.flag_ref), channel_id=1, source_target_pairs={{0,16},{16,0},{1,17},{17,1},{2,18},{18,2},{3,19},{19,3},{4,20},{20... | collective-permute-start | bytes 24584 | tf_op jit(solution)/shard_map/ppermute | solution.py:370
  26.7 3.6 %collective-permute-start.2 = (bf16[256,128]{1,0:T(8,128)(2,1)S(1)}, bf16[256,128]{1,0:T(8,128)(2,1)S(1)}, u32[]{:S(2)}, u32[]{:S(2)}) collective-permute-start(bf16[256,128]{1,0:T(8,128)(2,1)S(1)} %get-tuple-element.45.y_ref), channel_id=1, source_target_pairs={{0,16},{16,0},{1,17},{17,1},{2,18},{18,2},{3,19},{19,3},{4,20},{20... | collective-permute-start | bytes 196616 | tf_op jit(solution)/shard_map/ppermute | solution.py:376
  30.3 9.4 %collective-permute-start.5 = (bf16[2,256,128]{2,1,0:T(8,128)(2,1)S(1)}, bf16[2,256,128]{2,1,0:T(8,128)(2,1)S(1)}, u32[]{:S(2)}, u32[]{:S(2)}) collective-permute-start(bf16[2,256,128]{2,1,0:T(8,128)(2,1)S(1)} %join_kernel.1.pair_ref), channel_id=1, source_target_pairs={{0,64},{32,96},{64,128},{96,160},{128,192},{160,224},{192,0},{224,... | collective-permute-start | bytes 393224 | tf_op jit(solution)/shard_map/ppermute | solution.py:323
  36.4 7.4 %collective-permute-start.3 = (bf16[2,256,128]{2,1,0:T(8,128)(2,1)S(1)}, bf16[2,256,128]{2,1,0:T(8,128)(2,1)S(1)}, u32[]{:S(2)}, u32[]{:S(2)}) collective-permute-start(bf16[2,256,128]{2,1,0:T(8,128)(2,1)S(1)} %join_kernel.1.pair_ref), channel_id=1, source_target_pairs={{0,32},{32,64},{64,96},{96,128},{128,160},{160,192},{192,224},{224... | collective-permute-start | bytes 393224 | tf_op jit(solution)/shard_map/ppermute | solution.py:323
  39.7 6.7 %collective-permute-start.6 = (bf16[2,256,128]{2,1,0:T(8,128)(2,1)S(1)}, bf16[2,256,128]{2,1,0:T(8,128)(2,1)S(1)}, u32[]{:S(2)}, u32[]{:S(2)}) collective-permute-start(bf16[2,256,128]{2,1,0:T(8,128)(2,1)S(1)} %collective-permute-done.5.pair_ref.two_ref), channel_id=1, source_target_pairs={{0,32},{32,64},{64,96},{96,128},{128,160},{160,192},{192,224},{224... | collective-permute-start | bytes 393224 | tf_op jit(solution)/shard_map/ppermute | solution.py:323
  42.0 4.4 %collective-permute-start.7 = (bf16[256,128]{1,0:T(8,128)(2,1)S(1)}, bf16[256,128]{1,0:T(8,128)(2,1)S(1)}, u32[]{:S(2)}, u32[]{:S(2)}) collective-permute-start(bf16[256,128]{1,0:T(8,128)(2,1)S(1)} %half_kernel.1), channel_id=1, source_target_pairs={{0,64},{32,96},{64,128},{96,160},{128,192},{160,224},{192,0},{224,... | collective-permute-start | bytes 196616 | tf_op jit(solution)/shard_map/ppermute | solution.py:323
  46.9 3.6 %collective-permute-start.8 = (f32[256,128]{1,0:T(8,128)S(1)}, f32[256,128]{1,0:T(8,128)S(1)}, u32[]{:S(2)}, u32[]{:S(2)}) collective-permute-start(f32[256,128]{1,0:T(8,128)S(1)} %get-tuple-element.51), channel_id=1, source_target_pairs={{0,16},{16,0},{1,17},{17,1},{2,18},{18,2},{3,19},{19,3},{4,20},{20... | collective-permute-start | bytes 393224 | tf_op jit(solution)/shard_map/ppermute | solution.py:394
  51.3 1.4 %collective-permute-start.9 = (bf16[384,256]{1,0:T(8,128)(2,1)S(1)}, bf16[384,256]{1,0:T(8,128)(2,1)S(1)}, u32[]{:S(2)}, u32[]{:S(2)}) collective-permute-start(bf16[384,256]{1,0:T(8,128)(2,1)S(1)} %get-tuple-element.54.both_ref), channel_id=1, source_target_pairs={{0,16},{16,0},{1,17},{17,1},{2,18},{18,2},{3,19},{19,3},{4,20},{20... | collective-permute-start | bytes 589832 | tf_op jit(solution)/shard_map/ppermute | solution.py:417
  53.4 6.1 %collective-permute-start.10 = (bf16[2,128,256]{2,1,0:T(8,128)(2,1)S(1)}, bf16[2,128,256]{2,1,0:T(8,128)(2,1)S(1)}, u32[]{:S(2)}, u32[]{:S(2)}) collective-permute-start(bf16[2,128,256]{2,1,0:T(8,128)(2,1)S(1)} %get-tuple-element.57), channel_id=1, source_target_pairs={{0,32},{32,64},{64,96},{96,128},{128,160},{160,192},{192,224},{224... | collective-permute-start | bytes 393224 | tf_op jit(solution)/shard_map/ppermute | solution.py:323
  54.5 5.0 %collective-permute-start.11 = (bf16[128,256]{1,0:T(8,128)(2,1)S(1)}, bf16[128,256]{1,0:T(8,128)(2,1)S(1)}, u32[]{:S(2)}, u32[]{:S(2)}) collective-permute-start(bf16[128,256]{1,0:T(8,128)(2,1)S(1)} %get-tuple-element.58), channel_id=1, source_target_pairs={{0,64},{32,96},{64,128},{96,160},{128,192},{160,224},{192,0},{224,... | collective-permute-start | bytes 196616 | tf_op jit(solution)/shard_map/ppermute | solution.py:323
  57.2 6.2 %collective-permute-start.13 = (bf16[2,128,256]{2,1,0:T(8,128)(2,1)S(1)}, bf16[2,128,256]{2,1,0:T(8,128)(2,1)S(1)}, u32[]{:S(2)}, u32[]{:S(2)}) collective-permute-start(bf16[2,128,256]{2,1,0:T(8,128)(2,1)S(1)} %get-tuple-element.59), channel_id=1, source_target_pairs={{0,32},{32,64},{64,96},{96,128},{128,160},{160,192},{192,224},{224... | collective-permute-start | bytes 393224 | tf_op jit(solution)/shard_map/ppermute | solution.py:323
  59.5 7.1 %collective-permute-start.12 = (bf16[2,128,256]{2,1,0:T(8,128)(2,1)S(1)}, bf16[2,128,256]{2,1,0:T(8,128)(2,1)S(1)}, u32[]{:S(2)}, u32[]{:S(2)}) collective-permute-start(bf16[2,128,256]{2,1,0:T(8,128)(2,1)S(1)} %relay_kernel.2), channel_id=1, source_target_pairs={{0,64},{32,96},{64,128},{96,160},{128,192},{160,224},{192,0},{224,... | collective-permute-start | bytes 393224 | tf_op jit(solution)/shard_map/ppermute | solution.py:323
  66.7 2.6 %collective-permute-start.14 = (f32[128,256]{1,0:T(8,128)S(1)}, f32[128,256]{1,0:T(8,128)S(1)}, u32[]{:S(2)}, u32[]{:S(2)}) collective-permute-start(f32[128,256]{1,0:T(8,128)S(1)} %get-tuple-element.61), channel_id=1, source_target_pairs={{0,16},{16,0},{1,17},{17,1},{2,18},{18,2},{3,19},{19,3},{4,20},{20... | collective-permute-start | bytes 393224 | tf_op jit(solution)/shard_map/ppermute | solution.py:413
  69.9 2.0 %collective-permute-start.15 = (bf16[8,256,128]{2,1,0:T(8,128)(2,1)S(1)}, bf16[8,256,128]{2,1,0:T(8,128)(2,1)S(1)}, u32[]{:S(2)}, u32[]{:S(2)}) collective-permute-start(bf16[8,256,128]{2,1,0:T(8,128)(2,1)S(1)} %get-tuple-element.63), channel_id=1, source_target_pairs={{0,16},{16,0},{1,17},{17,1},{2,18},{18,2},{3,19},{19,3},{4,20},{20... | collective-permute-start | bytes 1572872 | tf_op jit(solution)/shard_map/ppermute | solution.py:426
  72.0 22.0 %all-to-all-start.1 = ((bf16[16,128,256]{2,1,0:T(8,128)(2,1)}), bf16[16,128,256]{2,1,0:T(8,128)(2,1)S(1)}, u32[]{:S(2)}, u32[]{:S(2)}) async-start(bf16[16,128,256]{2,1,0:T(8,128)(2,1)} %get-tuple-element.72), calls=%async_computation.1 | async-start | bytes 2097152 | tf_op jit(solution)/shard_map/all_to_all | solution.py:442
  75.6 8.7 %collective-permute-start.16 = (bf16[2,256,128]{2,1,0:T(8,128)(2,1)S(1)}, bf16[2,256,128]{2,1,0:T(8,128)(2,1)S(1)}, u32[]{:S(2)}, u32[]{:S(2)}) collective-permute-start(bf16[2,256,128]{2,1,0:T(8,128)(2,1)S(1)} %get-tuple-element.67), channel_id=1, source_target_pairs={{0,32},{32,64},{64,96},{96,128},{128,160},{160,192},{192,224},{224... | collective-permute-start | bytes 393224 | tf_op jit(solution)/shard_map/ppermute | solution.py:323
  78.6 5.8 %collective-permute-start.17 = (bf16[256,128]{1,0:T(8,128)(2,1)S(1)}, bf16[256,128]{1,0:T(8,128)(2,1)S(1)}, u32[]{:S(2)}, u32[]{:S(2)}) collective-permute-start(bf16[256,128]{1,0:T(8,128)(2,1)S(1)} %get-tuple-element.68), channel_id=1, source_target_pairs={{0,64},{32,96},{64,128},{96,160},{128,192},{160,224},{192,0},{224,... | collective-permute-start | bytes 196616 | tf_op jit(solution)/shard_map/ppermute | solution.py:323
  83.0 5.6 %collective-permute-start.19 = (bf16[2,256,128]{2,1,0:T(8,128)(2,1)S(1)}, bf16[2,256,128]{2,1,0:T(8,128)(2,1)S(1)}, u32[]{:S(2)}, u32[]{:S(2)}) collective-permute-start(bf16[2,256,128]{2,1,0:T(8,128)(2,1)S(1)} %get-tuple-element.69), channel_id=1, source_target_pairs={{0,32},{32,64},{64,96},{96,128},{128,160},{160,192},{192,224},{224... | collective-permute-start | bytes 393224 | tf_op jit(solution)/shard_map/ppermute | solution.py:323
  84.4 6.5 %collective-permute-start.18 = (bf16[2,256,128]{2,1,0:T(8,128)(2,1)S(1)}, bf16[2,256,128]{2,1,0:T(8,128)(2,1)S(1)}, u32[]{:S(2)}, u32[]{:S(2)}) collective-permute-start(bf16[2,256,128]{2,1,0:T(8,128)(2,1)S(1)} %relay_kernel.3), channel_id=1, source_target_pairs={{0,64},{32,96},{64,128},{96,160},{128,192},{160,224},{192,0},{224,... | collective-permute-start | bytes 393224 | tf_op jit(solution)/shard_map/ppermute | solution.py:323
  91.0 4.0 %collective-permute-start.20 = (f32[256,128]{1,0:T(8,128)S(1)}, f32[256,128]{1,0:T(8,128)S(1)}, u32[]{:S(2)}, u32[]{:S(2)}) collective-permute-start(f32[256,128]{1,0:T(8,128)S(1)} %get-tuple-element.71), channel_id=1, source_target_pairs={{0,16},{16,0},{1,17},{17,1},{2,18},{18,2},{3,19},{19,3},{4,20},{20... | collective-permute-start | bytes 393224 | tf_op jit(solution)/shard_map/ppermute | solution.py:413

commit v17 on v16

--- a/solution.py
+++ b/solution.py
@@ -194,23 +194,23 @@
     mine_ref[...] = summed([adj_ref[owner] for owner in found], flag_ref, blocks, found)
 
 
-def activation_kernel(inv_ref, mine_ref, came_ref, z_ref, og_ref, out_ref, both_ref):
+def activation_kernel(inv_ref, mine_ref, came_ref, z_ref, og_ref, out_ref, gt_ref, scaled_ref):
     inverse = inv_ref[...]
     z = z_ref[...] + inverse * (mine_ref[...] + came_ref[...])
     sig = 1.0 / (1.0 + jnp.exp(-z))
     grad = (og_ref[...].astype(F32) * sig * (1.0 + z * (1.0 - sig))).astype(BF16).astype(F32)
-    both_ref[0:T, :] = grad.T.astype(BF16)
-    both_ref[T:, :] = halves((grad * inverse).T)
+    scaled_ref[...] = halves((grad * inverse).T)
+    gt_ref[...] = grad.T.astype(BF16)
     out_ref[...] = (z * sig).astype(BF16)
 
 
 def transpose_kernel(
-    flag_ref, flag_pair_ref, adj_ref, adj_pair_ref, adj_back_ref, both_ref, both_pair_ref,
+    flag_ref, flag_pair_ref, adj_ref, adj_pair_ref, adj_back_ref, scaled_ref, scaled_pair_ref,
     far_ref, three_ref, one_ref, two_ref, own_ref,
 ):
     found = owners(lax.axis_index("z"), lax.axis_index("c"), flag_ref.shape[0] // 2)
     adj_pair = [adj_pair_ref[len(found) - 2]] + [adj_back_ref[slot] for slot in range(len(found) - 1)]
-    left = jnp.concatenate([both_ref[T:, :], both_pair_ref[T:, :]], axis=1)
+    left = jnp.concatenate([scaled_ref[...], scaled_pair_ref[...]], axis=1)
 
     def block(slot):
         parts = []
@@ -228,13 +228,13 @@
     own_ref[...] = block(7)
 
 
-def weight_grad_kernel(mine_ref, came_ref, both_ref, x_ref, bt_ref, keep_ref, send_ref):
+def weight_grad_kernel(mine_ref, came_ref, gt_ref, x_ref, bt_ref, keep_ref, send_ref):
     core = lax.axis_index("c")
     here = lax.axis_index("z")
     chips = keep_ref.shape[0]
     split = halves(mine_ref[...] + came_ref[...])
     bt_ref[...] = split[0:T]
-    left = jnp.concatenate([both_ref[0:T, :], split], axis=0)
+    left = jnp.concatenate([gt_ref[...], split], axis=0)
     slots = zip(owners(here, core, chips), owners(here, 1 - core, chips))
     for slot, (ours, theirs) in enumerate(slots):
         total = dot(left, jnp.concatenate([x_ref[ours], x_ref[theirs]], axis=1))
@@ -245,8 +245,8 @@
         send_ref[slot, T:] = (sent[T : 2 * T] + sent[2 * T :]).astype(BF16)
 
 
-def feature_grad_kernel(both_ref, bt_ref, ws_ref, wn_ref, pay_ref, buf, sems):
-    right = jnp.concatenate([both_ref[0:T, :], bt_ref[...]], axis=0)
+def feature_grad_kernel(gt_ref, bt_ref, ws_ref, wn_ref, pay_ref, buf, sems):
+    right = jnp.concatenate([gt_ref[...], bt_ref[...]], axis=0)
     copies = []
     for part in range(pay_ref.shape[0]):
         span = slice(part * T, (part + 1) * T)
@@ -393,10 +393,10 @@
     )
     came = lax.ppermute(theirs, "c", swap)
     (z_self,) = call(self_kernel, (x_all, w_self), [((rows, T), F32)])
-    output, both = call(
+    output, gt, scaled = call(
         activation_kernel,
         (inverse, mine, came, z_self, out_grad),
-        [((rows, T), BF16), ((3 * T, rows), BF16)],
+        [((rows, T), BF16), ((T, rows), BF16), ((2 * T, rows), BF16)],
     )
 
     def sends(block):
@@ -414,19 +414,19 @@
 
     parts_sent = call(
         transpose_kernel,
-        (flags, flags_pair, adj, adj_pair, adj_back, both, lax.ppermute(both, "c", swap)),
+        (flags, flags_pair, adj, adj_pair, adj_back, scaled, lax.ppermute(scaled, "c", swap)),
         sends((T, rows)),
     )
     mine, came = reduce(*parts_sent)
     bt, keep, send = call(
         weight_grad_kernel,
-        (mine, came, both, x_all),
+        (mine, came, gt, x_all),
         [((T, rows), BF16), ((chips, 2 * T, T), F32), ((chips, 2 * T, T), BF16)],
     )
     came = lax.ppermute(send, "c", swap)
     (p_pay,) = call(
         feature_grad_kernel,
-        (both, bt, w_self, w_neigh),
+        (gt, bt, w_self, w_neigh),
         [((parts, T, rows), BF16)],
         out_specs=[HBM],
         scratch=[pltpu.VMEM((parts, T, rows), BF16), pltpu.SemaphoreType.DMA((parts,))],

time: 96 us -> 95.9 us (level)
  no operation moved by 1% of the time
where the time goes in v17:
time: 95.9 us; the launch traced here: 95.6 us
  starting transfers between devices  56.8 us (59%)
  waiting for transfers between devices  24.7 us (26%)
  Pallas kernels  12.7 us (13%)
  between operations  1.43 us (1%)
    ppermute x12, starting transfers between devices, along(): return lax.ppermute(value, ('z', 'c'), pairs)  32.3 us
    pallas_call x19, Pallas kernels, call(): pl.pallas_call(kernel, out_shape=shapes, in_specs=in_specs or [VMEM] * le...  12.7 us
    ppermute x12, waiting for transfers between devices, along(): return lax.ppermute(value, ('z', 'c'), pairs)  11.1 us
    all_to_all x1, waiting for transfers between devices, per_device(): x_all = lax.all_to_all(x_pay, 'f', 0, 0, tiled=True)  8.52 us
    all_to_all x1, starting transfers between devices, per_device(): x_all = lax.all_to_all(x_pay, 'f', 0, 0, tiled=True)  7.6 us
    ppermute x2, starting transfers between devices, reduce(): return (mine, lax.ppermute(theirs, 'c', swap))  4.65 us
    all_to_all x1, starting transfers between devices, per_device(): p_all = lax.all_to_all(p_pay, 'f', 0, 0, tiled=True)  3.66 us
    ppermute x1, starting transfers between devices, per_device(): lax.ppermute(y, 'c', swap)  2.7 us
  transfers between devices with their start and end apart: 23, of which 15 were waited for; matrix products, arithmetic and copies ran while one was open for 0% of the time, Pallas kernels for 8%

profile of v17, /device:TPU:1, one launch (start us, length us, event | category | flops | bytes accessed | tf_op | source)
XLA Modules:
  0.0 95.6 jit_solution(11331878787246654840)
XLA Ops:
  0.6 2.0 %spread_kernel.1 = bf16[16,256,128]{2,1,0:T(8,128)(2,1)} custom-call(bf16[256,128]{1,0:T(8,128)(2,1)} %x_hbm.1), custom_call_target="tpu_custom_call" | custom-call | tf_op jit(solution)/shard_map/spread_kernel/pallas_call | solution.py:308
  2.7 7.6 %all-to-all-start = ((bf16[16,256,128]{2,1,0:T(8,128)(2,1)}), bf16[16,256,128]{2,1,0:T(8,128)(2,1)S(1)}, u32[]{:S(2)}, u32[]{:S(2)}) async-start(bf16[16,256,128]{2,1,0:T(8,128)(2,1)} %spread_kernel.1), calls=%async_computation | async-start | bytes 2097152 | tf_op jit(solution)/shard_map/all_to_all | solution.py:340
  10.9 3.0 %adjacency_kernel.1 = (bf16[16,256,128]{2,1,0:T(8,128)(2,1)S(1)}, bf16[7,256,128]{2,1,0:T(8,128)(2,1)}, bf16[7,256,128]{2,1,0:T(8,128)(2,1)}, f32[256,128]{1,0:T(8,128)S(1)}, f32[16,128]{1,0:T(8,128)S(1)}) custom-call(s32[1]{0:T(128)S(6)} %copy.22.count_ref, s32[1,80]{1,0:T(1,128)} %dst_hbm.1, s32[1,80]{1,0:T(1,128)} %src_hbm.1, s32[80,128,128]{2,1,0:T(8,128)} %bitcast.1), custom_call_target="tpu_custom_call" | custom-call | tf_op jit(solution)/shard_map/adjacency_kernel/pallas_call | solution.py:308
  14.0 1.9 %collective-permute-start.1 = (bf16[7,256,128]{2,1,0:T(8,128)(2,1)}, bf16[7,256,128]{2,1,0:T(8,128)(2,1)}, u32[]{:S(2)}, u32[]{:S(2)}) collective-permute-start(bf16[7,256,128]{2,1,0:T(8,128)(2,1)} %get-tuple-element.43), channel_id=1, source_target_pairs={{0,16},{16,0},{1,17},{17,1},{2,18},{18,2},{3,19},{19,3},{4,20},{20... | collective-permute-start | bytes 1376264 | tf_op jit(solution)/shard_map/ppermute | solution.py:367
  16.5 1.0 collective-permute-done.pair_flag_ref
  17.7 8.5 %all-to-all-done.x_ref = bf16[16,256,128]{2,1,0:T(8,128)(2,1)S(1)} async-done(((bf16[16,256,128]{2,1,0:T(8,128)(2,1)}), bf16[16,256,128]{2,1,0:T(8,128)(2,1)S(1)}, u32[]{:S(2)}, u32[]{:S(2)}) %all-to-all-start) | async-done | bytes 1048608 | tf_op jit(solution)/shard_map/all_to_all | solution.py:340
  26.7 2.7 %collective-permute-start.2 = (bf16[256,128]{1,0:T(8,128)(2,1)S(1)}, bf16[256,128]{1,0:T(8,128)(2,1)S(1)}, u32[]{:S(2)}, u32[]{:S(2)}) collective-permute-start(bf16[256,128]{1,0:T(8,128)(2,1)S(1)} %get-tuple-element.46.y_ref), channel_id=1, source_target_pairs={{0,16},{16,0},{1,17},{17,1},{2,18},{18,2},{3,19},{19,3},{4,20},{20... | collective-permute-start | bytes 196616 | tf_op jit(solution)/shard_map/ppermute | solution.py:376
  29.4 0.9 collective-permute-done.2.y_pair_ref
  30.3 6.1 %collective-permute-start.5 = (bf16[2,256,128]{2,1,0:T(8,128)(2,1)S(1)}, bf16[2,256,128]{2,1,0:T(8,128)(2,1)S(1)}, u32[]{:S(2)}, u32[]{:S(2)}) collective-permute-start(bf16[2,256,128]{2,1,0:T(8,128)(2,1)S(1)} %join_kernel.1.pair_ref), channel_id=1, source_target_pairs={{0,64},{32,96},{64,128},{96,160},{128,192},{160,224},{192,0},{224,... | collective-permute-start | bytes 393224 | tf_op jit(solution)/shard_map/ppermute | solution.py:323
  37.1 2.6 %collective-permute-done.5.pair_ref.two_ref = bf16[2,256,128]{2,1,0:T(8,128)(2,1)S(1)} collective-permute-done((bf16[2,256,128]{2,1,0:T(8,128)(2,1)S(1)}, bf16[2,256,128]{2,1,0:T(8,128)(2,1)S(1)}, u32[]{:S(2)}, u32[]{:S(2)}) %collective-permute-start.5) | collective-permute-done | bytes 131104 | tf_op jit(solution)/shard_map/ppermute | solution.py:323
  39.7 2.3 %collective-permute-start.6 = (bf16[2,256,128]{2,1,0:T(8,128)(2,1)S(1)}, bf16[2,256,128]{2,1,0:T(8,128)(2,1)S(1)}, u32[]{:S(2)}, u32[]{:S(2)}) collective-permute-start(bf16[2,256,128]{2,1,0:T(8,128)(2,1)S(1)} %collective-permute-done.5.pair_ref.two_ref), channel_id=1, source_target_pairs={{0,32},{32,64},{64,96},{96,128},{128,160},{160,192},{192,224},{224... | collective-permute-start | bytes 393224 | tf_op jit(solution)/shard_map/ppermute | solution.py:323
  42.0 1.8 %collective-permute-start.7 = (bf16[256,128]{1,0:T(8,128)(2,1)S(1)}, bf16[256,128]{1,0:T(8,128)(2,1)S(1)}, u32[]{:S(2)}, u32[]{:S(2)}) collective-permute-start(bf16[256,128]{1,0:T(8,128)(2,1)S(1)} %half_kernel.1), channel_id=1, source_target_pairs={{0,64},{32,96},{64,128},{96,160},{128,192},{160,224},{192,0},{224,... | collective-permute-start | bytes 196616 | tf_op jit(solution)/shard_map/ppermute | solution.py:323
  43.8 1.2 %fetch_kernel.1 = (bf16[2,256,128]{2,1,0:T(8,128)(2,1)S(1)}, bf16[7,256,128]{2,1,0:T(8,128)(2,1)S(1)}, bf16[7,256,128]{2,1,0:T(8,128)(2,1)S(1)}) custom-call(bf16[2,256,128]{2,1,0:T(8,128)(2,1)S(1)} %collective-permute-done.3.one_ref, bf16[7,256,128]{2,1,0:T(8,128)(2,1)} %get-tuple-element.47.pair_hbm, ...), custom_call_target="tpu_custom_call", output_to_operand_aliasing={{0}: (0, {})} | custom-call | tf_op jit(solution)/shard_map/fetch_kernel/pallas_call | solution.py:308
  45.0 1.4 %collective-permute-done.7.far_ref = bf16[256,128]{1,0:T(8,128)(2,1)S(1)} collective-permute-done((bf16[256,128]{1,0:T(8,128)(2,1)S(1)}, bf16[256,128]{1,0:T(8,128)(2,1)S(1)}, u32[]{:S(2)}, u32[]{:S(2)}) %collective-permute-start.7) | collective-permute-done | bytes 65568 | tf_op jit(solution)/shard_map/ppermute | solution.py:323
  46.9 2.7 %collective-permute-start.8 = (f32[256,128]{1,0:T(8,128)S(1)}, f32[256,128]{1,0:T(8,128)S(1)}, u32[]{:S(2)}, u32[]{:S(2)}) collective-permute-start(f32[256,128]{1,0:T(8,128)S(1)} %get-tuple-element.52), channel_id=1, source_target_pairs={{0,16},{16,0},{1,17},{17,1},{2,18},{18,2},{3,19},{19,3},{4,20},{20... | collective-permute-start | bytes 393224 | tf_op jit(solution)/shard_map/ppermute | solution.py:394
  51.6 1.0 %collective-permute-done.9.scaled_pair_ref = bf16[256,256]{1,0:T(8,128)(2,1)S(1)} collective-permute-done((bf16[256,256]{1,0:T(8,128)(2,1)S(1)}, bf16[256,256]{1,0:T(8,128)(2,1)S(1)}, u32[]{:S(2)}, u32[]{:S(2)}) %collective-permute-start.9) | collective-permute-done | bytes 131104 | tf_op jit(solution)/shard_map/ppermute | solution.py:417
  53.3 1.0 %collective-permute-start.10 = (bf16[2,128,256]{2,1,0:T(8,128)(2,1)S(1)}, bf16[2,128,256]{2,1,0:T(8,128)(2,1)S(1)}, u32[]{:S(2)}, u32[]{:S(2)}) collective-permute-start(bf16[2,128,256]{2,1,0:T(8,128)(2,1)S(1)} %get-tuple-element.58), channel_id=1, source_target_pairs={{0,32},{32,64},{64,96},{96,128},{128,160},{160,192},{192,224},{224... | collective-permute-start | bytes 393224 | tf_op jit(solution)/shard_map/ppermute | solution.py:323
  54.4 2.7 %collective-permute-start.11 = (bf16[128,256]{1,0:T(8,128)(2,1)S(1)}, bf16[128,256]{1,0:T(8,128)(2,1)S(1)}, u32[]{:S(2)}, u32[]{:S(2)}) collective-permute-start(bf16[128,256]{1,0:T(8,128)(2,1)S(1)} %get-tuple-element.59), channel_id=1, source_target_pairs={{0,64},{32,96},{64,128},{96,160},{128,192},{160,224},{192,0},{224,... | collective-permute-start | bytes 196616 | tf_op jit(solution)/shard_map/ppermute | solution.py:323
  57.1 1.9 %collective-permute-start.13 = (bf16[2,128,256]{2,1,0:T(8,128)(2,1)S(1)}, bf16[2,128,256]{2,1,0:T(8,128)(2,1)S(1)}, u32[]{:S(2)}, u32[]{:S(2)}) collective-permute-start(bf16[2,128,256]{2,1,0:T(8,128)(2,1)S(1)} %get-tuple-element.60), channel_id=1, source_target_pairs={{0,32},{32,64},{64,96},{96,128},{128,160},{160,192},{192,224},{224... | collective-permute-start | bytes 393224 | tf_op jit(solution)/shard_map/ppermute | solution.py:323
  59.4 3.9 %collective-permute-start.12 = (bf16[2,128,256]{2,1,0:T(8,128)(2,1)S(1)}, bf16[2,128,256]{2,1,0:T(8,128)(2,1)S(1)}, u32[]{:S(2)}, u32[]{:S(2)}) collective-permute-start(bf16[2,128,256]{2,1,0:T(8,128)(2,1)S(1)} %relay_kernel.2), channel_id=1, source_target_pairs={{0,64},{32,96},{64,128},{96,160},{128,192},{160,224},{192,0},{224,... | collective-permute-start | bytes 393224 | tf_op jit(solution)/shard_map/ppermute | solution.py:323
  63.3 3.2 %collective-permute-done.12.two_ref = bf16[2,128,256]{2,1,0:T(8,128)(2,1)S(1)} collective-permute-done((bf16[2,128,256]{2,1,0:T(8,128)(2,1)S(1)}, bf16[2,128,256]{2,1,0:T(8,128)(2,1)S(1)}, u32[]{:S(2)}, u32[]{:S(2)}) %collective-permute-start.12) | collective-permute-done | bytes 131104 | tf_op jit(solution)/shard_map/ppermute | solution.py:323
  66.6 1.6 %collective-permute-start.14 = (f32[128,256]{1,0:T(8,128)S(1)}, f32[128,256]{1,0:T(8,128)S(1)}, u32[]{:S(2)}, u32[]{:S(2)}) collective-permute-start(f32[128,256]{1,0:T(8,128)S(1)} %get-tuple-element.62), channel_id=1, source_target_pairs={{0,16},{16,0},{1,17},{17,1},{2,18},{18,2},{3,19},{19,3},{4,20},{20... | collective-permute-start | bytes 393224 | tf_op jit(solution)/shard_map/ppermute | solution.py:413
  68.2 1.0 %collective-permute-done.14.came_ref = f32[128,256]{1,0:T(8,128)S(1)} collective-permute-done((f32[128,256]{1,0:T(8,128)S(1)}, f32[128,256]{1,0:T(8,128)S(1)}, u32[]{:S(2)}, u32[]{:S(2)}) %collective-permute-start.14) | collective-permute-done | bytes 131104 | tf_op jit(solution)/shard_map/ppermute | solution.py:413
  70.2 1.3 %feature_grad_kernel.1.payload_ref = bf16[16,128,256]{2,1,0:T(8,128)(2,1)} custom-call(bf16[128,256]{1,0:T(8,128)(2,1)S(1)} %get-tuple-element.63.gt_ref, bf16[128,256]{1,0:T(8,128)(2,1)S(1)} %get-tuple-element.66.bt_ref, bf16[2048,128]{1,0:T(8,128)(2,1)S(1)} %copy-done, bf16[2048,128]{1,0:T(8,128)(2,1)S(1)} %copy-done.1), custom_call_target="tpu_custom_call" | custom-call | tf_op jit(solution)/shard_map/feature_grad_kernel/pallas_call | solution.py:308
  71.9 3.7 %all-to-all-start.1 = ((bf16[16,128,256]{2,1,0:T(8,128)(2,1)}), bf16[16,128,256]{2,1,0:T(8,128)(2,1)S(1)}, u32[]{:S(2)}, u32[]{:S(2)}) async-start(bf16[16,128,256]{2,1,0:T(8,128)(2,1)} %get-tuple-element.74), calls=%async_computation.1 | async-start | bytes 2097152 | tf_op jit(solution)/shard_map/all_to_all | solution.py:442
  75.5 2.9 %collective-permute-start.16 = (bf16[2,256,128]{2,1,0:T(8,128)(2,1)S(1)}, bf16[2,256,128]{2,1,0:T(8,128)(2,1)S(1)}, u32[]{:S(2)}, u32[]{:S(2)}) collective-permute-start(bf16[2,256,128]{2,1,0:T(8,128)(2,1)S(1)} %get-tuple-element.69), channel_id=1, source_target_pairs={{0,32},{32,64},{64,96},{96,128},{128,160},{160,192},{192,224},{224... | collective-permute-start | bytes 393224 | tf_op jit(solution)/shard_map/ppermute | solution.py:323
  78.5 4.5 %collective-permute-start.17 = (bf16[256,128]{1,0:T(8,128)(2,1)S(1)}, bf16[256,128]{1,0:T(8,128)(2,1)S(1)}, u32[]{:S(2)}, u32[]{:S(2)}) collective-permute-start(bf16[256,128]{1,0:T(8,128)(2,1)S(1)} %get-tuple-element.70), channel_id=1, source_target_pairs={{0,64},{32,96},{64,128},{96,160},{128,192},{160,224},{192,0},{224,... | collective-permute-start | bytes 196616 | tf_op jit(solution)/shard_map/ppermute | solution.py:323
  83.1 1.2 %collective-permute-done.17.far_ref = bf16[256,128]{1,0:T(8,128)(2,1)S(1)} collective-permute-done((bf16[256,128]{1,0:T(8,128)(2,1)S(1)}, bf16[256,128]{1,0:T(8,128)(2,1)S(1)}, u32[]{:S(2)}, u32[]{:S(2)}) %collective-permute-start.17) | collective-permute-done | bytes 65568 | tf_op jit(solution)/shard_map/ppermute | solution.py:323
  84.3 4.3 %collective-permute-start.18 = (bf16[2,256,128]{2,1,0:T(8,128)(2,1)S(1)}, bf16[2,256,128]{2,1,0:T(8,128)(2,1)S(1)}, u32[]{:S(2)}, u32[]{:S(2)}) collective-permute-start(bf16[2,256,128]{2,1,0:T(8,128)(2,1)S(1)} %relay_kernel.3), channel_id=1, source_target_pairs={{0,64},{32,96},{64,128},{96,160},{128,192},{160,224},{192,0},{224,... | collective-permute-start | bytes 393224 | tf_op jit(solution)/shard_map/ppermute | solution.py:323
  88.6 2.2 %collective-permute-done.18.two_ref = bf16[2,256,128]{2,1,0:T(8,128)(2,1)S(1)} collective-permute-done((bf16[2,256,128]{2,1,0:T(8,128)(2,1)S(1)}, bf16[2,256,128]{2,1,0:T(8,128)(2,1)S(1)}, u32[]{:S(2)}, u32[]{:S(2)}) %collective-permute-start.18) | collective-permute-done | bytes 131104 | tf_op jit(solution)/shard_map/ppermute | solution.py:323
  90.9 3.0 %collective-permute-start.20 = (f32[256,128]{1,0:T(8,128)S(1)}, f32[256,128]{1,0:T(8,128)S(1)}, u32[]{:S(2)}, u32[]{:S(2)}) collective-permute-start(f32[256,128]{1,0:T(8,128)S(1)} %get-tuple-element.73), channel_id=1, source_target_pairs={{0,16},{16,0},{1,17},{17,1},{2,18},{18,2},{3,19},{19,3},{4,20},{20... | collective-permute-start | bytes 393224 | tf_op jit(solution)/shard_map/ppermute | solution.py:413
  93.9 0.8 sum_kernel.1.done_ref
  (39 shorter events, 8.1 us)
Async XLA Ops:
  0.6 25.6 %copy-start.1 = (bf16[2048,128]{1,0:T(8,128)(2,1)S(1)}, bf16[2048,128]{1,0:T(8,128)(2,1)}, u32[]{:S(2)}) copy-start(bf16[2048,128]{1,0:T(8,128)(2,1)} %wn_ref.1) | copy-start | bytes 1572868
  2.7 23.6 %all-to-all-start = ((bf16[16,256,128]{2,1,0:T(8,128)(2,1)}), bf16[16,256,128]{2,1,0:T(8,128)(2,1)S(1)}, u32[]{:S(2)}, u32[]{:S(2)}) async-start(bf16[16,256,128]{2,1,0:T(8,128)(2,1)} %spread_kernel.1), calls=%async_computation | async-start | bytes 2097152 | tf_op jit(solution)/shard_map/all_to_all | solution.py:340
  10.9 38.6 %copy-start = (bf16[2048,128]{1,0:T(8,128)(2,1)S(1)}, bf16[2048,128]{1,0:T(8,128)(2,1)}, u32[]{:S(2)}) copy-start(bf16[2048,128]{1,0:T(8,128)(2,1)} %ws_ref.1) | copy-start | bytes 1572868
  10.9 39.6 %copy-start.2 = (bf16[256,128]{1,0:T(8,128)(2,1)S(1)}, bf16[256,128]{1,0:T(8,128)(2,1)}, u32[]{:S(2)}) copy-start(bf16[256,128]{1,0:T(8,128)(2,1)} %og_ref.1) | copy-start | bytes 196612
  14.0 3.7 %collective-permute-start.1 = (bf16[7,256,128]{2,1,0:T(8,128)(2,1)}, bf16[7,256,128]{2,1,0:T(8,128)(2,1)}, u32[]{:S(2)}, u32[]{:S(2)}) collective-permute-start(bf16[7,256,128]{2,1,0:T(8,128)(2,1)} %get-tuple-element.43), channel_id=1, source_target_pairs={{0,16},{16,0},{1,17},{17,1},{2,18},{18,2},{3,19},{19,3},{4,20},{20... | collective-permute-start | bytes 1376264 | tf_op jit(solution)/shard_map/ppermute | solution.py:367
  15.9 27.9 %collective-permute-start.4 = (bf16[7,256,128]{2,1,0:T(8,128)(2,1)}, bf16[7,256,128]{2,1,0:T(8,128)(2,1)}, u32[]{:S(2)}, u32[]{:S(2)}) collective-permute-start(bf16[7,256,128]{2,1,0:T(8,128)(2,1)} %get-tuple-element.48), channel_id=1, source_target_pairs={{0,16},{16,0},{1,17},{17,1},{2,18},{18,2},{3,19},{19,3},{4,20},{20... | collective-permute-start | bytes 1376264 | tf_op jit(solution)/shard_map/ppermute | solution.py:367
  16.0 1.4 %collective-permute-start = (f32[16,128]{1,0:T(8,128)S(1)}, f32[16,128]{1,0:T(8,128)S(1)}, u32[]{:S(2)}, u32[]{:S(2)}) collective-permute-start(f32[16,128]{1,0:T(8,128)S(1)} %get-tuple-element.42.flag_ref), channel_id=1, source_target_pairs={{0,16},{16,0},{1,17},{17,1},{2,18},{18,2},{3,19},{19,3},{4,20},{20... | collective-permute-start | bytes 24584 | tf_op jit(solution)/shard_map/ppermute | solution.py:370
  26.7 3.6 %collective-permute-start.2 = (bf16[256,128]{1,0:T(8,128)(2,1)S(1)}, bf16[256,128]{1,0:T(8,128)(2,1)S(1)}, u32[]{:S(2)}, u32[]{:S(2)}) collective-permute-start(bf16[256,128]{1,0:T(8,128)(2,1)S(1)} %get-tuple-element.46.y_ref), channel_id=1, source_target_pairs={{0,16},{16,0},{1,17},{17,1},{2,18},{18,2},{3,19},{19,3},{4,20},{20... | collective-permute-start | bytes 196616 | tf_op jit(solution)/shard_map/ppermute | solution.py:376
  30.3 9.4 %collective-permute-start.5 = (bf16[2,256,128]{2,1,0:T(8,128)(2,1)S(1)}, bf16[2,256,128]{2,1,0:T(8,128)(2,1)S(1)}, u32[]{:S(2)}, u32[]{:S(2)}) collective-permute-start(bf16[2,256,128]{2,1,0:T(8,128)(2,1)S(1)} %join_kernel.1.pair_ref), channel_id=1, source_target_pairs={{0,64},{32,96},{64,128},{96,160},{128,192},{160,224},{192,0},{224,... | collective-permute-start | bytes 393224 | tf_op jit(solution)/shard_map/ppermute | solution.py:323
  36.4 7.4 %collective-permute-start.3 = (bf16[2,256,128]{2,1,0:T(8,128)(2,1)S(1)}, bf16[2,256,128]{2,1,0:T(8,128)(2,1)S(1)}, u32[]{:S(2)}, u32[]{:S(2)}) collective-permute-start(bf16[2,256,128]{2,1,0:T(8,128)(2,1)S(1)} %join_kernel.1.pair_ref), channel_id=1, source_target_pairs={{0,32},{32,64},{64,96},{96,128},{128,160},{160,192},{192,224},{224... | collective-permute-start | bytes 393224 | tf_op jit(solution)/shard_map/ppermute | solution.py:323
  39.7 6.7 %collective-permute-start.6 = (bf16[2,256,128]{2,1,0:T(8,128)(2,1)S(1)}, bf16[2,256,128]{2,1,0:T(8,128)(2,1)S(1)}, u32[]{:S(2)}, u32[]{:S(2)}) collective-permute-start(bf16[2,256,128]{2,1,0:T(8,128)(2,1)S(1)} %collective-permute-done.5.pair_ref.two_ref), channel_id=1, source_target_pairs={{0,32},{32,64},{64,96},{96,128},{128,160},{160,192},{192,224},{224... | collective-permute-start | bytes 393224 | tf_op jit(solution)/shard_map/ppermute | solution.py:323
  42.0 4.4 %collective-permute-start.7 = (bf16[256,128]{1,0:T(8,128)(2,1)S(1)}, bf16[256,128]{1,0:T(8,128)(2,1)S(1)}, u32[]{:S(2)}, u32[]{:S(2)}) collective-permute-start(bf16[256,128]{1,0:T(8,128)(2,1)S(1)} %half_kernel.1), channel_id=1, source_target_pairs={{0,64},{32,96},{64,128},{96,160},{128,192},{160,224},{192,0},{224,... | collective-permute-start | bytes 196616 | tf_op jit(solution)/shard_map/ppermute | solution.py:323
  46.9 3.6 %collective-permute-start.8 = (f32[256,128]{1,0:T(8,128)S(1)}, f32[256,128]{1,0:T(8,128)S(1)}, u32[]{:S(2)}, u32[]{:S(2)}) collective-permute-start(f32[256,128]{1,0:T(8,128)S(1)} %get-tuple-element.52), channel_id=1, source_target_pairs={{0,16},{16,0},{1,17},{17,1},{2,18},{18,2},{3,19},{19,3},{4,20},{20... | collective-permute-start | bytes 393224 | tf_op jit(solution)/shard_map/ppermute | solution.py:394
  51.3 1.3 %collective-permute-start.9 = (bf16[256,256]{1,0:T(8,128)(2,1)S(1)}, bf16[256,256]{1,0:T(8,128)(2,1)S(1)}, u32[]{:S(2)}, u32[]{:S(2)}) collective-permute-start(bf16[256,256]{1,0:T(8,128)(2,1)S(1)} %get-tuple-element.55.scaled_ref), channel_id=1, source_target_pairs={{0,16},{16,0},{1,17},{17,1},{2,18},{18,2},{3,19},{19,3},{4,20},{20... | collective-permute-start | bytes 393224 | tf_op jit(solution)/shard_map/ppermute | solution.py:417
  53.3 6.1 %collective-permute-start.10 = (bf16[2,128,256]{2,1,0:T(8,128)(2,1)S(1)}, bf16[2,128,256]{2,1,0:T(8,128)(2,1)S(1)}, u32[]{:S(2)}, u32[]{:S(2)}) collective-permute-start(bf16[2,128,256]{2,1,0:T(8,128)(2,1)S(1)} %get-tuple-element.58), channel_id=1, source_target_pairs={{0,32},{32,64},{64,96},{96,128},{128,160},{160,192},{192,224},{224... | collective-permute-start | bytes 393224 | tf_op jit(solution)/shard_map/ppermute | solution.py:323
  54.4 5.0 %collective-permute-start.11 = (bf16[128,256]{1,0:T(8,128)(2,1)S(1)}, bf16[128,256]{1,0:T(8,128)(2,1)S(1)}, u32[]{:S(2)}, u32[]{:S(2)}) collective-permute-start(bf16[128,256]{1,0:T(8,128)(2,1)S(1)} %get-tuple-element.59), channel_id=1, source_target_pairs={{0,64},{32,96},{64,128},{96,160},{128,192},{160,224},{192,0},{224,... | collective-permute-start | bytes 196616 | tf_op jit(solution)/shard_map/ppermute | solution.py:323
  57.1 6.2 %collective-permute-start.13 = (bf16[2,128,256]{2,1,0:T(8,128)(2,1)S(1)}, bf16[2,128,256]{2,1,0:T(8,128)(2,1)S(1)}, u32[]{:S(2)}, u32[]{:S(2)}) collective-permute-start(bf16[2,128,256]{2,1,0:T(8,128)(2,1)S(1)} %get-tuple-element.60), channel_id=1, source_target_pairs={{0,32},{32,64},{64,96},{96,128},{128,160},{160,192},{192,224},{224... | collective-permute-start | bytes 393224 | tf_op jit(solution)/shard_map/ppermute | solution.py:323
  59.4 7.1 %collective-permute-start.12 = (bf16[2,128,256]{2,1,0:T(8,128)(2,1)S(1)}, bf16[2,128,256]{2,1,0:T(8,128)(2,1)S(1)}, u32[]{:S(2)}, u32[]{:S(2)}) collective-permute-start(bf16[2,128,256]{2,1,0:T(8,128)(2,1)S(1)} %relay_kernel.2), channel_id=1, source_target_pairs={{0,64},{32,96},{64,128},{96,160},{128,192},{160,224},{192,0},{224,... | collective-permute-start | bytes 393224 | tf_op jit(solution)/shard_map/ppermute | solution.py:323
  66.6 2.6 %collective-permute-start.14 = (f32[128,256]{1,0:T(8,128)S(1)}, f32[128,256]{1,0:T(8,128)S(1)}, u32[]{:S(2)}, u32[]{:S(2)}) collective-permute-start(f32[128,256]{1,0:T(8,128)S(1)} %get-tuple-element.62), channel_id=1, source_target_pairs={{0,16},{16,0},{1,17},{17,1},{2,18},{18,2},{3,19},{19,3},{4,20},{20... | collective-permute-start | bytes 393224 | tf_op jit(solution)/shard_map/ppermute | solution.py:413
  69.8 2.0 %collective-permute-start.15 = (bf16[8,256,128]{2,1,0:T(8,128)(2,1)S(1)}, bf16[8,256,128]{2,1,0:T(8,128)(2,1)S(1)}, u32[]{:S(2)}, u32[]{:S(2)}) collective-permute-start(bf16[8,256,128]{2,1,0:T(8,128)(2,1)S(1)} %get-tuple-element.65), channel_id=1, source_target_pairs={{0,16},{16,0},{1,17},{17,1},{2,18},{18,2},{3,19},{19,3},{4,20},{20... | collective-permute-start | bytes 1572872 | tf_op jit(solution)/shard_map/ppermute | solution.py:426
  71.9 22.0 %all-to-all-start.1 = ((bf16[16,128,256]{2,1,0:T(8,128)(2,1)}), bf16[16,128,256]{2,1,0:T(8,128)(2,1)S(1)}, u32[]{:S(2)}, u32[]{:S(2)}) async-start(bf16[16,128,256]{2,1,0:T(8,128)(2,1)} %get-tuple-element.74), calls=%async_computation.1 | async-start | bytes 2097152 | tf_op jit(solution)/shard_map/all_to_all | solution.py:442
  75.5 8.8 %collective-permute-start.16 = (bf16[2,256,128]{2,1,0:T(8,128)(2,1)S(1)}, bf16[2,256,128]{2,1,0:T(8,128)(2,1)S(1)}, u32[]{:S(2)}, u32[]{:S(2)}) collective-permute-start(bf16[2,256,128]{2,1,0:T(8,128)(2,1)S(1)} %get-tuple-element.69), channel_id=1, source_target_pairs={{0,32},{32,64},{64,96},{96,128},{128,160},{160,192},{192,224},{224... | collective-permute-start | bytes 393224 | tf_op jit(solution)/shard_map/ppermute | solution.py:323
  78.5 5.8 %collective-permute-start.17 = (bf16[256,128]{1,0:T(8,128)(2,1)S(1)}, bf16[256,128]{1,0:T(8,128)(2,1)S(1)}, u32[]{:S(2)}, u32[]{:S(2)}) collective-permute-start(bf16[256,128]{1,0:T(8,128)(2,1)S(1)} %get-tuple-element.70), channel_id=1, source_target_pairs={{0,64},{32,96},{64,128},{96,160},{128,192},{160,224},{192,0},{224,... | collective-permute-start | bytes 196616 | tf_op jit(solution)/shard_map/ppermute | solution.py:323
  83.0 5.6 %collective-permute-start.19 = (bf16[2,256,128]{2,1,0:T(8,128)(2,1)S(1)}, bf16[2,256,128]{2,1,0:T(8,128)(2,1)S(1)}, u32[]{:S(2)}, u32[]{:S(2)}) collective-permute-start(bf16[2,256,128]{2,1,0:T(8,128)(2,1)S(1)} %get-tuple-element.71), channel_id=1, source_target_pairs={{0,32},{32,64},{64,96},{96,128},{128,160},{160,192},{192,224},{224... | collective-permute-start | bytes 393224 | tf_op jit(solution)/shard_map/ppermute | solution.py:323
  84.3 6.5 %collective-permute-start.18 = (bf16[2,256,128]{2,1,0:T(8,128)(2,1)S(1)}, bf16[2,256,128]{2,1,0:T(8,128)(2,1)S(1)}, u32[]{:S(2)}, u32[]{:S(2)}) collective-permute-start(bf16[2,256,128]{2,1,0:T(8,128)(2,1)S(1)} %relay_kernel.3), channel_id=1, source_target_pairs={{0,64},{32,96},{64,128},{96,160},{128,192},{160,224},{192,0},{224,... | collective-permute-start | bytes 393224 | tf_op jit(solution)/shard_map/ppermute | solution.py:323
  90.9 4.0 %collective-permute-start.20 = (f32[256,128]{1,0:T(8,128)S(1)}, f32[256,128]{1,0:T(8,128)S(1)}, u32[]{:S(2)}, u32[]{:S(2)}) collective-permute-start(f32[256,128]{1,0:T(8,128)S(1)} %get-tuple-element.73), channel_id=1, source_target_pairs={{0,16},{16,0},{1,17},{17,1},{2,18},{18,2},{3,19},{19,3},{4,20},{20... | collective-permute-start | bytes 393224 | tf_op jit(solution)/shard_map/ppermute | solution.py:413
